TPU v7x, 32 devices: a whole 2x2x4 slice. The times are simulated.
32 devices in a mesh: factor: 4 (over y, core), load: 8 (over z, x).
Axes of the slice: x: 2, y: 2, z: 4, core: 2. Of those that a mesh axis runs over, the one named last changes fastest.
Arguments:
- b_panel: bfloat16 [2048, 2048], P('factor', 'load'), may hold values from -6 to 6
- b_update: bfloat16 [8192, 2048], P('factor', 'load'), may hold values from -6 to 6
- panel_inverse: bfloat16 [2048, 2048], P('factor'), as said below
- update_factor: bfloat16 [8192, 2048], P('factor'), may hold values from -0.125 to 0.125
- update_solution: bfloat16 [8192, 2048], P(('factor', 'load')), may hold values from -3 to 3
- axle_weights: bfloat16 [3072, 2048], P('load'), may hold values from -0.125 to 0.125
Outputs:
- update_rhs: bfloat16 [8192, 2048], P('factor', 'load')
- panel_solution: bfloat16 [2048, 2048], P('factor', 'load')
- config_response: float32 [3072, 2048], P('load', 'factor')
Inputs may be any that keep to these rules, and one draw needn't show every extreme that they name: panel_inverse is zero above the diagonal and its diagonal lies between 1 and 2.
All inputs are finite; a program needn't handle non-finite values.
Results may differ from a plain program's by a relative error of at most 0.0052.
Values may be sent and summed in bfloat16 or wider, within the bound.
No kernel may reach another device: no remote copies, remote signals or barrier semaphores. Data moves between devices by JAX's collectives and lax.ppermute only.
A program may use at most 64 MiB of HBM per device.

v0:
```python
import functools

import jax
import jax.numpy as jnp
from jax import lax
from jax.experimental import pallas as pl
from jax.experimental.pallas import tpu as pltpu
from jax.sharding import PartitionSpec as P

BF16 = jnp.bfloat16
F32 = jnp.float32


VMEM = pl.BlockSpec(memory_space=pltpu.VMEM)
SMEM = pl.BlockSpec(memory_space=pltpu.SMEM)


def call(kernel, at, operands, outs, flops):
    shapes = [jax.ShapeDtypeStruct(shape, kind) for shape, kind in outs]
    moved = sum(v.size * v.dtype.itemsize for v in list(operands) + shapes)
    return pl.pallas_call(
        kernel,
        out_shape=shapes,
        in_specs=[SMEM] + [VMEM] * len(operands),
        out_specs=[VMEM] * len(shapes),
        compiler_params=pltpu.CompilerParams(vmem_limit_bytes=16 * 2**20),
        cost_estimate=pl.CostEstimate(flops=flops, bytes_accessed=moved, transcendentals=0),
    )(at, *operands)


def part(index, size):
    return pl.ds(pl.multiple_of(index * size, size), size)


def dot(a, b):
    return jnp.dot(a, b, preferred_element_type=F32)


def forward_kernel(at_ref, inverse_ref, *refs):
    blocks, out_ref = refs[:-1], refs[-1]
    rows = out_ref.shape[0]
    total = None
    for j, block in enumerate(blocks):
        term = dot(inverse_ref[:, part(at_ref[j], rows)], block[...])
        total = term if total is None else total + term
    out_ref[...] = total.astype(out_ref.dtype)


def update_kernel(at_ref, factor_ref, rhs_ref, *refs):
    blocks, (out_ref, turned_ref) = refs[:-2], refs[-2:]
    rows = blocks[0].shape[0]
    turned_ref[0] = blocks[0][...].T
    turned_ref[1] = blocks[2][...].T

    @pl.loop(0, out_ref.shape[0] // rows)
    def _(i):
        here = part(i, rows)
        total = rhs_ref[here, :].astype(F32)
        for j, block in enumerate(blocks):
            total = total - dot(factor_ref[here, part(at_ref[j], rows)], block[...])
        out_ref[here, :] = total.astype(out_ref.dtype)


def split_kernel(at_ref, solved_ref, *outs):
    cols = outs[0].shape[0]
    for j, out_ref in enumerate(outs):
        out_ref[...] = solved_ref[:, part(at_ref[j], cols)].T


def hold_kernel(factor_ref, out_ref, sem):
    copy = pltpu.make_async_copy(factor_ref, out_ref, sem)
    copy.start()
    copy.wait()


def coupled_kernel(panel_blocks, row_blocks, first, at_ref, factor_ref, *refs):
    pieces, out_ref = refs[-1 - len(row_blocks) : -1], refs[-1]
    depth, width = pieces[0].shape[1], out_ref.shape[2]
    for j, b in enumerate(panel_blocks):
        cols = part(at_ref[b], width)
        total = None if first is None else refs[0][first[j]]
        for k, piece in zip(row_blocks, pieces):
            term = dot(piece[...], factor_ref[part(at_ref[k], depth), cols])
            total = term if total is None else total + term
        out_ref[j] = total.astype(out_ref.dtype)


def reduce_kernel(at_ref, turned_ref, kept_ref, core_ref, across_ref, own_ref, other_ref, reduced_ref, send_ref):
    rows = send_ref.shape[1]
    for j in range(2):
        coupled = kept_ref[j] + core_ref[j].astype(F32) + across_ref[1 - j].astype(F32)
        reduced_ref[j] = (turned_ref[j].astype(F32) - coupled).astype(reduced_ref.dtype)
    solved = dot(reduced_ref[0], own_ref[:, part(at_ref[0], rows)]) + dot(
        reduced_ref[1], other_ref[:, part(at_ref[1], rows)]
    )
    send_ref[...] = solved.astype(send_ref.dtype)


def solve_kernel(at_ref, reduced_ref, own_ref, other_ref, keep_ref):
    rows = keep_ref.shape[1]
    keep_ref[...] = dot(reduced_ref[0], own_ref[:, part(at_ref[0], rows)]) + dot(
        reduced_ref[1], other_ref[:, part(at_ref[1], rows)]
    )


def config_near_kernel(at_ref, axle_ref, *refs):
    shards, out_ref = refs[:-1], refs[-1]
    cols = shards[0].shape[0]
    total = None
    for j, shard in enumerate(shards):
        term = dot(axle_ref[:, part(at_ref[j], cols)], shard[...])
        total = term if total is None else total + term
    out_ref[...] = total


def config_far_kernel(at_ref, axle_ref, near_ref, c_ref, cx_ref, b_ref, bx_ref, e_ref, ex_ref, out_ref):
    cols = c_ref.shape[0]
    middle = at_ref[8] == 1
    total = near_ref[...]
    shards = [
        c_ref[...],
        cx_ref[...],
        jnp.where(middle, b_ref[...], e_ref[...]),
        jnp.where(middle, bx_ref[...], ex_ref[...]),
    ]
    for j, shard in enumerate(shards):
        total = total + dot(axle_ref[:, part(at_ref[4 + j], cols)], shard)
    out_ref[...] = total


def by_xor(value, axis, size, bits):
    return lax.ppermute(value, axis, [(i, i ^ bits) for i in range(size)])


def small_slice(b_panel, b_update, panel_inverse, update_factor, update_solution, axle_weights):
    factors, loads = 4, 8
    rows = panel_inverse.shape[0]
    updates, panel = update_factor.shape
    cols = b_panel.shape[1]
    f, at_load = lax.axis_index("factor"), lax.axis_index("load")
    core = f & 1
    at_factor = f ^ jnp.arange(factors, dtype=jnp.int32)

    spread = at_load ^ jnp.arange(loads, dtype=jnp.int32)

    depth = update_solution.shape[0]
    pieces = call(split_kernel, spread, [update_solution], [((cols, depth), BF16)] * loads, 0)
    near = [pieces[0]] + [by_xor(pieces[k], "load", loads, k) for k in (1, 2, 3)]
    far = [by_xor(pieces[k], "load", loads, k) for k in (4, 5, 6, 7)]
    held = pl.pallas_call(
        hold_kernel,
        out_shape=jax.ShapeDtypeStruct((updates, panel), BF16),
        in_specs=[pl.BlockSpec(memory_space=pltpu.MemorySpace.HBM)],
        out_specs=VMEM,
        scratch_shapes=[pltpu.SemaphoreType.DMA],
        compiler_params=pltpu.CompilerParams(vmem_limit_bytes=16 * 2**20),
        cost_estimate=pl.CostEstimate(flops=0, bytes_accessed=2 * updates * panel, transcendentals=0),
    )(update_factor)

    up, down = [(0, 2), (1, 3)], [(2, 0), (3, 1)]
    b_core = by_xor(b_panel, "factor", factors, 1)
    b_across = lax.ppermute(b_panel, "factor", up)
    b_far = lax.ppermute(b_across, "factor", [(2, 3), (3, 2)])
    inverse_other = lax.ppermute(panel_inverse[:, : 2 * rows], "factor", down)
    (forward,) = call(
        forward_kernel,
        at_factor,
        [panel_inverse, b_panel, b_core, b_across, b_far],
        [((rows, cols), BF16)],
        2 * rows * panel * cols,
    )
    forward_core = by_xor(forward, "factor", factors, 1)
    forward_across = by_xor(forward, "factor", factors, 2)
    forward_far = by_xor(forward_across, "factor", factors, 1)
    far[3], inverse_other, forward_core, forward_across, forward_far = lax.optimization_barrier(
        (far[3], inverse_other, forward_core, forward_across, forward_far)
    )
    update_rhs, forward_t = call(
        update_kernel,
        at_factor,
        [held, b_update, forward, forward_core, forward_across, forward_far],
        [((updates, cols), BF16), ((2, cols, rows), BF16)],
        2 * updates * panel * cols,
    )

    pair = (2, cols, rows)
    at_coupled = jnp.concatenate([at_factor, spread])

    def coupled(panel_blocks, row_blocks, first, before, blocks, kind):
        shape = (len(panel_blocks), cols, rows)
        (out,) = call(
            functools.partial(coupled_kernel, panel_blocks, row_blocks, first),
            at_coupled,
            [held] + before + blocks,
            [(shape, kind)],
            2 * cols * rows * depth * len(panel_blocks) * len(row_blocks),
        )
        return out

    begun = coupled((1, 3, 0, 2), (4, 5, 6, 7), None, [], near, F32)
    send = coupled((1, 3), (8, 9, 10, 11), (0, 1), [begun], far, BF16)
    from_core = by_xor(send, "factor", factors, 1)
    kept = coupled((0, 2), (8, 9, 10, 11), (2, 3), [begun], far, F32)
    send = (kept + from_core.astype(F32)).astype(BF16)
    from_across = by_xor(send, "factor", factors, 2)

    work = 4 * cols * rows * rows
    reduced, send = call(
        reduce_kernel,
        jnp.stack([f ^ 1, core ^ 1]),
        [forward_t, kept, from_core, from_across, panel_inverse, inverse_other],
        [(pair, BF16), ((cols, rows), BF16)],
        work,
    )
    from_core = by_xor(send, "factor", factors, 1)
    (keep,) = call(
        solve_kernel,
        jnp.stack([f, core]),
        [reduced, panel_inverse, inverse_other],
        [((cols, rows), F32)],
        work,
    )
    solution_t = (keep + from_core.astype(F32)).astype(BF16)
    panel_solution = solution_t.T

    middle, ends = (2, 3, 4, 5), (0, 1, 6, 7)

    def hop(value, places, bits):
        return lax.ppermute(value, "load", [(i, i ^ bits) for i in places])

    everyone = middle + ends
    own = solution_t
    a = hop(own, everyone, 2)
    b = hop(own, middle, 6)
    own_x = hop(own, everyone, 1)
    c = hop(a, middle, 6)
    a_x = hop(a, everyone, 1)
    d = hop(b, middle, 2)
    b_x = hop(b, middle, 1)
    e = hop(c, middle, 2)
    in_middle = (at_load >= 2) & (at_load < 6)
    c = jnp.where(in_middle, c, d)
    c_x = hop(c, everyone, 1)
    e_x = hop(e, ends, 1)

    axle_at = jnp.concatenate([spread, in_middle.astype(jnp.int32)[None]])
    response = [((axle_weights.shape[0], rows), F32)]
    work = axle_weights.size * rows
    (begun,) = call(config_near_kernel, axle_at, [axle_weights, own, own_x, a, a_x], response, work)
    (config_response,) = call(
        config_far_kernel, axle_at, [axle_weights, begun, c, c_x, b, b_x, e, e_x], response, work
    )
    return (update_rhs, panel_solution, config_response)


def any_slice(b_panel, b_update, panel_inverse, update_factor, update_solution, axle_weights):
    b_all = lax.all_gather(b_panel, "factor", axis=0, tiled=True)
    forward = jnp.dot(panel_inverse, b_all, preferred_element_type=F32).astype(BF16)
    forward_all = lax.all_gather(forward, "factor", axis=0, tiled=True)
    lowered = jnp.dot(update_factor, forward_all, preferred_element_type=F32)
    update_rhs = (b_update.astype(F32) - lowered).astype(BF16)
    regrouped = lax.all_to_all(update_solution, "load", split_axis=1, concat_axis=0, tiled=True)
    over_rows = (((0,), (0,)), ((), ()))
    coupled = lax.psum_scatter(
        lax.dot_general(update_factor, regrouped, over_rows, preferred_element_type=F32),
        "factor",
        scatter_dimension=0,
        tiled=True,
    )
    reduced = (forward.astype(F32) - coupled).astype(BF16)
    panel_solution = lax.psum_scatter(
        lax.dot_general(panel_inverse, reduced, over_rows, preferred_element_type=F32),
        "factor",
        scatter_dimension=0,
        tiled=True,
    ).astype(BF16)
    config_response = lax.dot_general(
        axle_weights,
        lax.all_gather(panel_solution, "load", axis=1, tiled=True),
        (((1,), (1,)), ((), ())),
        preferred_element_type=F32,
    )
    return (update_rhs, panel_solution, config_response)


def solution(mesh):
    in_specs = (
        P("factor", "load"),
        P("factor", "load"),
        P("factor", None),
        P("factor", None),
        P(("factor", "load"), None),
        P("load", None),
    )
    out_specs = (P("factor", "load"), P("factor", "load"), P("load", "factor"))
    small = mesh.shape["factor"] == 4 and mesh.shape["load"] == 8
    local = small_slice if small else any_slice
    return jax.shard_map(local, mesh=mesh, in_specs=in_specs, out_specs=out_specs, check_vma=False)
```

profile of v0, /device:TPU:10, one launch (start us, length us, event | category | flops | bytes accessed | tf_op | source)
XLA Modules:
  0.0 127.8 jit_solution(16815053537112578332)
XLA Ops:
  0.6 3.6 %collective-permute-start.1 = (bf16[512,256]{1,0:T(8,128)(2,1)}, bf16[512,256]{1,0:T(8,128)(2,1)S(1)}, u32[]{:S(2)}, u32[]{:S(2)}) collective-permute-start(bf16[512,256]{1,0:T(8,128)(2,1)} %refs_0_.1), channel_id=1, source_target_pairs={{0,16},{8,24},{1,17},{9,25},{2,18},{10,26},{3,19},{11,27},{4,20},{... | collective-permute-start | bytes 786440 | tf_op jit(solution)/shard_map/ppermute | solution.py:162
  4.2 2.3 %slice.3 = bf16[512,1024]{1,0:T(8,128)(2,1)} slice(bf16[512,2048]{1,0:T(8,128)(2,1)} %own_ref.3), slice={[0:512], [0:1024]} | slice | bytes 2097152 | tf_op jit(solution)/shard_map/slice | solution.py:164
  7.9 2.2 %collective-permute-done.1.refs_2_ = bf16[512,256]{1,0:T(8,128)(2,1)S(1)} collective-permute-done((bf16[512,256]{1,0:T(8,128)(2,1)}, bf16[512,256]{1,0:T(8,128)(2,1)S(1)}, u32[]{:S(2)}, u32[]{:S(2)}) %collective-permute-start.1) | collective-permute-done | bytes 262176 | tf_op jit(solution)/shard_map/ppermute | solution.py:162
  14.2 1.8 %shard_map.86.refs_0_ = bf16[512,256]{1,0:T(8,128)(2,1)S(1)} custom-call(s32[4]{0:T(128)S(1)} %iota_xor_fusion.1.at_ref, bf16[512,2048]{1,0:T(8,128)(2,1)S(1)} %copy-done.2, bf16[512,256]{1,0:T(8,128)(2,1)S(1)} %copy-done.11, bf16[512,256]{1,0:T(8,128)(2,1)} %collective-permute-done.refs_1_, bf16[512,256]{1,0:T(8,128)(2,1)S(1)} %copy-done.13, ...), custom_call_target="tpu_custom_call" | custom-call | flops 536870912 | bytes 3407872 | tf_op jit(solution)/shard_map/pallas_call | solution.py:21
  15.9 3.8 %collective-permute-start.6 = (bf16[512,256]{1,0:T(8,128)(2,1)S(1)}, bf16[512,256]{1,0:T(8,128)(2,1)S(1)}, u32[]{:S(2)}, u32[]{:S(2)}) collective-permute-start(bf16[512,256]{1,0:T(8,128)(2,1)S(1)} %shard_map.86.refs_0_), channel_id=1, source_target_pairs={{0,16},{8,24},{16,0},{24,8},{1,17},{9,25},{17,1},{25,9},{2,18},{10... | collective-permute-start | bytes 786440 | tf_op jit(solution)/shard_map/ppermute | solution.py:132
  22.6 4.3 %collective-permute-done.10.refs_3_ = bf16[256,256]{1,0:T(8,128)(2,1)S(1)} collective-permute-done((bf16[256,256]{1,0:T(8,128)(2,1)S(1)}, bf16[256,256]{1,0:T(8,128)(2,1)S(1)}, u32[]{:S(2)}, u32[]{:S(2)}) %collective-permute-start.10) | collective-permute-done | bytes 131104 | tf_op jit(solution)/shard_map/ppermute | solution.py:132
  27.4 1.5 %collective-permute-done.8.refs_1_ = bf16[256,256]{1,0:T(8,128)(2,1)S(1)} collective-permute-done((bf16[256,256]{1,0:T(8,128)(2,1)S(1)}, bf16[256,256]{1,0:T(8,128)(2,1)S(1)}, u32[]{:S(2)}, u32[]{:S(2)}) %collective-permute-start.8) | collective-permute-done | bytes 131104 | tf_op jit(solution)/shard_map/ppermute | solution.py:132
  28.9 2.3 %collective-permute-start.3 = (bf16[256,256]{1,0:T(8,128)(2,1)S(1)}, bf16[256,256]{1,0:T(8,128)(2,1)S(1)}, u32[]{:S(2)}, u32[]{:S(2)}) collective-permute-start(bf16[256,256]{1,0:T(8,128)(2,1)S(1)} %get-tuple-element.20), channel_id=1, source_target_pairs={{0,7},{1,6},{2,5},{3,4},{4,3},{5,2},{6,1},{7,0},{8,15},{9,14},{10,... | collective-permute-start | bytes 393224 | tf_op jit(solution)/shard_map/ppermute | solution.py:132
  31.2 7.6 %collective-permute-done.6.refs_2_ = bf16[512,256]{1,0:T(8,128)(2,1)S(1)} collective-permute-done((bf16[512,256]{1,0:T(8,128)(2,1)S(1)}, bf16[512,256]{1,0:T(8,128)(2,1)S(1)}, u32[]{:S(2)}, u32[]{:S(2)}) %collective-permute-start.6) | collective-permute-done | bytes 262176 | tf_op jit(solution)/shard_map/ppermute | solution.py:132
  38.8 2.7 %collective-permute-start.11 = (bf16[256,256]{1,0:T(8,128)(2,1)S(1)}, bf16[256,256]{1,0:T(8,128)(2,1)S(1)}, u32[]{:S(2)}, u32[]{:S(2)}) collective-permute-start(bf16[256,256]{1,0:T(8,128)(2,1)S(1)} %get-tuple-element.30), channel_id=1, source_target_pairs={{0,4},{1,5},{2,6},{3,7},{4,0},{5,1},{6,2},{7,3},{8,12},{9,13},{10,... | collective-permute-start | bytes 393224 | tf_op jit(solution)/shard_map/ppermute | solution.py:132
  41.8 1.6 %collective-permute-start.13 = (bf16[256,256]{1,0:T(8,128)(2,1)S(1)}, bf16[256,256]{1,0:T(8,128)(2,1)S(1)}, u32[]{:S(2)}, u32[]{:S(2)}) collective-permute-start(bf16[256,256]{1,0:T(8,128)(2,1)S(1)} %get-tuple-element.32), channel_id=1, source_target_pairs={{0,6},{1,7},{2,4},{3,5},{4,2},{5,3},{6,0},{7,1},{8,14},{9,15},{10,... | collective-permute-start | bytes 393224 | tf_op jit(solution)/shard_map/ppermute | solution.py:132
  43.5 3.4 %copy-done.3 = bf16[2048,2048]{1,0:T(8,128)(2,1)S(1)} copy-done((bf16[2048,2048]{1,0:T(8,128)(2,1)S(1)}, bf16[2048,2048]{1,0:T(8,128)(2,1)}, u32[]{:S(2)}) %copy-start.3) | copy-done | bytes 8388632
  47.4 1.8 %shard_map.89.refs_0_ = f32[4,256,512]{2,1,0:T(8,128)S(1)} custom-call(s32[12]{0:T(128)S(1)} %pad_add_fusion.2.at_ref, bf16[2048,2048]{1,0:T(8,128)(2,1)S(1)} %shard_map.85.factor_ref, bf16[256,256]{1,0:T(8,128)(2,1)S(1)} %get-tuple-element.26.refs_0_, bf16[256,256]{1,0:T(8,128)(2,1)S(1)} %collective-permute-done.8.refs_1_, ...), custom_call_target="tpu_custom_call" | custom-call | flops 1073741824 | bytes 11010048 | tf_op jit(solution)/shard_map/pallas_call | solution.py:21
  49.3 3.9 %collective-permute-done.11.refs_1_ = bf16[256,256]{1,0:T(8,128)(2,1)S(1)} collective-permute-done((bf16[256,256]{1,0:T(8,128)(2,1)S(1)}, bf16[256,256]{1,0:T(8,128)(2,1)S(1)}, u32[]{:S(2)}, u32[]{:S(2)}) %collective-permute-start.11) | collective-permute-done | bytes 131104 | tf_op jit(solution)/shard_map/ppermute | solution.py:132
  53.2 2.8 %collective-permute-done.12.refs_2_ = bf16[256,256]{1,0:T(8,128)(2,1)S(1)} collective-permute-done((bf16[256,256]{1,0:T(8,128)(2,1)S(1)}, bf16[256,256]{1,0:T(8,128)(2,1)S(1)}, u32[]{:S(2)}, u32[]{:S(2)}) %collective-permute-start.12) | collective-permute-done | bytes 131104 | tf_op jit(solution)/shard_map/ppermute | solution.py:132
  56.0 2.8 %collective-permute-done.13.refs_3_ = bf16[256,256]{1,0:T(8,128)(2,1)S(1)} collective-permute-done((bf16[256,256]{1,0:T(8,128)(2,1)S(1)}, bf16[256,256]{1,0:T(8,128)(2,1)S(1)}, u32[]{:S(2)}, u32[]{:S(2)}) %collective-permute-start.13) | collective-permute-done | bytes 131104 | tf_op jit(solution)/shard_map/ppermute | solution.py:132
  63.9 3.4 %copy-done.1 = bf16[2048,2048]{1,0:T(8,128)(2,1)S(1)} copy-done((bf16[2048,2048]{1,0:T(8,128)(2,1)S(1)}, bf16[2048,2048]{1,0:T(8,128)(2,1)}, u32[]{:S(2)}) %copy-start.1) | copy-done | bytes 8388632
  71.4 4.6 %shard_map.88 = (bf16[2048,256]{1,0:T(8,128)(2,1)}, bf16[2,256,512]{2,1,0:T(8,128)(2,1)S(1)}) custom-call(s32[4]{0:T(128)S(1)} %iota_xor_fusion.1.at_ref, bf16[2048,2048]{1,0:T(8,128)(2,1)S(1)} %copy-done.1, bf16[2048,256]{1,0:T(8,128)(2,1)S(1)} %copy-done.10, bf16[512,256]{1,0:T(8,128)(2,1)S(1)} %shard_map.86.refs_0_, bf16[512,256]{1,0:T(8,128)(2,1)S(1)} %copy-done.17, ...), custom_call_target="tpu_custom_call" | custom-call | flops 2147483648 | bytes 12058624 | tf_op jit(solution)/shard_map/pallas_call | solution.py:21
  76.0 2.1 %collective-permute-done.15.across_ref = bf16[2,256,512]{2,1,0:T(8,128)(2,1)} collective-permute-done((bf16[2,256,512]{2,1,0:T(8,128)(2,1)}, bf16[2,256,512]{2,1,0:T(8,128)(2,1)}, u32[]{:S(2)}, u32[]{:S(2)}) %collective-permute-start.15) | collective-permute-done | bytes 524320 | tf_op jit(solution)/shard_map/ppermute | solution.py:132
  78.1 1.6 %shard_map.92 = (bf16[2,256,512]{2,1,0:T(8,128)(2,1)S(1)}, bf16[256,512]{1,0:T(8,128)(2,1)S(1)}) custom-call(s32[2]{0:T(128)S(1)} %pad_add_fusion.1.at_ref, bf16[2,256,512]{2,1,0:T(8,128)(2,1)S(1)} %get-tuple-element.25.turned_ref, f32[2,256,512]{2,1,0:T(8,128)S(1)} %shard_map.90.kept_ref, bf16[2,256,512]{2,1,0:T(8,128)(2,1)S(1)} %copy-done.8, ...), custom_call_target="tpu_custom_call" | custom-call | flops 268435456 | bytes 6553600 | tf_op jit(solution)/shard_map/pallas_call | solution.py:21
  81.5 4.4 %collective-permute-start.21 = (bf16[256,512]{1,0:T(8,128)(2,1)S(1)}, bf16[256,512]{1,0:T(8,128)(2,1)S(1)}, u32[]{:S(2)}, u32[]{:S(2)}) collective-permute-start(bf16[256,512]{1,0:T(8,128)(2,1)S(1)} %add_convert_fusion.1.refs_0_), channel_id=1, source_target_pairs={{2,4},{3,5},{4,2},{5,3},{10,12},{11,13},{12,10},{13,11},{18,20},{1... | collective-permute-start | bytes 786440 | tf_op jit(solution)/shard_map/ppermute | solution.py:229
  85.8 4.0 %collective-permute-done.18.refs_2_ = bf16[256,512]{1,0:T(8,128)(2,1)S(1)} collective-permute-done((bf16[256,512]{1,0:T(8,128)(2,1)S(1)}, bf16[256,512]{1,0:T(8,128)(2,1)S(1)}, u32[]{:S(2)}, u32[]{:S(2)}) %collective-permute-start.18) | collective-permute-done | bytes 262176 | tf_op jit(solution)/shard_map/ppermute | solution.py:229
  89.8 4.4 %collective-permute-start.20 = (bf16[256,512]{1,0:T(8,128)(2,1)S(1)}, bf16[256,512]{1,0:T(8,128)(2,1)}, u32[]{:S(2)}, u32[]{:S(2)}) collective-permute-start(bf16[256,512]{1,0:T(8,128)(2,1)S(1)} %collective-permute-done.18.refs_2_), channel_id=1, source_target_pairs={{2,4},{3,5},{4,2},{5,3},{10,12},{11,13},{12,10},{13,11},{18,20},{1... | collective-permute-start | bytes 786440 | tf_op jit(solution)/shard_map/ppermute | solution.py:229
  94.2 2.0 %collective-permute-start.22 = (bf16[256,512]{1,0:T(8,128)(2,1)S(1)}, bf16[256,512]{1,0:T(8,128)(2,1)}, u32[]{:S(2)}, u32[]{:S(2)}) collective-permute-start(bf16[256,512]{1,0:T(8,128)(2,1)S(1)} %collective-permute-done.21.b_ref), channel_id=1, source_target_pairs={{2,0},{3,1},{4,6},{5,7},{10,8},{11,9},{12,14},{13,15},{18,16},{19,... | collective-permute-start | bytes 786440 | tf_op jit(solution)/shard_map/ppermute | solution.py:229
  96.2 3.8 %collective-permute-done.20 = bf16[256,512]{1,0:T(8,128)(2,1)} collective-permute-done((bf16[256,512]{1,0:T(8,128)(2,1)S(1)}, bf16[256,512]{1,0:T(8,128)(2,1)}, u32[]{:S(2)}, u32[]{:S(2)}) %collective-permute-start.20) | collective-permute-done | bytes 262176 | tf_op jit(solution)/shard_map/ppermute | solution.py:229
  103.4 2.4 %collective-permute-start.24 = (bf16[256,512]{1,0:T(8,128)(2,1)S(1)}, bf16[256,512]{1,0:T(8,128)(2,1)S(1)}, u32[]{:S(2)}, u32[]{:S(2)}) collective-permute-start(bf16[256,512]{1,0:T(8,128)(2,1)S(1)} %collective-permute-done.21.b_ref), channel_id=1, source_target_pairs={{2,3},{3,2},{4,5},{5,4},{10,11},{11,10},{12,13},{13,12},{18,19},{1... | collective-permute-start | bytes 786440 | tf_op jit(solution)/shard_map/ppermute | solution.py:229
  106.9 1.5 %collective-permute-start.23 = (bf16[256,512]{1,0:T(8,128)(2,1)S(1)}, bf16[256,512]{1,0:T(8,128)(2,1)}, u32[]{:S(2)}, u32[]{:S(2)}) collective-permute-start(bf16[256,512]{1,0:T(8,128)(2,1)S(1)} %broadcast_select_fusion.c_ref), channel_id=1, source_target_pairs={{2,3},{3,2},{4,5},{5,4},{0,1},{1,0},{6,7},{7,6},{10,11},{11,10},{1... | collective-permute-start | bytes 786440 | tf_op jit(solution)/shard_map/ppermute | solution.py:229
  110.7 5.6 %collective-permute-done.19.refs_3_ = bf16[256,512]{1,0:T(8,128)(2,1)} collective-permute-done((bf16[256,512]{1,0:T(8,128)(2,1)S(1)}, bf16[256,512]{1,0:T(8,128)(2,1)}, u32[]{:S(2)}, u32[]{:S(2)}) %collective-permute-start.19) | collective-permute-done | bytes 262176 | tf_op jit(solution)/shard_map/ppermute | solution.py:229
  116.4 1.5 %shard_map.94.near_ref = f32[384,512]{1,0:T(8,128)S(1)} custom-call(s32[9]{0:T(128)S(1)} %pad_add_fusion.3.at_ref, bf16[384,2048]{1,0:T(8,128)(2,1)S(1)} %copy-done.4, bf16[256,512]{1,0:T(8,128)(2,1)S(1)} %add_convert_fusion.1.refs_0_, bf16[256,512]{1,0:T(8,128)(2,1)S(1)} %collective-permute-done.17.refs_1_, ...), custom_call_target="tpu_custom_call" | custom-call | flops 402653184 | bytes 3407872 | tf_op jit(solution)/shard_map/pallas_call | solution.py:21
  117.9 4.0 %collective-permute-done.24.bx_ref = bf16[256,512]{1,0:T(8,128)(2,1)S(1)} collective-permute-done((bf16[256,512]{1,0:T(8,128)(2,1)S(1)}, bf16[256,512]{1,0:T(8,128)(2,1)S(1)}, u32[]{:S(2)}, u32[]{:S(2)}) %collective-permute-start.24) | collective-permute-done | bytes 262176 | tf_op jit(solution)/shard_map/ppermute | solution.py:229
  121.9 3.4 %collective-permute-done.23.cx_ref = bf16[256,512]{1,0:T(8,128)(2,1)} collective-permute-done((bf16[256,512]{1,0:T(8,128)(2,1)S(1)}, bf16[256,512]{1,0:T(8,128)(2,1)}, u32[]{:S(2)}, u32[]{:S(2)}) %collective-permute-start.23) | collective-permute-done | bytes 262176 | tf_op jit(solution)/shard_map/ppermute | solution.py:229
  125.3 2.5 %shard_map.95 = f32[384,512]{1,0:T(8,128)} custom-call(s32[9]{0:T(128)S(1)} %pad_add_fusion.3.at_ref, bf16[384,2048]{1,0:T(8,128)(2,1)S(1)} %copy-done.4, f32[384,512]{1,0:T(8,128)S(1)} %shard_map.94.near_ref, bf16[256,512]{1,0:T(8,128)(2,1)S(1)} %broadcast_select_fusion.c_ref, bf16[256,512]{1,0:T(8,128)(2,1)} %collective-permute-done.23.cx_ref, ...), custom_call_target="tpu_custom_call" | custom-call | flops 402653184 | bytes 4718592 | tf_op jit(solution)/shard_map/pallas_call | solution.py:21
  (84 shorter events, 27.3 us)
Async XLA Ops:
  0.6 11.5 %copy-start.2 = (bf16[512,2048]{1,0:T(8,128)(2,1)S(1)}, bf16[512,2048]{1,0:T(8,128)(2,1)}, u32[]{:S(2)}) copy-start(bf16[512,2048]{1,0:T(8,128)(2,1)} %own_ref.3) | copy-start | bytes 6291460
  0.6 9.4 %collective-permute-start.1 = (bf16[512,256]{1,0:T(8,128)(2,1)}, bf16[512,256]{1,0:T(8,128)(2,1)S(1)}, u32[]{:S(2)}, u32[]{:S(2)}) collective-permute-start(bf16[512,256]{1,0:T(8,128)(2,1)} %refs_0_.1), channel_id=1, source_target_pairs={{0,16},{8,24},{1,17},{9,25},{2,18},{10,26},{3,19},{11,27},{4,20},{... | collective-permute-start | bytes 786440 | tf_op jit(solution)/shard_map/ppermute | solution.py:162
  6.5 42.8 %collective-permute-start.4 = (bf16[512,1024]{1,0:T(8,128)(2,1)}, bf16[512,1024]{1,0:T(8,128)(2,1)S(1)}, u32[]{:S(2)}, u32[]{:S(2)}) collective-permute-start(bf16[512,1024]{1,0:T(8,128)(2,1)} %slice.3), channel_id=1, source_target_pairs={{16,0},{24,8},{17,1},{25,9},{18,2},{26,10},{19,3},{27,11},{20,4},{... | collective-permute-start | bytes 3145736 | tf_op jit(solution)/shard_map/ppermute | solution.py:164
  7.8 4.4 %collective-permute-start = (bf16[512,256]{1,0:T(8,128)(2,1)}, bf16[512,256]{1,0:T(8,128)(2,1)}, u32[]{:S(2)}, u32[]{:S(2)}) collective-permute-start(bf16[512,256]{1,0:T(8,128)(2,1)} %refs_0_.1), channel_id=1, source_target_pairs={{0,8},{8,0},{16,24},{24,16},{1,9},{9,1},{17,25},{25,17},{2,10},{10... | collective-permute-start | bytes 786440 | tf_op jit(solution)/shard_map/ppermute | solution.py:132
  10.1 2.1 %collective-permute-start.2 = (bf16[512,256]{1,0:T(8,128)(2,1)S(1)}, bf16[512,256]{1,0:T(8,128)(2,1)}, u32[]{:S(2)}, u32[]{:S(2)}) collective-permute-start(bf16[512,256]{1,0:T(8,128)(2,1)S(1)} %collective-permute-done.1.refs_2_), channel_id=1, source_target_pairs={{16,24},{24,16},{17,25},{25,17},{18,26},{26,18},{19,27},{27,19},{2... | collective-permute-start | bytes 786440 | tf_op jit(solution)/shard_map/ppermute | solution.py:163
  15.9 22.9 %collective-permute-start.6 = (bf16[512,256]{1,0:T(8,128)(2,1)S(1)}, bf16[512,256]{1,0:T(8,128)(2,1)S(1)}, u32[]{:S(2)}, u32[]{:S(2)}) collective-permute-start(bf16[512,256]{1,0:T(8,128)(2,1)S(1)} %shard_map.86.refs_0_), channel_id=1, source_target_pairs={{0,16},{8,24},{16,0},{24,8},{1,17},{9,25},{17,1},{25,9},{2,18},{10... | collective-permute-start | bytes 786440 | tf_op jit(solution)/shard_map/ppermute | solution.py:132
  20.6 6.3 %collective-permute-start.10 = (bf16[256,256]{1,0:T(8,128)(2,1)S(1)}, bf16[256,256]{1,0:T(8,128)(2,1)S(1)}, u32[]{:S(2)}, u32[]{:S(2)}) collective-permute-start(bf16[256,256]{1,0:T(8,128)(2,1)S(1)} %get-tuple-element.29), channel_id=1, source_target_pairs={{0,3},{1,2},{2,1},{3,0},{4,7},{5,6},{6,5},{7,4},{8,11},{9,10},{10,... | collective-permute-start | bytes 393224 | tf_op jit(solution)/shard_map/ppermute | solution.py:132
  21.1 7.8 %collective-permute-start.8 = (bf16[256,256]{1,0:T(8,128)(2,1)S(1)}, bf16[256,256]{1,0:T(8,128)(2,1)S(1)}, u32[]{:S(2)}, u32[]{:S(2)}) collective-permute-start(bf16[256,256]{1,0:T(8,128)(2,1)S(1)} %get-tuple-element.27), channel_id=1, source_target_pairs={{0,1},{1,0},{2,3},{3,2},{4,5},{5,4},{6,7},{7,6},{8,9},{9,8},{10,11... | collective-permute-start | bytes 393224 | tf_op jit(solution)/shard_map/ppermute | solution.py:132
  22.6 19.2 %collective-permute-start.5 = (bf16[512,256]{1,0:T(8,128)(2,1)S(1)}, bf16[512,256]{1,0:T(8,128)(2,1)S(1)}, u32[]{:S(2)}, u32[]{:S(2)}) collective-permute-start(bf16[512,256]{1,0:T(8,128)(2,1)S(1)} %shard_map.86.refs_0_), channel_id=1, source_target_pairs={{0,8},{8,0},{16,24},{24,16},{1,9},{9,1},{17,25},{25,17},{2,10},{10... | collective-permute-start | bytes 786440 | tf_op jit(solution)/shard_map/ppermute | solution.py:132
  26.9 11.9 %collective-permute-start.9 = (bf16[256,256]{1,0:T(8,128)(2,1)S(1)}, bf16[256,256]{1,0:T(8,128)(2,1)S(1)}, u32[]{:S(2)}, u32[]{:S(2)}) collective-permute-start(bf16[256,256]{1,0:T(8,128)(2,1)S(1)} %get-tuple-element.28), channel_id=1, source_target_pairs={{0,2},{1,3},{2,0},{3,1},{4,6},{5,7},{6,4},{7,5},{8,10},{9,11},{10,... | collective-permute-start | bytes 393224 | tf_op jit(solution)/shard_map/ppermute | solution.py:132
  28.9 12.6 %collective-permute-start.3 = (bf16[256,256]{1,0:T(8,128)(2,1)S(1)}, bf16[256,256]{1,0:T(8,128)(2,1)S(1)}, u32[]{:S(2)}, u32[]{:S(2)}) collective-permute-start(bf16[256,256]{1,0:T(8,128)(2,1)S(1)} %get-tuple-element.20), channel_id=1, source_target_pairs={{0,7},{1,6},{2,5},{3,4},{4,3},{5,2},{6,1},{7,0},{8,15},{9,14},{10,... | collective-permute-start | bytes 393224 | tf_op jit(solution)/shard_map/ppermute | solution.py:132
  38.8 10.4 %collective-permute-start.7 = (bf16[512,256]{1,0:T(8,128)(2,1)S(1)}, bf16[512,256]{1,0:T(8,128)(2,1)S(1)}, u32[]{:S(2)}, u32[]{:S(2)}) collective-permute-start(bf16[512,256]{1,0:T(8,128)(2,1)S(1)} %collective-permute-done.6.refs_2_), channel_id=1, source_target_pairs={{0,8},{8,0},{16,24},{24,16},{1,9},{9,1},{17,25},{25,17},{2,10},{10... | collective-permute-start | bytes 786440 | tf_op jit(solution)/shard_map/ppermute | solution.py:132
  38.8 14.4 %collective-permute-start.11 = (bf16[256,256]{1,0:T(8,128)(2,1)S(1)}, bf16[256,256]{1,0:T(8,128)(2,1)S(1)}, u32[]{:S(2)}, u32[]{:S(2)}) collective-permute-start(bf16[256,256]{1,0:T(8,128)(2,1)S(1)} %get-tuple-element.30), channel_id=1, source_target_pairs={{0,4},{1,5},{2,6},{3,7},{4,0},{5,1},{6,2},{7,3},{8,12},{9,13},{10,... | collective-permute-start | bytes 393224 | tf_op jit(solution)/shard_map/ppermute | solution.py:132
  41.5 14.5 %collective-permute-start.12 = (bf16[256,256]{1,0:T(8,128)(2,1)S(1)}, bf16[256,256]{1,0:T(8,128)(2,1)S(1)}, u32[]{:S(2)}, u32[]{:S(2)}) collective-permute-start(bf16[256,256]{1,0:T(8,128)(2,1)S(1)} %get-tuple-element.31), channel_id=1, source_target_pairs={{0,5},{1,4},{2,7},{3,6},{4,1},{5,0},{6,3},{7,2},{8,13},{9,12},{10,... | collective-permute-start | bytes 393224 | tf_op jit(solution)/shard_map/ppermute | solution.py:132
  41.8 17.0 %collective-permute-start.13 = (bf16[256,256]{1,0:T(8,128)(2,1)S(1)}, bf16[256,256]{1,0:T(8,128)(2,1)S(1)}, u32[]{:S(2)}, u32[]{:S(2)}) collective-permute-start(bf16[256,256]{1,0:T(8,128)(2,1)S(1)} %get-tuple-element.32), channel_id=1, source_target_pairs={{0,6},{1,7},{2,4},{3,5},{4,2},{5,3},{6,0},{7,1},{8,14},{9,15},{10,... | collective-permute-start | bytes 393224 | tf_op jit(solution)/shard_map/ppermute | solution.py:132
  47.4 12.8 %copy-start = (bf16[2048,2048]{1,0:T(8,128)(2,1)}, bf16[2048,2048]{1,0:T(8,128)(2,1)S(1)}, u32[]{:S(2)}) copy-start(bf16[2048,2048]{1,0:T(8,128)(2,1)S(1)} %shard_map.85.factor_ref) | copy-start | bytes 25165828
  49.3 10.8 %copy-start.18 = (bf16[512,256]{1,0:T(8,128)(2,1)}, bf16[512,256]{1,0:T(8,128)(2,1)S(1)}, u32[]{:S(2)}) copy-start(bf16[512,256]{1,0:T(8,128)(2,1)S(1)} %collective-permute-done.7.refs_3_) | copy-start | bytes 786436
  49.3 10.8 %copy-start.5 = (bf16[512,1024]{1,0:T(8,128)(2,1)}, bf16[512,1024]{1,0:T(8,128)(2,1)S(1)}, u32[]{:S(2)}) copy-start(bf16[512,1024]{1,0:T(8,128)(2,1)S(1)} %collective-permute-done.4.other_ref) | copy-start | bytes 3145732
  60.1 2.0 %collective-permute-start.14 = (bf16[2,256,512]{2,1,0:T(8,128)(2,1)S(1)}, bf16[2,256,512]{2,1,0:T(8,128)(2,1)S(1)}, u32[]{:S(2)}, u32[]{:S(2)}) collective-permute-start(bf16[2,256,512]{2,1,0:T(8,128)(2,1)S(1)} %shard_map.91), channel_id=1, source_target_pairs={{0,8},{8,0},{16,24},{24,16},{1,9},{9,1},{17,25},{25,17},{2,10},{10... | collective-permute-start | bytes 1572872 | tf_op jit(solution)/shard_map/ppermute | solution.py:132
  63.9 14.3 %collective-permute-start.15 = (bf16[2,256,512]{2,1,0:T(8,128)(2,1)}, bf16[2,256,512]{2,1,0:T(8,128)(2,1)}, u32[]{:S(2)}, u32[]{:S(2)}) collective-permute-start(bf16[2,256,512]{2,1,0:T(8,128)(2,1)} %add_convert_fusion), channel_id=1, source_target_pairs={{0,16},{8,24},{16,0},{24,8},{1,17},{9,25},{17,1},{25,9},{2,18},{10... | collective-permute-start | bytes 1572872 | tf_op jit(solution)/shard_map/ppermute | solution.py:132
  79.7 1.6 %collective-permute-start.16 = (bf16[256,512]{1,0:T(8,128)(2,1)S(1)}, bf16[256,512]{1,0:T(8,128)(2,1)S(1)}, u32[]{:S(2)}, u32[]{:S(2)}) collective-permute-start(bf16[256,512]{1,0:T(8,128)(2,1)S(1)} %get-tuple-element.36), channel_id=1, source_target_pairs={{0,8},{8,0},{16,24},{24,16},{1,9},{9,1},{17,25},{25,17},{2,10},{10... | collective-permute-start | bytes 786440 | tf_op jit(solution)/shard_map/ppermute | solution.py:132
  80.9 35.5 %copy-start.4 = (bf16[384,2048]{1,0:T(8,128)(2,1)S(1)}, bf16[384,2048]{1,0:T(8,128)(2,1)}, u32[]{:S(2)}) copy-start(bf16[384,2048]{1,0:T(8,128)(2,1)} %axle_ref.3) | copy-start | bytes 4718596
  81.4 8.4 %collective-permute-start.18 = (bf16[256,512]{1,0:T(8,128)(2,1)S(1)}, bf16[256,512]{1,0:T(8,128)(2,1)S(1)}, u32[]{:S(2)}, u32[]{:S(2)}) collective-permute-start(bf16[256,512]{1,0:T(8,128)(2,1)S(1)} %add_convert_fusion.1.refs_0_), channel_id=1, source_target_pairs={{2,0},{3,1},{4,6},{5,7},{0,2},{1,3},{6,4},{7,5},{10,8},{11,9},{12,... | collective-permute-start | bytes 786440 | tf_op jit(solution)/shard_map/ppermute | solution.py:229
  81.5 12.7 %collective-permute-start.21 = (bf16[256,512]{1,0:T(8,128)(2,1)S(1)}, bf16[256,512]{1,0:T(8,128)(2,1)S(1)}, u32[]{:S(2)}, u32[]{:S(2)}) collective-permute-start(bf16[256,512]{1,0:T(8,128)(2,1)S(1)} %add_convert_fusion.1.refs_0_), channel_id=1, source_target_pairs={{2,4},{3,5},{4,2},{5,3},{10,12},{11,13},{12,10},{13,11},{18,20},{1... | collective-permute-start | bytes 786440 | tf_op jit(solution)/shard_map/ppermute | solution.py:229
  89.8 10.2 %collective-permute-start.20 = (bf16[256,512]{1,0:T(8,128)(2,1)S(1)}, bf16[256,512]{1,0:T(8,128)(2,1)}, u32[]{:S(2)}, u32[]{:S(2)}) collective-permute-start(bf16[256,512]{1,0:T(8,128)(2,1)S(1)} %collective-permute-done.18.refs_2_), channel_id=1, source_target_pairs={{2,4},{3,5},{4,2},{5,3},{10,12},{11,13},{12,10},{13,11},{18,20},{1... | collective-permute-start | bytes 786440 | tf_op jit(solution)/shard_map/ppermute | solution.py:229
  94.2 11.7 %collective-permute-start.22 = (bf16[256,512]{1,0:T(8,128)(2,1)S(1)}, bf16[256,512]{1,0:T(8,128)(2,1)}, u32[]{:S(2)}, u32[]{:S(2)}) collective-permute-start(bf16[256,512]{1,0:T(8,128)(2,1)S(1)} %collective-permute-done.21.b_ref), channel_id=1, source_target_pairs={{2,0},{3,1},{4,6},{5,7},{10,8},{11,9},{12,14},{13,15},{18,16},{19,... | collective-permute-start | bytes 786440 | tf_op jit(solution)/shard_map/ppermute | solution.py:229
  100.0 8.4 %collective-permute-start.25 = (bf16[256,512]{1,0:T(8,128)(2,1)}, bf16[256,512]{1,0:T(8,128)(2,1)S(1)}, u32[]{:S(2)}, u32[]{:S(2)}) collective-permute-start(bf16[256,512]{1,0:T(8,128)(2,1)} %collective-permute-done.20), channel_id=1, source_target_pairs={{2,0},{3,1},{4,6},{5,7},{10,8},{11,9},{12,14},{13,15},{18,16},{19,... | collective-permute-start | bytes 786440 | tf_op jit(solution)/shard_map/ppermute | solution.py:229
  101.3 9.4 %collective-permute-start.17 = (bf16[256,512]{1,0:T(8,128)(2,1)S(1)}, bf16[256,512]{1,0:T(8,128)(2,1)S(1)}, u32[]{:S(2)}, u32[]{:S(2)}) collective-permute-start(bf16[256,512]{1,0:T(8,128)(2,1)S(1)} %add_convert_fusion.1.refs_0_), channel_id=1, source_target_pairs={{2,3},{3,2},{4,5},{5,4},{0,1},{1,0},{6,7},{7,6},{10,11},{11,10},{1... | collective-permute-start | bytes 786440 | tf_op jit(solution)/shard_map/ppermute | solution.py:229
  102.0 14.4 %collective-permute-start.19 = (bf16[256,512]{1,0:T(8,128)(2,1)S(1)}, bf16[256,512]{1,0:T(8,128)(2,1)}, u32[]{:S(2)}, u32[]{:S(2)}) collective-permute-start(bf16[256,512]{1,0:T(8,128)(2,1)S(1)} %collective-permute-done.18.refs_2_), channel_id=1, source_target_pairs={{2,3},{3,2},{4,5},{5,4},{0,1},{1,0},{6,7},{7,6},{10,11},{11,10},{1... | collective-permute-start | bytes 786440 | tf_op jit(solution)/shard_map/ppermute | solution.py:229
  103.4 18.5 %collective-permute-start.24 = (bf16[256,512]{1,0:T(8,128)(2,1)S(1)}, bf16[256,512]{1,0:T(8,128)(2,1)S(1)}, u32[]{:S(2)}, u32[]{:S(2)}) collective-permute-start(bf16[256,512]{1,0:T(8,128)(2,1)S(1)} %collective-permute-done.21.b_ref), channel_id=1, source_target_pairs={{2,3},{3,2},{4,5},{5,4},{10,11},{11,10},{12,13},{13,12},{18,19},{1... | collective-permute-start | bytes 786440 | tf_op jit(solution)/shard_map/ppermute | solution.py:229
  106.9 18.4 %collective-permute-start.23 = (bf16[256,512]{1,0:T(8,128)(2,1)S(1)}, bf16[256,512]{1,0:T(8,128)(2,1)}, u32[]{:S(2)}, u32[]{:S(2)}) collective-permute-start(bf16[256,512]{1,0:T(8,128)(2,1)S(1)} %broadcast_select_fusion.c_ref), channel_id=1, source_target_pairs={{2,3},{3,2},{4,5},{5,4},{0,1},{1,0},{6,7},{7,6},{10,11},{11,10},{1... | collective-permute-start | bytes 786440 | tf_op jit(solution)/shard_map/ppermute | solution.py:229
  108.4 16.8 %collective-permute-start.26 = (bf16[256,512]{1,0:T(8,128)(2,1)S(1)}, bf16[256,512]{1,0:T(8,128)(2,1)}, u32[]{:S(2)}, u32[]{:S(2)}) collective-permute-start(bf16[256,512]{1,0:T(8,128)(2,1)S(1)} %collective-permute-done.25.e_ref), channel_id=1, source_target_pairs={{0,1},{1,0},{6,7},{7,6},{8,9},{9,8},{14,15},{15,14},{16,17},{17,16... | collective-permute-start | bytes 786440 | tf_op jit(solution)/shard_map/ppermute | solution.py:229
  (15 other events, 49.6 us)
where the time goes:
time: 128 us
  waiting for transfers between devices  49.1 us (38%)
  starting transfers between devices  39.1 us (31%)
  Pallas kernels  18.7 us (15%)
  local copies, waits for them, and re-layouts  17.5 us (14%)
  other arithmetic  2.38 us (2%)
    ppermute x14, waiting for transfers between devices, by_xor(): return lax.ppermute(value, axis, [(i, i ^ bits) for i in range(size)])  26.1 us
    ppermute x10, waiting for transfers between devices, hop(): return lax.ppermute(value, 'load', [(i, i ^ bits) for i in places])  20.8 us
    ppermute x10, starting transfers between devices, hop(): return lax.ppermute(value, 'load', [(i, i ^ bits) for i in places])  19.6 us
    pallas_call x10, Pallas kernels, call(): pl.pallas_call(kernel, out_shape=shapes, in_specs=[SMEM] + [VMEM] * len(o...  18.2 us
    unnamed x41, local copies, waits for them, and re-layouts  15.2 us
    ppermute x14, starting transfers between devices, by_xor(): return lax.ppermute(value, axis, [(i, i ^ bits) for i in range(size)])  13.3 us
    ppermute x1, starting transfers between devices, small_slice(): b_across = lax.ppermute(b_panel, 'factor', up)  3.57 us
  transfers between devices with their start and end apart: 27, of which 15 were waited for; matrix products, arithmetic and copies ran while one was open for 3% of the time, Pallas kernels for 10%

commit v1 on v0

v1 whole, which is shorter than its diff:
```python
import functools

import jax
import jax.numpy as jnp
from jax import lax
from jax.experimental import pallas as pl
from jax.experimental.pallas import tpu as pltpu
from jax.sharding import PartitionSpec as P

BF16 = jnp.bfloat16
F32 = jnp.float32


VMEM = pl.BlockSpec(memory_space=pltpu.VMEM)
SMEM = pl.BlockSpec(memory_space=pltpu.SMEM)


def call(kernel, at, operands, outs, flops):
    at = [] if at is None else [at]
    shapes = [jax.ShapeDtypeStruct(shape, kind) for shape, kind in outs]
    moved = sum(v.size * v.dtype.itemsize for v in list(operands) + shapes)
    return pl.pallas_call(
        kernel,
        out_shape=shapes,
        in_specs=[SMEM] * len(at) + [VMEM] * len(operands),
        out_specs=[VMEM] * len(shapes),
        compiler_params=pltpu.CompilerParams(vmem_limit_bytes=16 * 2**20),
        cost_estimate=pl.CostEstimate(flops=flops, bytes_accessed=moved, transcendentals=0),
    )(*at, *operands)


def part(index, size):
    return pl.ds(pl.multiple_of(index * size, size), size)


def dot(a, b):
    return jnp.dot(a, b, preferred_element_type=F32)


def forward_kernel(inverse_ref, b_ref, out_ref):
    out_ref[...] = dot(inverse_ref[...], b_ref[...]).astype(out_ref.dtype)


def update_kernel(factor_ref, rhs_ref, forward_ref, out_ref):
    rows = 512

    @pl.loop(0, out_ref.shape[0] // rows)
    def _(i):
        here = part(i, rows)
        total = rhs_ref[here, :].astype(F32) - dot(factor_ref[here, :], forward_ref[...])
        out_ref[here, :] = total.astype(out_ref.dtype)


def split_kernel(at_ref, solved_ref, *outs):
    cols = outs[0].shape[0]
    for j, out_ref in enumerate(outs):
        out_ref[...] = solved_ref[:, part(at_ref[j], cols)].T


def hold_kernel(factor_ref, out_ref, sem):
    copy = pltpu.make_async_copy(factor_ref, out_ref, sem)
    copy.start()
    copy.wait()


def coupled_kernel(panel_blocks, row_blocks, first, at_ref, factor_ref, *refs):
    pieces, out_ref = refs[-1 - len(row_blocks) : -1], refs[-1]
    depth, width = pieces[0].shape[1], out_ref.shape[2]
    for j, b in enumerate(panel_blocks):
        cols = part(at_ref[b], width)
        total = None if first is None else refs[0][first[j]]
        for k, piece in zip(row_blocks, pieces):
            term = dot(piece[...], factor_ref[part(at_ref[k], depth), cols])
            total = term if total is None else total + term
        out_ref[j] = total.astype(out_ref.dtype)


def reduce_kernel(at_ref, forward_ref, kept_ref, core_ref, across_ref, inverse_ref, reduced_ref, send_ref):
    rows = reduced_ref.shape[1]
    coupled = kept_ref[0] + core_ref[0].astype(F32) + across_ref[...].astype(F32)
    reduced_ref[...] = (forward_ref[...].astype(F32).T - coupled).astype(reduced_ref.dtype)
    for j, b in enumerate((1, 3)):
        send_ref[j] = dot(reduced_ref[...], inverse_ref[:, part(at_ref[b], rows)]).astype(send_ref.dtype)


def solve_kernel(at_ref, reduced_ref, inverse_ref, kept_ref):
    rows = kept_ref.shape[2]
    for j, b in enumerate((0, 2)):
        kept_ref[j] = dot(reduced_ref[...], inverse_ref[:, part(at_ref[b], rows)])


def config_kernel(first, at_ref, axle_ref, *refs):
    out_ref = refs[-1]
    total, shards = (None, refs[:-1]) if first == 0 else (refs[0][...], refs[1:-1])
    cols = shards[0].shape[0]
    for j, shard in enumerate(shards):
        term = dot(axle_ref[:, part(at_ref[first + j], cols)], shard[...])
        total = term if total is None else total + term
    out_ref[...] = total


def by_xor(value, axis, size, bits):
    return lax.ppermute(value, axis, [(i, i ^ bits) for i in range(size)])


def small_slice(b_panel, b_update, panel_inverse, update_factor, update_solution, axle_weights):
    factors, loads = 4, 8
    rows = panel_inverse.shape[0]
    updates, panel = update_factor.shape
    cols = b_panel.shape[1]
    f, at_load = lax.axis_index("factor"), lax.axis_index("load")
    at_factor = f ^ jnp.arange(factors, dtype=jnp.int32)

    spread = at_load ^ jnp.arange(loads, dtype=jnp.int32)

    depth = update_solution.shape[0]
    pieces = call(split_kernel, spread, [update_solution], [((cols, depth), BF16)] * loads, 0)
    early = [pieces[0]] + [by_xor(pieces[k], "load", loads, k) for k in (4, 5, 6)]
    late = [by_xor(pieces[k], "load", loads, k) for k in (7, 1, 2, 3)]
    held = pl.pallas_call(
        hold_kernel,
        out_shape=jax.ShapeDtypeStruct((updates, panel), BF16),
        in_specs=[pl.BlockSpec(memory_space=pltpu.MemorySpace.HBM)],
        out_specs=VMEM,
        scratch_shapes=[pltpu.SemaphoreType.DMA],
        compiler_params=pltpu.CompilerParams(vmem_limit_bytes=16 * 2**20),
        cost_estimate=pl.CostEstimate(flops=0, bytes_accessed=2 * updates * panel, transcendentals=0),
    )(update_factor)

    (forward,) = call(
        forward_kernel,
        None,
        [panel_inverse, lax.all_gather(b_panel, "factor", axis=0, tiled=True)],
        [((rows, cols), BF16)],
        2 * rows * panel * cols,
    )
    late[0], forward = lax.optimization_barrier((late[0], forward))
    forward_all = lax.all_gather(forward, "factor", axis=0, tiled=True)

    pair = (2, cols, rows)
    at_coupled = jnp.concatenate([at_factor, spread])

    def coupled(panel_blocks, row_blocks, first, before, blocks, kind):
        shape = (len(panel_blocks), cols, rows)
        (out,) = call(
            functools.partial(coupled_kernel, panel_blocks, row_blocks, first),
            at_coupled,
            [held] + before + blocks,
            [(shape, kind)],
            2 * cols * rows * depth * len(panel_blocks) * len(row_blocks),
        )
        return out

    begun = coupled((1, 3, 0, 2), (4, 8, 9, 10), None, [], early, F32)
    send = coupled((1, 3), (11, 5, 6, 7), (0, 1), [begun], late, BF16)
    from_core = by_xor(send, "factor", factors, 1)
    kept = coupled((0, 2), (11, 5, 6, 7), (2, 3), [begun], late, F32)
    send = (kept[1] + from_core[1].astype(F32)).astype(BF16)
    from_across = by_xor(send, "factor", factors, 2)
    from_across, forward_all = lax.optimization_barrier((from_across, forward_all))

    reduced, send = call(
        reduce_kernel,
        at_factor,
        [forward, kept, from_core, from_across, panel_inverse],
        [((cols, rows), BF16), (pair, BF16)],
        4 * cols * rows * rows,
    )
    from_core = by_xor(send, "factor", factors, 1)
    (kept,) = call(
        solve_kernel, at_factor, [reduced, panel_inverse], [(pair, F32)], 4 * cols * rows * rows
    )
    send = (kept[1] + from_core[1].astype(F32)).astype(BF16)
    from_across = lax.ppermute(send, "factor", [(2, 0), (3, 1)])
    (update_rhs,) = call(
        update_kernel,
        None,
        [held, b_update, forward_all],
        [((updates, cols), BF16)],
        2 * updates * panel * cols,
    )
    from_across, update_rhs = lax.optimization_barrier((from_across, update_rhs))
    solution_t = (kept[0] + from_core[0].astype(F32) + from_across.astype(F32)).astype(BF16)
    panel_solution = solution_t.T

    middle = (2, 3, 4, 5)
    own = solution_t
    own_x = by_xor(own, "load", loads, 1)
    a = by_xor(own, "load", loads, 2)
    b = by_xor(own, "load", loads, 6)
    own_x, a = lax.optimization_barrier((own_x, a))
    a_x = by_xor(a, "load", loads, 1)
    c = lax.ppermute(a, "load", [(i, i ^ 6) for i in middle])
    d = lax.ppermute(b, "load", [(i, i ^ 2) for i in middle])
    b_x = by_xor(b, "load", loads, 1)
    c = jnp.where((at_load >= 2) & (at_load < 6), c, d)
    c_x = by_xor(c, "load", loads, 1)

    axle_at = at_load ^ jnp.array([0, 1, 2, 3, 6, 7, 4, 5], jnp.int32)
    response = [((axle_weights.shape[0], rows), F32)]
    work = axle_weights.size * rows
    (begun,) = call(
        functools.partial(config_kernel, 0),
        axle_at,
        [axle_weights, own, own_x, a, a_x, b, b_x],
        response,
        3 * work // 2,
    )
    (config_response,) = call(
        functools.partial(config_kernel, 6), axle_at, [axle_weights, begun, c, c_x], response, work // 2
    )
    return (update_rhs, panel_solution, config_response)


def any_slice(b_panel, b_update, panel_inverse, update_factor, update_solution, axle_weights):
    b_all = lax.all_gather(b_panel, "factor", axis=0, tiled=True)
    forward = jnp.dot(panel_inverse, b_all, preferred_element_type=F32).astype(BF16)
    forward_all = lax.all_gather(forward, "factor", axis=0, tiled=True)
    lowered = jnp.dot(update_factor, forward_all, preferred_element_type=F32)
    update_rhs = (b_update.astype(F32) - lowered).astype(BF16)
    regrouped = lax.all_to_all(update_solution, "load", split_axis=1, concat_axis=0, tiled=True)
    over_rows = (((0,), (0,)), ((), ()))
    coupled = lax.psum_scatter(
        lax.dot_general(update_factor, regrouped, over_rows, preferred_element_type=F32),
        "factor",
        scatter_dimension=0,
        tiled=True,
    )
    reduced = (forward.astype(F32) - coupled).astype(BF16)
    panel_solution = lax.psum_scatter(
        lax.dot_general(panel_inverse, reduced, over_rows, preferred_element_type=F32),
        "factor",
        scatter_dimension=0,
        tiled=True,
    ).astype(BF16)
    config_response = lax.dot_general(
        axle_weights,
        lax.all_gather(panel_solution, "load", axis=1, tiled=True),
        (((1,), (1,)), ((), ())),
        preferred_element_type=F32,
    )
    return (update_rhs, panel_solution, config_response)


def solution(mesh):
    in_specs = (
        P("factor", "load"),
        P("factor", "load"),
        P("factor", None),
        P("factor", None),
        P(("factor", "load"), None),
        P("load", None),
    )
    out_specs = (P("factor", "load"), P("factor", "load"), P("load", "factor"))
    small = mesh.shape["factor"] == 4 and mesh.shape["load"] == 8
    local = small_slice if small else any_slice
    return jax.shard_map(local, mesh=mesh, in_specs=in_specs, out_specs=out_specs, check_vma=False)
```

time: 128 us -> 128 us (level)
  the two profiles are of different devices: /device:TPU:10 before, /device:TPU:0 now
where the time goes in v1:
time: 128 us
  waiting for transfers between devices  55 us (43%)
  starting transfers between devices  27.5 us (21%)
  Pallas kernels  17.2 us (13%)
  between operations  14.3 us (11%)
  local copies, waits for them, and re-layouts  12.6 us (10%)
  other arithmetic  1.32 us (1%)
    ppermute x16, waiting for transfers between devices, by_xor(): return lax.ppermute(value, axis, [(i, i ^ bits) for i in range(size)])  33.7 us
    ppermute x16, starting transfers between devices, by_xor(): return lax.ppermute(value, axis, [(i, i ^ bits) for i in range(size)])  23.5 us
    pallas_call x10, Pallas kernels, call(): pl.pallas_call(kernel, out_shape=shapes, in_specs=[SMEM] * len(at) + [VME...  16.6 us
    all_gather x1, waiting for transfers between devices, small_slice(): lax.all_gather(b_panel, 'factor', axis=0, tiled=True)  12.9 us
    unnamed x27, local copies, waits for them, and re-layouts  12.6 us
    ppermute x1, waiting for transfers between devices, small_slice(): d = lax.ppermute(b, 'load', [(i, i ^ 2) for i in middle])  4.97 us
    ppermute x1, waiting for transfers between devices, small_slice(): from_across = lax.ppermute(send, 'factor', [(2, 0), (3, 1)])  2.64 us
  transfers between devices with their start and end apart: 21, of which 13 were waited for; matrix products, arithmetic and copies ran while one was open for 2% of the time, Pallas kernels for 10%

profile of v1, /device:TPU:0, one launch (start us, length us, event | category | flops | bytes accessed | tf_op | source)
XLA Modules:
  0.0 127.8 jit_solution(13962604789920386656)
XLA Ops:
  10.1 6.0 %collective-permute-start = (bf16[256,256]{1,0:T(8,128)(2,1)S(1)}, bf16[256,256]{1,0:T(8,128)(2,1)S(1)}, u32[]{:S(2)}, u32[]{:S(2)}) collective-permute-start(bf16[256,256]{1,0:T(8,128)(2,1)S(1)} %get-tuple-element.21), channel_id=1, source_target_pairs={{0,7},{1,6},{2,5},{3,4},{4,3},{5,2},{6,1},{7,0},{8,15},{9,14},{10,... | collective-permute-start | bytes 393224 | tf_op jit(solution)/shard_map/ppermute | solution.py:103
  16.1 12.9 %all-gather.3.cloned.1.call-done.b_ref = bf16[2048,256]{1,0:T(8,128)(2,1)} async-done(((bf16[512,256]{1,0:T(8,128)(2,1)}), bf16[2048,256]{1,0:T(8,128)(2,1)}) %all-gather.3.cloned.1.call-update) | async-done | bytes 1048592 | tf_op jit(solution)/shard_map/all_gather | solution.py:133
  29.0 1.6 %copy-done.2 = bf16[512,2048]{1,0:T(8,128)(2,1)S(1)} copy-done((bf16[512,2048]{1,0:T(8,128)(2,1)S(1)}, bf16[512,2048]{1,0:T(8,128)(2,1)}, u32[]{:S(2)}) %copy-start.2) | copy-done | bytes 2097176
  30.6 1.2 copy-done.9
  31.8 1.4 %shard_map.95.forward_ref = bf16[512,256]{1,0:T(8,128)(2,1)} custom-call(bf16[512,2048]{1,0:T(8,128)(2,1)S(1)} %copy-done.2, bf16[2048,256]{1,0:T(8,128)(2,1)S(1)} %copy-done.9), custom_call_target="tpu_custom_call" | custom-call | flops 536870912 | bytes 3407872 | tf_op jit(solution)/shard_map/pallas_call | solution.py:22
  33.3 2.5 %collective-permute-start.1 = (bf16[256,256]{1,0:T(8,128)(2,1)S(1)}, bf16[256,256]{1,0:T(8,128)(2,1)S(1)}, u32[]{:S(2)}, u32[]{:S(2)}) collective-permute-start(bf16[256,256]{1,0:T(8,128)(2,1)S(1)} %get-tuple-element.24), channel_id=1, source_target_pairs={{0,4},{1,5},{2,6},{3,7},{4,0},{5,1},{6,2},{7,3},{8,12},{9,13},{10,... | collective-permute-start | bytes 393224 | tf_op jit(solution)/shard_map/ppermute | solution.py:103
  35.7 1.5 %collective-permute-start.2 = (bf16[256,256]{1,0:T(8,128)(2,1)S(1)}, bf16[256,256]{1,0:T(8,128)(2,1)S(1)}, u32[]{:S(2)}, u32[]{:S(2)}) collective-permute-start(bf16[256,256]{1,0:T(8,128)(2,1)S(1)} %get-tuple-element.25), channel_id=1, source_target_pairs={{0,5},{1,4},{2,7},{3,6},{4,1},{5,0},{6,3},{7,2},{8,13},{9,12},{10,... | collective-permute-start | bytes 393224 | tf_op jit(solution)/shard_map/ppermute | solution.py:103
  37.2 3.3 %collective-permute-start.3 = (bf16[256,256]{1,0:T(8,128)(2,1)S(1)}, bf16[256,256]{1,0:T(8,128)(2,1)S(1)}, u32[]{:S(2)}, u32[]{:S(2)}) collective-permute-start(bf16[256,256]{1,0:T(8,128)(2,1)S(1)} %get-tuple-element.26), channel_id=1, source_target_pairs={{0,6},{1,7},{2,4},{3,5},{4,2},{5,3},{6,0},{7,1},{8,14},{9,15},{10,... | collective-permute-start | bytes 393224 | tf_op jit(solution)/shard_map/ppermute | solution.py:103
  41.1 8.0 %collective-permute-done.1.refs_1_ = bf16[256,256]{1,0:T(8,128)(2,1)S(1)} collective-permute-done((bf16[256,256]{1,0:T(8,128)(2,1)S(1)}, bf16[256,256]{1,0:T(8,128)(2,1)S(1)}, u32[]{:S(2)}, u32[]{:S(2)}) %collective-permute-start.1) | collective-permute-done | bytes 131104 | tf_op jit(solution)/shard_map/ppermute | solution.py:103
  49.9 3.4 %copy-done.4 = bf16[2048,2048]{1,0:T(8,128)(2,1)S(1)} copy-done((bf16[2048,2048]{1,0:T(8,128)(2,1)S(1)}, bf16[2048,2048]{1,0:T(8,128)(2,1)}, u32[]{:S(2)}) %copy-start.4) | copy-done | bytes 8388632
  53.9 1.8 %shard_map.97.refs_0_ = f32[4,256,512]{2,1,0:T(8,128)S(1)} custom-call(s32[12]{0:T(128)S(1)} %pad_add_fusion.at_ref, bf16[2048,2048]{1,0:T(8,128)(2,1)S(1)} %shard_map.96.factor_ref, bf16[256,256]{1,0:T(8,128)(2,1)S(1)} %get-tuple-element.23.refs_0_, bf16[256,256]{1,0:T(8,128)(2,1)S(1)} %collective-permute-done.1.refs_1_, ...), custom_call_target="tpu_custom_call" | custom-call | flops 1073741824 | bytes 11010048 | tf_op jit(solution)/shard_map/pallas_call | solution.py:22
  56.6 1.3 shard_map.99
  58.0 1.3 shard_map.98.kept_ref
  61.3 7.8 %collective-permute-done.8.across_ref = bf16[256,512]{1,0:T(8,128)(2,1)S(1)} collective-permute-done((bf16[256,512]{1,0:T(8,128)(2,1)S(1)}, bf16[256,512]{1,0:T(8,128)(2,1)S(1)}, u32[]{:S(2)}, u32[]{:S(2)}) %collective-permute-start.8) | collective-permute-done | bytes 262176 | tf_op jit(solution)/shard_map/ppermute | solution.py:103
  70.2 1.6 %shard_map.100 = (bf16[256,512]{1,0:T(8,128)(2,1)S(1)}, bf16[2,256,512]{2,1,0:T(8,128)(2,1)S(1)}) custom-call(s32[4]{0:T(128)S(1)} %iota_xor_fusion.1.at_ref, bf16[512,256]{1,0:T(8,128)(2,1)} %shard_map.95.forward_ref, f32[2,256,512]{2,1,0:T(8,128)S(1)} %shard_map.98.kept_ref, bf16[2,256,512]{2,1,0:T(8,128)(2,1)S(1)} %copy-done.7, ...), custom_call_target="tpu_custom_call" | custom-call | flops 268435456 | bytes 4980736 | tf_op jit(solution)/shard_map/pallas_call | solution.py:22
  73.9 1.3 %collective-permute-start.10 = (bf16[256,512]{1,0:T(8,128)(2,1)S(1)}, bf16[256,512]{1,0:T(8,128)(2,1)S(1)}, u32[]{:S(2)}, u32[]{:S(2)}) collective-permute-start(bf16[256,512]{1,0:T(8,128)(2,1)S(1)} %fusion.6), channel_id=1, source_target_pairs={{16,0},{24,8},{17,1},{25,9},{18,2},{26,10},{19,3},{27,11},{20,4},{... | collective-permute-start | bytes 786440 | tf_op jit(solution)/shard_map/ppermute | solution.py:174
  76.4 1.2 copy-done.11
  77.6 3.8 %shard_map.102 = bf16[2048,256]{1,0:T(8,128)(2,1)} custom-call(bf16[2048,2048]{1,0:T(8,128)(2,1)S(1)} %copy-done.1, bf16[2048,256]{1,0:T(8,128)(2,1)S(1)} %copy-done.10, bf16[2048,256]{1,0:T(8,128)(2,1)S(1)} %copy-done.11), custom_call_target="tpu_custom_call" | custom-call | flops 2147483648 | bytes 11534336 | tf_op jit(solution)/shard_map/pallas_call | solution.py:22
  81.5 2.6 %collective-permute-done.10 = bf16[256,512]{1,0:T(8,128)(2,1)S(1)} collective-permute-done((bf16[256,512]{1,0:T(8,128)(2,1)S(1)}, bf16[256,512]{1,0:T(8,128)(2,1)S(1)}, u32[]{:S(2)}, u32[]{:S(2)}) %collective-permute-start.10) | collective-permute-done | bytes 262176 | tf_op jit(solution)/shard_map/ppermute | solution.py:174
  84.7 1.4 %collective-permute-start.12 = (bf16[256,512]{1,0:T(8,128)(2,1)S(1)}, bf16[256,512]{1,0:T(8,128)(2,1)S(1)}, u32[]{:S(2)}, u32[]{:S(2)}) collective-permute-start(bf16[256,512]{1,0:T(8,128)(2,1)S(1)} %fusion.2.refs_0_), channel_id=1, source_target_pairs={{0,2},{1,3},{2,0},{3,1},{4,6},{5,7},{6,4},{7,5},{8,10},{9,11},{10,... | collective-permute-start | bytes 786440 | tf_op jit(solution)/shard_map/ppermute | solution.py:103
  86.1 2.7 %collective-permute-start.14 = (bf16[256,512]{1,0:T(8,128)(2,1)S(1)}, bf16[256,512]{1,0:T(8,128)(2,1)S(1)}, u32[]{:S(2)}, u32[]{:S(2)}) collective-permute-start(bf16[256,512]{1,0:T(8,128)(2,1)S(1)} %fusion.2.refs_0_), channel_id=1, source_target_pairs={{0,6},{1,7},{2,4},{3,5},{4,2},{5,3},{6,0},{7,1},{8,14},{9,15},{10,... | collective-permute-start | bytes 786440 | tf_op jit(solution)/shard_map/ppermute | solution.py:103
  88.8 3.0 %collective-permute-done.11.refs_1_ = bf16[256,512]{1,0:T(8,128)(2,1)S(1)} collective-permute-done((bf16[256,512]{1,0:T(8,128)(2,1)S(1)}, bf16[256,512]{1,0:T(8,128)(2,1)S(1)}, u32[]{:S(2)}, u32[]{:S(2)}) %collective-permute-start.11) | collective-permute-done | bytes 262176 | tf_op jit(solution)/shard_map/ppermute | solution.py:103
  92.9 1.4 %collective-permute-start.16 = (bf16[256,512]{1,0:T(8,128)(2,1)S(1)}, bf16[256,512]{1,0:T(8,128)(2,1)}, u32[]{:S(2)}, u32[]{:S(2)}) collective-permute-start(bf16[256,512]{1,0:T(8,128)(2,1)S(1)} %collective-permute-done.12.refs_2_), channel_id=1, source_target_pairs={{2,4},{3,5},{4,2},{5,3},{10,12},{11,13},{12,10},{13,11},{18,20},{1... | collective-permute-start | bytes 786440 | tf_op jit(solution)/shard_map/ppermute | solution.py:193
  94.2 5.5 %collective-permute-done.14.refs_4_ = bf16[256,512]{1,0:T(8,128)(2,1)S(1)} collective-permute-done((bf16[256,512]{1,0:T(8,128)(2,1)S(1)}, bf16[256,512]{1,0:T(8,128)(2,1)S(1)}, u32[]{:S(2)}, u32[]{:S(2)}) %collective-permute-start.14) | collective-permute-done | bytes 262176 | tf_op jit(solution)/shard_map/ppermute | solution.py:103
  99.7 1.3 %collective-permute-start.17 = (bf16[256,512]{1,0:T(8,128)(2,1)S(1)}, bf16[256,512]{1,0:T(8,128)(2,1)}, u32[]{:S(2)}, u32[]{:S(2)}) collective-permute-start(bf16[256,512]{1,0:T(8,128)(2,1)S(1)} %collective-permute-done.14.refs_4_), channel_id=1, source_target_pairs={{2,0},{3,1},{4,6},{5,7},{10,8},{11,9},{12,14},{13,15},{18,16},{19,... | collective-permute-start | bytes 786440 | tf_op jit(solution)/shard_map/ppermute | solution.py:194
  101.0 1.5 %collective-permute-start.13 = (bf16[256,512]{1,0:T(8,128)(2,1)S(1)}, bf16[256,512]{1,0:T(8,128)(2,1)S(1)}, u32[]{:S(2)}, u32[]{:S(2)}) collective-permute-start(bf16[256,512]{1,0:T(8,128)(2,1)S(1)} %collective-permute-done.12.refs_2_), channel_id=1, source_target_pairs={{0,1},{1,0},{2,3},{3,2},{4,5},{5,4},{6,7},{7,6},{8,9},{9,8},{10,11... | collective-permute-start | bytes 786440 | tf_op jit(solution)/shard_map/ppermute | solution.py:103
  103.1 5.0 %collective-permute-done.17 = bf16[256,512]{1,0:T(8,128)(2,1)} collective-permute-done((bf16[256,512]{1,0:T(8,128)(2,1)S(1)}, bf16[256,512]{1,0:T(8,128)(2,1)}, u32[]{:S(2)}, u32[]{:S(2)}) %collective-permute-start.17) | collective-permute-done | bytes 262176 | tf_op jit(solution)/shard_map/ppermute | solution.py:194
  109.1 1.5 %collective-permute-start.18 = (bf16[256,512]{1,0:T(8,128)(2,1)S(1)}, bf16[256,512]{1,0:T(8,128)(2,1)}, u32[]{:S(2)}, u32[]{:S(2)}) collective-permute-start(bf16[256,512]{1,0:T(8,128)(2,1)S(1)} %broadcast_select_fusion.refs_1_), channel_id=1, source_target_pairs={{0,1},{1,0},{2,3},{3,2},{4,5},{5,4},{6,7},{7,6},{8,9},{9,8},{10,11... | collective-permute-start | bytes 786440 | tf_op jit(solution)/shard_map/ppermute | solution.py:103
  111.5 4.3 %collective-permute-done.15.refs_5_ = bf16[256,512]{1,0:T(8,128)(2,1)S(1)} collective-permute-done((bf16[256,512]{1,0:T(8,128)(2,1)S(1)}, bf16[256,512]{1,0:T(8,128)(2,1)S(1)}, u32[]{:S(2)}, u32[]{:S(2)}) %collective-permute-start.15) | collective-permute-done | bytes 262176 | tf_op jit(solution)/shard_map/ppermute | solution.py:103
  115.8 1.3 %shard_map.103.refs_0_ = f32[384,512]{1,0:T(8,128)S(1)} custom-call(s32[8]{0:T(128)S(1)} %broadcast_xor_fusion.at_ref, bf16[384,2048]{1,0:T(8,128)(2,1)S(1)} %copy-done.5, bf16[256,512]{1,0:T(8,128)(2,1)S(1)} %fusion.2.refs_0_, bf16[256,512]{1,0:T(8,128)(2,1)S(1)} %collective-permute-done.11.refs_1_, bf16[256,512]{1,0:T(8,128)(2,1)S(1)} %collective-permute-done.12.refs_2_, ...), custom_call_target="tpu_custom_call" | custom-call | flops 603979776 | bytes 3932160 | tf_op jit(solution)/shard_map/pallas_call | solution.py:22
  117.1 1.6 %collective-permute-done.18.refs_2_ = bf16[256,512]{1,0:T(8,128)(2,1)} collective-permute-done((bf16[256,512]{1,0:T(8,128)(2,1)S(1)}, bf16[256,512]{1,0:T(8,128)(2,1)}, u32[]{:S(2)}, u32[]{:S(2)}) %collective-permute-start.18) | collective-permute-done | bytes 262176 | tf_op jit(solution)/shard_map/ppermute | solution.py:103
  118.7 2.2 %shard_map.104 = f32[384,512]{1,0:T(8,128)} custom-call(s32[8]{0:T(128)S(1)} %broadcast_xor_fusion.at_ref, bf16[384,2048]{1,0:T(8,128)(2,1)S(1)} %copy-done.5, f32[384,512]{1,0:T(8,128)S(1)} %shard_map.103.refs_0_, bf16[256,512]{1,0:T(8,128)(2,1)S(1)} %broadcast_select_fusion.refs_1_, bf16[256,512]{1,0:T(8,128)(2,1)} %collective-permute-done.18.refs_2_), custom_call_target="tpu_custom_call" | custom-call | flops 201326592 | bytes 3670016 | tf_op jit(solution)/shard_map/pallas_call | solution.py:22
  (58 shorter events, 16.2 us)
Async XLA Ops:
  7.2 21.9 %all-gather.3.cloned.1.call-start = ((), (), s32[]{:S(2)}) async-start(), calls=%async_computation | async-start | bytes 1310720 | tf_op jit(solution)/shard_map/all_gather | solution.py:133
  7.9 61.2 %all-gather.5.cloned.1.call-start = ((), (), s32[]{:S(2)}) async-start(), calls=%async_computation.1 | async-start | bytes 1310720 | tf_op jit(solution)/shard_map/all_gather | solution.py:138
  8.0 1.2 copy-start.8
  10.1 23.2 %collective-permute-start = (bf16[256,256]{1,0:T(8,128)(2,1)S(1)}, bf16[256,256]{1,0:T(8,128)(2,1)S(1)}, u32[]{:S(2)}, u32[]{:S(2)}) collective-permute-start(bf16[256,256]{1,0:T(8,128)(2,1)S(1)} %get-tuple-element.21), channel_id=1, source_target_pairs={{0,7},{1,6},{2,5},{3,4},{4,3},{5,2},{6,1},{7,0},{8,15},{9,14},{10,... | collective-permute-start | bytes 393224 | tf_op jit(solution)/shard_map/ppermute | solution.py:103
  29.0 1.6 %copy-start.2 = (bf16[512,2048]{1,0:T(8,128)(2,1)S(1)}, bf16[512,2048]{1,0:T(8,128)(2,1)}, u32[]{:S(2)}) copy-start(bf16[512,2048]{1,0:T(8,128)(2,1)} %inverse_ref.5) | copy-start | bytes 6291460
  30.6 1.2 copy-start.9
  33.3 15.8 %collective-permute-start.1 = (bf16[256,256]{1,0:T(8,128)(2,1)S(1)}, bf16[256,256]{1,0:T(8,128)(2,1)S(1)}, u32[]{:S(2)}, u32[]{:S(2)}) collective-permute-start(bf16[256,256]{1,0:T(8,128)(2,1)S(1)} %get-tuple-element.24), channel_id=1, source_target_pairs={{0,4},{1,5},{2,6},{3,7},{4,0},{5,1},{6,2},{7,3},{8,12},{9,13},{10,... | collective-permute-start | bytes 393224 | tf_op jit(solution)/shard_map/ppermute | solution.py:103
  35.7 18.1 %collective-permute-start.2 = (bf16[256,256]{1,0:T(8,128)(2,1)S(1)}, bf16[256,256]{1,0:T(8,128)(2,1)S(1)}, u32[]{:S(2)}, u32[]{:S(2)}) collective-permute-start(bf16[256,256]{1,0:T(8,128)(2,1)S(1)} %get-tuple-element.25), channel_id=1, source_target_pairs={{0,5},{1,4},{2,7},{3,6},{4,1},{5,0},{6,3},{7,2},{8,13},{9,12},{10,... | collective-permute-start | bytes 393224 | tf_op jit(solution)/shard_map/ppermute | solution.py:103
  37.2 16.7 %collective-permute-start.3 = (bf16[256,256]{1,0:T(8,128)(2,1)S(1)}, bf16[256,256]{1,0:T(8,128)(2,1)S(1)}, u32[]{:S(2)}, u32[]{:S(2)}) collective-permute-start(bf16[256,256]{1,0:T(8,128)(2,1)S(1)} %get-tuple-element.26), channel_id=1, source_target_pairs={{0,6},{1,7},{2,4},{3,5},{4,2},{5,3},{6,0},{7,1},{8,14},{9,15},{10,... | collective-permute-start | bytes 393224 | tf_op jit(solution)/shard_map/ppermute | solution.py:103
  40.5 15.2 %collective-permute-start.4 = (bf16[256,256]{1,0:T(8,128)(2,1)S(1)}, bf16[256,256]{1,0:T(8,128)(2,1)S(1)}, u32[]{:S(2)}, u32[]{:S(2)}) collective-permute-start(bf16[256,256]{1,0:T(8,128)(2,1)S(1)} %get-tuple-element.28), channel_id=1, source_target_pairs={{0,1},{1,0},{2,3},{3,2},{4,5},{5,4},{6,7},{7,6},{8,9},{9,8},{10,11... | collective-permute-start | bytes 393224 | tf_op jit(solution)/shard_map/ppermute | solution.py:103
  41.1 14.7 %collective-permute-start.5 = (bf16[256,256]{1,0:T(8,128)(2,1)S(1)}, bf16[256,256]{1,0:T(8,128)(2,1)S(1)}, u32[]{:S(2)}, u32[]{:S(2)}) collective-permute-start(bf16[256,256]{1,0:T(8,128)(2,1)S(1)} %get-tuple-element.29), channel_id=1, source_target_pairs={{0,2},{1,3},{2,0},{3,1},{4,6},{5,7},{6,4},{7,5},{8,10},{9,11},{10,... | collective-permute-start | bytes 393224 | tf_op jit(solution)/shard_map/ppermute | solution.py:103
  49.1 7.5 %collective-permute-start.6 = (bf16[256,256]{1,0:T(8,128)(2,1)S(1)}, bf16[256,256]{1,0:T(8,128)(2,1)S(1)}, u32[]{:S(2)}, u32[]{:S(2)}) collective-permute-start(bf16[256,256]{1,0:T(8,128)(2,1)S(1)} %get-tuple-element.30), channel_id=1, source_target_pairs={{0,3},{1,2},{2,1},{3,0},{4,7},{5,6},{6,5},{7,4},{8,11},{9,10},{10,... | collective-permute-start | bytes 393224 | tf_op jit(solution)/shard_map/ppermute | solution.py:103
  49.9 3.4 %copy-start.4 = (bf16[2048,2048]{1,0:T(8,128)(2,1)S(1)}, bf16[2048,2048]{1,0:T(8,128)(2,1)}, u32[]{:S(2)}) copy-start(bf16[2048,2048]{1,0:T(8,128)(2,1)} %factor_ref.1) | copy-start | bytes 25165828
  53.8 4.2 %copy-start = (bf16[2048,2048]{1,0:T(8,128)(2,1)}, bf16[2048,2048]{1,0:T(8,128)(2,1)S(1)}, u32[]{:S(2)}) copy-start(bf16[2048,2048]{1,0:T(8,128)(2,1)S(1)} %shard_map.96.factor_ref) | copy-start | bytes 25165828
  57.9 2.0 %collective-permute-start.7 = (bf16[2,256,512]{2,1,0:T(8,128)(2,1)S(1)}, bf16[2,256,512]{2,1,0:T(8,128)(2,1)S(1)}, u32[]{:S(2)}, u32[]{:S(2)}) collective-permute-start(bf16[2,256,512]{2,1,0:T(8,128)(2,1)S(1)} %shard_map.99), channel_id=1, source_target_pairs={{0,8},{8,0},{16,24},{24,16},{1,9},{9,1},{17,25},{25,17},{2,10},{10... | collective-permute-start | bytes 1572872 | tf_op jit(solution)/shard_map/ppermute | solution.py:103
  58.0 11.1 %copy-start.3 = (bf16[512,2048]{1,0:T(8,128)(2,1)S(1)}, bf16[512,2048]{1,0:T(8,128)(2,1)}, u32[]{:S(2)}) copy-start(bf16[512,2048]{1,0:T(8,128)(2,1)} %inverse_ref.5) | copy-start | bytes 6291460
  60.8 8.3 %collective-permute-start.8 = (bf16[256,512]{1,0:T(8,128)(2,1)S(1)}, bf16[256,512]{1,0:T(8,128)(2,1)S(1)}, u32[]{:S(2)}, u32[]{:S(2)}) collective-permute-start(bf16[256,512]{1,0:T(8,128)(2,1)S(1)} %fusion.5), channel_id=1, source_target_pairs={{0,16},{8,24},{16,0},{24,8},{1,17},{9,25},{17,1},{25,9},{2,18},{10... | collective-permute-start | bytes 786440 | tf_op jit(solution)/shard_map/ppermute | solution.py:103
  70.2 5.0 %copy-start.1 = (bf16[2048,2048]{1,0:T(8,128)(2,1)S(1)}, bf16[2048,2048]{1,0:T(8,128)(2,1)}, u32[]{:S(2)}) copy-start(bf16[2048,2048]{1,0:T(8,128)(2,1)} %copy-done) | copy-start | bytes 25165828
  71.8 2.0 %collective-permute-start.9 = (bf16[2,256,512]{2,1,0:T(8,128)(2,1)S(1)}, bf16[2,256,512]{2,1,0:T(8,128)(2,1)S(1)}, u32[]{:S(2)}, u32[]{:S(2)}) collective-permute-start(bf16[2,256,512]{2,1,0:T(8,128)(2,1)S(1)} %get-tuple-element.33), channel_id=1, source_target_pairs={{0,8},{8,0},{16,24},{24,16},{1,9},{9,1},{17,25},{25,17},{2,10},{10... | collective-permute-start | bytes 1572872 | tf_op jit(solution)/shard_map/ppermute | solution.py:103
  73.9 10.2 %collective-permute-start.10 = (bf16[256,512]{1,0:T(8,128)(2,1)S(1)}, bf16[256,512]{1,0:T(8,128)(2,1)S(1)}, u32[]{:S(2)}, u32[]{:S(2)}) collective-permute-start(bf16[256,512]{1,0:T(8,128)(2,1)S(1)} %fusion.6), channel_id=1, source_target_pairs={{16,0},{24,8},{17,1},{25,9},{18,2},{26,10},{19,3},{27,11},{20,4},{... | collective-permute-start | bytes 786440 | tf_op jit(solution)/shard_map/ppermute | solution.py:174
  75.2 1.2 copy-start.10
  76.4 1.2 copy-start.11
  81.4 29.2 %copy-start.12 = (s32[8]{0:T(128)S(1)}, s32[8]{0:T(128)}, u32[]{:S(2)}) copy-start(s32[8]{0:T(128)} %constant.14.clone) | copy-start | bytes 100
  81.5 34.3 %copy-start.5 = (bf16[384,2048]{1,0:T(8,128)(2,1)S(1)}, bf16[384,2048]{1,0:T(8,128)(2,1)}, u32[]{:S(2)}) copy-start(bf16[384,2048]{1,0:T(8,128)(2,1)} %axle_ref.3) | copy-start | bytes 4718596
  84.2 7.6 %collective-permute-start.11 = (bf16[256,512]{1,0:T(8,128)(2,1)S(1)}, bf16[256,512]{1,0:T(8,128)(2,1)S(1)}, u32[]{:S(2)}, u32[]{:S(2)}) collective-permute-start(bf16[256,512]{1,0:T(8,128)(2,1)S(1)} %fusion.2.refs_0_), channel_id=1, source_target_pairs={{0,1},{1,0},{2,3},{3,2},{4,5},{5,4},{6,7},{7,6},{8,9},{9,8},{10,11... | collective-permute-start | bytes 786440 | tf_op jit(solution)/shard_map/ppermute | solution.py:103
  84.7 8.2 %collective-permute-start.12 = (bf16[256,512]{1,0:T(8,128)(2,1)S(1)}, bf16[256,512]{1,0:T(8,128)(2,1)S(1)}, u32[]{:S(2)}, u32[]{:S(2)}) collective-permute-start(bf16[256,512]{1,0:T(8,128)(2,1)S(1)} %fusion.2.refs_0_), channel_id=1, source_target_pairs={{0,2},{1,3},{2,0},{3,1},{4,6},{5,7},{6,4},{7,5},{8,10},{9,11},{10,... | collective-permute-start | bytes 786440 | tf_op jit(solution)/shard_map/ppermute | solution.py:103
  86.1 13.6 %collective-permute-start.14 = (bf16[256,512]{1,0:T(8,128)(2,1)S(1)}, bf16[256,512]{1,0:T(8,128)(2,1)S(1)}, u32[]{:S(2)}, u32[]{:S(2)}) collective-permute-start(bf16[256,512]{1,0:T(8,128)(2,1)S(1)} %fusion.2.refs_0_), channel_id=1, source_target_pairs={{0,6},{1,7},{2,4},{3,5},{4,2},{5,3},{6,0},{7,1},{8,14},{9,15},{10,... | collective-permute-start | bytes 786440 | tf_op jit(solution)/shard_map/ppermute | solution.py:103
  92.9 10.3 %collective-permute-start.16 = (bf16[256,512]{1,0:T(8,128)(2,1)S(1)}, bf16[256,512]{1,0:T(8,128)(2,1)}, u32[]{:S(2)}, u32[]{:S(2)}) collective-permute-start(bf16[256,512]{1,0:T(8,128)(2,1)S(1)} %collective-permute-done.12.refs_2_), channel_id=1, source_target_pairs={{2,4},{3,5},{4,2},{5,3},{10,12},{11,13},{12,10},{13,11},{18,20},{1... | collective-permute-start | bytes 786440 | tf_op jit(solution)/shard_map/ppermute | solution.py:193
  99.7 8.4 %collective-permute-start.17 = (bf16[256,512]{1,0:T(8,128)(2,1)S(1)}, bf16[256,512]{1,0:T(8,128)(2,1)}, u32[]{:S(2)}, u32[]{:S(2)}) collective-permute-start(bf16[256,512]{1,0:T(8,128)(2,1)S(1)} %collective-permute-done.14.refs_4_), channel_id=1, source_target_pairs={{2,0},{3,1},{4,6},{5,7},{10,8},{11,9},{12,14},{13,15},{18,16},{19,... | collective-permute-start | bytes 786440 | tf_op jit(solution)/shard_map/ppermute | solution.py:194
  101.0 10.4 %collective-permute-start.13 = (bf16[256,512]{1,0:T(8,128)(2,1)S(1)}, bf16[256,512]{1,0:T(8,128)(2,1)S(1)}, u32[]{:S(2)}, u32[]{:S(2)}) collective-permute-start(bf16[256,512]{1,0:T(8,128)(2,1)S(1)} %collective-permute-done.12.refs_2_), channel_id=1, source_target_pairs={{0,1},{1,0},{2,3},{3,2},{4,5},{5,4},{6,7},{7,6},{8,9},{9,8},{10,11... | collective-permute-start | bytes 786440 | tf_op jit(solution)/shard_map/ppermute | solution.py:103
  102.6 13.2 %collective-permute-start.15 = (bf16[256,512]{1,0:T(8,128)(2,1)S(1)}, bf16[256,512]{1,0:T(8,128)(2,1)S(1)}, u32[]{:S(2)}, u32[]{:S(2)}) collective-permute-start(bf16[256,512]{1,0:T(8,128)(2,1)S(1)} %collective-permute-done.14.refs_4_), channel_id=1, source_target_pairs={{0,1},{1,0},{2,3},{3,2},{4,5},{5,4},{6,7},{7,6},{8,9},{9,8},{10,11... | collective-permute-start | bytes 786440 | tf_op jit(solution)/shard_map/ppermute | solution.py:103
  109.1 9.6 %collective-permute-start.18 = (bf16[256,512]{1,0:T(8,128)(2,1)S(1)}, bf16[256,512]{1,0:T(8,128)(2,1)}, u32[]{:S(2)}, u32[]{:S(2)}) collective-permute-start(bf16[256,512]{1,0:T(8,128)(2,1)S(1)} %broadcast_select_fusion.refs_1_), channel_id=1, source_target_pairs={{0,1},{1,0},{2,3},{3,2},{4,5},{5,4},{6,7},{7,6},{8,9},{9,8},{10,11... | collective-permute-start | bytes 786440 | tf_op jit(solution)/shard_map/ppermute | solution.py:103
  (2 other events, 1.8 us)
Sparse Core Ops, SparseCore 0:
  9.6 19.4 all-gather.2
  33.4 16.7 all-gather.4

commit v2 on v1

--- a/solution.py
+++ b/solution.py
@@ -37,17 +37,26 @@
     return jnp.dot(a, b, preferred_element_type=F32)
 
 
-def forward_kernel(inverse_ref, b_ref, out_ref):
-    out_ref[...] = dot(inverse_ref[...], b_ref[...]).astype(out_ref.dtype)
-
-
-def update_kernel(factor_ref, rhs_ref, forward_ref, out_ref):
-    rows = 512
+def forward_kernel(at_ref, inverse_ref, *refs):
+    blocks, out_ref = refs[:-1], refs[-1]
+    rows = out_ref.shape[0]
+    total = None
+    for j, block in enumerate(blocks):
+        term = dot(inverse_ref[:, part(at_ref[j], rows)], block[...])
+        total = term if total is None else total + term
+    out_ref[...] = total.astype(out_ref.dtype)
+
+
+def update_kernel(at_ref, factor_ref, rhs_ref, *refs):
+    blocks, out_ref = refs[:-1], refs[-1]
+    rows = blocks[0].shape[0]
 
     @pl.loop(0, out_ref.shape[0] // rows)
     def _(i):
         here = part(i, rows)
-        total = rhs_ref[here, :].astype(F32) - dot(factor_ref[here, :], forward_ref[...])
+        total = rhs_ref[here, :].astype(F32)
+        for j, block in enumerate(blocks):
+            total = total - dot(factor_ref[here, part(at_ref[j], rows)], block[...])
         out_ref[here, :] = total.astype(out_ref.dtype)
 
 
@@ -115,8 +124,11 @@
 
     depth = update_solution.shape[0]
     pieces = call(split_kernel, spread, [update_solution], [((cols, depth), BF16)] * loads, 0)
-    early = [pieces[0]] + [by_xor(pieces[k], "load", loads, k) for k in (4, 5, 6)]
-    late = [by_xor(pieces[k], "load", loads, k) for k in (7, 1, 2, 3)]
+    early, late = [pieces[0]], [by_xor(pieces[7], "load", loads, 7)]
+    for k in (4, 5, 6):
+        block, piece = lax.optimization_barrier((by_xor(pieces[k], "load", loads, k), pieces[k - 3]))
+        early.append(block)
+        late.append(by_xor(piece, "load", loads, k - 3))
     held = pl.pallas_call(
         hold_kernel,
         out_shape=jax.ShapeDtypeStruct((updates, panel), BF16),
@@ -127,15 +139,17 @@
         cost_estimate=pl.CostEstimate(flops=0, bytes_accessed=2 * updates * panel, transcendentals=0),
     )(update_factor)
 
+    b_across = lax.ppermute(b_panel, "factor", [(0, 2), (1, 3)])
+    b_core = by_xor(b_panel, "factor", factors, 1)
+    b_far = lax.ppermute(b_across, "factor", [(2, 3), (3, 2)])
     (forward,) = call(
         forward_kernel,
-        None,
-        [panel_inverse, lax.all_gather(b_panel, "factor", axis=0, tiled=True)],
+        at_factor,
+        [panel_inverse, b_panel, b_core, b_across, b_far],
         [((rows, cols), BF16)],
         2 * rows * panel * cols,
     )
-    late[0], forward = lax.optimization_barrier((late[0], forward))
-    forward_all = lax.all_gather(forward, "factor", axis=0, tiled=True)
+    late[3], forward = lax.optimization_barrier((late[3], forward))
 
     pair = (2, cols, rows)
     at_coupled = jnp.concatenate([at_factor, spread])
@@ -157,7 +171,6 @@
     kept = coupled((0, 2), (11, 5, 6, 7), (2, 3), [begun], late, F32)
     send = (kept[1] + from_core[1].astype(F32)).astype(BF16)
     from_across = by_xor(send, "factor", factors, 2)
-    from_across, forward_all = lax.optimization_barrier((from_across, forward_all))
 
     reduced, send = call(
         reduce_kernel,
@@ -171,15 +184,18 @@
         solve_kernel, at_factor, [reduced, panel_inverse], [(pair, F32)], 4 * cols * rows * rows
     )
     send = (kept[1] + from_core[1].astype(F32)).astype(BF16)
+    send, forward = lax.optimization_barrier((send, forward))
     from_across = lax.ppermute(send, "factor", [(2, 0), (3, 1)])
+    forward_across = by_xor(forward, "factor", factors, 2)
+    forward_core = by_xor(forward, "factor", factors, 1)
+    forward_far = by_xor(forward_across, "factor", factors, 1)
     (update_rhs,) = call(
         update_kernel,
-        None,
-        [held, b_update, forward_all],
+        at_factor,
+        [held, b_update, forward, forward_core, forward_across, forward_far],
         [((updates, cols), BF16)],
         2 * updates * panel * cols,
     )
-    from_across, update_rhs = lax.optimization_barrier((from_across, update_rhs))
     solution_t = (kept[0] + from_core[0].astype(F32) + from_across.astype(F32)).astype(BF16)
     panel_solution = solution_t.T
 
@@ -190,6 +206,7 @@
     b = by_xor(own, "load", loads, 6)
     own_x, a = lax.optimization_barrier((own_x, a))
     a_x = by_xor(a, "load", loads, 1)
+    b, a_x = lax.optimization_barrier((b, a_x))
     c = lax.ppermute(a, "load", [(i, i ^ 6) for i in middle])
     d = lax.ppermute(b, "load", [(i, i ^ 2) for i in middle])
     b_x = by_xor(b, "load", loads, 1)

time: 128 us -> 104 us (0.81)
  between operations: 14.3 us -> 0.97 us
  waiting for transfers between devices: 55 us -> 45.7 us
  local copies, waits for them, and re-layouts: 12.6 us -> 9.55 us
    all_gather x2 -> x0, waiting for transfers between devices: 12.9 us -> none  [the longest x1 12.9 us: small_slice(): lax.all_gather(b_panel, 'factor', axis=0, tiled=True)]
    ppermute x1, waiting for transfers between devices: 2.64 us -> 8.94 us  [small_slice(): from_across = lax.ppermute(send, 'factor', [(2, 0), (3, 1)])]
    ppermute x0 -> x2, starting transfers between devices: none -> 5.56 us  [the longest x1 4.89 us: small_slice(): b_across = lax.ppermute(b_panel, 'factor', [(0, 2), (1, 3)])]
    ppermute x16 -> x20, starting transfers between devices: 23.5 us -> 19.7 us  [by_xor(): return lax.ppermute(value, axis, [(i, i ^ bits) for i in range(size)])]
    unnamed x27 -> x21, local copies, waits for them, and re-layouts: 12.6 us -> 9.55 us
    ppermute x16 -> x20, waiting for transfers between devices: 33.7 us -> 32.4 us  [by_xor(): return lax.ppermute(value, axis, [(i, i ^ bits) for i in range(size)])]
  transfers between devices with their start and end apart: 21 -> 25, of which waited for: 13 -> 12; matrix products, arithmetic and copies ran while one was open for 2% -> 2% of each run, Pallas kernels for 10% -> 13%
where the time goes in v2:
time: 104 us
  waiting for transfers between devices  45.7 us (44%)
  starting transfers between devices  28.5 us (27%)
  Pallas kernels  18 us (17%)
  local copies, waits for them, and re-layouts  9.55 us (9%)
  other arithmetic  1.32 us (1%)
    ppermute x20, waiting for transfers between devices, by_xor(): return lax.ppermute(value, axis, [(i, i ^ bits) for i in range(size)])  32.4 us
    ppermute x20, starting transfers between devices, by_xor(): return lax.ppermute(value, axis, [(i, i ^ bits) for i in range(size)])  19.7 us
    pallas_call x10, Pallas kernels, call(): pl.pallas_call(kernel, out_shape=shapes, in_specs=[SMEM] * len(at) + [VME...  17.4 us
    unnamed x21, local copies, waits for them, and re-layouts  9.55 us
    ppermute x1, waiting for transfers between devices, small_slice(): from_across = lax.ppermute(send, 'factor', [(2, 0), (3, 1)])  8.94 us
    ppermute x1, starting transfers between devices, small_slice(): b_across = lax.ppermute(b_panel, 'factor', [(0, 2), (1, 3)])  4.89 us
    ppermute x1, waiting for transfers between devices, small_slice(): d = lax.ppermute(b, 'load', [(i, i ^ 2) for i in middle])  4.31 us
  transfers between devices with their start and end apart: 25, of which 12 were waited for; matrix products, arithmetic and copies ran while one was open for 2% of the time, Pallas kernels for 13%

profile of v2, /device:TPU:0, one launch (start us, length us, event | category | flops | bytes accessed | tf_op | source)
XLA Modules:
  0.0 104.0 jit_solution(15532998841819731786)
XLA Ops:
  0.6 4.9 %collective-permute-start.3 = (bf16[512,256]{1,0:T(8,128)(2,1)}, bf16[512,256]{1,0:T(8,128)(2,1)S(1)}, u32[]{:S(2)}, u32[]{:S(2)}) collective-permute-start(bf16[512,256]{1,0:T(8,128)(2,1)} %refs_0_.1), channel_id=1, source_target_pairs={{0,16},{8,24},{1,17},{9,25},{2,18},{10,26},{3,19},{11,27},{4,20},{... | collective-permute-start | bytes 786440 | tf_op jit(solution)/shard_map/ppermute | solution.py:142
  5.6 1.2 %copy-done.6 = bf16[256,2048]{1,0:T(8,128)(2,1)S(1)} copy-done((bf16[256,2048]{1,0:T(8,128)(2,1)S(1)}, bf16[256,2048]{1,0:T(8,128)(2,1)}, u32[]{:S(2)}) %copy-start.6) | copy-done | bytes 1048600
  7.7 3.7 %collective-permute-start = (bf16[256,256]{1,0:T(8,128)(2,1)S(1)}, bf16[256,256]{1,0:T(8,128)(2,1)S(1)}, u32[]{:S(2)}, u32[]{:S(2)}) collective-permute-start(bf16[256,256]{1,0:T(8,128)(2,1)S(1)} %get-tuple-element.27), channel_id=1, source_target_pairs={{0,6},{1,7},{2,4},{3,5},{4,2},{5,3},{6,0},{7,1},{8,14},{9,15},{10,... | collective-permute-start | bytes 393224 | tf_op jit(solution)/shard_map/ppermute | solution.py:112
  11.4 3.8 %collective-permute-start.6 = (bf16[256,256]{1,0:T(8,128)(2,1)S(1)}, bf16[256,256]{1,0:T(8,128)(2,1)S(1)}, u32[]{:S(2)}, u32[]{:S(2)}) collective-permute-start(bf16[256,256]{1,0:T(8,128)(2,1)S(1)} %get-tuple-element.35), channel_id=1, source_target_pairs={{0,5},{1,4},{2,7},{3,6},{4,1},{5,0},{6,3},{7,2},{8,13},{9,12},{10,... | collective-permute-start | bytes 393224 | tf_op jit(solution)/shard_map/ppermute | solution.py:112
  15.9 3.4 %copy-done.3 = bf16[2048,2048]{1,0:T(8,128)(2,1)S(1)} copy-done((bf16[2048,2048]{1,0:T(8,128)(2,1)S(1)}, bf16[2048,2048]{1,0:T(8,128)(2,1)}, u32[]{:S(2)}) %copy-start.3) | copy-done | bytes 8388632
  20.6 8.5 %collective-permute-done.5.refs_1_ = bf16[256,256]{1,0:T(8,128)(2,1)S(1)} collective-permute-done((bf16[256,256]{1,0:T(8,128)(2,1)S(1)}, bf16[256,256]{1,0:T(8,128)(2,1)S(1)}, u32[]{:S(2)}, u32[]{:S(2)}) %collective-permute-start.5) | collective-permute-done | bytes 131104 | tf_op jit(solution)/shard_map/ppermute | solution.py:112
  29.7 3.1 %collective-permute-done.6.refs_2_ = bf16[256,256]{1,0:T(8,128)(2,1)S(1)} collective-permute-done((bf16[256,256]{1,0:T(8,128)(2,1)S(1)}, bf16[256,256]{1,0:T(8,128)(2,1)S(1)}, u32[]{:S(2)}, u32[]{:S(2)}) %collective-permute-start.6) | collective-permute-done | bytes 131104 | tf_op jit(solution)/shard_map/ppermute | solution.py:112
  33.4 1.8 %shard_map.97.refs_0_ = f32[4,256,512]{2,1,0:T(8,128)S(1)} custom-call(s32[12]{0:T(128)S(1)} %pad_add_fusion.at_ref, bf16[2048,2048]{1,0:T(8,128)(2,1)S(1)} %shard_map.94.factor_ref, bf16[256,256]{1,0:T(8,128)(2,1)S(1)} %get-tuple-element.31.refs_0_, bf16[256,256]{1,0:T(8,128)(2,1)S(1)} %collective-permute-done.5.refs_1_, ...), custom_call_target="tpu_custom_call" | custom-call | flops 1073741824 | bytes 11010048 | tf_op jit(solution)/shard_map/pallas_call | solution.py:22
  35.3 1.3 %shard_map.96.forward_ref.refs_0_ = bf16[512,256]{1,0:T(8,128)(2,1)S(1)} custom-call(s32[4]{0:T(128)S(1)} %iota_xor_fusion.1.at_ref, bf16[512,2048]{1,0:T(8,128)(2,1)S(1)} %copy-done.2, bf16[512,256]{1,0:T(8,128)(2,1)S(1)} %copy-done.7, bf16[512,256]{1,0:T(8,128)(2,1)S(1)} %collective-permute-done.2.refs_1_, ...), custom_call_target="tpu_custom_call" | custom-call | flops 536870912 | bytes 3407872 | tf_op jit(solution)/shard_map/pallas_call | solution.py:22
  36.6 1.5 %collective-permute-done.8.refs_2_ = bf16[256,256]{1,0:T(8,128)(2,1)S(1)} collective-permute-done((bf16[256,256]{1,0:T(8,128)(2,1)S(1)}, bf16[256,256]{1,0:T(8,128)(2,1)S(1)}, u32[]{:S(2)}, u32[]{:S(2)}) %collective-permute-start.8) | collective-permute-done | bytes 131104 | tf_op jit(solution)/shard_map/ppermute | solution.py:112
  38.4 1.3 %shard_map.99 = bf16[2,256,512]{2,1,0:T(8,128)(2,1)S(1)} custom-call(s32[12]{0:T(128)S(1)} %pad_add_fusion.at_ref, bf16[2048,2048]{1,0:T(8,128)(2,1)S(1)} %shard_map.94.factor_ref, f32[4,256,512]{2,1,0:T(8,128)S(1)} %shard_map.97.refs_0_, bf16[256,256]{1,0:T(8,128)(2,1)S(1)} %collective-permute-done.7.refs_1_, ...), custom_call_target="tpu_custom_call" | custom-call | flops 536870912 | bytes 11534336 | tf_op jit(solution)/shard_map/pallas_call | solution.py:22
  39.8 1.3 %shard_map.98.kept_ref = f32[2,256,512]{2,1,0:T(8,128)S(1)} custom-call(s32[12]{0:T(128)S(1)} %pad_add_fusion.at_ref, bf16[2048,2048]{1,0:T(8,128)(2,1)S(1)} %shard_map.94.factor_ref, f32[4,256,512]{2,1,0:T(8,128)S(1)} %shard_map.97.refs_0_, bf16[256,256]{1,0:T(8,128)(2,1)S(1)} %collective-permute-done.7.refs_1_, ...), custom_call_target="tpu_custom_call" | custom-call | flops 536870912 | bytes 12058624 | tf_op jit(solution)/shard_map/pallas_call | solution.py:22
  41.8 8.3 %collective-permute-done.11.across_ref = bf16[256,512]{1,0:T(8,128)(2,1)S(1)} collective-permute-done((bf16[256,512]{1,0:T(8,128)(2,1)S(1)}, bf16[256,512]{1,0:T(8,128)(2,1)S(1)}, u32[]{:S(2)}, u32[]{:S(2)}) %collective-permute-start.11) | collective-permute-done | bytes 262176 | tf_op jit(solution)/shard_map/ppermute | solution.py:112
  50.1 1.0 %shard_map.100 = (bf16[256,512]{1,0:T(8,128)(2,1)S(1)}, bf16[2,256,512]{2,1,0:T(8,128)(2,1)S(1)}) custom-call(s32[4]{0:T(128)S(1)} %iota_xor_fusion.1.at_ref, bf16[512,256]{1,0:T(8,128)(2,1)S(1)} %shard_map.96.forward_ref.refs_0_, f32[2,256,512]{2,1,0:T(8,128)S(1)} %shard_map.98.kept_ref, bf16[2,256,512]{2,1,0:T(8,128)(2,1)S(1)} %collective-permute-done.10.core_ref, ...), custom_call_target="tpu_custom_call" | custom-call | flops 268435456 | bytes 4980736 | tf_op jit(solution)/shard_map/pallas_call | solution.py:22
  53.2 1.3 %collective-permute-start.16 = (bf16[256,512]{1,0:T(8,128)(2,1)S(1)}, bf16[256,512]{1,0:T(8,128)(2,1)S(1)}, u32[]{:S(2)}, u32[]{:S(2)}) collective-permute-start(bf16[256,512]{1,0:T(8,128)(2,1)S(1)} %fusion.6), channel_id=1, source_target_pairs={{16,0},{24,8},{17,1},{25,9},{18,2},{26,10},{19,3},{27,11},{20,4},{... | collective-permute-start | bytes 786440 | tf_op jit(solution)/shard_map/ppermute | solution.py:188
  54.5 8.9 %collective-permute-done.16 = bf16[256,512]{1,0:T(8,128)(2,1)S(1)} collective-permute-done((bf16[256,512]{1,0:T(8,128)(2,1)S(1)}, bf16[256,512]{1,0:T(8,128)(2,1)S(1)}, u32[]{:S(2)}, u32[]{:S(2)}) %collective-permute-start.16) | collective-permute-done | bytes 262176 | tf_op jit(solution)/shard_map/ppermute | solution.py:188
  63.6 1.6 %collective-permute-start.17 = (bf16[256,512]{1,0:T(8,128)(2,1)S(1)}, bf16[256,512]{1,0:T(8,128)(2,1)S(1)}, u32[]{:S(2)}, u32[]{:S(2)}) collective-permute-start(bf16[256,512]{1,0:T(8,128)(2,1)S(1)} %fusion.2.refs_0_), channel_id=1, source_target_pairs={{0,1},{1,0},{2,3},{3,2},{4,5},{5,4},{6,7},{7,6},{8,9},{9,8},{10,11... | collective-permute-start | bytes 786440 | tf_op jit(solution)/shard_map/ppermute | solution.py:112
  65.2 1.6 %collective-permute-start.18 = (bf16[256,512]{1,0:T(8,128)(2,1)S(1)}, bf16[256,512]{1,0:T(8,128)(2,1)S(1)}, u32[]{:S(2)}, u32[]{:S(2)}) collective-permute-start(bf16[256,512]{1,0:T(8,128)(2,1)S(1)} %fusion.2.refs_0_), channel_id=1, source_target_pairs={{0,2},{1,3},{2,0},{3,1},{4,6},{5,7},{6,4},{7,5},{8,10},{9,11},{10,... | collective-permute-start | bytes 786440 | tf_op jit(solution)/shard_map/ppermute | solution.py:112
  66.8 2.2 %collective-permute-start.19 = (bf16[256,512]{1,0:T(8,128)(2,1)S(1)}, bf16[256,512]{1,0:T(8,128)(2,1)S(1)}, u32[]{:S(2)}, u32[]{:S(2)}) collective-permute-start(bf16[256,512]{1,0:T(8,128)(2,1)S(1)} %fusion.2.refs_0_), channel_id=1, source_target_pairs={{0,6},{1,7},{2,4},{3,5},{4,2},{5,3},{6,0},{7,1},{8,14},{9,15},{10,... | collective-permute-start | bytes 786440 | tf_op jit(solution)/shard_map/ppermute | solution.py:112
  68.9 2.2 %collective-permute-done.17.refs_1_ = bf16[256,512]{1,0:T(8,128)(2,1)S(1)} collective-permute-done((bf16[256,512]{1,0:T(8,128)(2,1)S(1)}, bf16[256,512]{1,0:T(8,128)(2,1)S(1)}, u32[]{:S(2)}, u32[]{:S(2)}) %collective-permute-start.17) | collective-permute-done | bytes 262176 | tf_op jit(solution)/shard_map/ppermute | solution.py:112
  71.2 2.4 %collective-permute-done.18.refs_2_ = bf16[256,512]{1,0:T(8,128)(2,1)S(1)} collective-permute-done((bf16[256,512]{1,0:T(8,128)(2,1)S(1)}, bf16[256,512]{1,0:T(8,128)(2,1)S(1)}, u32[]{:S(2)}, u32[]{:S(2)}) %collective-permute-start.18) | collective-permute-done | bytes 262176 | tf_op jit(solution)/shard_map/ppermute | solution.py:112
  73.5 1.2 %collective-permute-start.20 = (bf16[256,512]{1,0:T(8,128)(2,1)S(1)}, bf16[256,512]{1,0:T(8,128)(2,1)S(1)}, u32[]{:S(2)}, u32[]{:S(2)}) collective-permute-start(bf16[256,512]{1,0:T(8,128)(2,1)S(1)} %collective-permute-done.18.refs_2_), channel_id=1, source_target_pairs={{0,1},{1,0},{2,3},{3,2},{4,5},{5,4},{6,7},{7,6},{8,9},{9,8},{10,11... | collective-permute-start | bytes 786440 | tf_op jit(solution)/shard_map/ppermute | solution.py:112
  75.4 4.5 %collective-permute-done.19.refs_4_ = bf16[256,512]{1,0:T(8,128)(2,1)S(1)} collective-permute-done((bf16[256,512]{1,0:T(8,128)(2,1)S(1)}, bf16[256,512]{1,0:T(8,128)(2,1)S(1)}, u32[]{:S(2)}, u32[]{:S(2)}) %collective-permute-start.19) | collective-permute-done | bytes 262176 | tf_op jit(solution)/shard_map/ppermute | solution.py:112
  79.9 1.3 %collective-permute-start.23 = (bf16[256,512]{1,0:T(8,128)(2,1)S(1)}, bf16[256,512]{1,0:T(8,128)(2,1)}, u32[]{:S(2)}, u32[]{:S(2)}) collective-permute-start(bf16[256,512]{1,0:T(8,128)(2,1)S(1)} %collective-permute-done.19.refs_4_), channel_id=1, source_target_pairs={{2,0},{3,1},{4,6},{5,7},{10,8},{11,9},{12,14},{13,15},{18,16},{19,... | collective-permute-start | bytes 786440 | tf_op jit(solution)/shard_map/ppermute | solution.py:211
  81.8 1.5 %collective-permute-start.21 = (bf16[256,512]{1,0:T(8,128)(2,1)S(1)}, bf16[256,512]{1,0:T(8,128)(2,1)}, u32[]{:S(2)}, u32[]{:S(2)}) collective-permute-start(bf16[256,512]{1,0:T(8,128)(2,1)S(1)} %collective-permute-done.19.refs_4_), channel_id=1, source_target_pairs={{0,1},{1,0},{2,3},{3,2},{4,5},{5,4},{6,7},{7,6},{8,9},{9,8},{10,11... | collective-permute-start | bytes 786440 | tf_op jit(solution)/shard_map/ppermute | solution.py:112
  84.0 4.3 %collective-permute-done.23 = bf16[256,512]{1,0:T(8,128)(2,1)} collective-permute-done((bf16[256,512]{1,0:T(8,128)(2,1)S(1)}, bf16[256,512]{1,0:T(8,128)(2,1)}, u32[]{:S(2)}, u32[]{:S(2)}) %collective-permute-start.23) | collective-permute-done | bytes 262176 | tf_op jit(solution)/shard_map/ppermute | solution.py:211
  88.3 1.0 broadcast_select_fusion.refs_1_
  89.3 1.5 %collective-permute-start.24 = (bf16[256,512]{1,0:T(8,128)(2,1)S(1)}, bf16[256,512]{1,0:T(8,128)(2,1)}, u32[]{:S(2)}, u32[]{:S(2)}) collective-permute-start(bf16[256,512]{1,0:T(8,128)(2,1)S(1)} %broadcast_select_fusion.refs_1_), channel_id=1, source_target_pairs={{0,1},{1,0},{2,3},{3,2},{4,5},{5,4},{6,7},{7,6},{8,9},{9,8},{10,11... | collective-permute-start | bytes 786440 | tf_op jit(solution)/shard_map/ppermute | solution.py:112
  91.7 3.4 %copy-done.1 = bf16[2048,2048]{1,0:T(8,128)(2,1)S(1)} copy-done((bf16[2048,2048]{1,0:T(8,128)(2,1)S(1)}, bf16[2048,2048]{1,0:T(8,128)(2,1)}, u32[]{:S(2)}) %copy-start.1) | copy-done | bytes 8388632
  95.0 5.0 %shard_map.102 = bf16[2048,256]{1,0:T(8,128)(2,1)} custom-call(s32[4]{0:T(128)S(1)} %iota_xor_fusion.1.at_ref, bf16[2048,2048]{1,0:T(8,128)(2,1)S(1)} %copy-done.1, bf16[2048,256]{1,0:T(8,128)(2,1)S(1)} %copy-done.5, bf16[512,256]{1,0:T(8,128)(2,1)S(1)} %shard_map.96.forward_ref.refs_0_, bf16[512,256]{1,0:T(8,128)(2,1)S(1)} %collective-permute-done.13.refs_1_, ...), custom_call_target="tpu_custom_call" | custom-call | flops 2147483648 | bytes 11534336 | tf_op jit(solution)/shard_map/pallas_call | solution.py:22
  100.0 1.7 %shard_map.103.refs_0_ = f32[384,512]{1,0:T(8,128)S(1)} custom-call(s32[8]{0:T(128)S(1)} %broadcast_xor_fusion.at_ref, bf16[384,2048]{1,0:T(8,128)(2,1)S(1)} %copy-done.4, bf16[256,512]{1,0:T(8,128)(2,1)S(1)} %fusion.2.refs_0_, bf16[256,512]{1,0:T(8,128)(2,1)S(1)} %collective-permute-done.17.refs_1_, bf16[256,512]{1,0:T(8,128)(2,1)S(1)} %collective-permute-done.18.refs_2_, ...), custom_call_target="tpu_custom_call" | custom-call | flops 603979776 | bytes 3932160 | tf_op jit(solution)/shard_map/pallas_call | solution.py:22
  101.7 2.2 %shard_map.104 = f32[384,512]{1,0:T(8,128)} custom-call(s32[8]{0:T(128)S(1)} %broadcast_xor_fusion.at_ref, bf16[384,2048]{1,0:T(8,128)(2,1)S(1)} %copy-done.4, f32[384,512]{1,0:T(8,128)S(1)} %shard_map.103.refs_0_, bf16[256,512]{1,0:T(8,128)(2,1)S(1)} %broadcast_select_fusion.refs_1_, bf16[256,512]{1,0:T(8,128)(2,1)} %collective-permute-done.24.refs_2_), custom_call_target="tpu_custom_call" | custom-call | flops 201326592 | bytes 3670016 | tf_op jit(solution)/shard_map/pallas_call | solution.py:22
  (58 shorter events, 10.2 us)
Async XLA Ops:
  0.6 14.6 %collective-permute-start.3 = (bf16[512,256]{1,0:T(8,128)(2,1)}, bf16[512,256]{1,0:T(8,128)(2,1)S(1)}, u32[]{:S(2)}, u32[]{:S(2)}) collective-permute-start(bf16[512,256]{1,0:T(8,128)(2,1)} %refs_0_.1), channel_id=1, source_target_pairs={{0,16},{8,24},{1,17},{9,25},{2,18},{10,26},{3,19},{11,27},{4,20},{... | collective-permute-start | bytes 786440 | tf_op jit(solution)/shard_map/ppermute | solution.py:142
  5.5 27.9 %collective-permute-start.2 = (bf16[512,256]{1,0:T(8,128)(2,1)}, bf16[512,256]{1,0:T(8,128)(2,1)S(1)}, u32[]{:S(2)}, u32[]{:S(2)}) collective-permute-start(bf16[512,256]{1,0:T(8,128)(2,1)} %refs_0_.1), channel_id=1, source_target_pairs={{0,8},{8,0},{16,24},{24,16},{1,9},{9,1},{17,25},{25,17},{2,10},{10... | collective-permute-start | bytes 786440 | tf_op jit(solution)/shard_map/ppermute | solution.py:112
  7.7 12.3 %collective-permute-start = (bf16[256,256]{1,0:T(8,128)(2,1)S(1)}, bf16[256,256]{1,0:T(8,128)(2,1)S(1)}, u32[]{:S(2)}, u32[]{:S(2)}) collective-permute-start(bf16[256,256]{1,0:T(8,128)(2,1)S(1)} %get-tuple-element.27), channel_id=1, source_target_pairs={{0,6},{1,7},{2,4},{3,5},{4,2},{5,3},{6,0},{7,1},{8,14},{9,15},{10,... | collective-permute-start | bytes 393224 | tf_op jit(solution)/shard_map/ppermute | solution.py:112
  11.4 17.8 %collective-permute-start.5 = (bf16[256,256]{1,0:T(8,128)(2,1)S(1)}, bf16[256,256]{1,0:T(8,128)(2,1)S(1)}, u32[]{:S(2)}, u32[]{:S(2)}) collective-permute-start(bf16[256,256]{1,0:T(8,128)(2,1)S(1)} %get-tuple-element.32), channel_id=1, source_target_pairs={{0,4},{1,5},{2,6},{3,7},{4,0},{5,1},{6,2},{7,3},{8,12},{9,13},{10,... | collective-permute-start | bytes 393224 | tf_op jit(solution)/shard_map/ppermute | solution.py:112
  11.4 21.5 %collective-permute-start.6 = (bf16[256,256]{1,0:T(8,128)(2,1)S(1)}, bf16[256,256]{1,0:T(8,128)(2,1)S(1)}, u32[]{:S(2)}, u32[]{:S(2)}) collective-permute-start(bf16[256,256]{1,0:T(8,128)(2,1)S(1)} %get-tuple-element.35), channel_id=1, source_target_pairs={{0,5},{1,4},{2,7},{3,6},{4,1},{5,0},{6,3},{7,2},{8,13},{9,12},{10,... | collective-permute-start | bytes 393224 | tf_op jit(solution)/shard_map/ppermute | solution.py:112
  15.2 20.0 %collective-permute-start.4 = (bf16[512,256]{1,0:T(8,128)(2,1)S(1)}, bf16[512,256]{1,0:T(8,128)(2,1)S(1)}, u32[]{:S(2)}, u32[]{:S(2)}) collective-permute-start(bf16[512,256]{1,0:T(8,128)(2,1)S(1)} %collective-permute-done.3.refs_2_), channel_id=1, source_target_pairs={{16,24},{24,16},{17,25},{25,17},{18,26},{26,18},{19,27},{27,19},{2... | collective-permute-start | bytes 786440 | tf_op jit(solution)/shard_map/ppermute | solution.py:144
  15.9 3.4 %copy-start.3 = (bf16[2048,2048]{1,0:T(8,128)(2,1)S(1)}, bf16[2048,2048]{1,0:T(8,128)(2,1)}, u32[]{:S(2)}) copy-start(bf16[2048,2048]{1,0:T(8,128)(2,1)} %factor_ref.1) | copy-start | bytes 25165828
  19.9 19.9 %copy-start = (bf16[2048,2048]{1,0:T(8,128)(2,1)}, bf16[2048,2048]{1,0:T(8,128)(2,1)S(1)}, u32[]{:S(2)}) copy-start(bf16[2048,2048]{1,0:T(8,128)(2,1)S(1)} %shard_map.94.factor_ref) | copy-start | bytes 25165828
  20.0 16.6 %collective-permute-start.7 = (bf16[256,256]{1,0:T(8,128)(2,1)S(1)}, bf16[256,256]{1,0:T(8,128)(2,1)S(1)}, u32[]{:S(2)}, u32[]{:S(2)}) collective-permute-start(bf16[256,256]{1,0:T(8,128)(2,1)S(1)} %get-tuple-element.39), channel_id=1, source_target_pairs={{0,7},{1,6},{2,5},{3,4},{4,3},{5,2},{6,1},{7,0},{8,15},{9,14},{10,... | collective-permute-start | bytes 393224 | tf_op jit(solution)/shard_map/ppermute | solution.py:112
  29.1 7.4 %collective-permute-start.1 = (bf16[256,256]{1,0:T(8,128)(2,1)S(1)}, bf16[256,256]{1,0:T(8,128)(2,1)S(1)}, u32[]{:S(2)}, u32[]{:S(2)}) collective-permute-start(bf16[256,256]{1,0:T(8,128)(2,1)S(1)} %get-tuple-element.29), channel_id=1, source_target_pairs={{0,3},{1,2},{2,1},{3,0},{4,7},{5,6},{6,5},{7,4},{8,11},{9,10},{10,... | collective-permute-start | bytes 393224 | tf_op jit(solution)/shard_map/ppermute | solution.py:112
  32.9 5.2 %collective-permute-start.8 = (bf16[256,256]{1,0:T(8,128)(2,1)S(1)}, bf16[256,256]{1,0:T(8,128)(2,1)S(1)}, u32[]{:S(2)}, u32[]{:S(2)}) collective-permute-start(bf16[256,256]{1,0:T(8,128)(2,1)S(1)} %get-tuple-element.40), channel_id=1, source_target_pairs={{0,1},{1,0},{2,3},{3,2},{4,5},{5,4},{6,7},{7,6},{8,9},{9,8},{10,11... | collective-permute-start | bytes 393224 | tf_op jit(solution)/shard_map/ppermute | solution.py:112
  33.4 5.0 %collective-permute-start.9 = (bf16[256,256]{1,0:T(8,128)(2,1)S(1)}, bf16[256,256]{1,0:T(8,128)(2,1)S(1)}, u32[]{:S(2)}, u32[]{:S(2)}) collective-permute-start(bf16[256,256]{1,0:T(8,128)(2,1)S(1)} %get-tuple-element.41), channel_id=1, source_target_pairs={{0,2},{1,3},{2,0},{3,1},{4,6},{5,7},{6,4},{7,5},{8,10},{9,11},{10,... | collective-permute-start | bytes 393224 | tf_op jit(solution)/shard_map/ppermute | solution.py:112
  33.4 1.8 %copy-start.7 = (bf16[512,256]{1,0:T(8,128)(2,1)S(1)}, bf16[512,256]{1,0:T(8,128)(2,1)}, u32[]{:S(2)}) copy-start(bf16[512,256]{1,0:T(8,128)(2,1)} %refs_0_.1) | copy-start | bytes 786436
  39.7 2.0 %collective-permute-start.10 = (bf16[2,256,512]{2,1,0:T(8,128)(2,1)S(1)}, bf16[2,256,512]{2,1,0:T(8,128)(2,1)S(1)}, u32[]{:S(2)}, u32[]{:S(2)}) collective-permute-start(bf16[2,256,512]{2,1,0:T(8,128)(2,1)S(1)} %shard_map.99), channel_id=1, source_target_pairs={{0,8},{8,0},{16,24},{24,16},{1,9},{9,1},{17,25},{25,17},{2,10},{10... | collective-permute-start | bytes 1572872 | tf_op jit(solution)/shard_map/ppermute | solution.py:112
  41.7 8.4 %collective-permute-start.11 = (bf16[256,512]{1,0:T(8,128)(2,1)S(1)}, bf16[256,512]{1,0:T(8,128)(2,1)S(1)}, u32[]{:S(2)}, u32[]{:S(2)}) collective-permute-start(bf16[256,512]{1,0:T(8,128)(2,1)S(1)} %fusion.5), channel_id=1, source_target_pairs={{0,16},{8,24},{16,0},{24,8},{1,17},{9,25},{17,1},{25,9},{2,18},{10... | collective-permute-start | bytes 786440 | tf_op jit(solution)/shard_map/ppermute | solution.py:112
  51.2 2.0 %collective-permute-start.12 = (bf16[2,256,512]{2,1,0:T(8,128)(2,1)S(1)}, bf16[2,256,512]{2,1,0:T(8,128)(2,1)S(1)}, u32[]{:S(2)}, u32[]{:S(2)}) collective-permute-start(bf16[2,256,512]{2,1,0:T(8,128)(2,1)S(1)} %get-tuple-element.44), channel_id=1, source_target_pairs={{0,8},{8,0},{16,24},{24,16},{1,9},{9,1},{17,25},{25,17},{2,10},{10... | collective-permute-start | bytes 1572872 | tf_op jit(solution)/shard_map/ppermute | solution.py:112
  52.3 38.5 %copy-start.9 = (s32[8]{0:T(128)S(1)}, s32[8]{0:T(128)}, u32[]{:S(2)}) copy-start(s32[8]{0:T(128)} %constant.14.clone) | copy-start | bytes 100
  52.3 39.4 %copy-start.5 = (bf16[2048,256]{1,0:T(8,128)(2,1)S(1)}, bf16[2048,256]{1,0:T(8,128)(2,1)}, u32[]{:S(2)}) copy-start(bf16[2048,256]{1,0:T(8,128)(2,1)} %rhs_ref.1) | copy-start | bytes 3145732
  53.2 10.2 %collective-permute-start.16 = (bf16[256,512]{1,0:T(8,128)(2,1)S(1)}, bf16[256,512]{1,0:T(8,128)(2,1)S(1)}, u32[]{:S(2)}, u32[]{:S(2)}) collective-permute-start(bf16[256,512]{1,0:T(8,128)(2,1)S(1)} %fusion.6), channel_id=1, source_target_pairs={{16,0},{24,8},{17,1},{25,9},{18,2},{26,10},{19,3},{27,11},{20,4},{... | collective-permute-start | bytes 786440 | tf_op jit(solution)/shard_map/ppermute | solution.py:188
  63.6 7.6 %collective-permute-start.17 = (bf16[256,512]{1,0:T(8,128)(2,1)S(1)}, bf16[256,512]{1,0:T(8,128)(2,1)S(1)}, u32[]{:S(2)}, u32[]{:S(2)}) collective-permute-start(bf16[256,512]{1,0:T(8,128)(2,1)S(1)} %fusion.2.refs_0_), channel_id=1, source_target_pairs={{0,1},{1,0},{2,3},{3,2},{4,5},{5,4},{6,7},{7,6},{8,9},{9,8},{10,11... | collective-permute-start | bytes 786440 | tf_op jit(solution)/shard_map/ppermute | solution.py:112
  65.2 8.4 %collective-permute-start.18 = (bf16[256,512]{1,0:T(8,128)(2,1)S(1)}, bf16[256,512]{1,0:T(8,128)(2,1)S(1)}, u32[]{:S(2)}, u32[]{:S(2)}) collective-permute-start(bf16[256,512]{1,0:T(8,128)(2,1)S(1)} %fusion.2.refs_0_), channel_id=1, source_target_pairs={{0,2},{1,3},{2,0},{3,1},{4,6},{5,7},{6,4},{7,5},{8,10},{9,11},{10,... | collective-permute-start | bytes 786440 | tf_op jit(solution)/shard_map/ppermute | solution.py:112
  66.8 13.1 %collective-permute-start.19 = (bf16[256,512]{1,0:T(8,128)(2,1)S(1)}, bf16[256,512]{1,0:T(8,128)(2,1)S(1)}, u32[]{:S(2)}, u32[]{:S(2)}) collective-permute-start(bf16[256,512]{1,0:T(8,128)(2,1)S(1)} %fusion.2.refs_0_), channel_id=1, source_target_pairs={{0,6},{1,7},{2,4},{3,5},{4,2},{5,3},{6,0},{7,1},{8,14},{9,15},{10,... | collective-permute-start | bytes 786440 | tf_op jit(solution)/shard_map/ppermute | solution.py:112
  73.5 6.4 %collective-permute-start.20 = (bf16[256,512]{1,0:T(8,128)(2,1)S(1)}, bf16[256,512]{1,0:T(8,128)(2,1)S(1)}, u32[]{:S(2)}, u32[]{:S(2)}) collective-permute-start(bf16[256,512]{1,0:T(8,128)(2,1)S(1)} %collective-permute-done.18.refs_2_), channel_id=1, source_target_pairs={{0,1},{1,0},{2,3},{3,2},{4,5},{5,4},{6,7},{7,6},{8,9},{9,8},{10,11... | collective-permute-start | bytes 786440 | tf_op jit(solution)/shard_map/ppermute | solution.py:112
  74.7 6.6 %collective-permute-start.14 = (bf16[512,256]{1,0:T(8,128)(2,1)S(1)}, bf16[512,256]{1,0:T(8,128)(2,1)S(1)}, u32[]{:S(2)}, u32[]{:S(2)}) collective-permute-start(bf16[512,256]{1,0:T(8,128)(2,1)S(1)} %shard_map.96.forward_ref.refs_0_), channel_id=1, source_target_pairs={{0,16},{8,24},{16,0},{24,8},{1,17},{9,25},{17,1},{25,9},{2,18},{10... | collective-permute-start | bytes 786440 | tf_op jit(solution)/shard_map/ppermute | solution.py:112
  74.7 8.5 %collective-permute-start.22 = (bf16[256,512]{1,0:T(8,128)(2,1)S(1)}, bf16[256,512]{1,0:T(8,128)(2,1)S(1)}, u32[]{:S(2)}, u32[]{:S(2)}) collective-permute-start(bf16[256,512]{1,0:T(8,128)(2,1)S(1)} %collective-permute-done.18.refs_2_), channel_id=1, source_target_pairs={{2,4},{3,5},{4,2},{5,3},{10,12},{11,13},{12,10},{13,11},{18,20},{1... | collective-permute-start | bytes 786440 | tf_op jit(solution)/shard_map/ppermute | solution.py:210
  79.9 8.4 %collective-permute-start.23 = (bf16[256,512]{1,0:T(8,128)(2,1)S(1)}, bf16[256,512]{1,0:T(8,128)(2,1)}, u32[]{:S(2)}, u32[]{:S(2)}) collective-permute-start(bf16[256,512]{1,0:T(8,128)(2,1)S(1)} %collective-permute-done.19.refs_4_), channel_id=1, source_target_pairs={{2,0},{3,1},{4,6},{5,7},{10,8},{11,9},{12,14},{13,15},{18,16},{19,... | collective-permute-start | bytes 786440 | tf_op jit(solution)/shard_map/ppermute | solution.py:211
  81.2 10.4 %collective-permute-start.13 = (bf16[512,256]{1,0:T(8,128)(2,1)S(1)}, bf16[512,256]{1,0:T(8,128)(2,1)S(1)}, u32[]{:S(2)}, u32[]{:S(2)}) collective-permute-start(bf16[512,256]{1,0:T(8,128)(2,1)S(1)} %shard_map.96.forward_ref.refs_0_), channel_id=1, source_target_pairs={{0,8},{8,0},{16,24},{24,16},{1,9},{9,1},{17,25},{25,17},{2,10},{10... | collective-permute-start | bytes 786440 | tf_op jit(solution)/shard_map/ppermute | solution.py:112
  81.3 10.3 %collective-permute-start.15 = (bf16[512,256]{1,0:T(8,128)(2,1)S(1)}, bf16[512,256]{1,0:T(8,128)(2,1)}, u32[]{:S(2)}, u32[]{:S(2)}) collective-permute-start(bf16[512,256]{1,0:T(8,128)(2,1)S(1)} %collective-permute-done.14.refs_2_), channel_id=1, source_target_pairs={{0,8},{8,0},{16,24},{24,16},{1,9},{9,1},{17,25},{25,17},{2,10},{10... | collective-permute-start | bytes 786440 | tf_op jit(solution)/shard_map/ppermute | solution.py:112
  81.8 18.2 %collective-permute-start.21 = (bf16[256,512]{1,0:T(8,128)(2,1)S(1)}, bf16[256,512]{1,0:T(8,128)(2,1)}, u32[]{:S(2)}, u32[]{:S(2)}) collective-permute-start(bf16[256,512]{1,0:T(8,128)(2,1)S(1)} %collective-permute-done.19.refs_4_), channel_id=1, source_target_pairs={{0,1},{1,0},{2,3},{3,2},{4,5},{5,4},{6,7},{7,6},{8,9},{9,8},{10,11... | collective-permute-start | bytes 786440 | tf_op jit(solution)/shard_map/ppermute | solution.py:112
  89.3 12.5 %collective-permute-start.24 = (bf16[256,512]{1,0:T(8,128)(2,1)S(1)}, bf16[256,512]{1,0:T(8,128)(2,1)}, u32[]{:S(2)}, u32[]{:S(2)}) collective-permute-start(bf16[256,512]{1,0:T(8,128)(2,1)S(1)} %broadcast_select_fusion.refs_1_), channel_id=1, source_target_pairs={{0,1},{1,0},{2,3},{3,2},{4,5},{5,4},{6,7},{7,6},{8,9},{9,8},{10,11... | collective-permute-start | bytes 786440 | tf_op jit(solution)/shard_map/ppermute | solution.py:112
  91.6 3.4 %copy-start.1 = (bf16[2048,2048]{1,0:T(8,128)(2,1)S(1)}, bf16[2048,2048]{1,0:T(8,128)(2,1)}, u32[]{:S(2)}) copy-start(bf16[2048,2048]{1,0:T(8,128)(2,1)} %copy-done) | copy-start | bytes 25165828
  95.0 5.0 %copy-start.4 = (bf16[384,2048]{1,0:T(8,128)(2,1)S(1)}, bf16[384,2048]{1,0:T(8,128)(2,1)}, u32[]{:S(2)}) copy-start(bf16[384,2048]{1,0:T(8,128)(2,1)} %axle_ref.3) | copy-start | bytes 4718596
  (3 other events, 3.8 us)

commit v3 on v2

--- a/solution.py
+++ b/solution.py
@@ -72,39 +72,57 @@
     copy.wait()
 
 
-def coupled_kernel(panel_blocks, row_blocks, first, at_ref, factor_ref, *refs):
-    pieces, out_ref = refs[-1 - len(row_blocks) : -1], refs[-1]
+def coupled_kernel(panel_blocks, row_blocks, at_ref, factor_ref, *refs):
+    pieces, out_ref = refs[:-1], refs[-1]
     depth, width = pieces[0].shape[1], out_ref.shape[2]
     for j, b in enumerate(panel_blocks):
         cols = part(at_ref[b], width)
-        total = None if first is None else refs[0][first[j]]
+        total = None
         for k, piece in zip(row_blocks, pieces):
             term = dot(piece[...], factor_ref[part(at_ref[k], depth), cols])
             total = term if total is None else total + term
-        out_ref[j] = total.astype(out_ref.dtype)
-
-
-def reduce_kernel(at_ref, forward_ref, kept_ref, core_ref, across_ref, inverse_ref, reduced_ref, send_ref):
+        out_ref[j] = total
+
+
+def finish_kernel(panel_block, row_blocks, at_ref, factor_ref, begun_ref, *refs):
+    pieces, out_ref = refs[:-1], refs[-1]
+    depth, width = pieces[0].shape[1], out_ref.shape[1]
+    total = begun_ref[panel_block]
+    for k, piece in zip(row_blocks, pieces):
+        total = total + dot(piece[...], factor_ref[part(at_ref[k], depth), part(at_ref[panel_block], width)])
+    out_ref[...] = total.astype(out_ref.dtype)
+
+
+def reduce_kernel(block, at_ref, forward_ref, kept_ref, core_ref, across_ref, inverse_ref, reduced_ref, send_ref):
     rows = reduced_ref.shape[1]
-    coupled = kept_ref[0] + core_ref[0].astype(F32) + across_ref[...].astype(F32)
+    coupled = kept_ref[...] + core_ref[...].astype(F32) + across_ref[...].astype(F32)
     reduced_ref[...] = (forward_ref[...].astype(F32).T - coupled).astype(reduced_ref.dtype)
-    for j, b in enumerate((1, 3)):
-        send_ref[j] = dot(reduced_ref[...], inverse_ref[:, part(at_ref[b], rows)]).astype(send_ref.dtype)
-
-
-def solve_kernel(at_ref, reduced_ref, inverse_ref, kept_ref):
-    rows = kept_ref.shape[2]
-    for j, b in enumerate((0, 2)):
-        kept_ref[j] = dot(reduced_ref[...], inverse_ref[:, part(at_ref[b], rows)])
-
-
-def config_kernel(first, at_ref, axle_ref, *refs):
-    out_ref = refs[-1]
-    total, shards = (None, refs[:-1]) if first == 0 else (refs[0][...], refs[1:-1])
+    term = dot(reduced_ref[...], inverse_ref[:, part(at_ref[block], rows)])
+    send_ref[...] = term.astype(send_ref.dtype)
+
+
+def solve_kernel(block, at_ref, reduced_ref, inverse_ref, out_ref):
+    term = dot(reduced_ref[...], inverse_ref[:, part(at_ref[block], out_ref.shape[1])])
+    out_ref[...] = term.astype(out_ref.dtype)
+
+
+def config_near_kernel(at_ref, axle_ref, *refs):
+    shards, out_ref = refs[:-1], refs[-1]
     cols = shards[0].shape[0]
+    total = None
     for j, shard in enumerate(shards):
-        term = dot(axle_ref[:, part(at_ref[first + j], cols)], shard[...])
+        term = dot(axle_ref[:, part(at_ref[j], cols)], shard[...])
         total = term if total is None else total + term
+    out_ref[...] = total
+
+
+def config_far_kernel(at_ref, axle_ref, near_ref, c_ref, d_ref, cx_ref, dx_ref, out_ref):
+    cols = c_ref.shape[0]
+    middle = at_ref[8] == 1
+    total = near_ref[...]
+    for j, pair in ((6, (c_ref, d_ref)), (7, (cx_ref, dx_ref))):
+        shard = jnp.where(middle, pair[0][...], pair[1][...])
+        total = total + dot(axle_ref[:, part(at_ref[j], cols)], shard)
     out_ref[...] = total
 
 
@@ -124,6 +142,7 @@
 
     depth = update_solution.shape[0]
     pieces = call(split_kernel, spread, [update_solution], [((cols, depth), BF16)] * loads, 0)
+    *pieces, b_panel = lax.optimization_barrier((*pieces, b_panel))
     early, late = [pieces[0]], [by_xor(pieces[7], "load", loads, 7)]
     for k in (4, 5, 6):
         block, piece = lax.optimization_barrier((by_xor(pieces[k], "load", loads, k), pieces[k - 3]))
@@ -141,7 +160,7 @@
 
     b_across = lax.ppermute(b_panel, "factor", [(0, 2), (1, 3)])
     b_core = by_xor(b_panel, "factor", factors, 1)
-    b_far = lax.ppermute(b_across, "factor", [(2, 3), (3, 2)])
+    b_far = lax.ppermute(b_panel, "factor", [(0, 3), (1, 2)])
     (forward,) = call(
         forward_kernel,
         at_factor,
@@ -149,44 +168,59 @@
         [((rows, cols), BF16)],
         2 * rows * panel * cols,
     )
-    late[3], forward = lax.optimization_barrier((late[3], forward))
-
-    pair = (2, cols, rows)
+    forward_across = by_xor(forward, "factor", factors, 2)
+    late[3], forward_across = lax.optimization_barrier((late[3], forward_across))
+
+    block = (cols, rows)
     at_coupled = jnp.concatenate([at_factor, spread])
-
-    def coupled(panel_blocks, row_blocks, first, before, blocks, kind):
-        shape = (len(panel_blocks), cols, rows)
+    (begun,) = call(
+        functools.partial(coupled_kernel, (0, 1, 2, 3), (4, 8, 9, 10)),
+        at_coupled,
+        [held] + early,
+        [((factors,) + block, F32)],
+        2 * cols * depth * 4 * panel,
+    )
+
+    def coupled(panel_block, kind):
         (out,) = call(
-            functools.partial(coupled_kernel, panel_blocks, row_blocks, first),
+            functools.partial(finish_kernel, panel_block, (11, 5, 6, 7)),
             at_coupled,
-            [held] + before + blocks,
-            [(shape, kind)],
-            2 * cols * rows * depth * len(panel_blocks) * len(row_blocks),
+            [held, begun] + late,
+            [(block, kind)],
+            2 * cols * depth * 4 * rows,
         )
         return out
 
-    begun = coupled((1, 3, 0, 2), (4, 8, 9, 10), None, [], early, F32)
-    send = coupled((1, 3), (11, 5, 6, 7), (0, 1), [begun], late, BF16)
-    from_core = by_xor(send, "factor", factors, 1)
-    kept = coupled((0, 2), (11, 5, 6, 7), (2, 3), [begun], late, F32)
-    send = (kept[1] + from_core[1].astype(F32)).astype(BF16)
+    from_core = by_xor(coupled(3, BF16), "factor", factors, 1)
+    send = (coupled(2, F32) + from_core.astype(F32)).astype(BF16)
     from_across = by_xor(send, "factor", factors, 2)
-
+    from_core = by_xor(coupled(1, BF16), "factor", factors, 1)
+    kept = coupled(0, F32)
+
+    work = 2 * cols * rows * rows
     reduced, send = call(
-        reduce_kernel,
+        functools.partial(reduce_kernel, 3),
         at_factor,
         [forward, kept, from_core, from_across, panel_inverse],
-        [((cols, rows), BF16), (pair, BF16)],
-        4 * cols * rows * rows,
-    )
+        [(block, BF16), (block, BF16)],
+        work,
+    )
+
+    def solved(panel_block, kind):
+        (out,) = call(
+            functools.partial(solve_kernel, panel_block),
+            at_factor,
+            [reduced, panel_inverse],
+            [(block, kind)],
+            work,
+        )
+        return out
+
     from_core = by_xor(send, "factor", factors, 1)
-    (kept,) = call(
-        solve_kernel, at_factor, [reduced, panel_inverse], [(pair, F32)], 4 * cols * rows * rows
-    )
-    send = (kept[1] + from_core[1].astype(F32)).astype(BF16)
-    send, forward = lax.optimization_barrier((send, forward))
+    send = (solved(2, F32) + from_core.astype(F32)).astype(BF16)
     from_across = lax.ppermute(send, "factor", [(2, 0), (3, 1)])
-    forward_across = by_xor(forward, "factor", factors, 2)
+    from_core = by_xor(solved(1, BF16), "factor", factors, 1)
+    kept = solved(0, F32)
     forward_core = by_xor(forward, "factor", factors, 1)
     forward_far = by_xor(forward_across, "factor", factors, 1)
     (update_rhs,) = call(
@@ -196,7 +230,8 @@
         [((updates, cols), BF16)],
         2 * updates * panel * cols,
     )
-    solution_t = (kept[0] + from_core[0].astype(F32) + from_across.astype(F32)).astype(BF16)
+    from_across, update_rhs = lax.optimization_barrier((from_across, update_rhs))
+    solution_t = (kept + from_core.astype(F32) + from_across.astype(F32)).astype(BF16)
     panel_solution = solution_t.T
 
     middle = (2, 3, 4, 5)
@@ -210,21 +245,18 @@
     c = lax.ppermute(a, "load", [(i, i ^ 6) for i in middle])
     d = lax.ppermute(b, "load", [(i, i ^ 2) for i in middle])
     b_x = by_xor(b, "load", loads, 1)
-    c = jnp.where((at_load >= 2) & (at_load < 6), c, d)
-    c_x = by_xor(c, "load", loads, 1)
-
-    axle_at = at_load ^ jnp.array([0, 1, 2, 3, 6, 7, 4, 5], jnp.int32)
+    c_x = lax.ppermute(c, "load", [(i, i ^ 1) for i in middle])
+    d_x = lax.ppermute(d, "load", [(i, i ^ 1) for i in (0, 1, 6, 7)])
+
+    in_middle = ((at_load >= 2) & (at_load < 6)).astype(jnp.int32)
+    at_axle = jnp.concatenate([at_load ^ jnp.array([0, 1, 2, 3, 6, 7, 4, 5], jnp.int32), in_middle[None]])
     response = [((axle_weights.shape[0], rows), F32)]
     work = axle_weights.size * rows
     (begun,) = call(
-        functools.partial(config_kernel, 0),
-        axle_at,
-        [axle_weights, own, own_x, a, a_x, b, b_x],
-        response,
-        3 * work // 2,
+        config_near_kernel, at_axle, [axle_weights, own, own_x, a, a_x, b, b_x], response, 3 * work // 2
     )
     (config_response,) = call(
-        functools.partial(config_kernel, 6), axle_at, [axle_weights, begun, c, c_x], response, work // 2
+        config_far_kernel, at_axle, [axle_weights, begun, c, d, c_x, d_x], response, work // 2
     )
     return (update_rhs, panel_solution, config_response)
 

time: 104 us -> 101 us (0.971)
  waiting for transfers between devices: 45.7 us -> 31.7 us
  starting transfers between devices: 28.5 us -> 39.7 us
  Pallas kernels: 18 us -> 20.3 us
  local copies, waits for them, and re-layouts: 9.55 us -> 8 us
    ppermute x20 -> x21, waiting for transfers between devices: 32.4 us -> 17.5 us  [by_xor(): return lax.ppermute(value, axis, [(i, i ^ bits) for i in range(size)])]
    ppermute x20 -> x21, starting transfers between devices: 19.7 us -> 26.7 us  [by_xor(): return lax.ppermute(value, axis, [(i, i ^ bits) for i in range(size)])]
    ppermute x1 -> x3, waiting for transfers between devices: 0.01 us -> 6.48 us  [the longest x1 3.29 us: small_slice(): d_x = lax.ppermute(d, 'load', [(i, i ^ 1) for i in (0, 1, 6, 7)])]
    ppermute x1, waiting for transfers between devices: 8.94 us -> 2.6 us  [small_slice(): from_across = lax.ppermute(send, 'factor', [(2, 0), (3, 1)])]
    ppermute x1 -> x3, starting transfers between devices: 0.67 us -> 5.1 us  [the longest x1 2.36 us: small_slice(): d_x = lax.ppermute(d, 'load', [(i, i ^ 1) for i in (0, 1, 6, 7)])]
    pallas_call x10 -> x14, Pallas kernels: 17.4 us -> 19.8 us  [call(): pl.pallas_call(kernel, out_shape=shapes, in_specs=[SMEM] * len(at) + [VME...]
    unnamed x21 -> x17, local copies, waits for them, and re-layouts: 9.55 us -> 8 us
  transfers between devices with their start and end apart: 25 -> 28, of which waited for: 12 -> 10; matrix products, arithmetic and copies ran while one was open for 2% -> 1% of each run, Pallas kernels for 13% -> 15%
where the time goes in v3:
time: 101 us
  starting transfers between devices  39.7 us (39%)
  waiting for transfers between devices  31.7 us (31%)
  Pallas kernels  20.3 us (20%)
  local copies, waits for them, and re-layouts  8 us (8%)
    ppermute x21, starting transfers between devices, by_xor(): return lax.ppermute(value, axis, [(i, i ^ bits) for i in range(size)])  26.7 us
    pallas_call x14, Pallas kernels, call(): pl.pallas_call(kernel, out_shape=shapes, in_specs=[SMEM] * len(at) + [VME...  19.8 us
    ppermute x21, waiting for transfers between devices, by_xor(): return lax.ppermute(value, axis, [(i, i ^ bits) for i in range(size)])  17.5 us
    unnamed x17, local copies, waits for them, and re-layouts  8 us
    ppermute x1, waiting for transfers between devices, small_slice(): d = lax.ppermute(b, 'load', [(i, i ^ 2) for i in middle])  5.14 us
    ppermute x1, starting transfers between devices, small_slice(): b_across = lax.ppermute(b_panel, 'factor', [(0, 2), (1, 3)])  4.45 us
    ppermute x1, waiting for transfers between devices, small_slice(): d_x = lax.ppermute(d, 'load', [(i, i ^ 1) for i in (0, 1, 6, 7)])  3.29 us
    ppermute x1, waiting for transfers between devices, small_slice(): b_far = lax.ppermute(b_panel, 'factor', [(0, 3), (1, 2)])  3.19 us
  transfers between devices with their start and end apart: 28, of which 10 were waited for; matrix products, arithmetic and copies ran while one was open for 1% of the time, Pallas kernels for 15%

profile of v3, /device:TPU:0, one launch (start us, length us, event | category | flops | bytes accessed | tf_op | source)
XLA Modules:
  0.0 101.0 jit_solution(16400000919637579098)
XLA Ops:
  0.7 1.2 %copy-done.5 = bf16[256,2048]{1,0:T(8,128)(2,1)S(1)} copy-done((bf16[256,2048]{1,0:T(8,128)(2,1)S(1)}, bf16[256,2048]{1,0:T(8,128)(2,1)}, u32[]{:S(2)}) %copy-start.5) | copy-done | bytes 1048600
  3.3 4.5 %collective-permute-start.1 = (bf16[512,256]{1,0:T(8,128)(2,1)}, bf16[512,256]{1,0:T(8,128)(2,1)S(1)}, u32[]{:S(2)}, u32[]{:S(2)}) collective-permute-start(bf16[512,256]{1,0:T(8,128)(2,1)} %refs_0_), channel_id=1, source_target_pairs={{0,16},{8,24},{1,17},{9,25},{2,18},{10,26},{3,19},{11,27},{4,20},{... | collective-permute-start | bytes 786440 | tf_op jit(solution)/shard_map/ppermute | solution.py:161
  7.7 1.4 %collective-permute-start.2 = (bf16[512,256]{1,0:T(8,128)(2,1)}, bf16[512,256]{1,0:T(8,128)(2,1)S(1)}, u32[]{:S(2)}, u32[]{:S(2)}) collective-permute-start(bf16[512,256]{1,0:T(8,128)(2,1)} %refs_0_), channel_id=1, source_target_pairs={{0,24},{8,16},{1,25},{9,17},{2,26},{10,18},{3,27},{11,19},{4,28},{... | collective-permute-start | bytes 786440 | tf_op jit(solution)/shard_map/ppermute | solution.py:163
  9.1 2.7 %collective-permute-start.3 = (bf16[256,256]{1,0:T(8,128)(2,1)S(1)}, bf16[256,256]{1,0:T(8,128)(2,1)S(1)}, u32[]{:S(2)}, u32[]{:S(2)}) collective-permute-start(bf16[256,256]{1,0:T(8,128)(2,1)S(1)} %get-tuple-element.46), channel_id=1, source_target_pairs={{0,4},{1,5},{2,6},{3,7},{4,0},{5,1},{6,2},{7,3},{8,12},{9,13},{10,... | collective-permute-start | bytes 393224 | tf_op jit(solution)/shard_map/ppermute | solution.py:130
  11.8 1.3 %collective-permute-start.4 = (bf16[256,256]{1,0:T(8,128)(2,1)S(1)}, bf16[256,256]{1,0:T(8,128)(2,1)S(1)}, u32[]{:S(2)}, u32[]{:S(2)}) collective-permute-start(bf16[256,256]{1,0:T(8,128)(2,1)S(1)} %get-tuple-element.49), channel_id=1, source_target_pairs={{0,5},{1,4},{2,7},{3,6},{4,1},{5,0},{6,3},{7,2},{8,13},{9,12},{10,... | collective-permute-start | bytes 393224 | tf_op jit(solution)/shard_map/ppermute | solution.py:130
  13.0 3.6 %collective-permute-start.5 = (bf16[256,256]{1,0:T(8,128)(2,1)S(1)}, bf16[256,256]{1,0:T(8,128)(2,1)S(1)}, u32[]{:S(2)}, u32[]{:S(2)}) collective-permute-start(bf16[256,256]{1,0:T(8,128)(2,1)S(1)} %get-tuple-element.52), channel_id=1, source_target_pairs={{0,6},{1,7},{2,4},{3,5},{4,2},{5,3},{6,0},{7,1},{8,14},{9,15},{10,... | collective-permute-start | bytes 393224 | tf_op jit(solution)/shard_map/ppermute | solution.py:130
  16.6 3.2 %collective-permute-done.2.refs_3_ = bf16[512,256]{1,0:T(8,128)(2,1)S(1)} collective-permute-done((bf16[512,256]{1,0:T(8,128)(2,1)}, bf16[512,256]{1,0:T(8,128)(2,1)S(1)}, u32[]{:S(2)}, u32[]{:S(2)}) %collective-permute-start.2) | collective-permute-done | bytes 262176 | tf_op jit(solution)/shard_map/ppermute | solution.py:163
  19.8 1.6 %copy-done = bf16[512,2048]{1,0:T(8,128)(2,1)S(1)} copy-done((bf16[512,2048]{1,0:T(8,128)(2,1)S(1)}, bf16[512,2048]{1,0:T(8,128)(2,1)}, u32[]{:S(2)}) %copy-start) | copy-done | bytes 2097176
  22.4 1.3 %shard_map.95.forward_ref.refs_0_ = bf16[512,256]{1,0:T(8,128)(2,1)S(1)} custom-call(s32[4]{0:T(128)S(1)} %iota_xor_fusion.1.at_ref, bf16[512,2048]{1,0:T(8,128)(2,1)S(1)} %copy-done, bf16[512,256]{1,0:T(8,128)(2,1)S(1)} %copy-done.6, bf16[512,256]{1,0:T(8,128)(2,1)S(1)} %collective-permute-done.refs_1_, ...), custom_call_target="tpu_custom_call" | custom-call | flops 536870912 | bytes 3407872 | tf_op jit(solution)/shard_map/pallas_call | solution.py:22
  23.6 2.0 %collective-permute-start.10 = (bf16[512,256]{1,0:T(8,128)(2,1)S(1)}, bf16[512,256]{1,0:T(8,128)(2,1)S(1)}, u32[]{:S(2)}, u32[]{:S(2)}) collective-permute-start(bf16[512,256]{1,0:T(8,128)(2,1)S(1)} %shard_map.95.forward_ref.refs_0_), channel_id=1, source_target_pairs={{0,16},{8,24},{16,0},{24,8},{1,17},{9,25},{17,1},{25,9},{2,18},{10... | collective-permute-start | bytes 786440 | tf_op jit(solution)/shard_map/ppermute | solution.py:130
  25.7 4.5 %collective-permute-start.6 = (bf16[256,256]{1,0:T(8,128)(2,1)S(1)}, bf16[256,256]{1,0:T(8,128)(2,1)S(1)}, u32[]{:S(2)}, u32[]{:S(2)}) collective-permute-start(bf16[256,256]{1,0:T(8,128)(2,1)S(1)} %get-tuple-element.55), channel_id=1, source_target_pairs={{0,7},{1,6},{2,5},{3,4},{4,3},{5,2},{6,1},{7,0},{8,15},{9,14},{10,... | collective-permute-start | bytes 393224 | tf_op jit(solution)/shard_map/ppermute | solution.py:130
  30.8 1.3 %collective-permute-start.8 = (bf16[256,256]{1,0:T(8,128)(2,1)S(1)}, bf16[256,256]{1,0:T(8,128)(2,1)S(1)}, u32[]{:S(2)}, u32[]{:S(2)}) collective-permute-start(bf16[256,256]{1,0:T(8,128)(2,1)S(1)} %get-tuple-element.57), channel_id=1, source_target_pairs={{0,2},{1,3},{2,0},{3,1},{4,6},{5,7},{6,4},{7,5},{8,10},{9,11},{10,... | collective-permute-start | bytes 393224 | tf_op jit(solution)/shard_map/ppermute | solution.py:130
  32.1 1.7 %collective-permute-start.9 = (bf16[256,256]{1,0:T(8,128)(2,1)S(1)}, bf16[256,256]{1,0:T(8,128)(2,1)S(1)}, u32[]{:S(2)}, u32[]{:S(2)}) collective-permute-start(bf16[256,256]{1,0:T(8,128)(2,1)S(1)} %get-tuple-element.58), channel_id=1, source_target_pairs={{0,3},{1,2},{2,1},{3,0},{4,7},{5,6},{6,5},{7,4},{8,11},{9,10},{10,... | collective-permute-start | bytes 393224 | tf_op jit(solution)/shard_map/ppermute | solution.py:130
  33.8 3.4 %copy-done.2 = bf16[2048,2048]{1,0:T(8,128)(2,1)S(1)} copy-done((bf16[2048,2048]{1,0:T(8,128)(2,1)S(1)}, bf16[2048,2048]{1,0:T(8,128)(2,1)}, u32[]{:S(2)}) %copy-start.2) | copy-done | bytes 8388632
  37.8 1.8 %shard_map.97.begun_ref = f32[4,256,512]{2,1,0:T(8,128)S(1)} custom-call(s32[12]{0:T(128)S(1)} %pad_add_fusion.at_ref, bf16[2048,2048]{1,0:T(8,128)(2,1)S(1)} %shard_map.96.factor_ref, bf16[256,256]{1,0:T(8,128)(2,1)S(1)} %get-tuple-element.45.refs_0_, bf16[256,256]{1,0:T(8,128)(2,1)S(1)} %collective-permute-done.3.refs_1_, ...), custom_call_target="tpu_custom_call" | custom-call | flops 1073741824 | bytes 11010048 | tf_op jit(solution)/shard_map/pallas_call | solution.py:22
  45.0 6.9 %collective-permute-done.13.across_ref = bf16[256,512]{1,0:T(8,128)(2,1)S(1)} collective-permute-done((bf16[256,512]{1,0:T(8,128)(2,1)S(1)}, bf16[256,512]{1,0:T(8,128)(2,1)S(1)}, u32[]{:S(2)}, u32[]{:S(2)}) %collective-permute-start.13) | collective-permute-done | bytes 262176 | tf_op jit(solution)/shard_map/ppermute | solution.py:130
  54.5 1.4 %collective-permute-start.15 = (bf16[256,512]{1,0:T(8,128)(2,1)S(1)}, bf16[256,512]{1,0:T(8,128)(2,1)S(1)}, u32[]{:S(2)}, u32[]{:S(2)}) collective-permute-start(bf16[256,512]{1,0:T(8,128)(2,1)S(1)} %add_convert_fusion.1), channel_id=1, source_target_pairs={{16,0},{24,8},{17,1},{25,9},{18,2},{26,10},{19,3},{27,11},{20,4},{... | collective-permute-start | bytes 786440 | tf_op jit(solution)/shard_map/ppermute | solution.py:221
  57.2 4.4 %shard_map.104 = bf16[2048,256]{1,0:T(8,128)(2,1)} custom-call(s32[4]{0:T(128)S(1)} %iota_xor_fusion.1.at_ref, bf16[2048,2048]{1,0:T(8,128)(2,1)S(1)} %shard_map.96.factor_ref, bf16[2048,256]{1,0:T(8,128)(2,1)S(1)} %copy-done.4, bf16[512,256]{1,0:T(8,128)(2,1)S(1)} %shard_map.95.forward_ref.refs_0_, bf16[512,256]{1,0:T(8,128)(2,1)S(1)} %collective-permute-done.16.refs_1_, ...), custom_call_target="tpu_custom_call" | custom-call | flops 2147483648 | bytes 11534336 | tf_op jit(solution)/shard_map/pallas_call | solution.py:22
  62.5 2.6 %collective-permute-done.15 = bf16[256,512]{1,0:T(8,128)(2,1)S(1)} collective-permute-done((bf16[256,512]{1,0:T(8,128)(2,1)S(1)}, bf16[256,512]{1,0:T(8,128)(2,1)S(1)}, u32[]{:S(2)}, u32[]{:S(2)}) %collective-permute-start.15) | collective-permute-done | bytes 262176 | tf_op jit(solution)/shard_map/ppermute | solution.py:221
  65.2 1.5 %collective-permute-start.19 = (bf16[256,512]{1,0:T(8,128)(2,1)S(1)}, bf16[256,512]{1,0:T(8,128)(2,1)S(1)}, u32[]{:S(2)}, u32[]{:S(2)}) collective-permute-start(bf16[256,512]{1,0:T(8,128)(2,1)S(1)} %add_convert_fusion.refs_0_), channel_id=1, source_target_pairs={{0,1},{1,0},{2,3},{3,2},{4,5},{5,4},{6,7},{7,6},{8,9},{9,8},{10,11... | collective-permute-start | bytes 786440 | tf_op jit(solution)/shard_map/ppermute | solution.py:130
  66.7 1.7 %collective-permute-start.20 = (bf16[256,512]{1,0:T(8,128)(2,1)S(1)}, bf16[256,512]{1,0:T(8,128)(2,1)S(1)}, u32[]{:S(2)}, u32[]{:S(2)}) collective-permute-start(bf16[256,512]{1,0:T(8,128)(2,1)S(1)} %add_convert_fusion.refs_0_), channel_id=1, source_target_pairs={{0,2},{1,3},{2,0},{3,1},{4,6},{5,7},{6,4},{7,5},{8,10},{9,11},{10,... | collective-permute-start | bytes 786440 | tf_op jit(solution)/shard_map/ppermute | solution.py:130
  68.4 1.9 %collective-permute-start.21 = (bf16[256,512]{1,0:T(8,128)(2,1)S(1)}, bf16[256,512]{1,0:T(8,128)(2,1)S(1)}, u32[]{:S(2)}, u32[]{:S(2)}) collective-permute-start(bf16[256,512]{1,0:T(8,128)(2,1)S(1)} %add_convert_fusion.refs_0_), channel_id=1, source_target_pairs={{0,6},{1,7},{2,4},{3,5},{4,2},{5,3},{6,0},{7,1},{8,14},{9,15},{10,... | collective-permute-start | bytes 786440 | tf_op jit(solution)/shard_map/ppermute | solution.py:130
  70.3 2.7 %collective-permute-done.19.refs_1_ = bf16[256,512]{1,0:T(8,128)(2,1)S(1)} collective-permute-done((bf16[256,512]{1,0:T(8,128)(2,1)S(1)}, bf16[256,512]{1,0:T(8,128)(2,1)S(1)}, u32[]{:S(2)}, u32[]{:S(2)}) %collective-permute-start.19) | collective-permute-done | bytes 262176 | tf_op jit(solution)/shard_map/ppermute | solution.py:130
  73.0 2.2 %collective-permute-done.20.refs_2_ = bf16[256,512]{1,0:T(8,128)(2,1)S(1)} collective-permute-done((bf16[256,512]{1,0:T(8,128)(2,1)S(1)}, bf16[256,512]{1,0:T(8,128)(2,1)S(1)}, u32[]{:S(2)}, u32[]{:S(2)}) %collective-permute-start.20) | collective-permute-done | bytes 262176 | tf_op jit(solution)/shard_map/ppermute | solution.py:130
  76.4 5.3 %collective-permute-done.21.refs_4_ = bf16[256,512]{1,0:T(8,128)(2,1)S(1)} collective-permute-done((bf16[256,512]{1,0:T(8,128)(2,1)S(1)}, bf16[256,512]{1,0:T(8,128)(2,1)S(1)}, u32[]{:S(2)}, u32[]{:S(2)}) %collective-permute-start.21) | collective-permute-done | bytes 262176 | tf_op jit(solution)/shard_map/ppermute | solution.py:130
  81.7 1.3 %collective-permute-start.25 = (bf16[256,512]{1,0:T(8,128)(2,1)S(1)}, bf16[256,512]{1,0:T(8,128)(2,1)S(1)}, u32[]{:S(2)}, u32[]{:S(2)}) collective-permute-start(bf16[256,512]{1,0:T(8,128)(2,1)S(1)} %collective-permute-done.21.refs_4_), channel_id=1, source_target_pairs={{2,0},{3,1},{4,6},{5,7},{10,8},{11,9},{12,14},{13,15},{18,16},{19,... | collective-permute-start | bytes 786440 | tf_op jit(solution)/shard_map/ppermute | solution.py:246
  83.9 1.4 %collective-permute-start.26 = (bf16[256,512]{1,0:T(8,128)(2,1)S(1)}, bf16[256,512]{1,0:T(8,128)(2,1)}, u32[]{:S(2)}, u32[]{:S(2)}) collective-permute-start(bf16[256,512]{1,0:T(8,128)(2,1)S(1)} %collective-permute-done.24.c_ref), channel_id=1, source_target_pairs={{2,3},{3,2},{4,5},{5,4},{10,11},{11,10},{12,13},{13,12},{18,19},{1... | collective-permute-start | bytes 786440 | tf_op jit(solution)/shard_map/ppermute | solution.py:248
  85.2 5.1 %collective-permute-done.25.d_ref = bf16[256,512]{1,0:T(8,128)(2,1)S(1)} collective-permute-done((bf16[256,512]{1,0:T(8,128)(2,1)S(1)}, bf16[256,512]{1,0:T(8,128)(2,1)S(1)}, u32[]{:S(2)}, u32[]{:S(2)}) %collective-permute-start.25) | collective-permute-done | bytes 262176 | tf_op jit(solution)/shard_map/ppermute | solution.py:246
  90.4 2.4 %collective-permute-start.27 = (bf16[256,512]{1,0:T(8,128)(2,1)S(1)}, bf16[256,512]{1,0:T(8,128)(2,1)}, u32[]{:S(2)}, u32[]{:S(2)}) collective-permute-start(bf16[256,512]{1,0:T(8,128)(2,1)S(1)} %collective-permute-done.25.d_ref), channel_id=1, source_target_pairs={{0,1},{1,0},{6,7},{7,6},{8,9},{9,8},{14,15},{15,14},{16,17},{17,16... | collective-permute-start | bytes 786440 | tf_op jit(solution)/shard_map/ppermute | solution.py:249
  93.7 1.7 %shard_map.107.near_ref = f32[384,512]{1,0:T(8,128)S(1)} custom-call(s32[9]{0:T(128)S(1)} %pad_add_fusion.1.at_ref, bf16[384,2048]{1,0:T(8,128)(2,1)S(1)} %copy-done.3, bf16[256,512]{1,0:T(8,128)(2,1)S(1)} %add_convert_fusion.refs_0_, bf16[256,512]{1,0:T(8,128)(2,1)S(1)} %collective-permute-done.19.refs_1_, ...), custom_call_target="tpu_custom_call" | custom-call | flops 603979776 | bytes 3932160 | tf_op jit(solution)/shard_map/pallas_call | solution.py:22
  95.4 3.3 %collective-permute-done.27.dx_ref = bf16[256,512]{1,0:T(8,128)(2,1)} collective-permute-done((bf16[256,512]{1,0:T(8,128)(2,1)S(1)}, bf16[256,512]{1,0:T(8,128)(2,1)}, u32[]{:S(2)}, u32[]{:S(2)}) %collective-permute-start.27) | collective-permute-done | bytes 262176 | tf_op jit(solution)/shard_map/ppermute | solution.py:249
  98.7 2.3 %shard_map.108 = f32[384,512]{1,0:T(8,128)} custom-call(s32[9]{0:T(128)S(1)} %pad_add_fusion.1.at_ref, bf16[384,2048]{1,0:T(8,128)(2,1)S(1)} %copy-done.3, f32[384,512]{1,0:T(8,128)S(1)} %shard_map.107.near_ref, bf16[256,512]{1,0:T(8,128)(2,1)S(1)} %collective-permute-done.24.c_ref, bf16[256,512]{1,0:T(8,128)(2,1)S(1)} %collective-permute-done.25.d_ref, ...), custom_call_target="tpu_custom_call" | custom-call | flops 201326592 | bytes 4194304 | tf_op jit(solution)/shard_map/pallas_call | solution.py:22
  (64 shorter events, 16.7 us)
Async XLA Ops:
  2.7 10.3 %collective-permute-start = (bf16[512,256]{1,0:T(8,128)(2,1)}, bf16[512,256]{1,0:T(8,128)(2,1)S(1)}, u32[]{:S(2)}, u32[]{:S(2)}) collective-permute-start(bf16[512,256]{1,0:T(8,128)(2,1)} %refs_0_), channel_id=1, source_target_pairs={{0,8},{8,0},{16,24},{24,16},{1,9},{9,1},{17,25},{25,17},{2,10},{10... | collective-permute-start | bytes 786440 | tf_op jit(solution)/shard_map/ppermute | solution.py:130
  3.3 13.4 %collective-permute-start.1 = (bf16[512,256]{1,0:T(8,128)(2,1)}, bf16[512,256]{1,0:T(8,128)(2,1)S(1)}, u32[]{:S(2)}, u32[]{:S(2)}) collective-permute-start(bf16[512,256]{1,0:T(8,128)(2,1)} %refs_0_), channel_id=1, source_target_pairs={{0,16},{8,24},{1,17},{9,25},{2,18},{10,26},{3,19},{11,27},{4,20},{... | collective-permute-start | bytes 786440 | tf_op jit(solution)/shard_map/ppermute | solution.py:161
  7.7 12.1 %collective-permute-start.2 = (bf16[512,256]{1,0:T(8,128)(2,1)}, bf16[512,256]{1,0:T(8,128)(2,1)S(1)}, u32[]{:S(2)}, u32[]{:S(2)}) collective-permute-start(bf16[512,256]{1,0:T(8,128)(2,1)} %refs_0_), channel_id=1, source_target_pairs={{0,24},{8,16},{1,25},{9,17},{2,26},{10,18},{3,27},{11,19},{4,28},{... | collective-permute-start | bytes 786440 | tf_op jit(solution)/shard_map/ppermute | solution.py:163
  9.1 21.1 %collective-permute-start.3 = (bf16[256,256]{1,0:T(8,128)(2,1)S(1)}, bf16[256,256]{1,0:T(8,128)(2,1)S(1)}, u32[]{:S(2)}, u32[]{:S(2)}) collective-permute-start(bf16[256,256]{1,0:T(8,128)(2,1)S(1)} %get-tuple-element.46), channel_id=1, source_target_pairs={{0,4},{1,5},{2,6},{3,7},{4,0},{5,1},{6,2},{7,3},{8,12},{9,13},{10,... | collective-permute-start | bytes 393224 | tf_op jit(solution)/shard_map/ppermute | solution.py:130
  11.8 18.4 %collective-permute-start.4 = (bf16[256,256]{1,0:T(8,128)(2,1)S(1)}, bf16[256,256]{1,0:T(8,128)(2,1)S(1)}, u32[]{:S(2)}, u32[]{:S(2)}) collective-permute-start(bf16[256,256]{1,0:T(8,128)(2,1)S(1)} %get-tuple-element.49), channel_id=1, source_target_pairs={{0,5},{1,4},{2,7},{3,6},{4,1},{5,0},{6,3},{7,2},{8,13},{9,12},{10,... | collective-permute-start | bytes 393224 | tf_op jit(solution)/shard_map/ppermute | solution.py:130
  13.0 17.2 %collective-permute-start.5 = (bf16[256,256]{1,0:T(8,128)(2,1)S(1)}, bf16[256,256]{1,0:T(8,128)(2,1)S(1)}, u32[]{:S(2)}, u32[]{:S(2)}) collective-permute-start(bf16[256,256]{1,0:T(8,128)(2,1)S(1)} %get-tuple-element.52), channel_id=1, source_target_pairs={{0,6},{1,7},{2,4},{3,5},{4,2},{5,3},{6,0},{7,1},{8,14},{9,15},{10,... | collective-permute-start | bytes 393224 | tf_op jit(solution)/shard_map/ppermute | solution.py:130
  23.6 16.2 %collective-permute-start.10 = (bf16[512,256]{1,0:T(8,128)(2,1)S(1)}, bf16[512,256]{1,0:T(8,128)(2,1)S(1)}, u32[]{:S(2)}, u32[]{:S(2)}) collective-permute-start(bf16[512,256]{1,0:T(8,128)(2,1)S(1)} %shard_map.95.forward_ref.refs_0_), channel_id=1, source_target_pairs={{0,16},{8,24},{16,0},{24,8},{1,17},{9,25},{17,1},{25,9},{2,18},{10... | collective-permute-start | bytes 786440 | tf_op jit(solution)/shard_map/ppermute | solution.py:130
  25.7 14.2 %collective-permute-start.6 = (bf16[256,256]{1,0:T(8,128)(2,1)S(1)}, bf16[256,256]{1,0:T(8,128)(2,1)S(1)}, u32[]{:S(2)}, u32[]{:S(2)}) collective-permute-start(bf16[256,256]{1,0:T(8,128)(2,1)S(1)} %get-tuple-element.55), channel_id=1, source_target_pairs={{0,7},{1,6},{2,5},{3,4},{4,3},{5,2},{6,1},{7,0},{8,15},{9,14},{10,... | collective-permute-start | bytes 393224 | tf_op jit(solution)/shard_map/ppermute | solution.py:130
  30.2 9.6 %collective-permute-start.7 = (bf16[256,256]{1,0:T(8,128)(2,1)S(1)}, bf16[256,256]{1,0:T(8,128)(2,1)S(1)}, u32[]{:S(2)}, u32[]{:S(2)}) collective-permute-start(bf16[256,256]{1,0:T(8,128)(2,1)S(1)} %get-tuple-element.56), channel_id=1, source_target_pairs={{0,1},{1,0},{2,3},{3,2},{4,5},{5,4},{6,7},{7,6},{8,9},{9,8},{10,11... | collective-permute-start | bytes 393224 | tf_op jit(solution)/shard_map/ppermute | solution.py:130
  30.8 9.0 %collective-permute-start.8 = (bf16[256,256]{1,0:T(8,128)(2,1)S(1)}, bf16[256,256]{1,0:T(8,128)(2,1)S(1)}, u32[]{:S(2)}, u32[]{:S(2)}) collective-permute-start(bf16[256,256]{1,0:T(8,128)(2,1)S(1)} %get-tuple-element.57), channel_id=1, source_target_pairs={{0,2},{1,3},{2,0},{3,1},{4,6},{5,7},{6,4},{7,5},{8,10},{9,11},{10,... | collective-permute-start | bytes 393224 | tf_op jit(solution)/shard_map/ppermute | solution.py:130
  32.1 7.7 %collective-permute-start.9 = (bf16[256,256]{1,0:T(8,128)(2,1)S(1)}, bf16[256,256]{1,0:T(8,128)(2,1)S(1)}, u32[]{:S(2)}, u32[]{:S(2)}) collective-permute-start(bf16[256,256]{1,0:T(8,128)(2,1)S(1)} %get-tuple-element.58), channel_id=1, source_target_pairs={{0,3},{1,2},{2,1},{3,0},{4,7},{5,6},{6,5},{7,4},{8,11},{9,10},{10,... | collective-permute-start | bytes 393224 | tf_op jit(solution)/shard_map/ppermute | solution.py:130
  33.8 3.4 %copy-start.2 = (bf16[2048,2048]{1,0:T(8,128)(2,1)S(1)}, bf16[2048,2048]{1,0:T(8,128)(2,1)}, u32[]{:S(2)}) copy-start(bf16[2048,2048]{1,0:T(8,128)(2,1)} %factor_ref.1) | copy-start | bytes 25165828
  40.8 2.6 %collective-permute-start.12 = (bf16[256,512]{1,0:T(8,128)(2,1)S(1)}, bf16[256,512]{1,0:T(8,128)(2,1)S(1)}, u32[]{:S(2)}, u32[]{:S(2)}) collective-permute-start(bf16[256,512]{1,0:T(8,128)(2,1)S(1)} %shard_map.101), channel_id=1, source_target_pairs={{0,8},{8,0},{16,24},{24,16},{1,9},{9,1},{17,25},{25,17},{2,10},{10... | collective-permute-start | bytes 786440 | tf_op jit(solution)/shard_map/ppermute | solution.py:130
  41.9 3.1 %collective-permute-start.11 = (bf16[256,512]{1,0:T(8,128)(2,1)S(1)}, bf16[256,512]{1,0:T(8,128)(2,1)S(1)}, u32[]{:S(2)}, u32[]{:S(2)}) collective-permute-start(bf16[256,512]{1,0:T(8,128)(2,1)S(1)} %shard_map.99), channel_id=1, source_target_pairs={{0,8},{8,0},{16,24},{24,16},{1,9},{9,1},{17,25},{25,17},{2,10},{10... | collective-permute-start | bytes 786440 | tf_op jit(solution)/shard_map/ppermute | solution.py:130
  43.6 8.3 %copy-start.1 = (bf16[512,2048]{1,0:T(8,128)(2,1)S(1)}, bf16[512,2048]{1,0:T(8,128)(2,1)}, u32[]{:S(2)}) copy-start(bf16[512,2048]{1,0:T(8,128)(2,1)} %inverse_ref.9) | copy-start | bytes 6291460
  43.6 8.3 %collective-permute-start.13 = (bf16[256,512]{1,0:T(8,128)(2,1)S(1)}, bf16[256,512]{1,0:T(8,128)(2,1)S(1)}, u32[]{:S(2)}, u32[]{:S(2)}) collective-permute-start(bf16[256,512]{1,0:T(8,128)(2,1)S(1)} %add_convert_fusion.2), channel_id=1, source_target_pairs={{0,16},{8,24},{16,0},{24,8},{1,17},{9,25},{17,1},{25,9},{2,18},{10... | collective-permute-start | bytes 786440 | tf_op jit(solution)/shard_map/ppermute | solution.py:130
  52.8 1.6 %collective-permute-start.14 = (bf16[256,512]{1,0:T(8,128)(2,1)S(1)}, bf16[256,512]{1,0:T(8,128)(2,1)S(1)}, u32[]{:S(2)}, u32[]{:S(2)}) collective-permute-start(bf16[256,512]{1,0:T(8,128)(2,1)S(1)} %get-tuple-element.61), channel_id=1, source_target_pairs={{0,8},{8,0},{16,24},{24,16},{1,9},{9,1},{17,25},{25,17},{2,10},{10... | collective-permute-start | bytes 786440 | tf_op jit(solution)/shard_map/ppermute | solution.py:130
  52.9 4.3 %collective-permute-start.16 = (bf16[512,256]{1,0:T(8,128)(2,1)S(1)}, bf16[512,256]{1,0:T(8,128)(2,1)S(1)}, u32[]{:S(2)}, u32[]{:S(2)}) collective-permute-start(bf16[512,256]{1,0:T(8,128)(2,1)S(1)} %shard_map.95.forward_ref.refs_0_), channel_id=1, source_target_pairs={{0,8},{8,0},{16,24},{24,16},{1,9},{9,1},{17,25},{25,17},{2,10},{10... | collective-permute-start | bytes 786440 | tf_op jit(solution)/shard_map/ppermute | solution.py:130
  53.4 3.8 %collective-permute-start.17 = (bf16[512,256]{1,0:T(8,128)(2,1)S(1)}, bf16[512,256]{1,0:T(8,128)(2,1)S(1)}, u32[]{:S(2)}, u32[]{:S(2)}) collective-permute-start(bf16[512,256]{1,0:T(8,128)(2,1)S(1)} %collective-permute-done.10.refs_2_), channel_id=1, source_target_pairs={{0,8},{8,0},{16,24},{24,16},{1,9},{9,1},{17,25},{25,17},{2,10},{10... | collective-permute-start | bytes 786440 | tf_op jit(solution)/shard_map/ppermute | solution.py:130
  54.5 10.6 %collective-permute-start.15 = (bf16[256,512]{1,0:T(8,128)(2,1)S(1)}, bf16[256,512]{1,0:T(8,128)(2,1)S(1)}, u32[]{:S(2)}, u32[]{:S(2)}) collective-permute-start(bf16[256,512]{1,0:T(8,128)(2,1)S(1)} %add_convert_fusion.1), channel_id=1, source_target_pairs={{16,0},{24,8},{17,1},{25,9},{18,2},{26,10},{19,3},{27,11},{20,4},{... | collective-permute-start | bytes 786440 | tf_op jit(solution)/shard_map/ppermute | solution.py:221
  56.8 8.3 %collective-permute-start.18 = (bf16[256,512]{1,0:T(8,128)(2,1)S(1)}, bf16[256,512]{1,0:T(8,128)(2,1)S(1)}, u32[]{:S(2)}, u32[]{:S(2)}) collective-permute-start(bf16[256,512]{1,0:T(8,128)(2,1)S(1)} %shard_map.106), channel_id=1, source_target_pairs={{0,8},{8,0},{16,24},{24,16},{1,9},{9,1},{17,25},{25,17},{2,10},{10... | collective-permute-start | bytes 786440 | tf_op jit(solution)/shard_map/ppermute | solution.py:130
  61.6 31.1 %copy-start.7 = (s32[8]{0:T(128)S(1)}, s32[8]{0:T(128)}, u32[]{:S(2)}) copy-start(s32[8]{0:T(128)} %constant.14.clone) | copy-start | bytes 100
  61.6 32.1 %copy-start.3 = (bf16[384,2048]{1,0:T(8,128)(2,1)S(1)}, bf16[384,2048]{1,0:T(8,128)(2,1)}, u32[]{:S(2)}) copy-start(bf16[384,2048]{1,0:T(8,128)(2,1)} %axle_ref.3) | copy-start | bytes 4718596
  65.2 7.8 %collective-permute-start.19 = (bf16[256,512]{1,0:T(8,128)(2,1)S(1)}, bf16[256,512]{1,0:T(8,128)(2,1)S(1)}, u32[]{:S(2)}, u32[]{:S(2)}) collective-permute-start(bf16[256,512]{1,0:T(8,128)(2,1)S(1)} %add_convert_fusion.refs_0_), channel_id=1, source_target_pairs={{0,1},{1,0},{2,3},{3,2},{4,5},{5,4},{6,7},{7,6},{8,9},{9,8},{10,11... | collective-permute-start | bytes 786440 | tf_op jit(solution)/shard_map/ppermute | solution.py:130
  66.7 8.5 %collective-permute-start.20 = (bf16[256,512]{1,0:T(8,128)(2,1)S(1)}, bf16[256,512]{1,0:T(8,128)(2,1)S(1)}, u32[]{:S(2)}, u32[]{:S(2)}) collective-permute-start(bf16[256,512]{1,0:T(8,128)(2,1)S(1)} %add_convert_fusion.refs_0_), channel_id=1, source_target_pairs={{0,2},{1,3},{2,0},{3,1},{4,6},{5,7},{6,4},{7,5},{8,10},{9,11},{10,... | collective-permute-start | bytes 786440 | tf_op jit(solution)/shard_map/ppermute | solution.py:130
  68.4 13.3 %collective-permute-start.21 = (bf16[256,512]{1,0:T(8,128)(2,1)S(1)}, bf16[256,512]{1,0:T(8,128)(2,1)S(1)}, u32[]{:S(2)}, u32[]{:S(2)}) collective-permute-start(bf16[256,512]{1,0:T(8,128)(2,1)S(1)} %add_convert_fusion.refs_0_), channel_id=1, source_target_pairs={{0,6},{1,7},{2,4},{3,5},{4,2},{5,3},{6,0},{7,1},{8,14},{9,15},{10,... | collective-permute-start | bytes 786440 | tf_op jit(solution)/shard_map/ppermute | solution.py:130
  75.2 6.6 %collective-permute-start.22 = (bf16[256,512]{1,0:T(8,128)(2,1)S(1)}, bf16[256,512]{1,0:T(8,128)(2,1)S(1)}, u32[]{:S(2)}, u32[]{:S(2)}) collective-permute-start(bf16[256,512]{1,0:T(8,128)(2,1)S(1)} %collective-permute-done.20.refs_2_), channel_id=1, source_target_pairs={{0,1},{1,0},{2,3},{3,2},{4,5},{5,4},{6,7},{7,6},{8,9},{9,8},{10,11... | collective-permute-start | bytes 786440 | tf_op jit(solution)/shard_map/ppermute | solution.py:130
  75.7 8.2 %collective-permute-start.24 = (bf16[256,512]{1,0:T(8,128)(2,1)S(1)}, bf16[256,512]{1,0:T(8,128)(2,1)S(1)}, u32[]{:S(2)}, u32[]{:S(2)}) collective-permute-start(bf16[256,512]{1,0:T(8,128)(2,1)S(1)} %collective-permute-done.20.refs_2_), channel_id=1, source_target_pairs={{2,4},{3,5},{4,2},{5,3},{10,12},{11,13},{12,10},{13,11},{18,20},{1... | collective-permute-start | bytes 786440 | tf_op jit(solution)/shard_map/ppermute | solution.py:245
  81.7 8.7 %collective-permute-start.25 = (bf16[256,512]{1,0:T(8,128)(2,1)S(1)}, bf16[256,512]{1,0:T(8,128)(2,1)S(1)}, u32[]{:S(2)}, u32[]{:S(2)}) collective-permute-start(bf16[256,512]{1,0:T(8,128)(2,1)S(1)} %collective-permute-done.21.refs_4_), channel_id=1, source_target_pairs={{2,0},{3,1},{4,6},{5,7},{10,8},{11,9},{12,14},{13,15},{18,16},{19,... | collective-permute-start | bytes 786440 | tf_op jit(solution)/shard_map/ppermute | solution.py:246
  83.0 10.7 %collective-permute-start.23 = (bf16[256,512]{1,0:T(8,128)(2,1)S(1)}, bf16[256,512]{1,0:T(8,128)(2,1)}, u32[]{:S(2)}, u32[]{:S(2)}) collective-permute-start(bf16[256,512]{1,0:T(8,128)(2,1)S(1)} %collective-permute-done.21.refs_4_), channel_id=1, source_target_pairs={{0,1},{1,0},{2,3},{3,2},{4,5},{5,4},{6,7},{7,6},{8,9},{9,8},{10,11... | collective-permute-start | bytes 786440 | tf_op jit(solution)/shard_map/ppermute | solution.py:130
  83.9 11.6 %collective-permute-start.26 = (bf16[256,512]{1,0:T(8,128)(2,1)S(1)}, bf16[256,512]{1,0:T(8,128)(2,1)}, u32[]{:S(2)}, u32[]{:S(2)}) collective-permute-start(bf16[256,512]{1,0:T(8,128)(2,1)S(1)} %collective-permute-done.24.c_ref), channel_id=1, source_target_pairs={{2,3},{3,2},{4,5},{5,4},{10,11},{11,10},{12,13},{13,12},{18,19},{1... | collective-permute-start | bytes 786440 | tf_op jit(solution)/shard_map/ppermute | solution.py:248
  90.4 8.4 %collective-permute-start.27 = (bf16[256,512]{1,0:T(8,128)(2,1)S(1)}, bf16[256,512]{1,0:T(8,128)(2,1)}, u32[]{:S(2)}, u32[]{:S(2)}) collective-permute-start(bf16[256,512]{1,0:T(8,128)(2,1)S(1)} %collective-permute-done.25.d_ref), channel_id=1, source_target_pairs={{0,1},{1,0},{6,7},{7,6},{8,9},{9,8},{14,15},{15,14},{16,17},{17,16... | collective-permute-start | bytes 786440 | tf_op jit(solution)/shard_map/ppermute | solution.py:249
  (4 other events, 6.7 us)

commit v4 on v3

--- a/solution.py
+++ b/solution.py
@@ -106,23 +106,18 @@
     out_ref[...] = term.astype(out_ref.dtype)
 
 
-def config_near_kernel(at_ref, axle_ref, *refs):
-    shards, out_ref = refs[:-1], refs[-1]
+def config_kernel(first, at_ref, axle_ref, *refs):
+    out_ref = refs[-1]
+    total, shards = (None, refs[:-1]) if first == 0 else (refs[0][...], refs[1:-1])
     cols = shards[0].shape[0]
-    total = None
-    for j, shard in enumerate(shards):
-        term = dot(axle_ref[:, part(at_ref[j], cols)], shard[...])
+    middle = at_ref[8] == 1
+    singles = 4 if first == 0 else 0
+    values = [shard[...] for shard in shards[:singles]]
+    for inner, outer in zip(shards[singles::2], shards[singles + 1 :: 2]):
+        values.append(jnp.where(middle, inner[...], outer[...]))
+    for j, value in enumerate(values):
+        term = dot(axle_ref[:, part(at_ref[first + j], cols)], value)
         total = term if total is None else total + term
-    out_ref[...] = total
-
-
-def config_far_kernel(at_ref, axle_ref, near_ref, c_ref, d_ref, cx_ref, dx_ref, out_ref):
-    cols = c_ref.shape[0]
-    middle = at_ref[8] == 1
-    total = near_ref[...]
-    for j, pair in ((6, (c_ref, d_ref)), (7, (cx_ref, dx_ref))):
-        shard = jnp.where(middle, pair[0][...], pair[1][...])
-        total = total + dot(axle_ref[:, part(at_ref[j], cols)], shard)
     out_ref[...] = total
 
 
@@ -143,11 +138,12 @@
     depth = update_solution.shape[0]
     pieces = call(split_kernel, spread, [update_solution], [((cols, depth), BF16)] * loads, 0)
     *pieces, b_panel = lax.optimization_barrier((*pieces, b_panel))
-    early, late = [pieces[0]], [by_xor(pieces[7], "load", loads, 7)]
-    for k in (4, 5, 6):
-        block, piece = lax.optimization_barrier((by_xor(pieces[k], "load", loads, k), pieces[k - 3]))
-        early.append(block)
-        late.append(by_xor(piece, "load", loads, k - 3))
+    far = [by_xor(pieces[k], "load", loads, k) for k in (4, 5, 6, 7)]
+    far[0], pieces[1] = lax.optimization_barrier((far[0], pieces[1]))
+    far[1], pieces[2] = lax.optimization_barrier((far[1], pieces[2]))
+    far[2], far[3], pieces[3] = lax.optimization_barrier((far[2], far[3], pieces[3]))
+    early = [pieces[0]] + far
+    late = [by_xor(pieces[k], "load", loads, k) for k in (1, 2, 3)]
     held = pl.pallas_call(
         hold_kernel,
         out_shape=jax.ShapeDtypeStruct((updates, panel), BF16),
@@ -161,6 +157,7 @@
     b_across = lax.ppermute(b_panel, "factor", [(0, 2), (1, 3)])
     b_core = by_xor(b_panel, "factor", factors, 1)
     b_far = lax.ppermute(b_panel, "factor", [(0, 3), (1, 2)])
+    b_far, held = lax.optimization_barrier((b_far, held))
     (forward,) = call(
         forward_kernel,
         at_factor,
@@ -169,25 +166,25 @@
         2 * rows * panel * cols,
     )
     forward_across = by_xor(forward, "factor", factors, 2)
-    late[3], forward_across = lax.optimization_barrier((late[3], forward_across))
+    late[2], forward_across = lax.optimization_barrier((late[2], forward_across))
 
     block = (cols, rows)
     at_coupled = jnp.concatenate([at_factor, spread])
     (begun,) = call(
-        functools.partial(coupled_kernel, (0, 1, 2, 3), (4, 8, 9, 10)),
+        functools.partial(coupled_kernel, (0, 1, 2, 3), (4, 8, 9, 10, 11)),
         at_coupled,
         [held] + early,
         [((factors,) + block, F32)],
-        2 * cols * depth * 4 * panel,
+        2 * cols * depth * 5 * panel,
     )
 
     def coupled(panel_block, kind):
         (out,) = call(
-            functools.partial(finish_kernel, panel_block, (11, 5, 6, 7)),
+            functools.partial(finish_kernel, panel_block, (5, 6, 7)),
             at_coupled,
             [held, begun] + late,
             [(block, kind)],
-            2 * cols * depth * 4 * rows,
+            2 * cols * depth * 3 * rows,
         )
         return out
 
@@ -234,29 +231,42 @@
     solution_t = (kept + from_core.astype(F32) + from_across.astype(F32)).astype(BF16)
     panel_solution = solution_t.T
 
-    middle = (2, 3, 4, 5)
+    middle, ends = (2, 3, 4, 5), (0, 1, 6, 7)
+
+    def hop(value, places, bits):
+        return lax.ppermute(value, "load", [(i, i ^ bits) for i in places])
+
     own = solution_t
-    own_x = by_xor(own, "load", loads, 1)
-    a = by_xor(own, "load", loads, 2)
-    b = by_xor(own, "load", loads, 6)
-    own_x, a = lax.optimization_barrier((own_x, a))
-    a_x = by_xor(a, "load", loads, 1)
-    b, a_x = lax.optimization_barrier((b, a_x))
-    c = lax.ppermute(a, "load", [(i, i ^ 6) for i in middle])
-    d = lax.ppermute(b, "load", [(i, i ^ 2) for i in middle])
-    b_x = by_xor(b, "load", loads, 1)
-    c_x = lax.ppermute(c, "load", [(i, i ^ 1) for i in middle])
-    d_x = lax.ppermute(d, "load", [(i, i ^ 1) for i in (0, 1, 6, 7)])
+    b = hop(own, middle, 6)
+    a = hop(own, middle + ends, 2)
+    own_x = hop(own, middle + ends, 1)
+    b, a, own_x = lax.optimization_barrier((b, a, own_x))
+    c = hop(a, middle, 6)
+    d = hop(b, middle, 2)
+    a_x = hop(a, middle + ends, 1)
+    b_x = hop(b, middle, 1)
+    e = hop(own, ends, 6)
+    c_x = hop(c, middle, 1)
+    d_x = hop(d, ends, 1)
+    e_x = hop(e, ends, 1)
 
     in_middle = ((at_load >= 2) & (at_load < 6)).astype(jnp.int32)
-    at_axle = jnp.concatenate([at_load ^ jnp.array([0, 1, 2, 3, 6, 7, 4, 5], jnp.int32), in_middle[None]])
+    at_axle = jnp.concatenate([at_load ^ jnp.array([0, 1, 2, 3, 4, 6, 5, 7], jnp.int32), in_middle[None]])
     response = [((axle_weights.shape[0], rows), F32)]
-    work = axle_weights.size * rows
+    work = axle_weights.size * rows // 4
     (begun,) = call(
-        config_near_kernel, at_axle, [axle_weights, own, own_x, a, a_x, b, b_x], response, 3 * work // 2
+        functools.partial(config_kernel, 0),
+        at_axle,
+        [axle_weights, own, own_x, a, a_x, c, d, b, e],
+        response,
+        6 * work,
     )
     (config_response,) = call(
-        config_far_kernel, at_axle, [axle_weights, begun, c, d, c_x, d_x], response, work // 2
+        functools.partial(config_kernel, 6),
+        at_axle,
+        [axle_weights, begun, c_x, d_x, b_x, e_x],
+        response,
+        2 * work,
     )
     return (update_rhs, panel_solution, config_response)
 

time: 101 us -> 106 us (1.050)
  starting transfers between devices: 39.7 us -> 45.7 us
  local copies, waits for them, and re-layouts: 8 us -> 5.46 us
    ppermute x4 -> x11, starting transfers between devices: 5.67 us -> 20.3 us  [hop(): return lax.ppermute(value, 'load', [(i, i ^ bits) for i in places])]
    ppermute x21 -> x16, starting transfers between devices: 26.7 us -> 18.1 us  [by_xor(): return lax.ppermute(value, axis, [(i, i ^ bits) for i in range(size)])]
    ppermute x1, waiting for transfers between devices: 3.19 us -> 0.01 us  [small_slice(): b_far = lax.ppermute(b_panel, 'factor', [(0, 3), (1, 2)])]
    ppermute x1, starting transfers between devices: 1.38 us -> 4.54 us  [small_slice(): b_far = lax.ppermute(b_panel, 'factor', [(0, 3), (1, 2)])]
    ppermute x1, starting transfers between devices: 4.45 us -> 1.31 us  [small_slice(): b_across = lax.ppermute(b_panel, 'factor', [(0, 2), (1, 3)])]
    unnamed x17 -> x15, local copies, waits for them, and re-layouts: 8 us -> 5.46 us
    ppermute x4 -> x11, waiting for transfers between devices: 8.43 us -> 10.7 us  [hop(): return lax.ppermute(value, 'load', [(i, i ^ bits) for i in places])]
    ppermute x21 -> x16, waiting for transfers between devices: 17.5 us -> 19 us  [by_xor(): return lax.ppermute(value, axis, [(i, i ^ bits) for i in range(size)])]
  transfers between devices with their start and end apart: 28 -> 30, of which waited for: 10 -> 11; matrix products, arithmetic and copies ran while one was open for 1% -> 1% of each run, Pallas kernels for 15% -> 15%
where the time goes in v4:
time: 106 us; the launch traced here: 105 us
  starting transfers between devices  45.7 us (43%)
  waiting for transfers between devices  32.3 us (30%)
  Pallas kernels  20.5 us (19%)
  local copies, waits for them, and re-layouts  5.46 us (5%)
    ppermute x11, starting transfers between devices, hop(): return lax.ppermute(value, 'load', [(i, i ^ bits) for i in places])  20.3 us
    pallas_call x14, Pallas kernels, call(): pl.pallas_call(kernel, out_shape=shapes, in_specs=[SMEM] * len(at) + [VME...  19.9 us
    ppermute x16, waiting for transfers between devices, by_xor(): return lax.ppermute(value, axis, [(i, i ^ bits) for i in range(size)])  19 us
    ppermute x16, starting transfers between devices, by_xor(): return lax.ppermute(value, axis, [(i, i ^ bits) for i in range(size)])  18.1 us
    ppermute x11, waiting for transfers between devices, hop(): return lax.ppermute(value, 'load', [(i, i ^ bits) for i in places])  10.7 us
    unnamed x15, local copies, waits for them, and re-layouts  5.46 us
    ppermute x1, starting transfers between devices, small_slice(): b_far = lax.ppermute(b_panel, 'factor', [(0, 3), (1, 2)])  4.54 us
    ppermute x1, waiting for transfers between devices, small_slice(): from_across = lax.ppermute(send, 'factor', [(2, 0), (3, 1)])  2.61 us
  transfers between devices with their start and end apart: 30, of which 11 were waited for; matrix products, arithmetic and copies ran while one was open for 1% of the time, Pallas kernels for 15%

profile of v4, /device:TPU:0, one launch (start us, length us, event | category | flops | bytes accessed | tf_op | source)
XLA Modules:
  0.0 105.3 jit_solution(2897799580679282343)
XLA Ops:
  0.7 1.2 %copy-done.4 = bf16[256,2048]{1,0:T(8,128)(2,1)S(1)} copy-done((bf16[256,2048]{1,0:T(8,128)(2,1)S(1)}, bf16[256,2048]{1,0:T(8,128)(2,1)}, u32[]{:S(2)}) %copy-start.4) | copy-done | bytes 1048600
  3.3 4.5 %collective-permute-start.2 = (bf16[512,256]{1,0:T(8,128)(2,1)}, bf16[512,256]{1,0:T(8,128)(2,1)S(1)}, u32[]{:S(2)}, u32[]{:S(2)}) collective-permute-start(bf16[512,256]{1,0:T(8,128)(2,1)} %refs_0_), channel_id=1, source_target_pairs={{0,24},{8,16},{1,25},{9,17},{2,26},{10,18},{3,27},{11,19},{4,28},{... | collective-permute-start | bytes 786440 | tf_op jit(solution)/shard_map/ppermute | solution.py:159
  7.8 1.3 %collective-permute-start.1 = (bf16[512,256]{1,0:T(8,128)(2,1)}, bf16[512,256]{1,0:T(8,128)(2,1)S(1)}, u32[]{:S(2)}, u32[]{:S(2)}) collective-permute-start(bf16[512,256]{1,0:T(8,128)(2,1)} %refs_0_), channel_id=1, source_target_pairs={{0,16},{8,24},{1,17},{9,25},{2,18},{10,26},{3,19},{11,27},{4,20},{... | collective-permute-start | bytes 786440 | tf_op jit(solution)/shard_map/ppermute | solution.py:157
  9.1 2.7 %collective-permute-start.3 = (bf16[256,256]{1,0:T(8,128)(2,1)S(1)}, bf16[256,256]{1,0:T(8,128)(2,1)S(1)}, u32[]{:S(2)}, u32[]{:S(2)}) collective-permute-start(bf16[256,256]{1,0:T(8,128)(2,1)S(1)} %get-tuple-element.50), channel_id=1, source_target_pairs={{0,4},{1,5},{2,6},{3,7},{4,0},{5,1},{6,2},{7,3},{8,12},{9,13},{10,... | collective-permute-start | bytes 393224 | tf_op jit(solution)/shard_map/ppermute | solution.py:125
  11.8 1.3 %collective-permute-start.4 = (bf16[256,256]{1,0:T(8,128)(2,1)S(1)}, bf16[256,256]{1,0:T(8,128)(2,1)S(1)}, u32[]{:S(2)}, u32[]{:S(2)}) collective-permute-start(bf16[256,256]{1,0:T(8,128)(2,1)S(1)} %get-tuple-element.53), channel_id=1, source_target_pairs={{0,5},{1,4},{2,7},{3,6},{4,1},{5,0},{6,3},{7,2},{8,13},{9,12},{10,... | collective-permute-start | bytes 393224 | tf_op jit(solution)/shard_map/ppermute | solution.py:125
  13.0 3.4 %copy-done.1 = bf16[2048,2048]{1,0:T(8,128)(2,1)S(1)} copy-done((bf16[2048,2048]{1,0:T(8,128)(2,1)S(1)}, bf16[2048,2048]{1,0:T(8,128)(2,1)}, u32[]{:S(2)}) %copy-start.1) | copy-done | bytes 8388632
  17.0 3.7 %collective-permute-start.5 = (bf16[256,256]{1,0:T(8,128)(2,1)S(1)}, bf16[256,256]{1,0:T(8,128)(2,1)S(1)}, u32[]{:S(2)}, u32[]{:S(2)}) collective-permute-start(bf16[256,256]{1,0:T(8,128)(2,1)S(1)} %get-tuple-element.56), channel_id=1, source_target_pairs={{0,6},{1,7},{2,4},{3,5},{4,2},{5,3},{6,0},{7,1},{8,14},{9,15},{10,... | collective-permute-start | bytes 393224 | tf_op jit(solution)/shard_map/ppermute | solution.py:125
  20.9 1.3 %shard_map.96.forward_ref.refs_0_ = bf16[512,256]{1,0:T(8,128)(2,1)S(1)} custom-call(s32[4]{0:T(128)S(1)} %iota_xor_fusion.1.at_ref, bf16[512,2048]{1,0:T(8,128)(2,1)S(1)} %copy-done, bf16[512,256]{1,0:T(8,128)(2,1)S(1)} %copy-done.5, bf16[512,256]{1,0:T(8,128)(2,1)S(1)} %collective-permute-done.refs_1_, ...), custom_call_target="tpu_custom_call" | custom-call | flops 536870912 | bytes 3407872 | tf_op jit(solution)/shard_map/pallas_call | solution.py:22
  22.2 1.3 %collective-permute-start.10 = (bf16[512,256]{1,0:T(8,128)(2,1)S(1)}, bf16[512,256]{1,0:T(8,128)(2,1)S(1)}, u32[]{:S(2)}, u32[]{:S(2)}) collective-permute-start(bf16[512,256]{1,0:T(8,128)(2,1)S(1)} %shard_map.96.forward_ref.refs_0_), channel_id=1, source_target_pairs={{0,16},{8,24},{16,0},{24,8},{1,17},{9,25},{17,1},{25,9},{2,18},{10... | collective-permute-start | bytes 786440 | tf_op jit(solution)/shard_map/ppermute | solution.py:125
  23.5 4.2 %collective-permute-done.3.refs_1_ = bf16[256,256]{1,0:T(8,128)(2,1)S(1)} collective-permute-done((bf16[256,256]{1,0:T(8,128)(2,1)S(1)}, bf16[256,256]{1,0:T(8,128)(2,1)S(1)}, u32[]{:S(2)}, u32[]{:S(2)}) %collective-permute-start.3) | collective-permute-done | bytes 131104 | tf_op jit(solution)/shard_map/ppermute | solution.py:125
  27.7 3.7 %collective-permute-done.4.refs_2_ = bf16[256,256]{1,0:T(8,128)(2,1)S(1)} collective-permute-done((bf16[256,256]{1,0:T(8,128)(2,1)S(1)}, bf16[256,256]{1,0:T(8,128)(2,1)S(1)}, u32[]{:S(2)}, u32[]{:S(2)}) %collective-permute-start.4) | collective-permute-done | bytes 131104 | tf_op jit(solution)/shard_map/ppermute | solution.py:125
  32.0 5.5 %collective-permute-start.8 = (bf16[256,256]{1,0:T(8,128)(2,1)S(1)}, bf16[256,256]{1,0:T(8,128)(2,1)S(1)}, u32[]{:S(2)}, u32[]{:S(2)}) collective-permute-start(bf16[256,256]{1,0:T(8,128)(2,1)S(1)} %get-tuple-element.62), channel_id=1, source_target_pairs={{0,2},{1,3},{2,0},{3,1},{4,6},{5,7},{6,4},{7,5},{8,10},{9,11},{10,... | collective-permute-start | bytes 393224 | tf_op jit(solution)/shard_map/ppermute | solution.py:125
  38.3 2.1 %shard_map.97.begun_ref = f32[4,256,512]{2,1,0:T(8,128)S(1)} custom-call(s32[12]{0:T(128)S(1)} %pad_add_fusion.at_ref, bf16[2048,2048]{1,0:T(8,128)(2,1)S(1)} %shard_map.95.factor_ref, bf16[256,256]{1,0:T(8,128)(2,1)S(1)} %get-tuple-element.49.refs_0_, bf16[256,256]{1,0:T(8,128)(2,1)S(1)} %collective-permute-done.3.refs_1_, ...), custom_call_target="tpu_custom_call" | custom-call | flops 1342177280 | bytes 11141120 | tf_op jit(solution)/shard_map/pallas_call | solution.py:22
  40.4 3.6 %collective-permute-done.9.refs_2_ = bf16[256,256]{1,0:T(8,128)(2,1)S(1)} collective-permute-done((bf16[256,256]{1,0:T(8,128)(2,1)S(1)}, bf16[256,256]{1,0:T(8,128)(2,1)S(1)}, u32[]{:S(2)}, u32[]{:S(2)}) %collective-permute-start.9) | collective-permute-done | bytes 131104 | tf_op jit(solution)/shard_map/ppermute | solution.py:125
  45.0 0.9 shard_map.99
  48.5 7.3 %collective-permute-done.13.across_ref = bf16[256,512]{1,0:T(8,128)(2,1)S(1)} collective-permute-done((bf16[256,512]{1,0:T(8,128)(2,1)S(1)}, bf16[256,512]{1,0:T(8,128)(2,1)S(1)}, u32[]{:S(2)}, u32[]{:S(2)}) %collective-permute-start.13) | collective-permute-done | bytes 262176 | tf_op jit(solution)/shard_map/ppermute | solution.py:125
  58.4 1.4 %collective-permute-start.15 = (bf16[256,512]{1,0:T(8,128)(2,1)S(1)}, bf16[256,512]{1,0:T(8,128)(2,1)S(1)}, u32[]{:S(2)}, u32[]{:S(2)}) collective-permute-start(bf16[256,512]{1,0:T(8,128)(2,1)S(1)} %add_convert_fusion.1), channel_id=1, source_target_pairs={{16,0},{24,8},{17,1},{25,9},{18,2},{26,10},{19,3},{27,11},{20,4},{... | collective-permute-start | bytes 786440 | tf_op jit(solution)/shard_map/ppermute | solution.py:218
  61.1 4.4 %shard_map.104 = bf16[2048,256]{1,0:T(8,128)(2,1)} custom-call(s32[4]{0:T(128)S(1)} %iota_xor_fusion.1.at_ref, bf16[2048,2048]{1,0:T(8,128)(2,1)S(1)} %shard_map.95.factor_ref, bf16[2048,256]{1,0:T(8,128)(2,1)S(1)} %copy-done.3, bf16[512,256]{1,0:T(8,128)(2,1)S(1)} %shard_map.96.forward_ref.refs_0_, bf16[512,256]{1,0:T(8,128)(2,1)S(1)} %collective-permute-done.16.refs_1_, ...), custom_call_target="tpu_custom_call" | custom-call | flops 2147483648 | bytes 11534336 | tf_op jit(solution)/shard_map/pallas_call | solution.py:22
  66.4 2.6 %collective-permute-done.15 = bf16[256,512]{1,0:T(8,128)(2,1)S(1)} collective-permute-done((bf16[256,512]{1,0:T(8,128)(2,1)S(1)}, bf16[256,512]{1,0:T(8,128)(2,1)S(1)}, u32[]{:S(2)}, u32[]{:S(2)}) %collective-permute-start.15) | collective-permute-done | bytes 262176 | tf_op jit(solution)/shard_map/ppermute | solution.py:218
  69.8 6.1 %collective-permute-start.20 = (bf16[256,512]{1,0:T(8,128)(2,1)S(1)}, bf16[256,512]{1,0:T(8,128)(2,1)S(1)}, u32[]{:S(2)}, u32[]{:S(2)}) collective-permute-start(bf16[256,512]{1,0:T(8,128)(2,1)S(1)} %add_convert_fusion.refs_0_), channel_id=1, source_target_pairs={{2,0},{3,1},{4,6},{5,7},{0,2},{1,3},{6,4},{7,5},{10,8},{11,9},{12,... | collective-permute-start | bytes 786440 | tf_op jit(solution)/shard_map/ppermute | solution.py:237
  76.4 2.8 %collective-permute-start.25 = (bf16[256,512]{1,0:T(8,128)(2,1)S(1)}, bf16[256,512]{1,0:T(8,128)(2,1)S(1)}, u32[]{:S(2)}, u32[]{:S(2)}) collective-permute-start(bf16[256,512]{1,0:T(8,128)(2,1)S(1)} %add_convert_fusion.refs_0_), channel_id=1, source_target_pairs={{0,6},{1,7},{6,0},{7,1},{8,14},{9,15},{14,8},{15,9},{16,22},{17,23... | collective-permute-start | bytes 786440 | tf_op jit(solution)/shard_map/ppermute | solution.py:237
  79.2 3.4 %collective-permute-done.20.refs_2_ = bf16[256,512]{1,0:T(8,128)(2,1)S(1)} collective-permute-done((bf16[256,512]{1,0:T(8,128)(2,1)S(1)}, bf16[256,512]{1,0:T(8,128)(2,1)S(1)}, u32[]{:S(2)}, u32[]{:S(2)}) %collective-permute-start.20) | collective-permute-done | bytes 262176 | tf_op jit(solution)/shard_map/ppermute | solution.py:237
  83.7 1.3 %collective-permute-start.24 = (bf16[256,512]{1,0:T(8,128)(2,1)S(1)}, bf16[256,512]{1,0:T(8,128)(2,1)S(1)}, u32[]{:S(2)}, u32[]{:S(2)}) collective-permute-start(bf16[256,512]{1,0:T(8,128)(2,1)S(1)} %collective-permute-done.19.refs_6_), channel_id=1, source_target_pairs={{2,0},{3,1},{4,6},{5,7},{10,8},{11,9},{12,14},{13,15},{18,16},{19,... | collective-permute-start | bytes 786440 | tf_op jit(solution)/shard_map/ppermute | solution.py:237
  85.6 1.4 %collective-permute-start.28 = (bf16[256,512]{1,0:T(8,128)(2,1)S(1)}, bf16[256,512]{1,0:T(8,128)(2,1)}, u32[]{:S(2)}, u32[]{:S(2)}) collective-permute-start(bf16[256,512]{1,0:T(8,128)(2,1)S(1)} %collective-permute-done.19.refs_6_), channel_id=1, source_target_pairs={{2,3},{3,2},{4,5},{5,4},{10,11},{11,10},{12,13},{13,12},{18,19},{1... | collective-permute-start | bytes 786440 | tf_op jit(solution)/shard_map/ppermute | solution.py:237
  87.0 1.3 %collective-permute-done.25.refs_7_ = bf16[256,512]{1,0:T(8,128)(2,1)S(1)} collective-permute-done((bf16[256,512]{1,0:T(8,128)(2,1)S(1)}, bf16[256,512]{1,0:T(8,128)(2,1)S(1)}, u32[]{:S(2)}, u32[]{:S(2)}) %collective-permute-start.25) | collective-permute-done | bytes 262176 | tf_op jit(solution)/shard_map/ppermute | solution.py:237
  88.3 2.4 %collective-permute-start.29 = (bf16[256,512]{1,0:T(8,128)(2,1)S(1)}, bf16[256,512]{1,0:T(8,128)(2,1)}, u32[]{:S(2)}, u32[]{:S(2)}) collective-permute-start(bf16[256,512]{1,0:T(8,128)(2,1)S(1)} %collective-permute-done.25.refs_7_), channel_id=1, source_target_pairs={{0,1},{1,0},{6,7},{7,6},{8,9},{9,8},{14,15},{15,14},{16,17},{17,16... | collective-permute-start | bytes 786440 | tf_op jit(solution)/shard_map/ppermute | solution.py:237
  90.7 1.4 %collective-permute-start.26 = (bf16[256,512]{1,0:T(8,128)(2,1)S(1)}, bf16[256,512]{1,0:T(8,128)(2,1)}, u32[]{:S(2)}, u32[]{:S(2)}) collective-permute-start(bf16[256,512]{1,0:T(8,128)(2,1)S(1)} %collective-permute-done.23.refs_4_), channel_id=1, source_target_pairs={{2,3},{3,2},{4,5},{5,4},{10,11},{11,10},{12,13},{13,12},{18,19},{1... | collective-permute-start | bytes 786440 | tf_op jit(solution)/shard_map/ppermute | solution.py:237
  92.1 1.7 %collective-permute-done.24.refs_5_ = bf16[256,512]{1,0:T(8,128)(2,1)S(1)} collective-permute-done((bf16[256,512]{1,0:T(8,128)(2,1)S(1)}, bf16[256,512]{1,0:T(8,128)(2,1)S(1)}, u32[]{:S(2)}, u32[]{:S(2)}) %collective-permute-start.24) | collective-permute-done | bytes 262176 | tf_op jit(solution)/shard_map/ppermute | solution.py:237
  93.8 2.4 %collective-permute-start.27 = (bf16[256,512]{1,0:T(8,128)(2,1)S(1)}, bf16[256,512]{1,0:T(8,128)(2,1)}, u32[]{:S(2)}, u32[]{:S(2)}) collective-permute-start(bf16[256,512]{1,0:T(8,128)(2,1)S(1)} %collective-permute-done.24.refs_5_), channel_id=1, source_target_pairs={{0,1},{1,0},{6,7},{7,6},{8,9},{9,8},{14,15},{15,14},{16,17},{17,16... | collective-permute-start | bytes 786440 | tf_op jit(solution)/shard_map/ppermute | solution.py:237
  97.2 1.7 %shard_map.107.refs_0_ = f32[384,512]{1,0:T(8,128)S(1)} custom-call(s32[9]{0:T(128)S(1)} %pad_add_fusion.1.at_ref, bf16[384,2048]{1,0:T(8,128)(2,1)S(1)} %copy-done.2, bf16[256,512]{1,0:T(8,128)(2,1)S(1)} %add_convert_fusion.refs_0_, bf16[256,512]{1,0:T(8,128)(2,1)S(1)} %collective-permute-done.21.refs_1_, ...), custom_call_target="tpu_custom_call" | custom-call | flops 603979776 | bytes 4456448 | tf_op jit(solution)/shard_map/pallas_call | solution.py:22
  99.0 3.9 %collective-permute-done.27.refs_2_ = bf16[256,512]{1,0:T(8,128)(2,1)} collective-permute-done((bf16[256,512]{1,0:T(8,128)(2,1)S(1)}, bf16[256,512]{1,0:T(8,128)(2,1)}, u32[]{:S(2)}, u32[]{:S(2)}) %collective-permute-start.27) | collective-permute-done | bytes 262176 | tf_op jit(solution)/shard_map/ppermute | solution.py:237
  102.8 2.5 %shard_map.108 = f32[384,512]{1,0:T(8,128)} custom-call(s32[9]{0:T(128)S(1)} %pad_add_fusion.1.at_ref, bf16[384,2048]{1,0:T(8,128)(2,1)S(1)} %copy-done.2, f32[384,512]{1,0:T(8,128)S(1)} %shard_map.107.refs_0_, bf16[256,512]{1,0:T(8,128)(2,1)} %collective-permute-done.26.refs_1_, bf16[256,512]{1,0:T(8,128)(2,1)} %collective-permute-done.27.refs_2_, ...), custom_call_target="tpu_custom_call" | custom-call | flops 201326592 | bytes 4194304 | tf_op jit(solution)/shard_map/pallas_call | solution.py:22
  (66 shorter events, 15.7 us)
Async XLA Ops:
  2.7 14.3 %collective-permute-start = (bf16[512,256]{1,0:T(8,128)(2,1)}, bf16[512,256]{1,0:T(8,128)(2,1)S(1)}, u32[]{:S(2)}, u32[]{:S(2)}) collective-permute-start(bf16[512,256]{1,0:T(8,128)(2,1)} %refs_0_), channel_id=1, source_target_pairs={{0,8},{8,0},{16,24},{24,16},{1,9},{9,1},{17,25},{25,17},{2,10},{10... | collective-permute-start | bytes 786440 | tf_op jit(solution)/shard_map/ppermute | solution.py:125
  3.3 17.4 %collective-permute-start.2 = (bf16[512,256]{1,0:T(8,128)(2,1)}, bf16[512,256]{1,0:T(8,128)(2,1)S(1)}, u32[]{:S(2)}, u32[]{:S(2)}) collective-permute-start(bf16[512,256]{1,0:T(8,128)(2,1)} %refs_0_), channel_id=1, source_target_pairs={{0,24},{8,16},{1,25},{9,17},{2,26},{10,18},{3,27},{11,19},{4,28},{... | collective-permute-start | bytes 786440 | tf_op jit(solution)/shard_map/ppermute | solution.py:159
  7.8 13.1 %collective-permute-start.1 = (bf16[512,256]{1,0:T(8,128)(2,1)}, bf16[512,256]{1,0:T(8,128)(2,1)S(1)}, u32[]{:S(2)}, u32[]{:S(2)}) collective-permute-start(bf16[512,256]{1,0:T(8,128)(2,1)} %refs_0_), channel_id=1, source_target_pairs={{0,16},{8,24},{1,17},{9,25},{2,18},{10,26},{3,19},{11,27},{4,20},{... | collective-permute-start | bytes 786440 | tf_op jit(solution)/shard_map/ppermute | solution.py:157
  9.1 18.5 %collective-permute-start.3 = (bf16[256,256]{1,0:T(8,128)(2,1)S(1)}, bf16[256,256]{1,0:T(8,128)(2,1)S(1)}, u32[]{:S(2)}, u32[]{:S(2)}) collective-permute-start(bf16[256,256]{1,0:T(8,128)(2,1)S(1)} %get-tuple-element.50), channel_id=1, source_target_pairs={{0,4},{1,5},{2,6},{3,7},{4,0},{5,1},{6,2},{7,3},{8,12},{9,13},{10,... | collective-permute-start | bytes 393224 | tf_op jit(solution)/shard_map/ppermute | solution.py:125
  11.8 19.6 %collective-permute-start.4 = (bf16[256,256]{1,0:T(8,128)(2,1)S(1)}, bf16[256,256]{1,0:T(8,128)(2,1)S(1)}, u32[]{:S(2)}, u32[]{:S(2)}) collective-permute-start(bf16[256,256]{1,0:T(8,128)(2,1)S(1)} %get-tuple-element.53), channel_id=1, source_target_pairs={{0,5},{1,4},{2,7},{3,6},{4,1},{5,0},{6,3},{7,2},{8,13},{9,12},{10,... | collective-permute-start | bytes 393224 | tf_op jit(solution)/shard_map/ppermute | solution.py:125
  17.0 14.4 %collective-permute-start.5 = (bf16[256,256]{1,0:T(8,128)(2,1)S(1)}, bf16[256,256]{1,0:T(8,128)(2,1)S(1)}, u32[]{:S(2)}, u32[]{:S(2)}) collective-permute-start(bf16[256,256]{1,0:T(8,128)(2,1)S(1)} %get-tuple-element.56), channel_id=1, source_target_pairs={{0,6},{1,7},{2,4},{3,5},{4,2},{5,3},{6,0},{7,1},{8,14},{9,15},{10,... | collective-permute-start | bytes 393224 | tf_op jit(solution)/shard_map/ppermute | solution.py:125
  20.7 10.7 %collective-permute-start.6 = (bf16[256,256]{1,0:T(8,128)(2,1)S(1)}, bf16[256,256]{1,0:T(8,128)(2,1)S(1)}, u32[]{:S(2)}, u32[]{:S(2)}) collective-permute-start(bf16[256,256]{1,0:T(8,128)(2,1)S(1)} %get-tuple-element.57), channel_id=1, source_target_pairs={{0,7},{1,6},{2,5},{3,4},{4,3},{5,2},{6,1},{7,0},{8,15},{9,14},{10,... | collective-permute-start | bytes 393224 | tf_op jit(solution)/shard_map/ppermute | solution.py:125
  22.2 21.8 %collective-permute-start.10 = (bf16[512,256]{1,0:T(8,128)(2,1)S(1)}, bf16[512,256]{1,0:T(8,128)(2,1)S(1)}, u32[]{:S(2)}, u32[]{:S(2)}) collective-permute-start(bf16[512,256]{1,0:T(8,128)(2,1)S(1)} %shard_map.96.forward_ref.refs_0_), channel_id=1, source_target_pairs={{0,16},{8,24},{16,0},{24,8},{1,17},{9,25},{17,1},{25,9},{2,18},{10... | collective-permute-start | bytes 786440 | tf_op jit(solution)/shard_map/ppermute | solution.py:125
  31.4 12.6 %collective-permute-start.7 = (bf16[256,256]{1,0:T(8,128)(2,1)S(1)}, bf16[256,256]{1,0:T(8,128)(2,1)S(1)}, u32[]{:S(2)}, u32[]{:S(2)}) collective-permute-start(bf16[256,256]{1,0:T(8,128)(2,1)S(1)} %get-tuple-element.61), channel_id=1, source_target_pairs={{0,1},{1,0},{2,3},{3,2},{4,5},{5,4},{6,7},{7,6},{8,9},{9,8},{10,11... | collective-permute-start | bytes 393224 | tf_op jit(solution)/shard_map/ppermute | solution.py:125
  32.0 12.0 %collective-permute-start.8 = (bf16[256,256]{1,0:T(8,128)(2,1)S(1)}, bf16[256,256]{1,0:T(8,128)(2,1)S(1)}, u32[]{:S(2)}, u32[]{:S(2)}) collective-permute-start(bf16[256,256]{1,0:T(8,128)(2,1)S(1)} %get-tuple-element.62), channel_id=1, source_target_pairs={{0,2},{1,3},{2,0},{3,1},{4,6},{5,7},{6,4},{7,5},{8,10},{9,11},{10,... | collective-permute-start | bytes 393224 | tf_op jit(solution)/shard_map/ppermute | solution.py:125
  37.4 6.5 %collective-permute-start.9 = (bf16[256,256]{1,0:T(8,128)(2,1)S(1)}, bf16[256,256]{1,0:T(8,128)(2,1)S(1)}, u32[]{:S(2)}, u32[]{:S(2)}) collective-permute-start(bf16[256,256]{1,0:T(8,128)(2,1)S(1)} %get-tuple-element.63), channel_id=1, source_target_pairs={{0,3},{1,2},{2,1},{3,0},{4,7},{5,6},{6,5},{7,4},{8,11},{9,10},{10,... | collective-permute-start | bytes 393224 | tf_op jit(solution)/shard_map/ppermute | solution.py:125
  44.9 2.5 %collective-permute-start.12 = (bf16[256,512]{1,0:T(8,128)(2,1)S(1)}, bf16[256,512]{1,0:T(8,128)(2,1)S(1)}, u32[]{:S(2)}, u32[]{:S(2)}) collective-permute-start(bf16[256,512]{1,0:T(8,128)(2,1)S(1)} %shard_map.101), channel_id=1, source_target_pairs={{0,8},{8,0},{16,24},{24,16},{1,9},{9,1},{17,25},{25,17},{2,10},{10... | collective-permute-start | bytes 786440 | tf_op jit(solution)/shard_map/ppermute | solution.py:125
  45.9 2.6 %collective-permute-start.11 = (bf16[256,512]{1,0:T(8,128)(2,1)S(1)}, bf16[256,512]{1,0:T(8,128)(2,1)S(1)}, u32[]{:S(2)}, u32[]{:S(2)}) collective-permute-start(bf16[256,512]{1,0:T(8,128)(2,1)S(1)} %shard_map.99), channel_id=1, source_target_pairs={{0,8},{8,0},{16,24},{24,16},{1,9},{9,1},{17,25},{25,17},{2,10},{10... | collective-permute-start | bytes 786440 | tf_op jit(solution)/shard_map/ppermute | solution.py:125
  47.5 8.3 %collective-permute-start.13 = (bf16[256,512]{1,0:T(8,128)(2,1)S(1)}, bf16[256,512]{1,0:T(8,128)(2,1)S(1)}, u32[]{:S(2)}, u32[]{:S(2)}) collective-permute-start(bf16[256,512]{1,0:T(8,128)(2,1)S(1)} %add_convert_fusion.2), channel_id=1, source_target_pairs={{0,16},{8,24},{16,0},{24,8},{1,17},{9,25},{17,1},{25,9},{2,18},{10... | collective-permute-start | bytes 786440 | tf_op jit(solution)/shard_map/ppermute | solution.py:125
  56.7 1.6 %collective-permute-start.14 = (bf16[256,512]{1,0:T(8,128)(2,1)S(1)}, bf16[256,512]{1,0:T(8,128)(2,1)S(1)}, u32[]{:S(2)}, u32[]{:S(2)}) collective-permute-start(bf16[256,512]{1,0:T(8,128)(2,1)S(1)} %get-tuple-element.66), channel_id=1, source_target_pairs={{0,8},{8,0},{16,24},{24,16},{1,9},{9,1},{17,25},{25,17},{2,10},{10... | collective-permute-start | bytes 786440 | tf_op jit(solution)/shard_map/ppermute | solution.py:125
  56.8 4.3 %collective-permute-start.16 = (bf16[512,256]{1,0:T(8,128)(2,1)S(1)}, bf16[512,256]{1,0:T(8,128)(2,1)S(1)}, u32[]{:S(2)}, u32[]{:S(2)}) collective-permute-start(bf16[512,256]{1,0:T(8,128)(2,1)S(1)} %shard_map.96.forward_ref.refs_0_), channel_id=1, source_target_pairs={{0,8},{8,0},{16,24},{24,16},{1,9},{9,1},{17,25},{25,17},{2,10},{10... | collective-permute-start | bytes 786440 | tf_op jit(solution)/shard_map/ppermute | solution.py:125
  57.3 3.8 %collective-permute-start.17 = (bf16[512,256]{1,0:T(8,128)(2,1)S(1)}, bf16[512,256]{1,0:T(8,128)(2,1)S(1)}, u32[]{:S(2)}, u32[]{:S(2)}) collective-permute-start(bf16[512,256]{1,0:T(8,128)(2,1)S(1)} %collective-permute-done.10.refs_2_), channel_id=1, source_target_pairs={{0,8},{8,0},{16,24},{24,16},{1,9},{9,1},{17,25},{25,17},{2,10},{10... | collective-permute-start | bytes 786440 | tf_op jit(solution)/shard_map/ppermute | solution.py:125
  58.4 10.6 %collective-permute-start.15 = (bf16[256,512]{1,0:T(8,128)(2,1)S(1)}, bf16[256,512]{1,0:T(8,128)(2,1)S(1)}, u32[]{:S(2)}, u32[]{:S(2)}) collective-permute-start(bf16[256,512]{1,0:T(8,128)(2,1)S(1)} %add_convert_fusion.1), channel_id=1, source_target_pairs={{16,0},{24,8},{17,1},{25,9},{18,2},{26,10},{19,3},{27,11},{20,4},{... | collective-permute-start | bytes 786440 | tf_op jit(solution)/shard_map/ppermute | solution.py:218
  60.7 8.3 %collective-permute-start.18 = (bf16[256,512]{1,0:T(8,128)(2,1)S(1)}, bf16[256,512]{1,0:T(8,128)(2,1)S(1)}, u32[]{:S(2)}, u32[]{:S(2)}) collective-permute-start(bf16[256,512]{1,0:T(8,128)(2,1)S(1)} %shard_map.106), channel_id=1, source_target_pairs={{0,8},{8,0},{16,24},{24,16},{1,9},{9,1},{17,25},{25,17},{2,10},{10... | collective-permute-start | bytes 786440 | tf_op jit(solution)/shard_map/ppermute | solution.py:125
  65.5 30.7 %copy-start.6 = (s32[8]{0:T(128)S(1)}, s32[8]{0:T(128)}, u32[]{:S(2)}) copy-start(s32[8]{0:T(128)} %constant.14.clone) | copy-start | bytes 100
  65.5 31.7 %copy-start.2 = (bf16[384,2048]{1,0:T(8,128)(2,1)S(1)}, bf16[384,2048]{1,0:T(8,128)(2,1)}, u32[]{:S(2)}) copy-start(bf16[384,2048]{1,0:T(8,128)(2,1)} %axle_ref.3) | copy-start | bytes 4718596
  69.1 10.1 %collective-permute-start.19 = (bf16[256,512]{1,0:T(8,128)(2,1)S(1)}, bf16[256,512]{1,0:T(8,128)(2,1)S(1)}, u32[]{:S(2)}, u32[]{:S(2)}) collective-permute-start(bf16[256,512]{1,0:T(8,128)(2,1)S(1)} %add_convert_fusion.refs_0_), channel_id=1, source_target_pairs={{2,4},{3,5},{4,2},{5,3},{10,12},{11,13},{12,10},{13,11},{18,20},{1... | collective-permute-start | bytes 786440 | tf_op jit(solution)/shard_map/ppermute | solution.py:237
  69.8 12.8 %collective-permute-start.20 = (bf16[256,512]{1,0:T(8,128)(2,1)S(1)}, bf16[256,512]{1,0:T(8,128)(2,1)S(1)}, u32[]{:S(2)}, u32[]{:S(2)}) collective-permute-start(bf16[256,512]{1,0:T(8,128)(2,1)S(1)} %add_convert_fusion.refs_0_), channel_id=1, source_target_pairs={{2,0},{3,1},{4,6},{5,7},{0,2},{1,3},{6,4},{7,5},{10,8},{11,9},{12,... | collective-permute-start | bytes 786440 | tf_op jit(solution)/shard_map/ppermute | solution.py:237
  75.9 7.2 %collective-permute-start.21 = (bf16[256,512]{1,0:T(8,128)(2,1)S(1)}, bf16[256,512]{1,0:T(8,128)(2,1)S(1)}, u32[]{:S(2)}, u32[]{:S(2)}) collective-permute-start(bf16[256,512]{1,0:T(8,128)(2,1)S(1)} %add_convert_fusion.refs_0_), channel_id=1, source_target_pairs={{2,3},{3,2},{4,5},{5,4},{0,1},{1,0},{6,7},{7,6},{10,11},{11,10},{1... | collective-permute-start | bytes 786440 | tf_op jit(solution)/shard_map/ppermute | solution.py:237
  76.4 11.9 %collective-permute-start.25 = (bf16[256,512]{1,0:T(8,128)(2,1)S(1)}, bf16[256,512]{1,0:T(8,128)(2,1)S(1)}, u32[]{:S(2)}, u32[]{:S(2)}) collective-permute-start(bf16[256,512]{1,0:T(8,128)(2,1)S(1)} %add_convert_fusion.refs_0_), channel_id=1, source_target_pairs={{0,6},{1,7},{6,0},{7,1},{8,14},{9,15},{14,8},{15,9},{16,22},{17,23... | collective-permute-start | bytes 786440 | tf_op jit(solution)/shard_map/ppermute | solution.py:237
  83.1 7.7 %collective-permute-start.23 = (bf16[256,512]{1,0:T(8,128)(2,1)S(1)}, bf16[256,512]{1,0:T(8,128)(2,1)S(1)}, u32[]{:S(2)}, u32[]{:S(2)}) collective-permute-start(bf16[256,512]{1,0:T(8,128)(2,1)S(1)} %collective-permute-done.20.refs_2_), channel_id=1, source_target_pairs={{2,4},{3,5},{4,2},{5,3},{10,12},{11,13},{12,10},{13,11},{18,20},{1... | collective-permute-start | bytes 786440 | tf_op jit(solution)/shard_map/ppermute | solution.py:237
  83.7 10.1 %collective-permute-start.24 = (bf16[256,512]{1,0:T(8,128)(2,1)S(1)}, bf16[256,512]{1,0:T(8,128)(2,1)S(1)}, u32[]{:S(2)}, u32[]{:S(2)}) collective-permute-start(bf16[256,512]{1,0:T(8,128)(2,1)S(1)} %collective-permute-done.19.refs_6_), channel_id=1, source_target_pairs={{2,0},{3,1},{4,6},{5,7},{10,8},{11,9},{12,14},{13,15},{18,16},{19,... | collective-permute-start | bytes 786440 | tf_op jit(solution)/shard_map/ppermute | solution.py:237
  85.0 12.2 %collective-permute-start.22 = (bf16[256,512]{1,0:T(8,128)(2,1)S(1)}, bf16[256,512]{1,0:T(8,128)(2,1)}, u32[]{:S(2)}, u32[]{:S(2)}) collective-permute-start(bf16[256,512]{1,0:T(8,128)(2,1)S(1)} %collective-permute-done.20.refs_2_), channel_id=1, source_target_pairs={{2,3},{3,2},{4,5},{5,4},{0,1},{1,0},{6,7},{7,6},{10,11},{11,10},{1... | collective-permute-start | bytes 786440 | tf_op jit(solution)/shard_map/ppermute | solution.py:237
  85.6 13.3 %collective-permute-start.28 = (bf16[256,512]{1,0:T(8,128)(2,1)S(1)}, bf16[256,512]{1,0:T(8,128)(2,1)}, u32[]{:S(2)}, u32[]{:S(2)}) collective-permute-start(bf16[256,512]{1,0:T(8,128)(2,1)S(1)} %collective-permute-done.19.refs_6_), channel_id=1, source_target_pairs={{2,3},{3,2},{4,5},{5,4},{10,11},{11,10},{12,13},{13,12},{18,19},{1... | collective-permute-start | bytes 786440 | tf_op jit(solution)/shard_map/ppermute | solution.py:237
  88.3 10.7 %collective-permute-start.29 = (bf16[256,512]{1,0:T(8,128)(2,1)S(1)}, bf16[256,512]{1,0:T(8,128)(2,1)}, u32[]{:S(2)}, u32[]{:S(2)}) collective-permute-start(bf16[256,512]{1,0:T(8,128)(2,1)S(1)} %collective-permute-done.25.refs_7_), channel_id=1, source_target_pairs={{0,1},{1,0},{6,7},{7,6},{8,9},{9,8},{14,15},{15,14},{16,17},{17,16... | collective-permute-start | bytes 786440 | tf_op jit(solution)/shard_map/ppermute | solution.py:237
  90.7 8.2 %collective-permute-start.26 = (bf16[256,512]{1,0:T(8,128)(2,1)S(1)}, bf16[256,512]{1,0:T(8,128)(2,1)}, u32[]{:S(2)}, u32[]{:S(2)}) collective-permute-start(bf16[256,512]{1,0:T(8,128)(2,1)S(1)} %collective-permute-done.23.refs_4_), channel_id=1, source_target_pairs={{2,3},{3,2},{4,5},{5,4},{10,11},{11,10},{12,13},{13,12},{18,19},{1... | collective-permute-start | bytes 786440 | tf_op jit(solution)/shard_map/ppermute | solution.py:237
  93.8 9.0 %collective-permute-start.27 = (bf16[256,512]{1,0:T(8,128)(2,1)S(1)}, bf16[256,512]{1,0:T(8,128)(2,1)}, u32[]{:S(2)}, u32[]{:S(2)}) collective-permute-start(bf16[256,512]{1,0:T(8,128)(2,1)S(1)} %collective-permute-done.24.refs_5_), channel_id=1, source_target_pairs={{0,1},{1,0},{6,7},{7,6},{8,9},{9,8},{14,15},{15,14},{16,17},{17,16... | collective-permute-start | bytes 786440 | tf_op jit(solution)/shard_map/ppermute | solution.py:237
  (5 other events, 16.4 us)

commit v5 on v3

--- a/solution.py
+++ b/solution.py
@@ -60,10 +60,10 @@
         out_ref[here, :] = total.astype(out_ref.dtype)
 
 
-def split_kernel(at_ref, solved_ref, *outs):
-    cols = outs[0].shape[0]
-    for j, out_ref in enumerate(outs):
-        out_ref[...] = solved_ref[:, part(at_ref[j], cols)].T
+def turn_kernel(solved_ref, out_ref):
+    cols = out_ref.shape[1]
+    for j in range(out_ref.shape[0]):
+        out_ref[j] = solved_ref[:, j * cols : (j + 1) * cols].T
 
 
 def hold_kernel(factor_ref, out_ref, sem):
@@ -72,24 +72,13 @@
     copy.wait()
 
 
-def coupled_kernel(panel_blocks, row_blocks, at_ref, factor_ref, *refs):
-    pieces, out_ref = refs[:-1], refs[-1]
-    depth, width = pieces[0].shape[1], out_ref.shape[2]
-    for j, b in enumerate(panel_blocks):
-        cols = part(at_ref[b], width)
-        total = None
-        for k, piece in zip(row_blocks, pieces):
-            term = dot(piece[...], factor_ref[part(at_ref[k], depth), cols])
-            total = term if total is None else total + term
-        out_ref[j] = total
-
-
-def finish_kernel(panel_block, row_blocks, at_ref, factor_ref, begun_ref, *refs):
-    pieces, out_ref = refs[:-1], refs[-1]
-    depth, width = pieces[0].shape[1], out_ref.shape[1]
-    total = begun_ref[panel_block]
-    for k, piece in zip(row_blocks, pieces):
-        total = total + dot(piece[...], factor_ref[part(at_ref[k], depth), part(at_ref[panel_block], width)])
+def coupled_kernel(panel_block, at_ref, factor_ref, solved_ref, out_ref):
+    pieces, _, depth = solved_ref.shape
+    cols = part(at_ref[panel_block], out_ref.shape[1])
+    total = None
+    for k in range(pieces):
+        term = dot(solved_ref[k], factor_ref[k * depth : (k + 1) * depth, cols])
+        total = term if total is None else total + term
     out_ref[...] = total.astype(out_ref.dtype)
 
 
@@ -106,23 +95,17 @@
     out_ref[...] = term.astype(out_ref.dtype)
 
 
-def config_near_kernel(at_ref, axle_ref, *refs):
-    shards, out_ref = refs[:-1], refs[-1]
-    cols = shards[0].shape[0]
-    total = None
+def config_kernel(first, singles, at_ref, axle_ref, *refs):
+    refs, out_ref = list(refs[:-1]), refs[-1]
+    total = None if first == 0 else refs.pop(0)[...]
+    cols = refs[0].shape[0]
+    middle = at_ref[8] == 1
+    shards = [ref[...] for ref in refs[:singles]]
+    for inner, outer in zip(refs[singles::2], refs[singles + 1 :: 2]):
+        shards.append(jnp.where(middle, inner[...], outer[...]))
     for j, shard in enumerate(shards):
-        term = dot(axle_ref[:, part(at_ref[j], cols)], shard[...])
+        term = dot(axle_ref[:, part(at_ref[first + j], cols)], shard)
         total = term if total is None else total + term
-    out_ref[...] = total
-
-
-def config_far_kernel(at_ref, axle_ref, near_ref, c_ref, d_ref, cx_ref, dx_ref, out_ref):
-    cols = c_ref.shape[0]
-    middle = at_ref[8] == 1
-    total = near_ref[...]
-    for j, pair in ((6, (c_ref, d_ref)), (7, (cx_ref, dx_ref))):
-        shard = jnp.where(middle, pair[0][...], pair[1][...])
-        total = total + dot(axle_ref[:, part(at_ref[j], cols)], shard)
     out_ref[...] = total
 
 
@@ -138,16 +121,10 @@
     f, at_load = lax.axis_index("factor"), lax.axis_index("load")
     at_factor = f ^ jnp.arange(factors, dtype=jnp.int32)
 
-    spread = at_load ^ jnp.arange(loads, dtype=jnp.int32)
-
     depth = update_solution.shape[0]
-    pieces = call(split_kernel, spread, [update_solution], [((cols, depth), BF16)] * loads, 0)
-    *pieces, b_panel = lax.optimization_barrier((*pieces, b_panel))
-    early, late = [pieces[0]], [by_xor(pieces[7], "load", loads, 7)]
-    for k in (4, 5, 6):
-        block, piece = lax.optimization_barrier((by_xor(pieces[k], "load", loads, k), pieces[k - 3]))
-        early.append(block)
-        late.append(by_xor(piece, "load", loads, k - 3))
+    (turned,) = call(turn_kernel, None, [update_solution], [((loads, cols, depth), BF16)], 0)
+    turned, b_panel = lax.optimization_barrier((turned, b_panel))
+    regrouped = lax.all_to_all(turned, "load", split_axis=0, concat_axis=0, tiled=True)
     held = pl.pallas_call(
         hold_kernel,
         out_shape=jax.ShapeDtypeStruct((updates, panel), BF16),
@@ -169,25 +146,17 @@
         2 * rows * panel * cols,
     )
     forward_across = by_xor(forward, "factor", factors, 2)
-    late[3], forward_across = lax.optimization_barrier((late[3], forward_across))
+    regrouped, held, forward_across = lax.optimization_barrier((regrouped, held, forward_across))
 
     block = (cols, rows)
-    at_coupled = jnp.concatenate([at_factor, spread])
-    (begun,) = call(
-        functools.partial(coupled_kernel, (0, 1, 2, 3), (4, 8, 9, 10)),
-        at_coupled,
-        [held] + early,
-        [((factors,) + block, F32)],
-        2 * cols * depth * 4 * panel,
-    )
 
     def coupled(panel_block, kind):
         (out,) = call(
-            functools.partial(finish_kernel, panel_block, (11, 5, 6, 7)),
-            at_coupled,
-            [held, begun] + late,
+            functools.partial(coupled_kernel, panel_block),
+            at_factor,
+            [held, regrouped],
             [(block, kind)],
-            2 * cols * depth * 4 * rows,
+            2 * updates * cols * rows,
         )
         return out
 
@@ -251,12 +220,16 @@
     in_middle = ((at_load >= 2) & (at_load < 6)).astype(jnp.int32)
     at_axle = jnp.concatenate([at_load ^ jnp.array([0, 1, 2, 3, 6, 7, 4, 5], jnp.int32), in_middle[None]])
     response = [((axle_weights.shape[0], rows), F32)]
-    work = axle_weights.size * rows
+    work = axle_weights.size * rows // 4
     (begun,) = call(
-        config_near_kernel, at_axle, [axle_weights, own, own_x, a, a_x, b, b_x], response, 3 * work // 2
+        functools.partial(config_kernel, 0, 6),
+        at_axle,
+        [axle_weights, own, own_x, a, a_x, b, b_x, c, d],
+        response,
+        7 * work,
     )
     (config_response,) = call(
-        config_far_kernel, at_axle, [axle_weights, begun, c, d, c_x, d_x], response, work // 2
+        functools.partial(config_kernel, 7, 0), at_axle, [axle_weights, begun, c_x, d_x], response, work
     )
     return (update_rhs, panel_solution, config_response)
 

time: 101 us -> 105 us (1.040)
  starting transfers between devices: 39.7 us -> 31.5 us
  local copies, waits for them, and re-layouts: 8 us -> 14.7 us
  waiting for transfers between devices: 31.7 us -> 37.2 us
    ppermute x21 -> x14, starting transfers between devices: 26.7 us -> 12.4 us  [by_xor(): return lax.ppermute(value, axis, [(i, i ^ bits) for i in range(size)])]
    all_to_all x0 -> x1, starting transfers between devices: none -> 7.25 us  [small_slice(): lax.all_to_all(turned, 'load', split_axis=0, concat_axis=0, tiled=True)]
    unnamed x17 -> x25, local copies, waits for them, and re-layouts: 8 us -> 14.7 us
    ppermute x1, waiting for transfers between devices: 0.01 us -> 5.48 us  [small_slice(): b_across = lax.ppermute(b_panel, 'factor', [(0, 2), (1, 3)])]
    ppermute x1, waiting for transfers between devices: 3.19 us -> 5.22 us  [small_slice(): b_far = lax.ppermute(b_panel, 'factor', [(0, 3), (1, 2)])]
    ppermute x21 -> x14, waiting for transfers between devices: 17.5 us -> 15.8 us  [by_xor(): return lax.ppermute(value, axis, [(i, i ^ bits) for i in range(size)])]
    pallas_call x14 -> x13, Pallas kernels: 19.8 us -> 19.5 us  [call(): pl.pallas_call(kernel, out_shape=shapes, in_specs=[SMEM] * len(at) + [VME...]
  transfers between devices with their start and end apart: 28 -> 22, of which waited for: 10 -> 10; matrix products, arithmetic and copies ran while one was open for 1% -> 1% of each run, Pallas kernels for 15% -> 14%
where the time goes in v5:
time: 105 us
  waiting for transfers between devices  37.2 us (35%)
  starting transfers between devices  31.5 us (30%)
  Pallas kernels  20 us (19%)
  local copies, waits for them, and re-layouts  14.7 us (14%)
    pallas_call x13, Pallas kernels, call(): pl.pallas_call(kernel, out_shape=shapes, in_specs=[SMEM] * len(at) + [VME...  19.5 us
    ppermute x14, waiting for transfers between devices, by_xor(): return lax.ppermute(value, axis, [(i, i ^ bits) for i in range(size)])  15.8 us
    unnamed x25, local copies, waits for them, and re-layouts  14.7 us
    ppermute x14, starting transfers between devices, by_xor(): return lax.ppermute(value, axis, [(i, i ^ bits) for i in range(size)])  12.4 us
    all_to_all x1, starting transfers between devices, small_slice(): lax.all_to_all(turned, 'load', split_axis=0, concat_axis=0, tiled=True)  7.25 us
    ppermute x1, waiting for transfers between devices, small_slice(): b_across = lax.ppermute(b_panel, 'factor', [(0, 2), (1, 3)])  5.48 us
    ppermute x1, waiting for transfers between devices, small_slice(): b_far = lax.ppermute(b_panel, 'factor', [(0, 3), (1, 2)])  5.22 us
    ppermute x1, waiting for transfers between devices, small_slice(): d = lax.ppermute(b, 'load', [(i, i ^ 2) for i in middle])  5.07 us
  transfers between devices with their start and end apart: 22, of which 10 were waited for; matrix products, arithmetic and copies ran while one was open for 1% of the time, Pallas kernels for 14%

profile of v5, /device:TPU:0, one launch (start us, length us, event | category | flops | bytes accessed | tf_op | source)
XLA Modules:
  0.0 104.7 jit_solution(15553437393339473542)
XLA Ops:
  1.9 1.3 %shard_map.94 = bf16[8,256,256]{2,1,0:T(8,128)(2,1)} custom-call(bf16[256,2048]{1,0:T(8,128)(2,1)S(1)} %copy-done.7), custom_call_target="tpu_custom_call" | custom-call | bytes 2097152 | tf_op jit(solution)/shard_map/pallas_call | solution.py:22
  3.2 7.3 %all-to-all-start = ((bf16[8,256,256]{2,1,0:T(8,128)(2,1)}), bf16[8,256,256]{2,1,0:T(8,128)(2,1)S(1)}, u32[]{:S(2)}, u32[]{:S(2)}) async-start(bf16[8,256,256]{2,1,0:T(8,128)(2,1)} %shard_map.94), calls=%async_computation | async-start | bytes 2097152 | tf_op jit(solution)/shard_map/all_to_all | solution.py:127
  10.4 3.4 %collective-permute-start.1 = (bf16[512,256]{1,0:T(8,128)(2,1)}, bf16[512,256]{1,0:T(8,128)(2,1)S(1)}, u32[]{:S(2)}, u32[]{:S(2)}) collective-permute-start(bf16[512,256]{1,0:T(8,128)(2,1)} %refs_0_), channel_id=1, source_target_pairs={{0,16},{8,24},{1,17},{9,25},{2,18},{10,26},{3,19},{11,27},{4,20},{... | collective-permute-start | bytes 786440 | tf_op jit(solution)/shard_map/ppermute | solution.py:138
  13.9 1.4 %collective-permute-start.2 = (bf16[512,256]{1,0:T(8,128)(2,1)}, bf16[512,256]{1,0:T(8,128)(2,1)S(1)}, u32[]{:S(2)}, u32[]{:S(2)}) collective-permute-start(bf16[512,256]{1,0:T(8,128)(2,1)} %refs_0_), channel_id=1, source_target_pairs={{0,24},{8,16},{1,25},{9,17},{2,26},{10,18},{3,27},{11,19},{4,28},{... | collective-permute-start | bytes 786440 | tf_op jit(solution)/shard_map/ppermute | solution.py:140
  15.3 5.5 %collective-permute-done.1.refs_2_ = bf16[512,256]{1,0:T(8,128)(2,1)S(1)} collective-permute-done((bf16[512,256]{1,0:T(8,128)(2,1)}, bf16[512,256]{1,0:T(8,128)(2,1)S(1)}, u32[]{:S(2)}, u32[]{:S(2)}) %collective-permute-start.1) | collective-permute-done | bytes 262176 | tf_op jit(solution)/shard_map/ppermute | solution.py:138
  20.8 5.2 %collective-permute-done.2.refs_3_ = bf16[512,256]{1,0:T(8,128)(2,1)S(1)} collective-permute-done((bf16[512,256]{1,0:T(8,128)(2,1)}, bf16[512,256]{1,0:T(8,128)(2,1)S(1)}, u32[]{:S(2)}, u32[]{:S(2)}) %collective-permute-start.2) | collective-permute-done | bytes 262176 | tf_op jit(solution)/shard_map/ppermute | solution.py:140
  26.0 1.6 %copy-done.2 = bf16[512,2048]{1,0:T(8,128)(2,1)S(1)} copy-done((bf16[512,2048]{1,0:T(8,128)(2,1)S(1)}, bf16[512,2048]{1,0:T(8,128)(2,1)}, u32[]{:S(2)}) %copy-start.2) | copy-done | bytes 2097176
  28.5 1.3 %shard_map.95.forward_ref.refs_0_ = bf16[512,256]{1,0:T(8,128)(2,1)S(1)} custom-call(s32[4]{0:T(128)S(1)} %iota_xor_fusion.at_ref, bf16[512,2048]{1,0:T(8,128)(2,1)S(1)} %copy-done.2, bf16[512,256]{1,0:T(8,128)(2,1)S(1)} %copy-done.8, bf16[512,256]{1,0:T(8,128)(2,1)S(1)} %collective-permute-done.refs_1_, ...), custom_call_target="tpu_custom_call" | custom-call | flops 536870912 | bytes 3407872 | tf_op jit(solution)/shard_map/pallas_call | solution.py:22
  29.8 2.0 %collective-permute-start.3 = (bf16[512,256]{1,0:T(8,128)(2,1)S(1)}, bf16[512,256]{1,0:T(8,128)(2,1)S(1)}, u32[]{:S(2)}, u32[]{:S(2)}) collective-permute-start(bf16[512,256]{1,0:T(8,128)(2,1)S(1)} %shard_map.95.forward_ref.refs_0_), channel_id=1, source_target_pairs={{0,16},{8,24},{16,0},{24,8},{1,17},{9,25},{17,1},{25,9},{2,18},{10... | collective-permute-start | bytes 786440 | tf_op jit(solution)/shard_map/ppermute | solution.py:113
  31.8 3.4 %copy-done.4 = bf16[2048,2048]{1,0:T(8,128)(2,1)S(1)} copy-done((bf16[2048,2048]{1,0:T(8,128)(2,1)S(1)}, bf16[2048,2048]{1,0:T(8,128)(2,1)}, u32[]{:S(2)}) %copy-start.4) | copy-done | bytes 8388632
  35.8 3.3 %copy-done = bf16[2048,2048]{1,0:T(8,128)(2,1)} copy-done((bf16[2048,2048]{1,0:T(8,128)(2,1)}, bf16[2048,2048]{1,0:T(8,128)(2,1)S(1)}, u32[]{:S(2)}) %copy-start) | copy-done | bytes 8388632
  39.1 3.4 %copy-done.1 = bf16[2048,2048]{1,0:T(8,128)(2,1)S(1)} copy-done((bf16[2048,2048]{1,0:T(8,128)(2,1)S(1)}, bf16[2048,2048]{1,0:T(8,128)(2,1)}, u32[]{:S(2)}) %copy-start.1) | copy-done | bytes 8388632
  42.4 1.3 %shard_map.100 = bf16[256,512]{1,0:T(8,128)(2,1)S(1)} custom-call(s32[4]{0:T(128)S(1)} %iota_xor_fusion.at_ref, bf16[2048,2048]{1,0:T(8,128)(2,1)S(1)} %copy-done.1, bf16[8,256,256]{2,1,0:T(8,128)(2,1)S(1)} %all-to-all-done.solved_ref), custom_call_target="tpu_custom_call" | custom-call | flops 536870912 | bytes 9699328 | tf_op jit(solution)/shard_map/pallas_call | solution.py:22
  44.0 1.3 %shard_map.98 = bf16[256,512]{1,0:T(8,128)(2,1)S(1)} custom-call(s32[4]{0:T(128)S(1)} %iota_xor_fusion.at_ref, bf16[2048,2048]{1,0:T(8,128)(2,1)S(1)} %copy-done.1, bf16[8,256,256]{2,1,0:T(8,128)(2,1)S(1)} %all-to-all-done.solved_ref), custom_call_target="tpu_custom_call" | custom-call | flops 536870912 | bytes 9699328 | tf_op jit(solution)/shard_map/pallas_call | solution.py:22
  47.0 1.6 %collective-permute-start.6 = (bf16[256,512]{1,0:T(8,128)(2,1)S(1)}, bf16[256,512]{1,0:T(8,128)(2,1)S(1)}, u32[]{:S(2)}, u32[]{:S(2)}) collective-permute-start(bf16[256,512]{1,0:T(8,128)(2,1)S(1)} %add_convert_fusion.2), channel_id=1, source_target_pairs={{0,16},{8,24},{16,0},{24,8},{1,17},{9,25},{17,1},{25,9},{2,18},{10... | collective-permute-start | bytes 786440 | tf_op jit(solution)/shard_map/ppermute | solution.py:113
  49.8 5.7 %collective-permute-done.6.across_ref = bf16[256,512]{1,0:T(8,128)(2,1)S(1)} collective-permute-done((bf16[256,512]{1,0:T(8,128)(2,1)S(1)}, bf16[256,512]{1,0:T(8,128)(2,1)S(1)}, u32[]{:S(2)}, u32[]{:S(2)}) %collective-permute-start.6) | collective-permute-done | bytes 262176 | tf_op jit(solution)/shard_map/ppermute | solution.py:113
  58.1 1.3 %collective-permute-start.8 = (bf16[256,512]{1,0:T(8,128)(2,1)S(1)}, bf16[256,512]{1,0:T(8,128)(2,1)S(1)}, u32[]{:S(2)}, u32[]{:S(2)}) collective-permute-start(bf16[256,512]{1,0:T(8,128)(2,1)S(1)} %add_convert_fusion.1), channel_id=1, source_target_pairs={{16,0},{24,8},{17,1},{25,9},{18,2},{26,10},{19,3},{27,11},{20,4},{... | collective-permute-start | bytes 786440 | tf_op jit(solution)/shard_map/ppermute | solution.py:190
  60.8 4.4 %shard_map.103 = bf16[2048,256]{1,0:T(8,128)(2,1)} custom-call(s32[4]{0:T(128)S(1)} %iota_xor_fusion.at_ref, bf16[2048,2048]{1,0:T(8,128)(2,1)S(1)} %bitcast.3, bf16[2048,256]{1,0:T(8,128)(2,1)S(1)} %copy-done.6, bf16[512,256]{1,0:T(8,128)(2,1)S(1)} %shard_map.95.forward_ref.refs_0_, bf16[512,256]{1,0:T(8,128)(2,1)S(1)} %collective-permute-done.9.refs_1_, ...), custom_call_target="tpu_custom_call" | custom-call | flops 2147483648 | bytes 11534336 | tf_op jit(solution)/shard_map/pallas_call | solution.py:22
  66.1 2.5 %collective-permute-done.8 = bf16[256,512]{1,0:T(8,128)(2,1)S(1)} collective-permute-done((bf16[256,512]{1,0:T(8,128)(2,1)S(1)}, bf16[256,512]{1,0:T(8,128)(2,1)S(1)}, u32[]{:S(2)}, u32[]{:S(2)}) %collective-permute-start.8) | collective-permute-done | bytes 262176 | tf_op jit(solution)/shard_map/ppermute | solution.py:190
  68.7 1.9 %collective-permute-start.12 = (bf16[256,512]{1,0:T(8,128)(2,1)S(1)}, bf16[256,512]{1,0:T(8,128)(2,1)S(1)}, u32[]{:S(2)}, u32[]{:S(2)}) collective-permute-start(bf16[256,512]{1,0:T(8,128)(2,1)S(1)} %add_convert_fusion.refs_0_), channel_id=1, source_target_pairs={{0,1},{1,0},{2,3},{3,2},{4,5},{5,4},{6,7},{7,6},{8,9},{9,8},{10,11... | collective-permute-start | bytes 786440 | tf_op jit(solution)/shard_map/ppermute | solution.py:113
  70.6 1.7 %collective-permute-start.13 = (bf16[256,512]{1,0:T(8,128)(2,1)S(1)}, bf16[256,512]{1,0:T(8,128)(2,1)S(1)}, u32[]{:S(2)}, u32[]{:S(2)}) collective-permute-start(bf16[256,512]{1,0:T(8,128)(2,1)S(1)} %add_convert_fusion.refs_0_), channel_id=1, source_target_pairs={{0,2},{1,3},{2,0},{3,1},{4,6},{5,7},{6,4},{7,5},{8,10},{9,11},{10,... | collective-permute-start | bytes 786440 | tf_op jit(solution)/shard_map/ppermute | solution.py:113
  72.3 2.4 %collective-permute-start.14 = (bf16[256,512]{1,0:T(8,128)(2,1)S(1)}, bf16[256,512]{1,0:T(8,128)(2,1)S(1)}, u32[]{:S(2)}, u32[]{:S(2)}) collective-permute-start(bf16[256,512]{1,0:T(8,128)(2,1)S(1)} %add_convert_fusion.refs_0_), channel_id=1, source_target_pairs={{0,6},{1,7},{2,4},{3,5},{4,2},{5,3},{6,0},{7,1},{8,14},{9,15},{10,... | collective-permute-start | bytes 786440 | tf_op jit(solution)/shard_map/ppermute | solution.py:113
  74.6 2.0 %collective-permute-done.12.refs_1_ = bf16[256,512]{1,0:T(8,128)(2,1)S(1)} collective-permute-done((bf16[256,512]{1,0:T(8,128)(2,1)S(1)}, bf16[256,512]{1,0:T(8,128)(2,1)S(1)}, u32[]{:S(2)}, u32[]{:S(2)}) %collective-permute-start.12) | collective-permute-done | bytes 262176 | tf_op jit(solution)/shard_map/ppermute | solution.py:113
  76.6 2.4 %collective-permute-done.13.refs_2_ = bf16[256,512]{1,0:T(8,128)(2,1)S(1)} collective-permute-done((bf16[256,512]{1,0:T(8,128)(2,1)S(1)}, bf16[256,512]{1,0:T(8,128)(2,1)S(1)}, u32[]{:S(2)}, u32[]{:S(2)}) %collective-permute-start.13) | collective-permute-done | bytes 262176 | tf_op jit(solution)/shard_map/ppermute | solution.py:113
  80.3 5.5 %collective-permute-done.14.refs_4_ = bf16[256,512]{1,0:T(8,128)(2,1)S(1)} collective-permute-done((bf16[256,512]{1,0:T(8,128)(2,1)S(1)}, bf16[256,512]{1,0:T(8,128)(2,1)S(1)}, u32[]{:S(2)}, u32[]{:S(2)}) %collective-permute-start.14) | collective-permute-done | bytes 262176 | tf_op jit(solution)/shard_map/ppermute | solution.py:113
  85.8 1.3 %collective-permute-start.18 = (bf16[256,512]{1,0:T(8,128)(2,1)S(1)}, bf16[256,512]{1,0:T(8,128)(2,1)S(1)}, u32[]{:S(2)}, u32[]{:S(2)}) collective-permute-start(bf16[256,512]{1,0:T(8,128)(2,1)S(1)} %collective-permute-done.14.refs_4_), channel_id=1, source_target_pairs={{2,0},{3,1},{4,6},{5,7},{10,8},{11,9},{12,14},{13,15},{18,16},{19,... | collective-permute-start | bytes 786440 | tf_op jit(solution)/shard_map/ppermute | solution.py:215
  87.7 1.4 %collective-permute-start.19 = (bf16[256,512]{1,0:T(8,128)(2,1)S(1)}, bf16[256,512]{1,0:T(8,128)(2,1)}, u32[]{:S(2)}, u32[]{:S(2)}) collective-permute-start(bf16[256,512]{1,0:T(8,128)(2,1)S(1)} %collective-permute-done.17.refs_6_), channel_id=1, source_target_pairs={{2,3},{3,2},{4,5},{5,4},{10,11},{11,10},{12,13},{13,12},{18,19},{1... | collective-permute-start | bytes 786440 | tf_op jit(solution)/shard_map/ppermute | solution.py:217
  89.1 5.1 %collective-permute-done.18.refs_7_ = bf16[256,512]{1,0:T(8,128)(2,1)S(1)} collective-permute-done((bf16[256,512]{1,0:T(8,128)(2,1)S(1)}, bf16[256,512]{1,0:T(8,128)(2,1)S(1)}, u32[]{:S(2)}, u32[]{:S(2)}) %collective-permute-start.18) | collective-permute-done | bytes 262176 | tf_op jit(solution)/shard_map/ppermute | solution.py:215
  94.1 2.4 %collective-permute-start.20 = (bf16[256,512]{1,0:T(8,128)(2,1)S(1)}, bf16[256,512]{1,0:T(8,128)(2,1)}, u32[]{:S(2)}, u32[]{:S(2)}) collective-permute-start(bf16[256,512]{1,0:T(8,128)(2,1)S(1)} %collective-permute-done.18.refs_7_), channel_id=1, source_target_pairs={{0,1},{1,0},{6,7},{7,6},{8,9},{9,8},{14,15},{15,14},{16,17},{17,16... | collective-permute-start | bytes 786440 | tf_op jit(solution)/shard_map/ppermute | solution.py:218
  97.5 1.8 %shard_map.106.refs_0_ = f32[384,512]{1,0:T(8,128)S(1)} custom-call(s32[9]{0:T(128)S(1)} %pad_add_fusion.at_ref, bf16[384,2048]{1,0:T(8,128)(2,1)S(1)} %copy-done.5, bf16[256,512]{1,0:T(8,128)(2,1)S(1)} %add_convert_fusion.refs_0_, bf16[256,512]{1,0:T(8,128)(2,1)S(1)} %collective-permute-done.12.refs_1_, ...), custom_call_target="tpu_custom_call" | custom-call | flops 704643072 | bytes 4456448 | tf_op jit(solution)/shard_map/pallas_call | solution.py:22
  99.4 3.1 %collective-permute-done.20.refs_2_ = bf16[256,512]{1,0:T(8,128)(2,1)} collective-permute-done((bf16[256,512]{1,0:T(8,128)(2,1)S(1)}, bf16[256,512]{1,0:T(8,128)(2,1)}, u32[]{:S(2)}, u32[]{:S(2)}) %collective-permute-start.20) | collective-permute-done | bytes 262176 | tf_op jit(solution)/shard_map/ppermute | solution.py:218
  102.5 2.2 %shard_map.107 = f32[384,512]{1,0:T(8,128)} custom-call(s32[9]{0:T(128)S(1)} %pad_add_fusion.at_ref, bf16[384,2048]{1,0:T(8,128)(2,1)S(1)} %copy-done.5, f32[384,512]{1,0:T(8,128)S(1)} %shard_map.106.refs_0_, bf16[256,512]{1,0:T(8,128)(2,1)} %collective-permute-done.19.refs_1_, bf16[256,512]{1,0:T(8,128)(2,1)} %collective-permute-done.20.refs_2_), custom_call_target="tpu_custom_call" | custom-call | flops 100663296 | bytes 3670016 | tf_op jit(solution)/shard_map/pallas_call | solution.py:22
  (58 shorter events, 13.6 us)
Async XLA Ops:
  3.2 35.9 %all-to-all-start = ((bf16[8,256,256]{2,1,0:T(8,128)(2,1)}), bf16[8,256,256]{2,1,0:T(8,128)(2,1)S(1)}, u32[]{:S(2)}, u32[]{:S(2)}) async-start(bf16[8,256,256]{2,1,0:T(8,128)(2,1)} %shard_map.94), calls=%async_computation | async-start | bytes 2097152 | tf_op jit(solution)/shard_map/all_to_all | solution.py:127
  10.4 4.9 %collective-permute-start = (bf16[512,256]{1,0:T(8,128)(2,1)}, bf16[512,256]{1,0:T(8,128)(2,1)S(1)}, u32[]{:S(2)}, u32[]{:S(2)}) collective-permute-start(bf16[512,256]{1,0:T(8,128)(2,1)} %refs_0_), channel_id=1, source_target_pairs={{0,8},{8,0},{16,24},{24,16},{1,9},{9,1},{17,25},{25,17},{2,10},{10... | collective-permute-start | bytes 786440 | tf_op jit(solution)/shard_map/ppermute | solution.py:113
  10.4 10.3 %collective-permute-start.1 = (bf16[512,256]{1,0:T(8,128)(2,1)}, bf16[512,256]{1,0:T(8,128)(2,1)S(1)}, u32[]{:S(2)}, u32[]{:S(2)}) collective-permute-start(bf16[512,256]{1,0:T(8,128)(2,1)} %refs_0_), channel_id=1, source_target_pairs={{0,16},{8,24},{1,17},{9,25},{2,18},{10,26},{3,19},{11,27},{4,20},{... | collective-permute-start | bytes 786440 | tf_op jit(solution)/shard_map/ppermute | solution.py:138
  13.9 12.1 %collective-permute-start.2 = (bf16[512,256]{1,0:T(8,128)(2,1)}, bf16[512,256]{1,0:T(8,128)(2,1)S(1)}, u32[]{:S(2)}, u32[]{:S(2)}) collective-permute-start(bf16[512,256]{1,0:T(8,128)(2,1)} %refs_0_), channel_id=1, source_target_pairs={{0,24},{8,16},{1,25},{9,17},{2,26},{10,18},{3,27},{11,19},{4,28},{... | collective-permute-start | bytes 786440 | tf_op jit(solution)/shard_map/ppermute | solution.py:140
  26.0 1.6 %copy-start.2 = (bf16[512,2048]{1,0:T(8,128)(2,1)S(1)}, bf16[512,2048]{1,0:T(8,128)(2,1)}, u32[]{:S(2)}) copy-start(bf16[512,2048]{1,0:T(8,128)(2,1)} %inverse_ref.9) | copy-start | bytes 6291460
  29.8 9.3 %collective-permute-start.3 = (bf16[512,256]{1,0:T(8,128)(2,1)S(1)}, bf16[512,256]{1,0:T(8,128)(2,1)S(1)}, u32[]{:S(2)}, u32[]{:S(2)}) collective-permute-start(bf16[512,256]{1,0:T(8,128)(2,1)S(1)} %shard_map.95.forward_ref.refs_0_), channel_id=1, source_target_pairs={{0,16},{8,24},{16,0},{24,8},{1,17},{9,25},{17,1},{25,9},{2,18},{10... | collective-permute-start | bytes 786440 | tf_op jit(solution)/shard_map/ppermute | solution.py:113
  31.8 3.4 %copy-start.4 = (bf16[2048,2048]{1,0:T(8,128)(2,1)S(1)}, bf16[2048,2048]{1,0:T(8,128)(2,1)}, u32[]{:S(2)}) copy-start(bf16[2048,2048]{1,0:T(8,128)(2,1)} %factor_ref.1) | copy-start | bytes 25165828
  35.8 3.3 %copy-start = (bf16[2048,2048]{1,0:T(8,128)(2,1)}, bf16[2048,2048]{1,0:T(8,128)(2,1)S(1)}, u32[]{:S(2)}) copy-start(bf16[2048,2048]{1,0:T(8,128)(2,1)S(1)} %shard_map.96.factor_ref) | copy-start | bytes 25165828
  39.1 3.4 %copy-start.1 = (bf16[2048,2048]{1,0:T(8,128)(2,1)S(1)}, bf16[2048,2048]{1,0:T(8,128)(2,1)}, u32[]{:S(2)}) copy-start(bf16[2048,2048]{1,0:T(8,128)(2,1)} %copy-done) | copy-start | bytes 25165828
  43.7 3.2 %collective-permute-start.5 = (bf16[256,512]{1,0:T(8,128)(2,1)S(1)}, bf16[256,512]{1,0:T(8,128)(2,1)S(1)}, u32[]{:S(2)}, u32[]{:S(2)}) collective-permute-start(bf16[256,512]{1,0:T(8,128)(2,1)S(1)} %shard_map.100), channel_id=1, source_target_pairs={{0,8},{8,0},{16,24},{24,16},{1,9},{9,1},{17,25},{25,17},{2,10},{10... | collective-permute-start | bytes 786440 | tf_op jit(solution)/shard_map/ppermute | solution.py:113
  45.3 10.3 %copy-start.3 = (bf16[512,2048]{1,0:T(8,128)(2,1)S(1)}, bf16[512,2048]{1,0:T(8,128)(2,1)}, u32[]{:S(2)}) copy-start(bf16[512,2048]{1,0:T(8,128)(2,1)} %inverse_ref.9) | copy-start | bytes 6291460
  45.3 4.5 %collective-permute-start.4 = (bf16[256,512]{1,0:T(8,128)(2,1)S(1)}, bf16[256,512]{1,0:T(8,128)(2,1)S(1)}, u32[]{:S(2)}, u32[]{:S(2)}) collective-permute-start(bf16[256,512]{1,0:T(8,128)(2,1)S(1)} %shard_map.98), channel_id=1, source_target_pairs={{0,8},{8,0},{16,24},{24,16},{1,9},{9,1},{17,25},{25,17},{2,10},{10... | collective-permute-start | bytes 786440 | tf_op jit(solution)/shard_map/ppermute | solution.py:113
  47.0 13.8 %slice-start = ((s8[8388608]{0:T(1024)(128)(4,1)}), s8[4194304]{0:T(1024)(128)(4,1)S(1)}, s32[]{:S(2)}) async-start(s8[8388608]{0:T(1024)(128)(4,1)} %bitcast.2), calls=%async_computation.1 | async-start | bytes 8388608
  47.0 13.8 %copy-start.6 = (bf16[2048,256]{1,0:T(8,128)(2,1)S(1)}, bf16[2048,256]{1,0:T(8,128)(2,1)}, u32[]{:S(2)}) copy-start(bf16[2048,256]{1,0:T(8,128)(2,1)} %rhs_ref.1) | copy-start | bytes 3145732
  47.0 8.5 %collective-permute-start.6 = (bf16[256,512]{1,0:T(8,128)(2,1)S(1)}, bf16[256,512]{1,0:T(8,128)(2,1)S(1)}, u32[]{:S(2)}, u32[]{:S(2)}) collective-permute-start(bf16[256,512]{1,0:T(8,128)(2,1)S(1)} %add_convert_fusion.2), channel_id=1, source_target_pairs={{0,16},{8,24},{16,0},{24,8},{1,17},{9,25},{17,1},{25,9},{2,18},{10... | collective-permute-start | bytes 786440 | tf_op jit(solution)/shard_map/ppermute | solution.py:113
  49.8 10.9 %slice-start.1 = ((s8[8388608]{0:T(1024)(128)(4,1)}), s8[4194304]{0:T(1024)(128)(4,1)S(1)}, s32[]{:S(2)}) async-start(s8[8388608]{0:T(1024)(128)(4,1)} %bitcast.2), calls=%async_computation.2 | async-start | bytes 8388608
  56.5 1.6 %collective-permute-start.7 = (bf16[256,512]{1,0:T(8,128)(2,1)S(1)}, bf16[256,512]{1,0:T(8,128)(2,1)S(1)}, u32[]{:S(2)}, u32[]{:S(2)}) collective-permute-start(bf16[256,512]{1,0:T(8,128)(2,1)S(1)} %get-tuple-element.21), channel_id=1, source_target_pairs={{0,8},{8,0},{16,24},{24,16},{1,9},{9,1},{17,25},{25,17},{2,10},{10... | collective-permute-start | bytes 786440 | tf_op jit(solution)/shard_map/ppermute | solution.py:113
  56.5 4.2 %collective-permute-start.9 = (bf16[512,256]{1,0:T(8,128)(2,1)S(1)}, bf16[512,256]{1,0:T(8,128)(2,1)S(1)}, u32[]{:S(2)}, u32[]{:S(2)}) collective-permute-start(bf16[512,256]{1,0:T(8,128)(2,1)S(1)} %shard_map.95.forward_ref.refs_0_), channel_id=1, source_target_pairs={{0,8},{8,0},{16,24},{24,16},{1,9},{9,1},{17,25},{25,17},{2,10},{10... | collective-permute-start | bytes 786440 | tf_op jit(solution)/shard_map/ppermute | solution.py:113
  57.0 3.7 %collective-permute-start.10 = (bf16[512,256]{1,0:T(8,128)(2,1)S(1)}, bf16[512,256]{1,0:T(8,128)(2,1)S(1)}, u32[]{:S(2)}, u32[]{:S(2)}) collective-permute-start(bf16[512,256]{1,0:T(8,128)(2,1)S(1)} %collective-permute-done.3.refs_2_), channel_id=1, source_target_pairs={{0,8},{8,0},{16,24},{24,16},{1,9},{9,1},{17,25},{25,17},{2,10},{10... | collective-permute-start | bytes 786440 | tf_op jit(solution)/shard_map/ppermute | solution.py:113
  58.1 10.4 %collective-permute-start.8 = (bf16[256,512]{1,0:T(8,128)(2,1)S(1)}, bf16[256,512]{1,0:T(8,128)(2,1)S(1)}, u32[]{:S(2)}, u32[]{:S(2)}) collective-permute-start(bf16[256,512]{1,0:T(8,128)(2,1)S(1)} %add_convert_fusion.1), channel_id=1, source_target_pairs={{16,0},{24,8},{17,1},{25,9},{18,2},{26,10},{19,3},{27,11},{20,4},{... | collective-permute-start | bytes 786440 | tf_op jit(solution)/shard_map/ppermute | solution.py:190
  60.3 36.3 %copy-start.9 = (s32[8]{0:T(128)S(1)}, s32[8]{0:T(128)}, u32[]{:S(2)}) copy-start(s32[8]{0:T(128)} %constant.14.clone) | copy-start | bytes 100
  60.3 37.2 %copy-start.5 = (bf16[384,2048]{1,0:T(8,128)(2,1)S(1)}, bf16[384,2048]{1,0:T(8,128)(2,1)}, u32[]{:S(2)}) copy-start(bf16[384,2048]{1,0:T(8,128)(2,1)} %axle_ref.3) | copy-start | bytes 4718596
  60.3 8.3 %collective-permute-start.11 = (bf16[256,512]{1,0:T(8,128)(2,1)S(1)}, bf16[256,512]{1,0:T(8,128)(2,1)S(1)}, u32[]{:S(2)}, u32[]{:S(2)}) collective-permute-start(bf16[256,512]{1,0:T(8,128)(2,1)S(1)} %shard_map.105), channel_id=1, source_target_pairs={{0,8},{8,0},{16,24},{24,16},{1,9},{9,1},{17,25},{25,17},{2,10},{10... | collective-permute-start | bytes 786440 | tf_op jit(solution)/shard_map/ppermute | solution.py:113
  68.7 7.9 %collective-permute-start.12 = (bf16[256,512]{1,0:T(8,128)(2,1)S(1)}, bf16[256,512]{1,0:T(8,128)(2,1)S(1)}, u32[]{:S(2)}, u32[]{:S(2)}) collective-permute-start(bf16[256,512]{1,0:T(8,128)(2,1)S(1)} %add_convert_fusion.refs_0_), channel_id=1, source_target_pairs={{0,1},{1,0},{2,3},{3,2},{4,5},{5,4},{6,7},{7,6},{8,9},{9,8},{10,11... | collective-permute-start | bytes 786440 | tf_op jit(solution)/shard_map/ppermute | solution.py:113
  70.6 8.4 %collective-permute-start.13 = (bf16[256,512]{1,0:T(8,128)(2,1)S(1)}, bf16[256,512]{1,0:T(8,128)(2,1)S(1)}, u32[]{:S(2)}, u32[]{:S(2)}) collective-permute-start(bf16[256,512]{1,0:T(8,128)(2,1)S(1)} %add_convert_fusion.refs_0_), channel_id=1, source_target_pairs={{0,2},{1,3},{2,0},{3,1},{4,6},{5,7},{6,4},{7,5},{8,10},{9,11},{10,... | collective-permute-start | bytes 786440 | tf_op jit(solution)/shard_map/ppermute | solution.py:113
  72.3 13.5 %collective-permute-start.14 = (bf16[256,512]{1,0:T(8,128)(2,1)S(1)}, bf16[256,512]{1,0:T(8,128)(2,1)S(1)}, u32[]{:S(2)}, u32[]{:S(2)}) collective-permute-start(bf16[256,512]{1,0:T(8,128)(2,1)S(1)} %add_convert_fusion.refs_0_), channel_id=1, source_target_pairs={{0,6},{1,7},{2,4},{3,5},{4,2},{5,3},{6,0},{7,1},{8,14},{9,15},{10,... | collective-permute-start | bytes 786440 | tf_op jit(solution)/shard_map/ppermute | solution.py:113
  79.0 6.8 %collective-permute-start.15 = (bf16[256,512]{1,0:T(8,128)(2,1)S(1)}, bf16[256,512]{1,0:T(8,128)(2,1)S(1)}, u32[]{:S(2)}, u32[]{:S(2)}) collective-permute-start(bf16[256,512]{1,0:T(8,128)(2,1)S(1)} %collective-permute-done.13.refs_2_), channel_id=1, source_target_pairs={{0,1},{1,0},{2,3},{3,2},{4,5},{5,4},{6,7},{7,6},{8,9},{9,8},{10,11... | collective-permute-start | bytes 786440 | tf_op jit(solution)/shard_map/ppermute | solution.py:113
  79.6 8.1 %collective-permute-start.17 = (bf16[256,512]{1,0:T(8,128)(2,1)S(1)}, bf16[256,512]{1,0:T(8,128)(2,1)S(1)}, u32[]{:S(2)}, u32[]{:S(2)}) collective-permute-start(bf16[256,512]{1,0:T(8,128)(2,1)S(1)} %collective-permute-done.13.refs_2_), channel_id=1, source_target_pairs={{2,4},{3,5},{4,2},{5,3},{10,12},{11,13},{12,10},{13,11},{18,20},{1... | collective-permute-start | bytes 786440 | tf_op jit(solution)/shard_map/ppermute | solution.py:214
  85.8 8.3 %collective-permute-start.18 = (bf16[256,512]{1,0:T(8,128)(2,1)S(1)}, bf16[256,512]{1,0:T(8,128)(2,1)S(1)}, u32[]{:S(2)}, u32[]{:S(2)}) collective-permute-start(bf16[256,512]{1,0:T(8,128)(2,1)S(1)} %collective-permute-done.14.refs_4_), channel_id=1, source_target_pairs={{2,0},{3,1},{4,6},{5,7},{10,8},{11,9},{12,14},{13,15},{18,16},{19,... | collective-permute-start | bytes 786440 | tf_op jit(solution)/shard_map/ppermute | solution.py:215
  87.1 10.5 %collective-permute-start.16 = (bf16[256,512]{1,0:T(8,128)(2,1)S(1)}, bf16[256,512]{1,0:T(8,128)(2,1)}, u32[]{:S(2)}, u32[]{:S(2)}) collective-permute-start(bf16[256,512]{1,0:T(8,128)(2,1)S(1)} %collective-permute-done.14.refs_4_), channel_id=1, source_target_pairs={{0,1},{1,0},{2,3},{3,2},{4,5},{5,4},{6,7},{7,6},{8,9},{9,8},{10,11... | collective-permute-start | bytes 786440 | tf_op jit(solution)/shard_map/ppermute | solution.py:113
  87.7 11.7 %collective-permute-start.19 = (bf16[256,512]{1,0:T(8,128)(2,1)S(1)}, bf16[256,512]{1,0:T(8,128)(2,1)}, u32[]{:S(2)}, u32[]{:S(2)}) collective-permute-start(bf16[256,512]{1,0:T(8,128)(2,1)S(1)} %collective-permute-done.17.refs_6_), channel_id=1, source_target_pairs={{2,3},{3,2},{4,5},{5,4},{10,11},{11,10},{12,13},{13,12},{18,19},{1... | collective-permute-start | bytes 786440 | tf_op jit(solution)/shard_map/ppermute | solution.py:217
  94.1 8.4 %collective-permute-start.20 = (bf16[256,512]{1,0:T(8,128)(2,1)S(1)}, bf16[256,512]{1,0:T(8,128)(2,1)}, u32[]{:S(2)}, u32[]{:S(2)}) collective-permute-start(bf16[256,512]{1,0:T(8,128)(2,1)S(1)} %collective-permute-done.18.refs_7_), channel_id=1, source_target_pairs={{0,1},{1,0},{6,7},{7,6},{8,9},{9,8},{14,15},{15,14},{16,17},{17,16... | collective-permute-start | bytes 786440 | tf_op jit(solution)/shard_map/ppermute | solution.py:218
  (2 other events, 2.2 us)

commit v6 on v3

--- a/solution.py
+++ b/solution.py
@@ -106,23 +106,17 @@
     out_ref[...] = term.astype(out_ref.dtype)
 
 
-def config_near_kernel(at_ref, axle_ref, *refs):
-    shards, out_ref = refs[:-1], refs[-1]
-    cols = shards[0].shape[0]
-    total = None
+def config_kernel(first, singles, at_ref, axle_ref, *refs):
+    refs, out_ref = list(refs[:-1]), refs[-1]
+    total = None if first == 0 else refs.pop(0)[...]
+    cols = refs[0].shape[0]
+    middle = at_ref[8] == 1
+    shards = [ref[...] for ref in refs[:singles]]
+    for inner, outer in zip(refs[singles::2], refs[singles + 1 :: 2]):
+        shards.append(jnp.where(middle, inner[...], outer[...]))
     for j, shard in enumerate(shards):
-        term = dot(axle_ref[:, part(at_ref[j], cols)], shard[...])
+        term = dot(axle_ref[:, part(at_ref[first + j], cols)], shard)
         total = term if total is None else total + term
-    out_ref[...] = total
-
-
-def config_far_kernel(at_ref, axle_ref, near_ref, c_ref, d_ref, cx_ref, dx_ref, out_ref):
-    cols = c_ref.shape[0]
-    middle = at_ref[8] == 1
-    total = near_ref[...]
-    for j, pair in ((6, (c_ref, d_ref)), (7, (cx_ref, dx_ref))):
-        shard = jnp.where(middle, pair[0][...], pair[1][...])
-        total = total + dot(axle_ref[:, part(at_ref[j], cols)], shard)
     out_ref[...] = total
 
 
@@ -143,11 +137,10 @@
     depth = update_solution.shape[0]
     pieces = call(split_kernel, spread, [update_solution], [((cols, depth), BF16)] * loads, 0)
     *pieces, b_panel = lax.optimization_barrier((*pieces, b_panel))
-    early, late = [pieces[0]], [by_xor(pieces[7], "load", loads, 7)]
-    for k in (4, 5, 6):
-        block, piece = lax.optimization_barrier((by_xor(pieces[k], "load", loads, k), pieces[k - 3]))
-        early.append(block)
-        late.append(by_xor(piece, "load", loads, k - 3))
+    early = [pieces[0]] + [by_xor(pieces[k], "load", loads, k) for k in (4, 5, 6)]
+    late = [by_xor(pieces[7], "load", loads, 7)]
+    early[1], *pieces[1:4] = lax.optimization_barrier((early[1], *pieces[1:4]))
+    late += [by_xor(pieces[k], "load", loads, k) for k in (1, 2, 3)]
     held = pl.pallas_call(
         hold_kernel,
         out_shape=jax.ShapeDtypeStruct((updates, panel), BF16),
@@ -193,6 +186,7 @@
 
     from_core = by_xor(coupled(3, BF16), "factor", factors, 1)
     send = (coupled(2, F32) + from_core.astype(F32)).astype(BF16)
+    send, late[0] = lax.optimization_barrier((send, late[0]))
     from_across = by_xor(send, "factor", factors, 2)
     from_core = by_xor(coupled(1, BF16), "factor", factors, 1)
     kept = coupled(0, F32)
@@ -251,12 +245,16 @@
     in_middle = ((at_load >= 2) & (at_load < 6)).astype(jnp.int32)
     at_axle = jnp.concatenate([at_load ^ jnp.array([0, 1, 2, 3, 6, 7, 4, 5], jnp.int32), in_middle[None]])
     response = [((axle_weights.shape[0], rows), F32)]
-    work = axle_weights.size * rows
+    work = axle_weights.size * rows // 4
     (begun,) = call(
-        config_near_kernel, at_axle, [axle_weights, own, own_x, a, a_x, b, b_x], response, 3 * work // 2
+        functools.partial(config_kernel, 0, 6),
+        at_axle,
+        [axle_weights, own, own_x, a, a_x, b, b_x, c, d],
+        response,
+        7 * work,
     )
     (config_response,) = call(
-        config_far_kernel, at_axle, [axle_weights, begun, c, d, c_x, d_x], response, work // 2
+        functools.partial(config_kernel, 7, 0), at_axle, [axle_weights, begun, c_x, d_x], response, work
     )
     return (update_rhs, panel_solution, config_response)
 

time: 101 us -> 101 us (level)
  starting transfers between devices: 39.7 us -> 37.7 us
  waiting for transfers between devices: 31.7 us -> 33.4 us
    ppermute x21, waiting for transfers between devices: 17.5 us -> 19.5 us  [by_xor(): return lax.ppermute(value, axis, [(i, i ^ bits) for i in range(size)])]
    ppermute x21, starting transfers between devices: 26.7 us -> 24.7 us  [by_xor(): return lax.ppermute(value, axis, [(i, i ^ bits) for i in range(size)])]
  transfers between devices with their start and end apart: 28 -> 28, of which waited for: 10 -> 13; matrix products, arithmetic and copies ran while one was open for 1% -> 1% of each run, Pallas kernels for 15% -> 14%
where the time goes in v6:
time: 101 us
  starting transfers between devices  37.7 us (37%)
  waiting for transfers between devices  33.4 us (33%)
  Pallas kernels  20.3 us (20%)
  local copies, waits for them, and re-layouts  8 us (8%)
    ppermute x21, starting transfers between devices, by_xor(): return lax.ppermute(value, axis, [(i, i ^ bits) for i in range(size)])  24.7 us
    pallas_call x14, Pallas kernels, call(): pl.pallas_call(kernel, out_shape=shapes, in_specs=[SMEM] * len(at) + [VME...  19.8 us
    ppermute x21, waiting for transfers between devices, by_xor(): return lax.ppermute(value, axis, [(i, i ^ bits) for i in range(size)])  19.5 us
    unnamed x17, local copies, waits for them, and re-layouts  8 us
    ppermute x1, waiting for transfers between devices, small_slice(): d = lax.ppermute(b, 'load', [(i, i ^ 2) for i in middle])  4.99 us
    ppermute x1, starting transfers between devices, small_slice(): b_across = lax.ppermute(b_panel, 'factor', [(0, 2), (1, 3)])  4.45 us
    ppermute x1, waiting for transfers between devices, small_slice(): b_far = lax.ppermute(b_panel, 'factor', [(0, 3), (1, 2)])  3.19 us
    ppermute x1, waiting for transfers between devices, small_slice(): d_x = lax.ppermute(d, 'load', [(i, i ^ 1) for i in (0, 1, 6, 7)])  3.1 us
  transfers between devices with their start and end apart: 28, of which 13 were waited for; matrix products, arithmetic and copies ran while one was open for 1% of the time, Pallas kernels for 14%

profile of v6, /device:TPU:0, one launch (start us, length us, event | category | flops | bytes accessed | tf_op | source)
XLA Modules:
  0.0 100.8 jit_solution(6042949257693216670)
XLA Ops:
  0.7 1.2 %copy-done.5 = bf16[256,2048]{1,0:T(8,128)(2,1)S(1)} copy-done((bf16[256,2048]{1,0:T(8,128)(2,1)S(1)}, bf16[256,2048]{1,0:T(8,128)(2,1)}, u32[]{:S(2)}) %copy-start.5) | copy-done | bytes 1048600
  3.3 4.5 %collective-permute-start.1 = (bf16[512,256]{1,0:T(8,128)(2,1)}, bf16[512,256]{1,0:T(8,128)(2,1)S(1)}, u32[]{:S(2)}, u32[]{:S(2)}) collective-permute-start(bf16[512,256]{1,0:T(8,128)(2,1)} %refs_0_), channel_id=1, source_target_pairs={{0,16},{8,24},{1,17},{9,25},{2,18},{10,26},{3,19},{11,27},{4,20},{... | collective-permute-start | bytes 786440 | tf_op jit(solution)/shard_map/ppermute | solution.py:154
  7.7 1.4 %collective-permute-start.2 = (bf16[512,256]{1,0:T(8,128)(2,1)}, bf16[512,256]{1,0:T(8,128)(2,1)S(1)}, u32[]{:S(2)}, u32[]{:S(2)}) collective-permute-start(bf16[512,256]{1,0:T(8,128)(2,1)} %refs_0_), channel_id=1, source_target_pairs={{0,24},{8,16},{1,25},{9,17},{2,26},{10,18},{3,27},{11,19},{4,28},{... | collective-permute-start | bytes 786440 | tf_op jit(solution)/shard_map/ppermute | solution.py:156
  9.1 2.7 %collective-permute-start.3 = (bf16[256,256]{1,0:T(8,128)(2,1)S(1)}, bf16[256,256]{1,0:T(8,128)(2,1)S(1)}, u32[]{:S(2)}, u32[]{:S(2)}) collective-permute-start(bf16[256,256]{1,0:T(8,128)(2,1)S(1)} %get-tuple-element.46), channel_id=1, source_target_pairs={{0,4},{1,5},{2,6},{3,7},{4,0},{5,1},{6,2},{7,3},{8,12},{9,13},{10,... | collective-permute-start | bytes 393224 | tf_op jit(solution)/shard_map/ppermute | solution.py:124
  11.8 1.3 %collective-permute-start.4 = (bf16[256,256]{1,0:T(8,128)(2,1)S(1)}, bf16[256,256]{1,0:T(8,128)(2,1)S(1)}, u32[]{:S(2)}, u32[]{:S(2)}) collective-permute-start(bf16[256,256]{1,0:T(8,128)(2,1)S(1)} %get-tuple-element.51), channel_id=1, source_target_pairs={{0,5},{1,4},{2,7},{3,6},{4,1},{5,0},{6,3},{7,2},{8,13},{9,12},{10,... | collective-permute-start | bytes 393224 | tf_op jit(solution)/shard_map/ppermute | solution.py:124
  13.0 3.6 %collective-permute-start.5 = (bf16[256,256]{1,0:T(8,128)(2,1)S(1)}, bf16[256,256]{1,0:T(8,128)(2,1)S(1)}, u32[]{:S(2)}, u32[]{:S(2)}) collective-permute-start(bf16[256,256]{1,0:T(8,128)(2,1)S(1)} %get-tuple-element.52), channel_id=1, source_target_pairs={{0,6},{1,7},{2,4},{3,5},{4,2},{5,3},{6,0},{7,1},{8,14},{9,15},{10,... | collective-permute-start | bytes 393224 | tf_op jit(solution)/shard_map/ppermute | solution.py:124
  16.6 3.2 %collective-permute-done.2.refs_3_ = bf16[512,256]{1,0:T(8,128)(2,1)S(1)} collective-permute-done((bf16[512,256]{1,0:T(8,128)(2,1)}, bf16[512,256]{1,0:T(8,128)(2,1)S(1)}, u32[]{:S(2)}, u32[]{:S(2)}) %collective-permute-start.2) | collective-permute-done | bytes 262176 | tf_op jit(solution)/shard_map/ppermute | solution.py:156
  19.8 1.6 %copy-done = bf16[512,2048]{1,0:T(8,128)(2,1)S(1)} copy-done((bf16[512,2048]{1,0:T(8,128)(2,1)S(1)}, bf16[512,2048]{1,0:T(8,128)(2,1)}, u32[]{:S(2)}) %copy-start) | copy-done | bytes 2097176
  22.4 1.3 %shard_map.95.forward_ref.refs_0_ = bf16[512,256]{1,0:T(8,128)(2,1)S(1)} custom-call(s32[4]{0:T(128)S(1)} %iota_xor_fusion.1.at_ref, bf16[512,2048]{1,0:T(8,128)(2,1)S(1)} %copy-done, bf16[512,256]{1,0:T(8,128)(2,1)S(1)} %copy-done.6, bf16[512,256]{1,0:T(8,128)(2,1)S(1)} %collective-permute-done.refs_1_, ...), custom_call_target="tpu_custom_call" | custom-call | flops 536870912 | bytes 3407872 | tf_op jit(solution)/shard_map/pallas_call | solution.py:22
  23.6 2.0 %collective-permute-start.10 = (bf16[512,256]{1,0:T(8,128)(2,1)S(1)}, bf16[512,256]{1,0:T(8,128)(2,1)S(1)}, u32[]{:S(2)}, u32[]{:S(2)}) collective-permute-start(bf16[512,256]{1,0:T(8,128)(2,1)S(1)} %shard_map.95.forward_ref.refs_0_), channel_id=1, source_target_pairs={{0,16},{8,24},{16,0},{24,8},{1,17},{9,25},{17,1},{25,9},{2,18},{10... | collective-permute-start | bytes 786440 | tf_op jit(solution)/shard_map/ppermute | solution.py:124
  25.7 4.5 %collective-permute-start.6 = (bf16[256,256]{1,0:T(8,128)(2,1)S(1)}, bf16[256,256]{1,0:T(8,128)(2,1)S(1)}, u32[]{:S(2)}, u32[]{:S(2)}) collective-permute-start(bf16[256,256]{1,0:T(8,128)(2,1)S(1)} %get-tuple-element.53), channel_id=1, source_target_pairs={{0,7},{1,6},{2,5},{3,4},{4,3},{5,2},{6,1},{7,0},{8,15},{9,14},{10,... | collective-permute-start | bytes 393224 | tf_op jit(solution)/shard_map/ppermute | solution.py:124
  30.8 2.9 %collective-permute-start.9 = (bf16[256,256]{1,0:T(8,128)(2,1)S(1)}, bf16[256,256]{1,0:T(8,128)(2,1)S(1)}, u32[]{:S(2)}, u32[]{:S(2)}) collective-permute-start(bf16[256,256]{1,0:T(8,128)(2,1)S(1)} %get-tuple-element.56), channel_id=1, source_target_pairs={{0,3},{1,2},{2,1},{3,0},{4,7},{5,6},{6,5},{7,4},{8,11},{9,10},{10,... | collective-permute-start | bytes 393224 | tf_op jit(solution)/shard_map/ppermute | solution.py:124
  33.8 3.4 %copy-done.2 = bf16[2048,2048]{1,0:T(8,128)(2,1)S(1)} copy-done((bf16[2048,2048]{1,0:T(8,128)(2,1)S(1)}, bf16[2048,2048]{1,0:T(8,128)(2,1)}, u32[]{:S(2)}) %copy-start.2) | copy-done | bytes 8388632
  37.7 1.8 %shard_map.97.begun_ref = f32[4,256,512]{2,1,0:T(8,128)S(1)} custom-call(s32[12]{0:T(128)S(1)} %pad_add_fusion.at_ref, bf16[2048,2048]{1,0:T(8,128)(2,1)S(1)} %shard_map.96.factor_ref, bf16[256,256]{1,0:T(8,128)(2,1)S(1)} %get-tuple-element.45.refs_0_, bf16[256,256]{1,0:T(8,128)(2,1)S(1)} %collective-permute-done.3.refs_1_, ...), custom_call_target="tpu_custom_call" | custom-call | flops 1073741824 | bytes 11010048 | tf_op jit(solution)/shard_map/pallas_call | solution.py:22
  40.0 1.0 shard_map.99
  42.7 1.0 shard_map.101
  45.3 7.2 %collective-permute-done.13.across_ref = bf16[256,512]{1,0:T(8,128)(2,1)S(1)} collective-permute-done((bf16[256,512]{1,0:T(8,128)(2,1)S(1)}, bf16[256,512]{1,0:T(8,128)(2,1)S(1)}, u32[]{:S(2)}, u32[]{:S(2)}) %collective-permute-start.13) | collective-permute-done | bytes 262176 | tf_op jit(solution)/shard_map/ppermute | solution.py:124
  55.0 1.4 %collective-permute-start.15 = (bf16[256,512]{1,0:T(8,128)(2,1)S(1)}, bf16[256,512]{1,0:T(8,128)(2,1)S(1)}, u32[]{:S(2)}, u32[]{:S(2)}) collective-permute-start(bf16[256,512]{1,0:T(8,128)(2,1)S(1)} %add_convert_fusion.1), channel_id=1, source_target_pairs={{16,0},{24,8},{17,1},{25,9},{18,2},{26,10},{19,3},{27,11},{20,4},{... | collective-permute-start | bytes 786440 | tf_op jit(solution)/shard_map/ppermute | solution.py:215
  57.8 4.4 %shard_map.104 = bf16[2048,256]{1,0:T(8,128)(2,1)} custom-call(s32[4]{0:T(128)S(1)} %iota_xor_fusion.1.at_ref, bf16[2048,2048]{1,0:T(8,128)(2,1)S(1)} %shard_map.96.factor_ref, bf16[2048,256]{1,0:T(8,128)(2,1)S(1)} %copy-done.4, bf16[512,256]{1,0:T(8,128)(2,1)S(1)} %shard_map.95.forward_ref.refs_0_, bf16[512,256]{1,0:T(8,128)(2,1)S(1)} %collective-permute-done.16.refs_1_, ...), custom_call_target="tpu_custom_call" | custom-call | flops 2147483648 | bytes 11534336 | tf_op jit(solution)/shard_map/pallas_call | solution.py:22
  63.0 2.6 %collective-permute-done.15 = bf16[256,512]{1,0:T(8,128)(2,1)S(1)} collective-permute-done((bf16[256,512]{1,0:T(8,128)(2,1)S(1)}, bf16[256,512]{1,0:T(8,128)(2,1)S(1)}, u32[]{:S(2)}, u32[]{:S(2)}) %collective-permute-start.15) | collective-permute-done | bytes 262176 | tf_op jit(solution)/shard_map/ppermute | solution.py:215
  65.8 1.3 %collective-permute-start.19 = (bf16[256,512]{1,0:T(8,128)(2,1)S(1)}, bf16[256,512]{1,0:T(8,128)(2,1)S(1)}, u32[]{:S(2)}, u32[]{:S(2)}) collective-permute-start(bf16[256,512]{1,0:T(8,128)(2,1)S(1)} %add_convert_fusion.refs_0_), channel_id=1, source_target_pairs={{0,1},{1,0},{2,3},{3,2},{4,5},{5,4},{6,7},{7,6},{8,9},{9,8},{10,11... | collective-permute-start | bytes 786440 | tf_op jit(solution)/shard_map/ppermute | solution.py:124
  67.1 1.7 %collective-permute-start.20 = (bf16[256,512]{1,0:T(8,128)(2,1)S(1)}, bf16[256,512]{1,0:T(8,128)(2,1)S(1)}, u32[]{:S(2)}, u32[]{:S(2)}) collective-permute-start(bf16[256,512]{1,0:T(8,128)(2,1)S(1)} %add_convert_fusion.refs_0_), channel_id=1, source_target_pairs={{0,2},{1,3},{2,0},{3,1},{4,6},{5,7},{6,4},{7,5},{8,10},{9,11},{10,... | collective-permute-start | bytes 786440 | tf_op jit(solution)/shard_map/ppermute | solution.py:124
  69.6 3.9 %collective-permute-done.19.refs_1_ = bf16[256,512]{1,0:T(8,128)(2,1)S(1)} collective-permute-done((bf16[256,512]{1,0:T(8,128)(2,1)S(1)}, bf16[256,512]{1,0:T(8,128)(2,1)S(1)}, u32[]{:S(2)}, u32[]{:S(2)}) %collective-permute-start.19) | collective-permute-done | bytes 262176 | tf_op jit(solution)/shard_map/ppermute | solution.py:124
  73.6 2.0 %collective-permute-done.20.refs_2_ = bf16[256,512]{1,0:T(8,128)(2,1)S(1)} collective-permute-done((bf16[256,512]{1,0:T(8,128)(2,1)S(1)}, bf16[256,512]{1,0:T(8,128)(2,1)S(1)}, u32[]{:S(2)}, u32[]{:S(2)}) %collective-permute-start.20) | collective-permute-done | bytes 262176 | tf_op jit(solution)/shard_map/ppermute | solution.py:124
  76.8 4.3 %collective-permute-done.21.refs_4_ = bf16[256,512]{1,0:T(8,128)(2,1)S(1)} collective-permute-done((bf16[256,512]{1,0:T(8,128)(2,1)S(1)}, bf16[256,512]{1,0:T(8,128)(2,1)S(1)}, u32[]{:S(2)}, u32[]{:S(2)}) %collective-permute-start.21) | collective-permute-done | bytes 262176 | tf_op jit(solution)/shard_map/ppermute | solution.py:124
  82.0 1.3 %collective-permute-start.25 = (bf16[256,512]{1,0:T(8,128)(2,1)S(1)}, bf16[256,512]{1,0:T(8,128)(2,1)S(1)}, u32[]{:S(2)}, u32[]{:S(2)}) collective-permute-start(bf16[256,512]{1,0:T(8,128)(2,1)S(1)} %collective-permute-done.21.refs_4_), channel_id=1, source_target_pairs={{2,0},{3,1},{4,6},{5,7},{10,8},{11,9},{12,14},{13,15},{18,16},{19,... | collective-permute-start | bytes 786440 | tf_op jit(solution)/shard_map/ppermute | solution.py:240
  83.9 1.4 %collective-permute-start.26 = (bf16[256,512]{1,0:T(8,128)(2,1)S(1)}, bf16[256,512]{1,0:T(8,128)(2,1)}, u32[]{:S(2)}, u32[]{:S(2)}) collective-permute-start(bf16[256,512]{1,0:T(8,128)(2,1)S(1)} %collective-permute-done.24.refs_6_), channel_id=1, source_target_pairs={{2,3},{3,2},{4,5},{5,4},{10,11},{11,10},{12,13},{13,12},{18,19},{1... | collective-permute-start | bytes 786440 | tf_op jit(solution)/shard_map/ppermute | solution.py:242
  85.2 5.0 %collective-permute-done.25.refs_7_ = bf16[256,512]{1,0:T(8,128)(2,1)S(1)} collective-permute-done((bf16[256,512]{1,0:T(8,128)(2,1)S(1)}, bf16[256,512]{1,0:T(8,128)(2,1)S(1)}, u32[]{:S(2)}, u32[]{:S(2)}) %collective-permute-start.25) | collective-permute-done | bytes 262176 | tf_op jit(solution)/shard_map/ppermute | solution.py:240
  90.2 2.4 %collective-permute-start.27 = (bf16[256,512]{1,0:T(8,128)(2,1)S(1)}, bf16[256,512]{1,0:T(8,128)(2,1)}, u32[]{:S(2)}, u32[]{:S(2)}) collective-permute-start(bf16[256,512]{1,0:T(8,128)(2,1)S(1)} %collective-permute-done.25.refs_7_), channel_id=1, source_target_pairs={{0,1},{1,0},{6,7},{7,6},{8,9},{9,8},{14,15},{15,14},{16,17},{17,16... | collective-permute-start | bytes 786440 | tf_op jit(solution)/shard_map/ppermute | solution.py:243
  93.6 1.8 %shard_map.107.refs_0_ = f32[384,512]{1,0:T(8,128)S(1)} custom-call(s32[9]{0:T(128)S(1)} %pad_add_fusion.1.at_ref, bf16[384,2048]{1,0:T(8,128)(2,1)S(1)} %copy-done.3, bf16[256,512]{1,0:T(8,128)(2,1)S(1)} %add_convert_fusion.refs_0_, bf16[256,512]{1,0:T(8,128)(2,1)S(1)} %collective-permute-done.19.refs_1_, ...), custom_call_target="tpu_custom_call" | custom-call | flops 704643072 | bytes 4456448 | tf_op jit(solution)/shard_map/pallas_call | solution.py:22
  95.5 3.1 %collective-permute-done.27.refs_2_ = bf16[256,512]{1,0:T(8,128)(2,1)} collective-permute-done((bf16[256,512]{1,0:T(8,128)(2,1)S(1)}, bf16[256,512]{1,0:T(8,128)(2,1)}, u32[]{:S(2)}, u32[]{:S(2)}) %collective-permute-start.27) | collective-permute-done | bytes 262176 | tf_op jit(solution)/shard_map/ppermute | solution.py:243
  98.6 2.2 %shard_map.108 = f32[384,512]{1,0:T(8,128)} custom-call(s32[9]{0:T(128)S(1)} %pad_add_fusion.1.at_ref, bf16[384,2048]{1,0:T(8,128)(2,1)S(1)} %copy-done.3, f32[384,512]{1,0:T(8,128)S(1)} %shard_map.107.refs_0_, bf16[256,512]{1,0:T(8,128)(2,1)} %collective-permute-done.26.refs_1_, bf16[256,512]{1,0:T(8,128)(2,1)} %collective-permute-done.27.refs_2_), custom_call_target="tpu_custom_call" | custom-call | flops 100663296 | bytes 3670016 | tf_op jit(solution)/shard_map/pallas_call | solution.py:22
  (64 shorter events, 16.4 us)
Async XLA Ops:
  2.7 10.3 %collective-permute-start = (bf16[512,256]{1,0:T(8,128)(2,1)}, bf16[512,256]{1,0:T(8,128)(2,1)S(1)}, u32[]{:S(2)}, u32[]{:S(2)}) collective-permute-start(bf16[512,256]{1,0:T(8,128)(2,1)} %refs_0_), channel_id=1, source_target_pairs={{0,8},{8,0},{16,24},{24,16},{1,9},{9,1},{17,25},{25,17},{2,10},{10... | collective-permute-start | bytes 786440 | tf_op jit(solution)/shard_map/ppermute | solution.py:124
  3.3 13.4 %collective-permute-start.1 = (bf16[512,256]{1,0:T(8,128)(2,1)}, bf16[512,256]{1,0:T(8,128)(2,1)S(1)}, u32[]{:S(2)}, u32[]{:S(2)}) collective-permute-start(bf16[512,256]{1,0:T(8,128)(2,1)} %refs_0_), channel_id=1, source_target_pairs={{0,16},{8,24},{1,17},{9,25},{2,18},{10,26},{3,19},{11,27},{4,20},{... | collective-permute-start | bytes 786440 | tf_op jit(solution)/shard_map/ppermute | solution.py:154
  7.7 12.1 %collective-permute-start.2 = (bf16[512,256]{1,0:T(8,128)(2,1)}, bf16[512,256]{1,0:T(8,128)(2,1)S(1)}, u32[]{:S(2)}, u32[]{:S(2)}) collective-permute-start(bf16[512,256]{1,0:T(8,128)(2,1)} %refs_0_), channel_id=1, source_target_pairs={{0,24},{8,16},{1,25},{9,17},{2,26},{10,18},{3,27},{11,19},{4,28},{... | collective-permute-start | bytes 786440 | tf_op jit(solution)/shard_map/ppermute | solution.py:156
  9.1 21.1 %collective-permute-start.3 = (bf16[256,256]{1,0:T(8,128)(2,1)S(1)}, bf16[256,256]{1,0:T(8,128)(2,1)S(1)}, u32[]{:S(2)}, u32[]{:S(2)}) collective-permute-start(bf16[256,256]{1,0:T(8,128)(2,1)S(1)} %get-tuple-element.46), channel_id=1, source_target_pairs={{0,4},{1,5},{2,6},{3,7},{4,0},{5,1},{6,2},{7,3},{8,12},{9,13},{10,... | collective-permute-start | bytes 393224 | tf_op jit(solution)/shard_map/ppermute | solution.py:124
  11.8 19.0 %collective-permute-start.4 = (bf16[256,256]{1,0:T(8,128)(2,1)S(1)}, bf16[256,256]{1,0:T(8,128)(2,1)S(1)}, u32[]{:S(2)}, u32[]{:S(2)}) collective-permute-start(bf16[256,256]{1,0:T(8,128)(2,1)S(1)} %get-tuple-element.51), channel_id=1, source_target_pairs={{0,5},{1,4},{2,7},{3,6},{4,1},{5,0},{6,3},{7,2},{8,13},{9,12},{10,... | collective-permute-start | bytes 393224 | tf_op jit(solution)/shard_map/ppermute | solution.py:124
  13.0 17.7 %collective-permute-start.5 = (bf16[256,256]{1,0:T(8,128)(2,1)S(1)}, bf16[256,256]{1,0:T(8,128)(2,1)S(1)}, u32[]{:S(2)}, u32[]{:S(2)}) collective-permute-start(bf16[256,256]{1,0:T(8,128)(2,1)S(1)} %get-tuple-element.52), channel_id=1, source_target_pairs={{0,6},{1,7},{2,4},{3,5},{4,2},{5,3},{6,0},{7,1},{8,14},{9,15},{10,... | collective-permute-start | bytes 393224 | tf_op jit(solution)/shard_map/ppermute | solution.py:124
  23.6 16.3 %collective-permute-start.10 = (bf16[512,256]{1,0:T(8,128)(2,1)S(1)}, bf16[512,256]{1,0:T(8,128)(2,1)S(1)}, u32[]{:S(2)}, u32[]{:S(2)}) collective-permute-start(bf16[512,256]{1,0:T(8,128)(2,1)S(1)} %shard_map.95.forward_ref.refs_0_), channel_id=1, source_target_pairs={{0,16},{8,24},{16,0},{24,8},{1,17},{9,25},{17,1},{25,9},{2,18},{10... | collective-permute-start | bytes 786440 | tf_op jit(solution)/shard_map/ppermute | solution.py:124
  25.7 14.3 %collective-permute-start.6 = (bf16[256,256]{1,0:T(8,128)(2,1)S(1)}, bf16[256,256]{1,0:T(8,128)(2,1)S(1)}, u32[]{:S(2)}, u32[]{:S(2)}) collective-permute-start(bf16[256,256]{1,0:T(8,128)(2,1)S(1)} %get-tuple-element.53), channel_id=1, source_target_pairs={{0,7},{1,6},{2,5},{3,4},{4,3},{5,2},{6,1},{7,0},{8,15},{9,14},{10,... | collective-permute-start | bytes 393224 | tf_op jit(solution)/shard_map/ppermute | solution.py:124
  30.2 9.8 %collective-permute-start.7 = (bf16[256,256]{1,0:T(8,128)(2,1)S(1)}, bf16[256,256]{1,0:T(8,128)(2,1)S(1)}, u32[]{:S(2)}, u32[]{:S(2)}) collective-permute-start(bf16[256,256]{1,0:T(8,128)(2,1)S(1)} %get-tuple-element.54), channel_id=1, source_target_pairs={{0,1},{1,0},{2,3},{3,2},{4,5},{5,4},{6,7},{7,6},{8,9},{9,8},{10,11... | collective-permute-start | bytes 393224 | tf_op jit(solution)/shard_map/ppermute | solution.py:124
  30.7 9.2 %collective-permute-start.8 = (bf16[256,256]{1,0:T(8,128)(2,1)S(1)}, bf16[256,256]{1,0:T(8,128)(2,1)S(1)}, u32[]{:S(2)}, u32[]{:S(2)}) collective-permute-start(bf16[256,256]{1,0:T(8,128)(2,1)S(1)} %get-tuple-element.55), channel_id=1, source_target_pairs={{0,2},{1,3},{2,0},{3,1},{4,6},{5,7},{6,4},{7,5},{8,10},{9,11},{10,... | collective-permute-start | bytes 393224 | tf_op jit(solution)/shard_map/ppermute | solution.py:124
  30.8 9.2 %collective-permute-start.9 = (bf16[256,256]{1,0:T(8,128)(2,1)S(1)}, bf16[256,256]{1,0:T(8,128)(2,1)S(1)}, u32[]{:S(2)}, u32[]{:S(2)}) collective-permute-start(bf16[256,256]{1,0:T(8,128)(2,1)S(1)} %get-tuple-element.56), channel_id=1, source_target_pairs={{0,3},{1,2},{2,1},{3,0},{4,7},{5,6},{6,5},{7,4},{8,11},{9,10},{10,... | collective-permute-start | bytes 393224 | tf_op jit(solution)/shard_map/ppermute | solution.py:124
  33.8 3.4 %copy-start.2 = (bf16[2048,2048]{1,0:T(8,128)(2,1)S(1)}, bf16[2048,2048]{1,0:T(8,128)(2,1)}, u32[]{:S(2)}) copy-start(bf16[2048,2048]{1,0:T(8,128)(2,1)} %factor_ref.1) | copy-start | bytes 25165828
  41.0 1.6 %collective-permute-start.11 = (bf16[256,512]{1,0:T(8,128)(2,1)S(1)}, bf16[256,512]{1,0:T(8,128)(2,1)S(1)}, u32[]{:S(2)}, u32[]{:S(2)}) collective-permute-start(bf16[256,512]{1,0:T(8,128)(2,1)S(1)} %shard_map.99), channel_id=1, source_target_pairs={{0,8},{8,0},{16,24},{24,16},{1,9},{9,1},{17,25},{25,17},{2,10},{10... | collective-permute-start | bytes 786440 | tf_op jit(solution)/shard_map/ppermute | solution.py:124
  43.6 8.8 %copy-start.1 = (bf16[512,2048]{1,0:T(8,128)(2,1)S(1)}, bf16[512,2048]{1,0:T(8,128)(2,1)}, u32[]{:S(2)}) copy-start(bf16[512,2048]{1,0:T(8,128)(2,1)} %inverse_ref.9) | copy-start | bytes 6291460
  43.7 1.6 %collective-permute-start.12 = (bf16[256,512]{1,0:T(8,128)(2,1)S(1)}, bf16[256,512]{1,0:T(8,128)(2,1)S(1)}, u32[]{:S(2)}, u32[]{:S(2)}) collective-permute-start(bf16[256,512]{1,0:T(8,128)(2,1)S(1)} %shard_map.101), channel_id=1, source_target_pairs={{0,8},{8,0},{16,24},{24,16},{1,9},{9,1},{17,25},{25,17},{2,10},{10... | collective-permute-start | bytes 786440 | tf_op jit(solution)/shard_map/ppermute | solution.py:124
  43.9 8.6 %collective-permute-start.13 = (bf16[256,512]{1,0:T(8,128)(2,1)S(1)}, bf16[256,512]{1,0:T(8,128)(2,1)S(1)}, u32[]{:S(2)}, u32[]{:S(2)}) collective-permute-start(bf16[256,512]{1,0:T(8,128)(2,1)S(1)} %add_convert_fusion.2), channel_id=1, source_target_pairs={{0,16},{8,24},{16,0},{24,8},{1,17},{9,25},{17,1},{25,9},{2,18},{10... | collective-permute-start | bytes 786440 | tf_op jit(solution)/shard_map/ppermute | solution.py:124
  53.4 1.6 %collective-permute-start.14 = (bf16[256,512]{1,0:T(8,128)(2,1)S(1)}, bf16[256,512]{1,0:T(8,128)(2,1)S(1)}, u32[]{:S(2)}, u32[]{:S(2)}) collective-permute-start(bf16[256,512]{1,0:T(8,128)(2,1)S(1)} %get-tuple-element.61), channel_id=1, source_target_pairs={{0,8},{8,0},{16,24},{24,16},{1,9},{9,1},{17,25},{25,17},{2,10},{10... | collective-permute-start | bytes 786440 | tf_op jit(solution)/shard_map/ppermute | solution.py:124
  53.4 4.3 %collective-permute-start.16 = (bf16[512,256]{1,0:T(8,128)(2,1)S(1)}, bf16[512,256]{1,0:T(8,128)(2,1)S(1)}, u32[]{:S(2)}, u32[]{:S(2)}) collective-permute-start(bf16[512,256]{1,0:T(8,128)(2,1)S(1)} %shard_map.95.forward_ref.refs_0_), channel_id=1, source_target_pairs={{0,8},{8,0},{16,24},{24,16},{1,9},{9,1},{17,25},{25,17},{2,10},{10... | collective-permute-start | bytes 786440 | tf_op jit(solution)/shard_map/ppermute | solution.py:124
  53.9 3.8 %collective-permute-start.17 = (bf16[512,256]{1,0:T(8,128)(2,1)S(1)}, bf16[512,256]{1,0:T(8,128)(2,1)S(1)}, u32[]{:S(2)}, u32[]{:S(2)}) collective-permute-start(bf16[512,256]{1,0:T(8,128)(2,1)S(1)} %collective-permute-done.10.refs_2_), channel_id=1, source_target_pairs={{0,8},{8,0},{16,24},{24,16},{1,9},{9,1},{17,25},{25,17},{2,10},{10... | collective-permute-start | bytes 786440 | tf_op jit(solution)/shard_map/ppermute | solution.py:124
  55.0 10.6 %collective-permute-start.15 = (bf16[256,512]{1,0:T(8,128)(2,1)S(1)}, bf16[256,512]{1,0:T(8,128)(2,1)S(1)}, u32[]{:S(2)}, u32[]{:S(2)}) collective-permute-start(bf16[256,512]{1,0:T(8,128)(2,1)S(1)} %add_convert_fusion.1), channel_id=1, source_target_pairs={{16,0},{24,8},{17,1},{25,9},{18,2},{26,10},{19,3},{27,11},{20,4},{... | collective-permute-start | bytes 786440 | tf_op jit(solution)/shard_map/ppermute | solution.py:215
  57.3 8.3 %collective-permute-start.18 = (bf16[256,512]{1,0:T(8,128)(2,1)S(1)}, bf16[256,512]{1,0:T(8,128)(2,1)S(1)}, u32[]{:S(2)}, u32[]{:S(2)}) collective-permute-start(bf16[256,512]{1,0:T(8,128)(2,1)S(1)} %shard_map.106), channel_id=1, source_target_pairs={{0,8},{8,0},{16,24},{24,16},{1,9},{9,1},{17,25},{25,17},{2,10},{10... | collective-permute-start | bytes 786440 | tf_op jit(solution)/shard_map/ppermute | solution.py:124
  62.2 30.5 %copy-start.7 = (s32[8]{0:T(128)S(1)}, s32[8]{0:T(128)}, u32[]{:S(2)}) copy-start(s32[8]{0:T(128)} %constant.14.clone) | copy-start | bytes 100
  62.2 31.4 %copy-start.3 = (bf16[384,2048]{1,0:T(8,128)(2,1)S(1)}, bf16[384,2048]{1,0:T(8,128)(2,1)}, u32[]{:S(2)}) copy-start(bf16[384,2048]{1,0:T(8,128)(2,1)} %axle_ref.3) | copy-start | bytes 4718596
  65.8 7.8 %collective-permute-start.19 = (bf16[256,512]{1,0:T(8,128)(2,1)S(1)}, bf16[256,512]{1,0:T(8,128)(2,1)S(1)}, u32[]{:S(2)}, u32[]{:S(2)}) collective-permute-start(bf16[256,512]{1,0:T(8,128)(2,1)S(1)} %add_convert_fusion.refs_0_), channel_id=1, source_target_pairs={{0,1},{1,0},{2,3},{3,2},{4,5},{5,4},{6,7},{7,6},{8,9},{9,8},{10,11... | collective-permute-start | bytes 786440 | tf_op jit(solution)/shard_map/ppermute | solution.py:124
  67.1 8.5 %collective-permute-start.20 = (bf16[256,512]{1,0:T(8,128)(2,1)S(1)}, bf16[256,512]{1,0:T(8,128)(2,1)S(1)}, u32[]{:S(2)}, u32[]{:S(2)}) collective-permute-start(bf16[256,512]{1,0:T(8,128)(2,1)S(1)} %add_convert_fusion.refs_0_), channel_id=1, source_target_pairs={{0,2},{1,3},{2,0},{3,1},{4,6},{5,7},{6,4},{7,5},{8,10},{9,11},{10,... | collective-permute-start | bytes 786440 | tf_op jit(solution)/shard_map/ppermute | solution.py:124
  68.8 12.3 %collective-permute-start.21 = (bf16[256,512]{1,0:T(8,128)(2,1)S(1)}, bf16[256,512]{1,0:T(8,128)(2,1)S(1)}, u32[]{:S(2)}, u32[]{:S(2)}) collective-permute-start(bf16[256,512]{1,0:T(8,128)(2,1)S(1)} %add_convert_fusion.refs_0_), channel_id=1, source_target_pairs={{0,6},{1,7},{2,4},{3,5},{4,2},{5,3},{6,0},{7,1},{8,14},{9,15},{10,... | collective-permute-start | bytes 786440 | tf_op jit(solution)/shard_map/ppermute | solution.py:124
  75.6 6.4 %collective-permute-start.22 = (bf16[256,512]{1,0:T(8,128)(2,1)S(1)}, bf16[256,512]{1,0:T(8,128)(2,1)S(1)}, u32[]{:S(2)}, u32[]{:S(2)}) collective-permute-start(bf16[256,512]{1,0:T(8,128)(2,1)S(1)} %collective-permute-done.20.refs_2_), channel_id=1, source_target_pairs={{0,1},{1,0},{2,3},{3,2},{4,5},{5,4},{6,7},{7,6},{8,9},{9,8},{10,11... | collective-permute-start | bytes 786440 | tf_op jit(solution)/shard_map/ppermute | solution.py:124
  76.1 7.7 %collective-permute-start.24 = (bf16[256,512]{1,0:T(8,128)(2,1)S(1)}, bf16[256,512]{1,0:T(8,128)(2,1)S(1)}, u32[]{:S(2)}, u32[]{:S(2)}) collective-permute-start(bf16[256,512]{1,0:T(8,128)(2,1)S(1)} %collective-permute-done.20.refs_2_), channel_id=1, source_target_pairs={{2,4},{3,5},{4,2},{5,3},{10,12},{11,13},{12,10},{13,11},{18,20},{1... | collective-permute-start | bytes 786440 | tf_op jit(solution)/shard_map/ppermute | solution.py:239
  82.0 8.3 %collective-permute-start.25 = (bf16[256,512]{1,0:T(8,128)(2,1)S(1)}, bf16[256,512]{1,0:T(8,128)(2,1)S(1)}, u32[]{:S(2)}, u32[]{:S(2)}) collective-permute-start(bf16[256,512]{1,0:T(8,128)(2,1)S(1)} %collective-permute-done.21.refs_4_), channel_id=1, source_target_pairs={{2,0},{3,1},{4,6},{5,7},{10,8},{11,9},{12,14},{13,15},{18,16},{19,... | collective-permute-start | bytes 786440 | tf_op jit(solution)/shard_map/ppermute | solution.py:240
  83.3 10.4 %collective-permute-start.23 = (bf16[256,512]{1,0:T(8,128)(2,1)S(1)}, bf16[256,512]{1,0:T(8,128)(2,1)}, u32[]{:S(2)}, u32[]{:S(2)}) collective-permute-start(bf16[256,512]{1,0:T(8,128)(2,1)S(1)} %collective-permute-done.21.refs_4_), channel_id=1, source_target_pairs={{0,1},{1,0},{2,3},{3,2},{4,5},{5,4},{6,7},{7,6},{8,9},{9,8},{10,11... | collective-permute-start | bytes 786440 | tf_op jit(solution)/shard_map/ppermute | solution.py:124
  83.9 11.6 %collective-permute-start.26 = (bf16[256,512]{1,0:T(8,128)(2,1)S(1)}, bf16[256,512]{1,0:T(8,128)(2,1)}, u32[]{:S(2)}, u32[]{:S(2)}) collective-permute-start(bf16[256,512]{1,0:T(8,128)(2,1)S(1)} %collective-permute-done.24.refs_6_), channel_id=1, source_target_pairs={{2,3},{3,2},{4,5},{5,4},{10,11},{11,10},{12,13},{13,12},{18,19},{1... | collective-permute-start | bytes 786440 | tf_op jit(solution)/shard_map/ppermute | solution.py:242
  90.2 8.4 %collective-permute-start.27 = (bf16[256,512]{1,0:T(8,128)(2,1)S(1)}, bf16[256,512]{1,0:T(8,128)(2,1)}, u32[]{:S(2)}, u32[]{:S(2)}) collective-permute-start(bf16[256,512]{1,0:T(8,128)(2,1)S(1)} %collective-permute-done.25.refs_7_), channel_id=1, source_target_pairs={{0,1},{1,0},{6,7},{7,6},{8,9},{9,8},{14,15},{15,14},{16,17},{17,16... | collective-permute-start | bytes 786440 | tf_op jit(solution)/shard_map/ppermute | solution.py:243
  (4 other events, 6.7 us)

commit v7 on v6

--- a/solution.py
+++ b/solution.py
@@ -153,7 +153,7 @@
 
     b_across = lax.ppermute(b_panel, "factor", [(0, 2), (1, 3)])
     b_core = by_xor(b_panel, "factor", factors, 1)
-    b_far = lax.ppermute(b_panel, "factor", [(0, 3), (1, 2)])
+    b_far = lax.ppermute(b_across, "factor", [(2, 3), (3, 2)])
     (forward,) = call(
         forward_kernel,
         at_factor,

time: 101 us -> 113 us (1.12)
  the two profiles are of different devices: /device:TPU:0 before, /device:TPU:24 now
where the time goes in v7:
time: 113 us
  waiting for transfers between devices  43.9 us (39%)
  starting transfers between devices  39.1 us (35%)
  Pallas kernels  20.3 us (18%)
  local copies, waits for them, and re-layouts  8 us (7%)
    ppermute x21, waiting for transfers between devices, by_xor(): return lax.ppermute(value, axis, [(i, i ^ bits) for i in range(size)])  28.9 us
    ppermute x21, starting transfers between devices, by_xor(): return lax.ppermute(value, axis, [(i, i ^ bits) for i in range(size)])  27.1 us
    pallas_call x14, Pallas kernels, call(): pl.pallas_call(kernel, out_shape=shapes, in_specs=[SMEM] * len(at) + [VME...  19.8 us
    unnamed x17, local copies, waits for them, and re-layouts  8 us
    ppermute x1, waiting for transfers between devices, small_slice(): b_across = lax.ppermute(b_panel, 'factor', [(0, 2), (1, 3)])  5.77 us
    ppermute x1, waiting for transfers between devices, small_slice(): d = lax.ppermute(b, 'load', [(i, i ^ 2) for i in middle])  4.29 us
    ppermute x1, starting transfers between devices, small_slice(): b_across = lax.ppermute(b_panel, 'factor', [(0, 2), (1, 3)])  3.44 us
    ppermute x1, starting transfers between devices, small_slice(): d_x = lax.ppermute(d, 'load', [(i, i ^ 1) for i in (0, 1, 6, 7)])  3.14 us
  transfers between devices with their start and end apart: 28, of which 11 were waited for; matrix products, arithmetic and copies ran while one was open for 1% of the time, Pallas kernels for 13%

profile of v7, /device:TPU:24, one launch (start us, length us, event | category | flops | bytes accessed | tf_op | source)
XLA Modules:
  0.0 112.7 jit_solution(8693559721820717451)
XLA Ops:
  0.7 1.2 %copy-done.5 = bf16[256,2048]{1,0:T(8,128)(2,1)S(1)} copy-done((bf16[256,2048]{1,0:T(8,128)(2,1)S(1)}, bf16[256,2048]{1,0:T(8,128)(2,1)}, u32[]{:S(2)}) %copy-start.5) | copy-done | bytes 1048600
  2.7 3.4 %collective-permute-start.1 = (bf16[512,256]{1,0:T(8,128)(2,1)}, bf16[512,256]{1,0:T(8,128)(2,1)S(1)}, u32[]{:S(2)}, u32[]{:S(2)}) collective-permute-start(bf16[512,256]{1,0:T(8,128)(2,1)} %refs_0_), channel_id=1, source_target_pairs={{0,16},{8,24},{1,17},{9,25},{2,18},{10,26},{3,19},{11,27},{4,20},{... | collective-permute-start | bytes 786440 | tf_op jit(solution)/shard_map/ppermute | solution.py:154
  6.3 5.8 %collective-permute-done.1.refs_2_ = bf16[512,256]{1,0:T(8,128)(2,1)S(1)} collective-permute-done((bf16[512,256]{1,0:T(8,128)(2,1)}, bf16[512,256]{1,0:T(8,128)(2,1)S(1)}, u32[]{:S(2)}, u32[]{:S(2)}) %collective-permute-start.1) | collective-permute-done | bytes 262176 | tf_op jit(solution)/shard_map/ppermute | solution.py:154
  13.1 3.5 %collective-permute-start.4 = (bf16[256,256]{1,0:T(8,128)(2,1)S(1)}, bf16[256,256]{1,0:T(8,128)(2,1)S(1)}, u32[]{:S(2)}, u32[]{:S(2)}) collective-permute-start(bf16[256,256]{1,0:T(8,128)(2,1)S(1)} %get-tuple-element.51), channel_id=1, source_target_pairs={{0,5},{1,4},{2,7},{3,6},{4,1},{5,0},{6,3},{7,2},{8,13},{9,12},{10,... | collective-permute-start | bytes 393224 | tf_op jit(solution)/shard_map/ppermute | solution.py:124
  16.9 1.6 %copy-done = bf16[512,2048]{1,0:T(8,128)(2,1)S(1)} copy-done((bf16[512,2048]{1,0:T(8,128)(2,1)S(1)}, bf16[512,2048]{1,0:T(8,128)(2,1)}, u32[]{:S(2)}) %copy-start) | copy-done | bytes 2097176
  19.4 1.3 %shard_map.95.forward_ref.refs_0_ = bf16[512,256]{1,0:T(8,128)(2,1)S(1)} custom-call(s32[4]{0:T(128)S(1)} %iota_xor_fusion.1.at_ref, bf16[512,2048]{1,0:T(8,128)(2,1)S(1)} %copy-done, bf16[512,256]{1,0:T(8,128)(2,1)S(1)} %copy-done.6, bf16[512,256]{1,0:T(8,128)(2,1)S(1)} %collective-permute-done.refs_1_, ...), custom_call_target="tpu_custom_call" | custom-call | flops 536870912 | bytes 3407872 | tf_op jit(solution)/shard_map/pallas_call | solution.py:22
  20.7 3.7 %collective-permute-start.10 = (bf16[512,256]{1,0:T(8,128)(2,1)S(1)}, bf16[512,256]{1,0:T(8,128)(2,1)S(1)}, u32[]{:S(2)}, u32[]{:S(2)}) collective-permute-start(bf16[512,256]{1,0:T(8,128)(2,1)S(1)} %shard_map.95.forward_ref.refs_0_), channel_id=1, source_target_pairs={{0,16},{8,24},{16,0},{24,8},{1,17},{9,25},{17,1},{25,9},{2,18},{10... | collective-permute-start | bytes 786440 | tf_op jit(solution)/shard_map/ppermute | solution.py:124
  24.4 3.6 %collective-permute-start.6 = (bf16[256,256]{1,0:T(8,128)(2,1)S(1)}, bf16[256,256]{1,0:T(8,128)(2,1)S(1)}, u32[]{:S(2)}, u32[]{:S(2)}) collective-permute-start(bf16[256,256]{1,0:T(8,128)(2,1)S(1)} %get-tuple-element.53), channel_id=1, source_target_pairs={{0,7},{1,6},{2,5},{3,4},{4,3},{5,2},{6,1},{7,0},{8,15},{9,14},{10,... | collective-permute-start | bytes 393224 | tf_op jit(solution)/shard_map/ppermute | solution.py:124
  27.9 1.5 %collective-permute-start.7 = (bf16[256,256]{1,0:T(8,128)(2,1)S(1)}, bf16[256,256]{1,0:T(8,128)(2,1)S(1)}, u32[]{:S(2)}, u32[]{:S(2)}) collective-permute-start(bf16[256,256]{1,0:T(8,128)(2,1)S(1)} %get-tuple-element.54), channel_id=1, source_target_pairs={{0,1},{1,0},{2,3},{3,2},{4,5},{5,4},{6,7},{7,6},{8,9},{9,8},{10,11... | collective-permute-start | bytes 393224 | tf_op jit(solution)/shard_map/ppermute | solution.py:124
  29.4 3.6 %collective-permute-done.4.refs_2_ = bf16[256,256]{1,0:T(8,128)(2,1)S(1)} collective-permute-done((bf16[256,256]{1,0:T(8,128)(2,1)S(1)}, bf16[256,256]{1,0:T(8,128)(2,1)S(1)}, u32[]{:S(2)}, u32[]{:S(2)}) %collective-permute-start.4) | collective-permute-done | bytes 131104 | tf_op jit(solution)/shard_map/ppermute | solution.py:124
  33.0 3.3 %collective-permute-start.9 = (bf16[256,256]{1,0:T(8,128)(2,1)S(1)}, bf16[256,256]{1,0:T(8,128)(2,1)S(1)}, u32[]{:S(2)}, u32[]{:S(2)}) collective-permute-start(bf16[256,256]{1,0:T(8,128)(2,1)S(1)} %get-tuple-element.56), channel_id=1, source_target_pairs={{0,3},{1,2},{2,1},{3,0},{4,7},{5,6},{6,5},{7,4},{8,11},{9,10},{10,... | collective-permute-start | bytes 393224 | tf_op jit(solution)/shard_map/ppermute | solution.py:124
  36.4 3.4 %copy-done.2 = bf16[2048,2048]{1,0:T(8,128)(2,1)S(1)} copy-done((bf16[2048,2048]{1,0:T(8,128)(2,1)S(1)}, bf16[2048,2048]{1,0:T(8,128)(2,1)}, u32[]{:S(2)}) %copy-start.2) | copy-done | bytes 8388632
  40.4 1.8 %shard_map.97.begun_ref = f32[4,256,512]{2,1,0:T(8,128)S(1)} custom-call(s32[12]{0:T(128)S(1)} %pad_add_fusion.at_ref, bf16[2048,2048]{1,0:T(8,128)(2,1)S(1)} %shard_map.96.factor_ref, bf16[256,256]{1,0:T(8,128)(2,1)S(1)} %get-tuple-element.45.refs_0_, bf16[256,256]{1,0:T(8,128)(2,1)S(1)} %collective-permute-done.3.refs_1_, ...), custom_call_target="tpu_custom_call" | custom-call | flops 1073741824 | bytes 11010048 | tf_op jit(solution)/shard_map/pallas_call | solution.py:22
  42.3 1.0 shard_map.99
  44.9 1.0 shard_map.101
  46.1 5.1 %collective-permute-start.13 = (bf16[256,512]{1,0:T(8,128)(2,1)S(1)}, bf16[256,512]{1,0:T(8,128)(2,1)S(1)}, u32[]{:S(2)}, u32[]{:S(2)}) collective-permute-start(bf16[256,512]{1,0:T(8,128)(2,1)S(1)} %add_convert_fusion.2), channel_id=1, source_target_pairs={{0,16},{8,24},{16,0},{24,8},{1,17},{9,25},{17,1},{25,9},{2,18},{10... | collective-permute-start | bytes 786440 | tf_op jit(solution)/shard_map/ppermute | solution.py:124
  52.3 5.8 %collective-permute-done.13.across_ref = bf16[256,512]{1,0:T(8,128)(2,1)S(1)} collective-permute-done((bf16[256,512]{1,0:T(8,128)(2,1)S(1)}, bf16[256,512]{1,0:T(8,128)(2,1)S(1)}, u32[]{:S(2)}, u32[]{:S(2)}) %collective-permute-start.13) | collective-permute-done | bytes 262176 | tf_op jit(solution)/shard_map/ppermute | solution.py:124
  60.7 1.4 %collective-permute-start.15 = (bf16[256,512]{1,0:T(8,128)(2,1)S(1)}, bf16[256,512]{1,0:T(8,128)(2,1)S(1)}, u32[]{:S(2)}, u32[]{:S(2)}) collective-permute-start(bf16[256,512]{1,0:T(8,128)(2,1)S(1)} %add_convert_fusion.1), channel_id=1, source_target_pairs={{16,0},{24,8},{17,1},{25,9},{18,2},{26,10},{19,3},{27,11},{20,4},{... | collective-permute-start | bytes 786440 | tf_op jit(solution)/shard_map/ppermute | solution.py:215
  63.4 4.4 %shard_map.104 = bf16[2048,256]{1,0:T(8,128)(2,1)} custom-call(s32[4]{0:T(128)S(1)} %iota_xor_fusion.1.at_ref, bf16[2048,2048]{1,0:T(8,128)(2,1)S(1)} %shard_map.96.factor_ref, bf16[2048,256]{1,0:T(8,128)(2,1)S(1)} %copy-done.4, bf16[512,256]{1,0:T(8,128)(2,1)S(1)} %shard_map.95.forward_ref.refs_0_, bf16[512,256]{1,0:T(8,128)(2,1)S(1)} %collective-permute-done.16.refs_1_, ...), custom_call_target="tpu_custom_call" | custom-call | flops 2147483648 | bytes 11534336 | tf_op jit(solution)/shard_map/pallas_call | solution.py:22
  68.7 2.6 %collective-permute-done.15 = bf16[256,512]{1,0:T(8,128)(2,1)S(1)} collective-permute-done((bf16[256,512]{1,0:T(8,128)(2,1)S(1)}, bf16[256,512]{1,0:T(8,128)(2,1)S(1)}, u32[]{:S(2)}, u32[]{:S(2)}) %collective-permute-start.15) | collective-permute-done | bytes 262176 | tf_op jit(solution)/shard_map/ppermute | solution.py:215
  72.9 6.3 %collective-permute-done.19.refs_1_ = bf16[256,512]{1,0:T(8,128)(2,1)S(1)} collective-permute-done((bf16[256,512]{1,0:T(8,128)(2,1)S(1)}, bf16[256,512]{1,0:T(8,128)(2,1)S(1)}, u32[]{:S(2)}, u32[]{:S(2)}) %collective-permute-start.19) | collective-permute-done | bytes 262176 | tf_op jit(solution)/shard_map/ppermute | solution.py:124
  79.2 5.9 %collective-permute-done.20.refs_2_ = bf16[256,512]{1,0:T(8,128)(2,1)S(1)} collective-permute-done((bf16[256,512]{1,0:T(8,128)(2,1)S(1)}, bf16[256,512]{1,0:T(8,128)(2,1)S(1)}, u32[]{:S(2)}, u32[]{:S(2)}) %collective-permute-start.20) | collective-permute-done | bytes 262176 | tf_op jit(solution)/shard_map/ppermute | solution.py:124
  85.1 1.5 %collective-permute-start.22 = (bf16[256,512]{1,0:T(8,128)(2,1)S(1)}, bf16[256,512]{1,0:T(8,128)(2,1)S(1)}, u32[]{:S(2)}, u32[]{:S(2)}) collective-permute-start(bf16[256,512]{1,0:T(8,128)(2,1)S(1)} %collective-permute-done.20.refs_2_), channel_id=1, source_target_pairs={{0,1},{1,0},{2,3},{3,2},{4,5},{5,4},{6,7},{7,6},{8,9},{9,8},{10,11... | collective-permute-start | bytes 786440 | tf_op jit(solution)/shard_map/ppermute | solution.py:124
  87.3 6.6 %collective-permute-done.22.refs_3_ = bf16[256,512]{1,0:T(8,128)(2,1)S(1)} collective-permute-done((bf16[256,512]{1,0:T(8,128)(2,1)S(1)}, bf16[256,512]{1,0:T(8,128)(2,1)S(1)}, u32[]{:S(2)}, u32[]{:S(2)}) %collective-permute-start.22) | collective-permute-done | bytes 262176 | tf_op jit(solution)/shard_map/ppermute | solution.py:124
  93.9 1.3 %collective-permute-start.25 = (bf16[256,512]{1,0:T(8,128)(2,1)S(1)}, bf16[256,512]{1,0:T(8,128)(2,1)S(1)}, u32[]{:S(2)}, u32[]{:S(2)}) collective-permute-start(bf16[256,512]{1,0:T(8,128)(2,1)S(1)} %collective-permute-done.21.refs_4_), channel_id=1, source_target_pairs={{2,0},{3,1},{4,6},{5,7},{10,8},{11,9},{12,14},{13,15},{18,16},{19,... | collective-permute-start | bytes 786440 | tf_op jit(solution)/shard_map/ppermute | solution.py:240
  95.2 1.3 %collective-permute-start.23 = (bf16[256,512]{1,0:T(8,128)(2,1)S(1)}, bf16[256,512]{1,0:T(8,128)(2,1)}, u32[]{:S(2)}, u32[]{:S(2)}) collective-permute-start(bf16[256,512]{1,0:T(8,128)(2,1)S(1)} %collective-permute-done.21.refs_4_), channel_id=1, source_target_pairs={{0,1},{1,0},{2,3},{3,2},{4,5},{5,4},{6,7},{7,6},{8,9},{9,8},{10,11... | collective-permute-start | bytes 786440 | tf_op jit(solution)/shard_map/ppermute | solution.py:124
  96.5 1.4 %collective-permute-start.26 = (bf16[256,512]{1,0:T(8,128)(2,1)S(1)}, bf16[256,512]{1,0:T(8,128)(2,1)}, u32[]{:S(2)}, u32[]{:S(2)}) collective-permute-start(bf16[256,512]{1,0:T(8,128)(2,1)S(1)} %collective-permute-done.24.refs_6_), channel_id=1, source_target_pairs={{2,3},{3,2},{4,5},{5,4},{10,11},{11,10},{12,13},{13,12},{18,19},{1... | collective-permute-start | bytes 786440 | tf_op jit(solution)/shard_map/ppermute | solution.py:242
  97.9 4.3 %collective-permute-done.25.refs_7_ = bf16[256,512]{1,0:T(8,128)(2,1)S(1)} collective-permute-done((bf16[256,512]{1,0:T(8,128)(2,1)S(1)}, bf16[256,512]{1,0:T(8,128)(2,1)S(1)}, u32[]{:S(2)}, u32[]{:S(2)}) %collective-permute-start.25) | collective-permute-done | bytes 262176 | tf_op jit(solution)/shard_map/ppermute | solution.py:240
  102.2 3.1 %collective-permute-start.27 = (bf16[256,512]{1,0:T(8,128)(2,1)S(1)}, bf16[256,512]{1,0:T(8,128)(2,1)}, u32[]{:S(2)}, u32[]{:S(2)}) collective-permute-start(bf16[256,512]{1,0:T(8,128)(2,1)S(1)} %collective-permute-done.25.refs_7_), channel_id=1, source_target_pairs={{0,1},{1,0},{6,7},{7,6},{8,9},{9,8},{14,15},{15,14},{16,17},{17,16... | collective-permute-start | bytes 786440 | tf_op jit(solution)/shard_map/ppermute | solution.py:243
  106.3 1.8 %shard_map.107.refs_0_ = f32[384,512]{1,0:T(8,128)S(1)} custom-call(s32[9]{0:T(128)S(1)} %pad_add_fusion.1.at_ref, bf16[384,2048]{1,0:T(8,128)(2,1)S(1)} %copy-done.3, bf16[256,512]{1,0:T(8,128)(2,1)S(1)} %add_convert_fusion.refs_0_, bf16[256,512]{1,0:T(8,128)(2,1)S(1)} %collective-permute-done.19.refs_1_, ...), custom_call_target="tpu_custom_call" | custom-call | flops 704643072 | bytes 4456448 | tf_op jit(solution)/shard_map/pallas_call | solution.py:22
  108.1 2.4 %collective-permute-done.27.refs_2_ = bf16[256,512]{1,0:T(8,128)(2,1)} collective-permute-done((bf16[256,512]{1,0:T(8,128)(2,1)S(1)}, bf16[256,512]{1,0:T(8,128)(2,1)}, u32[]{:S(2)}, u32[]{:S(2)}) %collective-permute-start.27) | collective-permute-done | bytes 262176 | tf_op jit(solution)/shard_map/ppermute | solution.py:243
  110.5 2.2 %shard_map.108 = f32[384,512]{1,0:T(8,128)} custom-call(s32[9]{0:T(128)S(1)} %pad_add_fusion.1.at_ref, bf16[384,2048]{1,0:T(8,128)(2,1)S(1)} %copy-done.3, f32[384,512]{1,0:T(8,128)S(1)} %shard_map.107.refs_0_, bf16[256,512]{1,0:T(8,128)(2,1)} %collective-permute-done.26.refs_1_, bf16[256,512]{1,0:T(8,128)(2,1)} %collective-permute-done.27.refs_2_), custom_call_target="tpu_custom_call" | custom-call | flops 100663296 | bytes 3670016 | tf_op jit(solution)/shard_map/pallas_call | solution.py:22
  (64 shorter events, 14.6 us)
Async XLA Ops:
  2.7 9.3 %collective-permute-start.1 = (bf16[512,256]{1,0:T(8,128)(2,1)}, bf16[512,256]{1,0:T(8,128)(2,1)S(1)}, u32[]{:S(2)}, u32[]{:S(2)}) collective-permute-start(bf16[512,256]{1,0:T(8,128)(2,1)} %refs_0_), channel_id=1, source_target_pairs={{0,16},{8,24},{1,17},{9,25},{2,18},{10,26},{3,19},{11,27},{4,20},{... | collective-permute-start | bytes 786440 | tf_op jit(solution)/shard_map/ppermute | solution.py:154
  6.2 10.7 %collective-permute-start = (bf16[512,256]{1,0:T(8,128)(2,1)}, bf16[512,256]{1,0:T(8,128)(2,1)S(1)}, u32[]{:S(2)}, u32[]{:S(2)}) collective-permute-start(bf16[512,256]{1,0:T(8,128)(2,1)} %refs_0_), channel_id=1, source_target_pairs={{0,8},{8,0},{16,24},{24,16},{1,9},{9,1},{17,25},{25,17},{2,10},{10... | collective-permute-start | bytes 786440 | tf_op jit(solution)/shard_map/ppermute | solution.py:124
  12.0 4.8 %collective-permute-start.2 = (bf16[512,256]{1,0:T(8,128)(2,1)S(1)}, bf16[512,256]{1,0:T(8,128)(2,1)S(1)}, u32[]{:S(2)}, u32[]{:S(2)}) collective-permute-start(bf16[512,256]{1,0:T(8,128)(2,1)S(1)} %collective-permute-done.1.refs_2_), channel_id=1, source_target_pairs={{16,24},{24,16},{17,25},{25,17},{18,26},{26,18},{19,27},{27,19},{2... | collective-permute-start | bytes 786440 | tf_op jit(solution)/shard_map/ppermute | solution.py:156
  12.7 15.2 %collective-permute-start.3 = (bf16[256,256]{1,0:T(8,128)(2,1)S(1)}, bf16[256,256]{1,0:T(8,128)(2,1)S(1)}, u32[]{:S(2)}, u32[]{:S(2)}) collective-permute-start(bf16[256,256]{1,0:T(8,128)(2,1)S(1)} %get-tuple-element.46), channel_id=1, source_target_pairs={{0,4},{1,5},{2,6},{3,7},{4,0},{5,1},{6,2},{7,3},{8,12},{9,13},{10,... | collective-permute-start | bytes 393224 | tf_op jit(solution)/shard_map/ppermute | solution.py:124
  13.1 19.9 %collective-permute-start.4 = (bf16[256,256]{1,0:T(8,128)(2,1)S(1)}, bf16[256,256]{1,0:T(8,128)(2,1)S(1)}, u32[]{:S(2)}, u32[]{:S(2)}) collective-permute-start(bf16[256,256]{1,0:T(8,128)(2,1)S(1)} %get-tuple-element.51), channel_id=1, source_target_pairs={{0,5},{1,4},{2,7},{3,6},{4,1},{5,0},{6,3},{7,2},{8,13},{9,12},{10,... | collective-permute-start | bytes 393224 | tf_op jit(solution)/shard_map/ppermute | solution.py:124
  16.6 16.4 %collective-permute-start.5 = (bf16[256,256]{1,0:T(8,128)(2,1)S(1)}, bf16[256,256]{1,0:T(8,128)(2,1)S(1)}, u32[]{:S(2)}, u32[]{:S(2)}) collective-permute-start(bf16[256,256]{1,0:T(8,128)(2,1)S(1)} %get-tuple-element.52), channel_id=1, source_target_pairs={{0,6},{1,7},{2,4},{3,5},{4,2},{5,3},{6,0},{7,1},{8,14},{9,15},{10,... | collective-permute-start | bytes 393224 | tf_op jit(solution)/shard_map/ppermute | solution.py:124
  20.7 21.6 %collective-permute-start.10 = (bf16[512,256]{1,0:T(8,128)(2,1)S(1)}, bf16[512,256]{1,0:T(8,128)(2,1)S(1)}, u32[]{:S(2)}, u32[]{:S(2)}) collective-permute-start(bf16[512,256]{1,0:T(8,128)(2,1)S(1)} %shard_map.95.forward_ref.refs_0_), channel_id=1, source_target_pairs={{0,16},{8,24},{16,0},{24,8},{1,17},{9,25},{17,1},{25,9},{2,18},{10... | collective-permute-start | bytes 786440 | tf_op jit(solution)/shard_map/ppermute | solution.py:124
  24.4 17.9 %collective-permute-start.6 = (bf16[256,256]{1,0:T(8,128)(2,1)S(1)}, bf16[256,256]{1,0:T(8,128)(2,1)S(1)}, u32[]{:S(2)}, u32[]{:S(2)}) collective-permute-start(bf16[256,256]{1,0:T(8,128)(2,1)S(1)} %get-tuple-element.53), channel_id=1, source_target_pairs={{0,7},{1,6},{2,5},{3,4},{4,3},{5,2},{6,1},{7,0},{8,15},{9,14},{10,... | collective-permute-start | bytes 393224 | tf_op jit(solution)/shard_map/ppermute | solution.py:124
  27.9 14.3 %collective-permute-start.7 = (bf16[256,256]{1,0:T(8,128)(2,1)S(1)}, bf16[256,256]{1,0:T(8,128)(2,1)S(1)}, u32[]{:S(2)}, u32[]{:S(2)}) collective-permute-start(bf16[256,256]{1,0:T(8,128)(2,1)S(1)} %get-tuple-element.54), channel_id=1, source_target_pairs={{0,1},{1,0},{2,3},{3,2},{4,5},{5,4},{6,7},{7,6},{8,9},{9,8},{10,11... | collective-permute-start | bytes 393224 | tf_op jit(solution)/shard_map/ppermute | solution.py:124
  33.0 9.2 %collective-permute-start.8 = (bf16[256,256]{1,0:T(8,128)(2,1)S(1)}, bf16[256,256]{1,0:T(8,128)(2,1)S(1)}, u32[]{:S(2)}, u32[]{:S(2)}) collective-permute-start(bf16[256,256]{1,0:T(8,128)(2,1)S(1)} %get-tuple-element.55), channel_id=1, source_target_pairs={{0,2},{1,3},{2,0},{3,1},{4,6},{5,7},{6,4},{7,5},{8,10},{9,11},{10,... | collective-permute-start | bytes 393224 | tf_op jit(solution)/shard_map/ppermute | solution.py:124
  33.0 9.2 %collective-permute-start.9 = (bf16[256,256]{1,0:T(8,128)(2,1)S(1)}, bf16[256,256]{1,0:T(8,128)(2,1)S(1)}, u32[]{:S(2)}, u32[]{:S(2)}) collective-permute-start(bf16[256,256]{1,0:T(8,128)(2,1)S(1)} %get-tuple-element.56), channel_id=1, source_target_pairs={{0,3},{1,2},{2,1},{3,0},{4,7},{5,6},{6,5},{7,4},{8,11},{9,10},{10,... | collective-permute-start | bytes 393224 | tf_op jit(solution)/shard_map/ppermute | solution.py:124
  36.4 3.4 %copy-start.2 = (bf16[2048,2048]{1,0:T(8,128)(2,1)S(1)}, bf16[2048,2048]{1,0:T(8,128)(2,1)}, u32[]{:S(2)}) copy-start(bf16[2048,2048]{1,0:T(8,128)(2,1)} %factor_ref.1) | copy-start | bytes 25165828
  43.3 1.6 %collective-permute-start.11 = (bf16[256,512]{1,0:T(8,128)(2,1)S(1)}, bf16[256,512]{1,0:T(8,128)(2,1)S(1)}, u32[]{:S(2)}, u32[]{:S(2)}) collective-permute-start(bf16[256,512]{1,0:T(8,128)(2,1)S(1)} %shard_map.99), channel_id=1, source_target_pairs={{0,8},{8,0},{16,24},{24,16},{1,9},{9,1},{17,25},{25,17},{2,10},{10... | collective-permute-start | bytes 786440 | tf_op jit(solution)/shard_map/ppermute | solution.py:124
  45.9 12.2 %copy-start.1 = (bf16[512,2048]{1,0:T(8,128)(2,1)S(1)}, bf16[512,2048]{1,0:T(8,128)(2,1)}, u32[]{:S(2)}) copy-start(bf16[512,2048]{1,0:T(8,128)(2,1)} %inverse_ref.9) | copy-start | bytes 6291460
  45.9 6.3 %collective-permute-start.12 = (bf16[256,512]{1,0:T(8,128)(2,1)S(1)}, bf16[256,512]{1,0:T(8,128)(2,1)S(1)}, u32[]{:S(2)}, u32[]{:S(2)}) collective-permute-start(bf16[256,512]{1,0:T(8,128)(2,1)S(1)} %shard_map.101), channel_id=1, source_target_pairs={{0,8},{8,0},{16,24},{24,16},{1,9},{9,1},{17,25},{25,17},{2,10},{10... | collective-permute-start | bytes 786440 | tf_op jit(solution)/shard_map/ppermute | solution.py:124
  46.1 11.9 %collective-permute-start.13 = (bf16[256,512]{1,0:T(8,128)(2,1)S(1)}, bf16[256,512]{1,0:T(8,128)(2,1)S(1)}, u32[]{:S(2)}, u32[]{:S(2)}) collective-permute-start(bf16[256,512]{1,0:T(8,128)(2,1)S(1)} %add_convert_fusion.2), channel_id=1, source_target_pairs={{0,16},{8,24},{16,0},{24,8},{1,17},{9,25},{17,1},{25,9},{2,18},{10... | collective-permute-start | bytes 786440 | tf_op jit(solution)/shard_map/ppermute | solution.py:124
  59.0 1.6 %collective-permute-start.14 = (bf16[256,512]{1,0:T(8,128)(2,1)S(1)}, bf16[256,512]{1,0:T(8,128)(2,1)S(1)}, u32[]{:S(2)}, u32[]{:S(2)}) collective-permute-start(bf16[256,512]{1,0:T(8,128)(2,1)S(1)} %get-tuple-element.61), channel_id=1, source_target_pairs={{0,8},{8,0},{16,24},{24,16},{1,9},{9,1},{17,25},{25,17},{2,10},{10... | collective-permute-start | bytes 786440 | tf_op jit(solution)/shard_map/ppermute | solution.py:124
  59.1 4.3 %collective-permute-start.16 = (bf16[512,256]{1,0:T(8,128)(2,1)S(1)}, bf16[512,256]{1,0:T(8,128)(2,1)S(1)}, u32[]{:S(2)}, u32[]{:S(2)}) collective-permute-start(bf16[512,256]{1,0:T(8,128)(2,1)S(1)} %shard_map.95.forward_ref.refs_0_), channel_id=1, source_target_pairs={{0,8},{8,0},{16,24},{24,16},{1,9},{9,1},{17,25},{25,17},{2,10},{10... | collective-permute-start | bytes 786440 | tf_op jit(solution)/shard_map/ppermute | solution.py:124
  59.6 3.8 %collective-permute-start.17 = (bf16[512,256]{1,0:T(8,128)(2,1)S(1)}, bf16[512,256]{1,0:T(8,128)(2,1)S(1)}, u32[]{:S(2)}, u32[]{:S(2)}) collective-permute-start(bf16[512,256]{1,0:T(8,128)(2,1)S(1)} %collective-permute-done.10.refs_2_), channel_id=1, source_target_pairs={{0,8},{8,0},{16,24},{24,16},{1,9},{9,1},{17,25},{25,17},{2,10},{10... | collective-permute-start | bytes 786440 | tf_op jit(solution)/shard_map/ppermute | solution.py:124
  60.7 10.6 %collective-permute-start.15 = (bf16[256,512]{1,0:T(8,128)(2,1)S(1)}, bf16[256,512]{1,0:T(8,128)(2,1)S(1)}, u32[]{:S(2)}, u32[]{:S(2)}) collective-permute-start(bf16[256,512]{1,0:T(8,128)(2,1)S(1)} %add_convert_fusion.1), channel_id=1, source_target_pairs={{16,0},{24,8},{17,1},{25,9},{18,2},{26,10},{19,3},{27,11},{20,4},{... | collective-permute-start | bytes 786440 | tf_op jit(solution)/shard_map/ppermute | solution.py:215
  63.0 8.3 %collective-permute-start.18 = (bf16[256,512]{1,0:T(8,128)(2,1)S(1)}, bf16[256,512]{1,0:T(8,128)(2,1)S(1)}, u32[]{:S(2)}, u32[]{:S(2)}) collective-permute-start(bf16[256,512]{1,0:T(8,128)(2,1)S(1)} %shard_map.106), channel_id=1, source_target_pairs={{0,8},{8,0},{16,24},{24,16},{1,9},{9,1},{17,25},{25,17},{2,10},{10... | collective-permute-start | bytes 786440 | tf_op jit(solution)/shard_map/ppermute | solution.py:124
  67.8 37.5 %copy-start.7 = (s32[8]{0:T(128)S(1)}, s32[8]{0:T(128)}, u32[]{:S(2)}) copy-start(s32[8]{0:T(128)} %constant.14.clone) | copy-start | bytes 100
  67.8 38.4 %copy-start.3 = (bf16[384,2048]{1,0:T(8,128)(2,1)S(1)}, bf16[384,2048]{1,0:T(8,128)(2,1)}, u32[]{:S(2)}) copy-start(bf16[384,2048]{1,0:T(8,128)(2,1)} %axle_ref.3) | copy-start | bytes 4718596
  71.4 7.8 %collective-permute-start.19 = (bf16[256,512]{1,0:T(8,128)(2,1)S(1)}, bf16[256,512]{1,0:T(8,128)(2,1)S(1)}, u32[]{:S(2)}, u32[]{:S(2)}) collective-permute-start(bf16[256,512]{1,0:T(8,128)(2,1)S(1)} %add_convert_fusion.refs_0_), channel_id=1, source_target_pairs={{0,1},{1,0},{2,3},{3,2},{4,5},{5,4},{6,7},{7,6},{8,9},{9,8},{10,11... | collective-permute-start | bytes 786440 | tf_op jit(solution)/shard_map/ppermute | solution.py:124
  72.0 13.1 %collective-permute-start.20 = (bf16[256,512]{1,0:T(8,128)(2,1)S(1)}, bf16[256,512]{1,0:T(8,128)(2,1)S(1)}, u32[]{:S(2)}, u32[]{:S(2)}) collective-permute-start(bf16[256,512]{1,0:T(8,128)(2,1)S(1)} %add_convert_fusion.refs_0_), channel_id=1, source_target_pairs={{0,2},{1,3},{2,0},{3,1},{4,6},{5,7},{6,4},{7,5},{8,10},{9,11},{10,... | collective-permute-start | bytes 786440 | tf_op jit(solution)/shard_map/ppermute | solution.py:124
  72.5 14.8 %collective-permute-start.21 = (bf16[256,512]{1,0:T(8,128)(2,1)S(1)}, bf16[256,512]{1,0:T(8,128)(2,1)S(1)}, u32[]{:S(2)}, u32[]{:S(2)}) collective-permute-start(bf16[256,512]{1,0:T(8,128)(2,1)S(1)} %add_convert_fusion.refs_0_), channel_id=1, source_target_pairs={{0,6},{1,7},{2,4},{3,5},{4,2},{5,3},{6,0},{7,1},{8,14},{9,15},{10,... | collective-permute-start | bytes 786440 | tf_op jit(solution)/shard_map/ppermute | solution.py:124
  85.1 8.8 %collective-permute-start.22 = (bf16[256,512]{1,0:T(8,128)(2,1)S(1)}, bf16[256,512]{1,0:T(8,128)(2,1)S(1)}, u32[]{:S(2)}, u32[]{:S(2)}) collective-permute-start(bf16[256,512]{1,0:T(8,128)(2,1)S(1)} %collective-permute-done.20.refs_2_), channel_id=1, source_target_pairs={{0,1},{1,0},{2,3},{3,2},{4,5},{5,4},{6,7},{7,6},{8,9},{9,8},{10,11... | collective-permute-start | bytes 786440 | tf_op jit(solution)/shard_map/ppermute | solution.py:124
  86.6 9.9 %collective-permute-start.24 = (bf16[256,512]{1,0:T(8,128)(2,1)S(1)}, bf16[256,512]{1,0:T(8,128)(2,1)S(1)}, u32[]{:S(2)}, u32[]{:S(2)}) collective-permute-start(bf16[256,512]{1,0:T(8,128)(2,1)S(1)} %collective-permute-done.20.refs_2_), channel_id=1, source_target_pairs={{2,4},{3,5},{4,2},{5,3},{10,12},{11,13},{12,10},{13,11},{18,20},{1... | collective-permute-start | bytes 786440 | tf_op jit(solution)/shard_map/ppermute | solution.py:239
  93.9 8.3 %collective-permute-start.25 = (bf16[256,512]{1,0:T(8,128)(2,1)S(1)}, bf16[256,512]{1,0:T(8,128)(2,1)S(1)}, u32[]{:S(2)}, u32[]{:S(2)}) collective-permute-start(bf16[256,512]{1,0:T(8,128)(2,1)S(1)} %collective-permute-done.21.refs_4_), channel_id=1, source_target_pairs={{2,0},{3,1},{4,6},{5,7},{10,8},{11,9},{12,14},{13,15},{18,16},{19,... | collective-permute-start | bytes 786440 | tf_op jit(solution)/shard_map/ppermute | solution.py:240
  95.2 11.1 %collective-permute-start.23 = (bf16[256,512]{1,0:T(8,128)(2,1)S(1)}, bf16[256,512]{1,0:T(8,128)(2,1)}, u32[]{:S(2)}, u32[]{:S(2)}) collective-permute-start(bf16[256,512]{1,0:T(8,128)(2,1)S(1)} %collective-permute-done.21.refs_4_), channel_id=1, source_target_pairs={{0,1},{1,0},{2,3},{3,2},{4,5},{5,4},{6,7},{7,6},{8,9},{9,8},{10,11... | collective-permute-start | bytes 786440 | tf_op jit(solution)/shard_map/ppermute | solution.py:124
  96.5 11.6 %collective-permute-start.26 = (bf16[256,512]{1,0:T(8,128)(2,1)S(1)}, bf16[256,512]{1,0:T(8,128)(2,1)}, u32[]{:S(2)}, u32[]{:S(2)}) collective-permute-start(bf16[256,512]{1,0:T(8,128)(2,1)S(1)} %collective-permute-done.24.refs_6_), channel_id=1, source_target_pairs={{2,3},{3,2},{4,5},{5,4},{10,11},{11,10},{12,13},{13,12},{18,19},{1... | collective-permute-start | bytes 786440 | tf_op jit(solution)/shard_map/ppermute | solution.py:242
  102.2 8.4 %collective-permute-start.27 = (bf16[256,512]{1,0:T(8,128)(2,1)S(1)}, bf16[256,512]{1,0:T(8,128)(2,1)}, u32[]{:S(2)}, u32[]{:S(2)}) collective-permute-start(bf16[256,512]{1,0:T(8,128)(2,1)S(1)} %collective-permute-done.25.refs_7_), channel_id=1, source_target_pairs={{0,1},{1,0},{6,7},{7,6},{8,9},{9,8},{14,15},{15,14},{16,17},{17,16... | collective-permute-start | bytes 786440 | tf_op jit(solution)/shard_map/ppermute | solution.py:243
  (4 other events, 6.7 us)

commit v8 on v6

--- a/solution.py
+++ b/solution.py
@@ -84,18 +84,19 @@
         out_ref[j] = total
 
 
-def finish_kernel(panel_block, row_blocks, at_ref, factor_ref, begun_ref, *refs):
+def finish_kernel(panel_blocks, row_blocks, at_ref, factor_ref, begun_ref, *refs):
     pieces, out_ref = refs[:-1], refs[-1]
-    depth, width = pieces[0].shape[1], out_ref.shape[1]
-    total = begun_ref[panel_block]
-    for k, piece in zip(row_blocks, pieces):
-        total = total + dot(piece[...], factor_ref[part(at_ref[k], depth), part(at_ref[panel_block], width)])
-    out_ref[...] = total.astype(out_ref.dtype)
+    depth, width = pieces[0].shape[1], out_ref.shape[2]
+    for j, b in enumerate(panel_blocks):
+        total = begun_ref[b]
+        for k, piece in zip(row_blocks, pieces):
+            total = total + dot(piece[...], factor_ref[part(at_ref[k], depth), part(at_ref[b], width)])
+        out_ref[j] = total.astype(out_ref.dtype)
 
 
 def reduce_kernel(block, at_ref, forward_ref, kept_ref, core_ref, across_ref, inverse_ref, reduced_ref, send_ref):
     rows = reduced_ref.shape[1]
-    coupled = kept_ref[...] + core_ref[...].astype(F32) + across_ref[...].astype(F32)
+    coupled = kept_ref[0] + core_ref[0].astype(F32) + across_ref[...].astype(F32)
     reduced_ref[...] = (forward_ref[...].astype(F32).T - coupled).astype(reduced_ref.dtype)
     term = dot(reduced_ref[...], inverse_ref[:, part(at_ref[block], rows)])
     send_ref[...] = term.astype(send_ref.dtype)
@@ -174,22 +175,19 @@
         2 * cols * depth * 4 * panel,
     )
 
-    def coupled(panel_block, kind):
+    def coupled(panel_blocks, kind):
         (out,) = call(
-            functools.partial(finish_kernel, panel_block, (11, 5, 6, 7)),
+            functools.partial(finish_kernel, panel_blocks, (11, 5, 6, 7)),
             at_coupled,
             [held, begun] + late,
-            [(block, kind)],
-            2 * cols * depth * 4 * rows,
+            [((len(panel_blocks),) + block, kind)],
+            2 * cols * depth * 4 * rows * len(panel_blocks),
         )
         return out
 
-    from_core = by_xor(coupled(3, BF16), "factor", factors, 1)
-    send = (coupled(2, F32) + from_core.astype(F32)).astype(BF16)
-    send, late[0] = lax.optimization_barrier((send, late[0]))
-    from_across = by_xor(send, "factor", factors, 2)
-    from_core = by_xor(coupled(1, BF16), "factor", factors, 1)
-    kept = coupled(0, F32)
+    from_core = by_xor(coupled((1, 3), BF16), "factor", factors, 1)
+    kept = coupled((0, 2), F32)
+    from_across = by_xor((kept[1] + from_core[1].astype(F32)).astype(BF16), "factor", factors, 2)
 
     work = 2 * cols * rows * rows
     reduced, send = call(

time: 101 us -> 100 us (0.990)
  Pallas kernels: 20.3 us -> 18.9 us
    pallas_call x14 -> x12, Pallas kernels: 19.8 us -> 18.3 us  [call(): pl.pallas_call(kernel, out_shape=shapes, in_specs=[SMEM] * len(at) + [VME...]
    ppermute x21 -> x20, waiting for transfers between devices: 19.5 us -> 20.4 us  [by_xor(): return lax.ppermute(value, axis, [(i, i ^ bits) for i in range(size)])]
    ppermute x21 -> x20, starting transfers between devices: 24.7 us -> 24.5 us  [by_xor(): return lax.ppermute(value, axis, [(i, i ^ bits) for i in range(size)])]
  transfers between devices with their start and end apart: 28 -> 27, of which waited for: 13 -> 12; matrix products, arithmetic and copies ran while one was open for 1% -> 1% of each run, Pallas kernels for 14% -> 14%
where the time goes in v8:
time: 100 us
  starting transfers between devices  37.5 us (38%)
  waiting for transfers between devices  34.3 us (34%)
  Pallas kernels  18.9 us (19%)
  local copies, waits for them, and re-layouts  8 us (8%)
    ppermute x20, starting transfers between devices, by_xor(): return lax.ppermute(value, axis, [(i, i ^ bits) for i in range(size)])  24.5 us
    ppermute x20, waiting for transfers between devices, by_xor(): return lax.ppermute(value, axis, [(i, i ^ bits) for i in range(size)])  20.4 us
    pallas_call x12, Pallas kernels, call(): pl.pallas_call(kernel, out_shape=shapes, in_specs=[SMEM] * len(at) + [VME...  18.3 us
    unnamed x17, local copies, waits for them, and re-layouts  8 us
    ppermute x1, waiting for transfers between devices, small_slice(): d = lax.ppermute(b, 'load', [(i, i ^ 2) for i in middle])  4.99 us
    ppermute x1, starting transfers between devices, small_slice(): b_across = lax.ppermute(b_panel, 'factor', [(0, 2), (1, 3)])  4.45 us
    ppermute x1, waiting for transfers between devices, small_slice(): b_far = lax.ppermute(b_panel, 'factor', [(0, 3), (1, 2)])  3.19 us
    ppermute x1, waiting for transfers between devices, small_slice(): d_x = lax.ppermute(d, 'load', [(i, i ^ 1) for i in (0, 1, 6, 7)])  3.1 us
  transfers between devices with their start and end apart: 27, of which 12 were waited for; matrix products, arithmetic and copies ran while one was open for 1% of the time, Pallas kernels for 14%

profile of v8, /device:TPU:0, one launch (start us, length us, event | category | flops | bytes accessed | tf_op | source)
XLA Modules:
  0.0 100.1 jit_solution(10392488755425737231)
XLA Ops:
  0.7 1.2 %copy-done.5 = bf16[256,2048]{1,0:T(8,128)(2,1)S(1)} copy-done((bf16[256,2048]{1,0:T(8,128)(2,1)S(1)}, bf16[256,2048]{1,0:T(8,128)(2,1)}, u32[]{:S(2)}) %copy-start.5) | copy-done | bytes 1048600
  3.3 4.5 %collective-permute-start.1 = (bf16[512,256]{1,0:T(8,128)(2,1)}, bf16[512,256]{1,0:T(8,128)(2,1)S(1)}, u32[]{:S(2)}, u32[]{:S(2)}) collective-permute-start(bf16[512,256]{1,0:T(8,128)(2,1)} %refs_0_), channel_id=1, source_target_pairs={{0,16},{8,24},{1,17},{9,25},{2,18},{10,26},{3,19},{11,27},{4,20},{... | collective-permute-start | bytes 786440 | tf_op jit(solution)/shard_map/ppermute | solution.py:155
  7.7 1.4 %collective-permute-start.2 = (bf16[512,256]{1,0:T(8,128)(2,1)}, bf16[512,256]{1,0:T(8,128)(2,1)S(1)}, u32[]{:S(2)}, u32[]{:S(2)}) collective-permute-start(bf16[512,256]{1,0:T(8,128)(2,1)} %refs_0_), channel_id=1, source_target_pairs={{0,24},{8,16},{1,25},{9,17},{2,26},{10,18},{3,27},{11,19},{4,28},{... | collective-permute-start | bytes 786440 | tf_op jit(solution)/shard_map/ppermute | solution.py:157
  9.1 2.7 %collective-permute-start.3 = (bf16[256,256]{1,0:T(8,128)(2,1)S(1)}, bf16[256,256]{1,0:T(8,128)(2,1)S(1)}, u32[]{:S(2)}, u32[]{:S(2)}) collective-permute-start(bf16[256,256]{1,0:T(8,128)(2,1)S(1)} %get-tuple-element.44), channel_id=1, source_target_pairs={{0,4},{1,5},{2,6},{3,7},{4,0},{5,1},{6,2},{7,3},{8,12},{9,13},{10,... | collective-permute-start | bytes 393224 | tf_op jit(solution)/shard_map/ppermute | solution.py:125
  11.8 1.3 %collective-permute-start.4 = (bf16[256,256]{1,0:T(8,128)(2,1)S(1)}, bf16[256,256]{1,0:T(8,128)(2,1)S(1)}, u32[]{:S(2)}, u32[]{:S(2)}) collective-permute-start(bf16[256,256]{1,0:T(8,128)(2,1)S(1)} %get-tuple-element.49), channel_id=1, source_target_pairs={{0,5},{1,4},{2,7},{3,6},{4,1},{5,0},{6,3},{7,2},{8,13},{9,12},{10,... | collective-permute-start | bytes 393224 | tf_op jit(solution)/shard_map/ppermute | solution.py:125
  13.0 3.6 %collective-permute-start.5 = (bf16[256,256]{1,0:T(8,128)(2,1)S(1)}, bf16[256,256]{1,0:T(8,128)(2,1)S(1)}, u32[]{:S(2)}, u32[]{:S(2)}) collective-permute-start(bf16[256,256]{1,0:T(8,128)(2,1)S(1)} %get-tuple-element.50), channel_id=1, source_target_pairs={{0,6},{1,7},{2,4},{3,5},{4,2},{5,3},{6,0},{7,1},{8,14},{9,15},{10,... | collective-permute-start | bytes 393224 | tf_op jit(solution)/shard_map/ppermute | solution.py:125
  16.6 3.2 %collective-permute-done.2.refs_3_ = bf16[512,256]{1,0:T(8,128)(2,1)S(1)} collective-permute-done((bf16[512,256]{1,0:T(8,128)(2,1)}, bf16[512,256]{1,0:T(8,128)(2,1)S(1)}, u32[]{:S(2)}, u32[]{:S(2)}) %collective-permute-start.2) | collective-permute-done | bytes 262176 | tf_op jit(solution)/shard_map/ppermute | solution.py:157
  19.8 1.6 %copy-done = bf16[512,2048]{1,0:T(8,128)(2,1)S(1)} copy-done((bf16[512,2048]{1,0:T(8,128)(2,1)S(1)}, bf16[512,2048]{1,0:T(8,128)(2,1)}, u32[]{:S(2)}) %copy-start) | copy-done | bytes 2097176
  22.4 1.3 %shard_map.95.forward_ref.refs_0_ = bf16[512,256]{1,0:T(8,128)(2,1)S(1)} custom-call(s32[4]{0:T(128)S(1)} %iota_xor_fusion.1.at_ref, bf16[512,2048]{1,0:T(8,128)(2,1)S(1)} %copy-done, bf16[512,256]{1,0:T(8,128)(2,1)S(1)} %copy-done.6, bf16[512,256]{1,0:T(8,128)(2,1)S(1)} %collective-permute-done.refs_1_, ...), custom_call_target="tpu_custom_call" | custom-call | flops 536870912 | bytes 3407872 | tf_op jit(solution)/shard_map/pallas_call | solution.py:22
  23.6 2.0 %collective-permute-start.10 = (bf16[512,256]{1,0:T(8,128)(2,1)S(1)}, bf16[512,256]{1,0:T(8,128)(2,1)S(1)}, u32[]{:S(2)}, u32[]{:S(2)}) collective-permute-start(bf16[512,256]{1,0:T(8,128)(2,1)S(1)} %shard_map.95.forward_ref.refs_0_), channel_id=1, source_target_pairs={{0,16},{8,24},{16,0},{24,8},{1,17},{9,25},{17,1},{25,9},{2,18},{10... | collective-permute-start | bytes 786440 | tf_op jit(solution)/shard_map/ppermute | solution.py:125
  25.7 4.5 %collective-permute-start.6 = (bf16[256,256]{1,0:T(8,128)(2,1)S(1)}, bf16[256,256]{1,0:T(8,128)(2,1)S(1)}, u32[]{:S(2)}, u32[]{:S(2)}) collective-permute-start(bf16[256,256]{1,0:T(8,128)(2,1)S(1)} %get-tuple-element.51), channel_id=1, source_target_pairs={{0,7},{1,6},{2,5},{3,4},{4,3},{5,2},{6,1},{7,0},{8,15},{9,14},{10,... | collective-permute-start | bytes 393224 | tf_op jit(solution)/shard_map/ppermute | solution.py:125
  30.8 2.9 %collective-permute-start.9 = (bf16[256,256]{1,0:T(8,128)(2,1)S(1)}, bf16[256,256]{1,0:T(8,128)(2,1)S(1)}, u32[]{:S(2)}, u32[]{:S(2)}) collective-permute-start(bf16[256,256]{1,0:T(8,128)(2,1)S(1)} %get-tuple-element.54), channel_id=1, source_target_pairs={{0,3},{1,2},{2,1},{3,0},{4,7},{5,6},{6,5},{7,4},{8,11},{9,10},{10,... | collective-permute-start | bytes 393224 | tf_op jit(solution)/shard_map/ppermute | solution.py:125
  33.8 3.4 %copy-done.2 = bf16[2048,2048]{1,0:T(8,128)(2,1)S(1)} copy-done((bf16[2048,2048]{1,0:T(8,128)(2,1)S(1)}, bf16[2048,2048]{1,0:T(8,128)(2,1)}, u32[]{:S(2)}) %copy-start.2) | copy-done | bytes 8388632
  37.7 1.8 %shard_map.97.begun_ref = f32[4,256,512]{2,1,0:T(8,128)S(1)} custom-call(s32[12]{0:T(128)S(1)} %pad_add_fusion.at_ref, bf16[2048,2048]{1,0:T(8,128)(2,1)S(1)} %shard_map.96.factor_ref, bf16[256,256]{1,0:T(8,128)(2,1)S(1)} %get-tuple-element.43.refs_0_, bf16[256,256]{1,0:T(8,128)(2,1)S(1)} %collective-permute-done.3.refs_1_, ...), custom_call_target="tpu_custom_call" | custom-call | flops 1073741824 | bytes 11010048 | tf_op jit(solution)/shard_map/pallas_call | solution.py:22
  40.0 1.3 %shard_map.99 = bf16[2,256,512]{2,1,0:T(8,128)(2,1)S(1)} custom-call(s32[12]{0:T(128)S(1)} %pad_add_fusion.at_ref, bf16[2048,2048]{1,0:T(8,128)(2,1)S(1)} %shard_map.96.factor_ref, f32[4,256,512]{2,1,0:T(8,128)S(1)} %shard_map.97.begun_ref, bf16[256,256]{1,0:T(8,128)(2,1)S(1)} %collective-permute-done.6.refs_0_, ...), custom_call_target="tpu_custom_call" | custom-call | flops 536870912 | bytes 11534336 | tf_op jit(solution)/shard_map/pallas_call | solution.py:22
  41.4 1.3 %shard_map.98.kept_ref = f32[2,256,512]{2,1,0:T(8,128)S(1)} custom-call(s32[12]{0:T(128)S(1)} %pad_add_fusion.at_ref, bf16[2048,2048]{1,0:T(8,128)(2,1)S(1)} %shard_map.96.factor_ref, f32[4,256,512]{2,1,0:T(8,128)S(1)} %shard_map.97.begun_ref, bf16[256,256]{1,0:T(8,128)(2,1)S(1)} %collective-permute-done.6.refs_0_, ...), custom_call_target="tpu_custom_call" | custom-call | flops 536870912 | bytes 12058624 | tf_op jit(solution)/shard_map/pallas_call | solution.py:22
  43.6 8.1 %collective-permute-done.12.across_ref = bf16[256,512]{1,0:T(8,128)(2,1)S(1)} collective-permute-done((bf16[256,512]{1,0:T(8,128)(2,1)S(1)}, bf16[256,512]{1,0:T(8,128)(2,1)S(1)}, u32[]{:S(2)}, u32[]{:S(2)}) %collective-permute-start.12) | collective-permute-done | bytes 262176 | tf_op jit(solution)/shard_map/ppermute | solution.py:125
  54.3 1.4 %collective-permute-start.14 = (bf16[256,512]{1,0:T(8,128)(2,1)S(1)}, bf16[256,512]{1,0:T(8,128)(2,1)S(1)}, u32[]{:S(2)}, u32[]{:S(2)}) collective-permute-start(bf16[256,512]{1,0:T(8,128)(2,1)S(1)} %add_convert_fusion.1), channel_id=1, source_target_pairs={{16,0},{24,8},{17,1},{25,9},{18,2},{26,10},{19,3},{27,11},{20,4},{... | collective-permute-start | bytes 786440 | tf_op jit(solution)/shard_map/ppermute | solution.py:213
  57.1 4.4 %shard_map.102 = bf16[2048,256]{1,0:T(8,128)(2,1)} custom-call(s32[4]{0:T(128)S(1)} %iota_xor_fusion.1.at_ref, bf16[2048,2048]{1,0:T(8,128)(2,1)S(1)} %shard_map.96.factor_ref, bf16[2048,256]{1,0:T(8,128)(2,1)S(1)} %copy-done.4, bf16[512,256]{1,0:T(8,128)(2,1)S(1)} %shard_map.95.forward_ref.refs_0_, bf16[512,256]{1,0:T(8,128)(2,1)S(1)} %collective-permute-done.15.refs_1_, ...), custom_call_target="tpu_custom_call" | custom-call | flops 2147483648 | bytes 11534336 | tf_op jit(solution)/shard_map/pallas_call | solution.py:22
  62.3 2.6 %collective-permute-done.14 = bf16[256,512]{1,0:T(8,128)(2,1)S(1)} collective-permute-done((bf16[256,512]{1,0:T(8,128)(2,1)S(1)}, bf16[256,512]{1,0:T(8,128)(2,1)S(1)}, u32[]{:S(2)}, u32[]{:S(2)}) %collective-permute-start.14) | collective-permute-done | bytes 262176 | tf_op jit(solution)/shard_map/ppermute | solution.py:213
  65.1 1.3 %collective-permute-start.18 = (bf16[256,512]{1,0:T(8,128)(2,1)S(1)}, bf16[256,512]{1,0:T(8,128)(2,1)S(1)}, u32[]{:S(2)}, u32[]{:S(2)}) collective-permute-start(bf16[256,512]{1,0:T(8,128)(2,1)S(1)} %add_convert_fusion.refs_0_), channel_id=1, source_target_pairs={{0,1},{1,0},{2,3},{3,2},{4,5},{5,4},{6,7},{7,6},{8,9},{9,8},{10,11... | collective-permute-start | bytes 786440 | tf_op jit(solution)/shard_map/ppermute | solution.py:125
  66.4 1.7 %collective-permute-start.19 = (bf16[256,512]{1,0:T(8,128)(2,1)S(1)}, bf16[256,512]{1,0:T(8,128)(2,1)S(1)}, u32[]{:S(2)}, u32[]{:S(2)}) collective-permute-start(bf16[256,512]{1,0:T(8,128)(2,1)S(1)} %add_convert_fusion.refs_0_), channel_id=1, source_target_pairs={{0,2},{1,3},{2,0},{3,1},{4,6},{5,7},{6,4},{7,5},{8,10},{9,11},{10,... | collective-permute-start | bytes 786440 | tf_op jit(solution)/shard_map/ppermute | solution.py:125
  68.9 3.9 %collective-permute-done.18.refs_1_ = bf16[256,512]{1,0:T(8,128)(2,1)S(1)} collective-permute-done((bf16[256,512]{1,0:T(8,128)(2,1)S(1)}, bf16[256,512]{1,0:T(8,128)(2,1)S(1)}, u32[]{:S(2)}, u32[]{:S(2)}) %collective-permute-start.18) | collective-permute-done | bytes 262176 | tf_op jit(solution)/shard_map/ppermute | solution.py:125
  72.9 2.0 %collective-permute-done.19.refs_2_ = bf16[256,512]{1,0:T(8,128)(2,1)S(1)} collective-permute-done((bf16[256,512]{1,0:T(8,128)(2,1)S(1)}, bf16[256,512]{1,0:T(8,128)(2,1)S(1)}, u32[]{:S(2)}, u32[]{:S(2)}) %collective-permute-start.19) | collective-permute-done | bytes 262176 | tf_op jit(solution)/shard_map/ppermute | solution.py:125
  76.1 4.3 %collective-permute-done.20.refs_4_ = bf16[256,512]{1,0:T(8,128)(2,1)S(1)} collective-permute-done((bf16[256,512]{1,0:T(8,128)(2,1)S(1)}, bf16[256,512]{1,0:T(8,128)(2,1)S(1)}, u32[]{:S(2)}, u32[]{:S(2)}) %collective-permute-start.20) | collective-permute-done | bytes 262176 | tf_op jit(solution)/shard_map/ppermute | solution.py:125
  81.3 1.3 %collective-permute-start.24 = (bf16[256,512]{1,0:T(8,128)(2,1)S(1)}, bf16[256,512]{1,0:T(8,128)(2,1)S(1)}, u32[]{:S(2)}, u32[]{:S(2)}) collective-permute-start(bf16[256,512]{1,0:T(8,128)(2,1)S(1)} %collective-permute-done.20.refs_4_), channel_id=1, source_target_pairs={{2,0},{3,1},{4,6},{5,7},{10,8},{11,9},{12,14},{13,15},{18,16},{19,... | collective-permute-start | bytes 786440 | tf_op jit(solution)/shard_map/ppermute | solution.py:238
  83.2 1.4 %collective-permute-start.25 = (bf16[256,512]{1,0:T(8,128)(2,1)S(1)}, bf16[256,512]{1,0:T(8,128)(2,1)}, u32[]{:S(2)}, u32[]{:S(2)}) collective-permute-start(bf16[256,512]{1,0:T(8,128)(2,1)S(1)} %collective-permute-done.23.refs_6_), channel_id=1, source_target_pairs={{2,3},{3,2},{4,5},{5,4},{10,11},{11,10},{12,13},{13,12},{18,19},{1... | collective-permute-start | bytes 786440 | tf_op jit(solution)/shard_map/ppermute | solution.py:240
  84.5 5.0 %collective-permute-done.24.refs_7_ = bf16[256,512]{1,0:T(8,128)(2,1)S(1)} collective-permute-done((bf16[256,512]{1,0:T(8,128)(2,1)S(1)}, bf16[256,512]{1,0:T(8,128)(2,1)S(1)}, u32[]{:S(2)}, u32[]{:S(2)}) %collective-permute-start.24) | collective-permute-done | bytes 262176 | tf_op jit(solution)/shard_map/ppermute | solution.py:238
  89.5 2.4 %collective-permute-start.26 = (bf16[256,512]{1,0:T(8,128)(2,1)S(1)}, bf16[256,512]{1,0:T(8,128)(2,1)}, u32[]{:S(2)}, u32[]{:S(2)}) collective-permute-start(bf16[256,512]{1,0:T(8,128)(2,1)S(1)} %collective-permute-done.24.refs_7_), channel_id=1, source_target_pairs={{0,1},{1,0},{6,7},{7,6},{8,9},{9,8},{14,15},{15,14},{16,17},{17,16... | collective-permute-start | bytes 786440 | tf_op jit(solution)/shard_map/ppermute | solution.py:241
  92.9 1.8 %shard_map.105.refs_0_ = f32[384,512]{1,0:T(8,128)S(1)} custom-call(s32[9]{0:T(128)S(1)} %pad_add_fusion.1.at_ref, bf16[384,2048]{1,0:T(8,128)(2,1)S(1)} %copy-done.3, bf16[256,512]{1,0:T(8,128)(2,1)S(1)} %add_convert_fusion.refs_0_, bf16[256,512]{1,0:T(8,128)(2,1)S(1)} %collective-permute-done.18.refs_1_, ...), custom_call_target="tpu_custom_call" | custom-call | flops 704643072 | bytes 4456448 | tf_op jit(solution)/shard_map/pallas_call | solution.py:22
  94.8 3.1 %collective-permute-done.26.refs_2_ = bf16[256,512]{1,0:T(8,128)(2,1)} collective-permute-done((bf16[256,512]{1,0:T(8,128)(2,1)S(1)}, bf16[256,512]{1,0:T(8,128)(2,1)}, u32[]{:S(2)}, u32[]{:S(2)}) %collective-permute-start.26) | collective-permute-done | bytes 262176 | tf_op jit(solution)/shard_map/ppermute | solution.py:241
  97.9 2.2 %shard_map.106 = f32[384,512]{1,0:T(8,128)} custom-call(s32[9]{0:T(128)S(1)} %pad_add_fusion.1.at_ref, bf16[384,2048]{1,0:T(8,128)(2,1)S(1)} %copy-done.3, f32[384,512]{1,0:T(8,128)S(1)} %shard_map.105.refs_0_, bf16[256,512]{1,0:T(8,128)(2,1)} %collective-permute-done.25.refs_1_, bf16[256,512]{1,0:T(8,128)(2,1)} %collective-permute-done.26.refs_2_), custom_call_target="tpu_custom_call" | custom-call | flops 100663296 | bytes 3670016 | tf_op jit(solution)/shard_map/pallas_call | solution.py:22
  (60 shorter events, 14.2 us)
Async XLA Ops:
  2.7 10.3 %collective-permute-start = (bf16[512,256]{1,0:T(8,128)(2,1)}, bf16[512,256]{1,0:T(8,128)(2,1)S(1)}, u32[]{:S(2)}, u32[]{:S(2)}) collective-permute-start(bf16[512,256]{1,0:T(8,128)(2,1)} %refs_0_), channel_id=1, source_target_pairs={{0,8},{8,0},{16,24},{24,16},{1,9},{9,1},{17,25},{25,17},{2,10},{10... | collective-permute-start | bytes 786440 | tf_op jit(solution)/shard_map/ppermute | solution.py:125
  3.3 13.4 %collective-permute-start.1 = (bf16[512,256]{1,0:T(8,128)(2,1)}, bf16[512,256]{1,0:T(8,128)(2,1)S(1)}, u32[]{:S(2)}, u32[]{:S(2)}) collective-permute-start(bf16[512,256]{1,0:T(8,128)(2,1)} %refs_0_), channel_id=1, source_target_pairs={{0,16},{8,24},{1,17},{9,25},{2,18},{10,26},{3,19},{11,27},{4,20},{... | collective-permute-start | bytes 786440 | tf_op jit(solution)/shard_map/ppermute | solution.py:155
  7.7 12.1 %collective-permute-start.2 = (bf16[512,256]{1,0:T(8,128)(2,1)}, bf16[512,256]{1,0:T(8,128)(2,1)S(1)}, u32[]{:S(2)}, u32[]{:S(2)}) collective-permute-start(bf16[512,256]{1,0:T(8,128)(2,1)} %refs_0_), channel_id=1, source_target_pairs={{0,24},{8,16},{1,25},{9,17},{2,26},{10,18},{3,27},{11,19},{4,28},{... | collective-permute-start | bytes 786440 | tf_op jit(solution)/shard_map/ppermute | solution.py:157
  9.1 21.1 %collective-permute-start.3 = (bf16[256,256]{1,0:T(8,128)(2,1)S(1)}, bf16[256,256]{1,0:T(8,128)(2,1)S(1)}, u32[]{:S(2)}, u32[]{:S(2)}) collective-permute-start(bf16[256,256]{1,0:T(8,128)(2,1)S(1)} %get-tuple-element.44), channel_id=1, source_target_pairs={{0,4},{1,5},{2,6},{3,7},{4,0},{5,1},{6,2},{7,3},{8,12},{9,13},{10,... | collective-permute-start | bytes 393224 | tf_op jit(solution)/shard_map/ppermute | solution.py:125
  11.8 19.0 %collective-permute-start.4 = (bf16[256,256]{1,0:T(8,128)(2,1)S(1)}, bf16[256,256]{1,0:T(8,128)(2,1)S(1)}, u32[]{:S(2)}, u32[]{:S(2)}) collective-permute-start(bf16[256,256]{1,0:T(8,128)(2,1)S(1)} %get-tuple-element.49), channel_id=1, source_target_pairs={{0,5},{1,4},{2,7},{3,6},{4,1},{5,0},{6,3},{7,2},{8,13},{9,12},{10,... | collective-permute-start | bytes 393224 | tf_op jit(solution)/shard_map/ppermute | solution.py:125
  13.0 17.7 %collective-permute-start.5 = (bf16[256,256]{1,0:T(8,128)(2,1)S(1)}, bf16[256,256]{1,0:T(8,128)(2,1)S(1)}, u32[]{:S(2)}, u32[]{:S(2)}) collective-permute-start(bf16[256,256]{1,0:T(8,128)(2,1)S(1)} %get-tuple-element.50), channel_id=1, source_target_pairs={{0,6},{1,7},{2,4},{3,5},{4,2},{5,3},{6,0},{7,1},{8,14},{9,15},{10,... | collective-permute-start | bytes 393224 | tf_op jit(solution)/shard_map/ppermute | solution.py:125
  23.6 16.3 %collective-permute-start.10 = (bf16[512,256]{1,0:T(8,128)(2,1)S(1)}, bf16[512,256]{1,0:T(8,128)(2,1)S(1)}, u32[]{:S(2)}, u32[]{:S(2)}) collective-permute-start(bf16[512,256]{1,0:T(8,128)(2,1)S(1)} %shard_map.95.forward_ref.refs_0_), channel_id=1, source_target_pairs={{0,16},{8,24},{16,0},{24,8},{1,17},{9,25},{17,1},{25,9},{2,18},{10... | collective-permute-start | bytes 786440 | tf_op jit(solution)/shard_map/ppermute | solution.py:125
  25.7 14.3 %collective-permute-start.6 = (bf16[256,256]{1,0:T(8,128)(2,1)S(1)}, bf16[256,256]{1,0:T(8,128)(2,1)S(1)}, u32[]{:S(2)}, u32[]{:S(2)}) collective-permute-start(bf16[256,256]{1,0:T(8,128)(2,1)S(1)} %get-tuple-element.51), channel_id=1, source_target_pairs={{0,7},{1,6},{2,5},{3,4},{4,3},{5,2},{6,1},{7,0},{8,15},{9,14},{10,... | collective-permute-start | bytes 393224 | tf_op jit(solution)/shard_map/ppermute | solution.py:125
  30.2 9.8 %collective-permute-start.7 = (bf16[256,256]{1,0:T(8,128)(2,1)S(1)}, bf16[256,256]{1,0:T(8,128)(2,1)S(1)}, u32[]{:S(2)}, u32[]{:S(2)}) collective-permute-start(bf16[256,256]{1,0:T(8,128)(2,1)S(1)} %get-tuple-element.52), channel_id=1, source_target_pairs={{0,1},{1,0},{2,3},{3,2},{4,5},{5,4},{6,7},{7,6},{8,9},{9,8},{10,11... | collective-permute-start | bytes 393224 | tf_op jit(solution)/shard_map/ppermute | solution.py:125
  30.7 9.2 %collective-permute-start.8 = (bf16[256,256]{1,0:T(8,128)(2,1)S(1)}, bf16[256,256]{1,0:T(8,128)(2,1)S(1)}, u32[]{:S(2)}, u32[]{:S(2)}) collective-permute-start(bf16[256,256]{1,0:T(8,128)(2,1)S(1)} %get-tuple-element.53), channel_id=1, source_target_pairs={{0,2},{1,3},{2,0},{3,1},{4,6},{5,7},{6,4},{7,5},{8,10},{9,11},{10,... | collective-permute-start | bytes 393224 | tf_op jit(solution)/shard_map/ppermute | solution.py:125
  30.8 9.2 %collective-permute-start.9 = (bf16[256,256]{1,0:T(8,128)(2,1)S(1)}, bf16[256,256]{1,0:T(8,128)(2,1)S(1)}, u32[]{:S(2)}, u32[]{:S(2)}) collective-permute-start(bf16[256,256]{1,0:T(8,128)(2,1)S(1)} %get-tuple-element.54), channel_id=1, source_target_pairs={{0,3},{1,2},{2,1},{3,0},{4,7},{5,6},{6,5},{7,4},{8,11},{9,10},{10,... | collective-permute-start | bytes 393224 | tf_op jit(solution)/shard_map/ppermute | solution.py:125
  33.8 3.4 %copy-start.2 = (bf16[2048,2048]{1,0:T(8,128)(2,1)S(1)}, bf16[2048,2048]{1,0:T(8,128)(2,1)}, u32[]{:S(2)}) copy-start(bf16[2048,2048]{1,0:T(8,128)(2,1)} %factor_ref.1) | copy-start | bytes 25165828
  41.3 2.0 %collective-permute-start.11 = (bf16[2,256,512]{2,1,0:T(8,128)(2,1)S(1)}, bf16[2,256,512]{2,1,0:T(8,128)(2,1)S(1)}, u32[]{:S(2)}, u32[]{:S(2)}) collective-permute-start(bf16[2,256,512]{2,1,0:T(8,128)(2,1)S(1)} %shard_map.99), channel_id=1, source_target_pairs={{0,8},{8,0},{16,24},{24,16},{1,9},{9,1},{17,25},{25,17},{2,10},{10... | collective-permute-start | bytes 1572872 | tf_op jit(solution)/shard_map/ppermute | solution.py:125
  41.3 10.4 %copy-start.1 = (bf16[512,2048]{1,0:T(8,128)(2,1)S(1)}, bf16[512,2048]{1,0:T(8,128)(2,1)}, u32[]{:S(2)}) copy-start(bf16[512,2048]{1,0:T(8,128)(2,1)} %inverse_ref.9) | copy-start | bytes 6291460
  43.3 8.4 %collective-permute-start.12 = (bf16[256,512]{1,0:T(8,128)(2,1)S(1)}, bf16[256,512]{1,0:T(8,128)(2,1)S(1)}, u32[]{:S(2)}, u32[]{:S(2)}) collective-permute-start(bf16[256,512]{1,0:T(8,128)(2,1)S(1)} %fusion.1), channel_id=1, source_target_pairs={{0,16},{8,24},{16,0},{24,8},{1,17},{9,25},{17,1},{25,9},{2,18},{10... | collective-permute-start | bytes 786440 | tf_op jit(solution)/shard_map/ppermute | solution.py:125
  52.7 1.6 %collective-permute-start.13 = (bf16[256,512]{1,0:T(8,128)(2,1)S(1)}, bf16[256,512]{1,0:T(8,128)(2,1)S(1)}, u32[]{:S(2)}, u32[]{:S(2)}) collective-permute-start(bf16[256,512]{1,0:T(8,128)(2,1)S(1)} %get-tuple-element.57), channel_id=1, source_target_pairs={{0,8},{8,0},{16,24},{24,16},{1,9},{9,1},{17,25},{25,17},{2,10},{10... | collective-permute-start | bytes 786440 | tf_op jit(solution)/shard_map/ppermute | solution.py:125
  52.7 4.3 %collective-permute-start.15 = (bf16[512,256]{1,0:T(8,128)(2,1)S(1)}, bf16[512,256]{1,0:T(8,128)(2,1)S(1)}, u32[]{:S(2)}, u32[]{:S(2)}) collective-permute-start(bf16[512,256]{1,0:T(8,128)(2,1)S(1)} %shard_map.95.forward_ref.refs_0_), channel_id=1, source_target_pairs={{0,8},{8,0},{16,24},{24,16},{1,9},{9,1},{17,25},{25,17},{2,10},{10... | collective-permute-start | bytes 786440 | tf_op jit(solution)/shard_map/ppermute | solution.py:125
  53.2 3.8 %collective-permute-start.16 = (bf16[512,256]{1,0:T(8,128)(2,1)S(1)}, bf16[512,256]{1,0:T(8,128)(2,1)S(1)}, u32[]{:S(2)}, u32[]{:S(2)}) collective-permute-start(bf16[512,256]{1,0:T(8,128)(2,1)S(1)} %collective-permute-done.10.refs_2_), channel_id=1, source_target_pairs={{0,8},{8,0},{16,24},{24,16},{1,9},{9,1},{17,25},{25,17},{2,10},{10... | collective-permute-start | bytes 786440 | tf_op jit(solution)/shard_map/ppermute | solution.py:125
  54.2 2.9 %copy-start.4 = (bf16[2048,256]{1,0:T(8,128)(2,1)S(1)}, bf16[2048,256]{1,0:T(8,128)(2,1)}, u32[]{:S(2)}) copy-start(bf16[2048,256]{1,0:T(8,128)(2,1)} %rhs_ref.1) | copy-start | bytes 3145732
  54.3 10.6 %collective-permute-start.14 = (bf16[256,512]{1,0:T(8,128)(2,1)S(1)}, bf16[256,512]{1,0:T(8,128)(2,1)S(1)}, u32[]{:S(2)}, u32[]{:S(2)}) collective-permute-start(bf16[256,512]{1,0:T(8,128)(2,1)S(1)} %add_convert_fusion.1), channel_id=1, source_target_pairs={{16,0},{24,8},{17,1},{25,9},{18,2},{26,10},{19,3},{27,11},{20,4},{... | collective-permute-start | bytes 786440 | tf_op jit(solution)/shard_map/ppermute | solution.py:213
  56.6 8.3 %collective-permute-start.17 = (bf16[256,512]{1,0:T(8,128)(2,1)S(1)}, bf16[256,512]{1,0:T(8,128)(2,1)S(1)}, u32[]{:S(2)}, u32[]{:S(2)}) collective-permute-start(bf16[256,512]{1,0:T(8,128)(2,1)S(1)} %shard_map.104), channel_id=1, source_target_pairs={{0,8},{8,0},{16,24},{24,16},{1,9},{9,1},{17,25},{25,17},{2,10},{10... | collective-permute-start | bytes 786440 | tf_op jit(solution)/shard_map/ppermute | solution.py:125
  61.5 30.5 %copy-start.7 = (s32[8]{0:T(128)S(1)}, s32[8]{0:T(128)}, u32[]{:S(2)}) copy-start(s32[8]{0:T(128)} %constant.14.clone) | copy-start | bytes 100
  61.5 31.4 %copy-start.3 = (bf16[384,2048]{1,0:T(8,128)(2,1)S(1)}, bf16[384,2048]{1,0:T(8,128)(2,1)}, u32[]{:S(2)}) copy-start(bf16[384,2048]{1,0:T(8,128)(2,1)} %axle_ref.3) | copy-start | bytes 4718596
  65.1 7.8 %collective-permute-start.18 = (bf16[256,512]{1,0:T(8,128)(2,1)S(1)}, bf16[256,512]{1,0:T(8,128)(2,1)S(1)}, u32[]{:S(2)}, u32[]{:S(2)}) collective-permute-start(bf16[256,512]{1,0:T(8,128)(2,1)S(1)} %add_convert_fusion.refs_0_), channel_id=1, source_target_pairs={{0,1},{1,0},{2,3},{3,2},{4,5},{5,4},{6,7},{7,6},{8,9},{9,8},{10,11... | collective-permute-start | bytes 786440 | tf_op jit(solution)/shard_map/ppermute | solution.py:125
  66.4 8.5 %collective-permute-start.19 = (bf16[256,512]{1,0:T(8,128)(2,1)S(1)}, bf16[256,512]{1,0:T(8,128)(2,1)S(1)}, u32[]{:S(2)}, u32[]{:S(2)}) collective-permute-start(bf16[256,512]{1,0:T(8,128)(2,1)S(1)} %add_convert_fusion.refs_0_), channel_id=1, source_target_pairs={{0,2},{1,3},{2,0},{3,1},{4,6},{5,7},{6,4},{7,5},{8,10},{9,11},{10,... | collective-permute-start | bytes 786440 | tf_op jit(solution)/shard_map/ppermute | solution.py:125
  68.1 12.3 %collective-permute-start.20 = (bf16[256,512]{1,0:T(8,128)(2,1)S(1)}, bf16[256,512]{1,0:T(8,128)(2,1)S(1)}, u32[]{:S(2)}, u32[]{:S(2)}) collective-permute-start(bf16[256,512]{1,0:T(8,128)(2,1)S(1)} %add_convert_fusion.refs_0_), channel_id=1, source_target_pairs={{0,6},{1,7},{2,4},{3,5},{4,2},{5,3},{6,0},{7,1},{8,14},{9,15},{10,... | collective-permute-start | bytes 786440 | tf_op jit(solution)/shard_map/ppermute | solution.py:125
  74.9 6.4 %collective-permute-start.21 = (bf16[256,512]{1,0:T(8,128)(2,1)S(1)}, bf16[256,512]{1,0:T(8,128)(2,1)S(1)}, u32[]{:S(2)}, u32[]{:S(2)}) collective-permute-start(bf16[256,512]{1,0:T(8,128)(2,1)S(1)} %collective-permute-done.19.refs_2_), channel_id=1, source_target_pairs={{0,1},{1,0},{2,3},{3,2},{4,5},{5,4},{6,7},{7,6},{8,9},{9,8},{10,11... | collective-permute-start | bytes 786440 | tf_op jit(solution)/shard_map/ppermute | solution.py:125
  75.4 7.7 %collective-permute-start.23 = (bf16[256,512]{1,0:T(8,128)(2,1)S(1)}, bf16[256,512]{1,0:T(8,128)(2,1)S(1)}, u32[]{:S(2)}, u32[]{:S(2)}) collective-permute-start(bf16[256,512]{1,0:T(8,128)(2,1)S(1)} %collective-permute-done.19.refs_2_), channel_id=1, source_target_pairs={{2,4},{3,5},{4,2},{5,3},{10,12},{11,13},{12,10},{13,11},{18,20},{1... | collective-permute-start | bytes 786440 | tf_op jit(solution)/shard_map/ppermute | solution.py:237
  81.3 8.3 %collective-permute-start.24 = (bf16[256,512]{1,0:T(8,128)(2,1)S(1)}, bf16[256,512]{1,0:T(8,128)(2,1)S(1)}, u32[]{:S(2)}, u32[]{:S(2)}) collective-permute-start(bf16[256,512]{1,0:T(8,128)(2,1)S(1)} %collective-permute-done.20.refs_4_), channel_id=1, source_target_pairs={{2,0},{3,1},{4,6},{5,7},{10,8},{11,9},{12,14},{13,15},{18,16},{19,... | collective-permute-start | bytes 786440 | tf_op jit(solution)/shard_map/ppermute | solution.py:238
  82.6 10.4 %collective-permute-start.22 = (bf16[256,512]{1,0:T(8,128)(2,1)S(1)}, bf16[256,512]{1,0:T(8,128)(2,1)}, u32[]{:S(2)}, u32[]{:S(2)}) collective-permute-start(bf16[256,512]{1,0:T(8,128)(2,1)S(1)} %collective-permute-done.20.refs_4_), channel_id=1, source_target_pairs={{0,1},{1,0},{2,3},{3,2},{4,5},{5,4},{6,7},{7,6},{8,9},{9,8},{10,11... | collective-permute-start | bytes 786440 | tf_op jit(solution)/shard_map/ppermute | solution.py:125
  83.2 11.6 %collective-permute-start.25 = (bf16[256,512]{1,0:T(8,128)(2,1)S(1)}, bf16[256,512]{1,0:T(8,128)(2,1)}, u32[]{:S(2)}, u32[]{:S(2)}) collective-permute-start(bf16[256,512]{1,0:T(8,128)(2,1)S(1)} %collective-permute-done.23.refs_6_), channel_id=1, source_target_pairs={{2,3},{3,2},{4,5},{5,4},{10,11},{11,10},{12,13},{13,12},{18,19},{1... | collective-permute-start | bytes 786440 | tf_op jit(solution)/shard_map/ppermute | solution.py:240
  89.5 8.4 %collective-permute-start.26 = (bf16[256,512]{1,0:T(8,128)(2,1)S(1)}, bf16[256,512]{1,0:T(8,128)(2,1)}, u32[]{:S(2)}, u32[]{:S(2)}) collective-permute-start(bf16[256,512]{1,0:T(8,128)(2,1)S(1)} %collective-permute-done.24.refs_7_), channel_id=1, source_target_pairs={{0,1},{1,0},{6,7},{7,6},{8,9},{9,8},{14,15},{15,14},{16,17},{17,16... | collective-permute-start | bytes 786440 | tf_op jit(solution)/shard_map/ppermute | solution.py:241
  (3 other events, 3.8 us)

commit v9 on v8

--- a/solution.py
+++ b/solution.py
@@ -37,12 +37,12 @@
     return jnp.dot(a, b, preferred_element_type=F32)
 
 
-def forward_kernel(at_ref, inverse_ref, *refs):
-    blocks, out_ref = refs[:-1], refs[-1]
+def forward_kernel(first, at_ref, inverse_ref, *refs):
+    refs, out_ref = list(refs[:-1]), refs[-1]
     rows = out_ref.shape[0]
-    total = None
-    for j, block in enumerate(blocks):
-        term = dot(inverse_ref[:, part(at_ref[j], rows)], block[...])
+    total = None if first == 0 else refs.pop(0)[...]
+    for j, block in enumerate(refs):
+        term = dot(inverse_ref[:, part(at_ref[first + j], rows)], block[...])
         total = term if total is None else total + term
     out_ref[...] = total.astype(out_ref.dtype)
 
@@ -155,12 +155,20 @@
     b_across = lax.ppermute(b_panel, "factor", [(0, 2), (1, 3)])
     b_core = by_xor(b_panel, "factor", factors, 1)
     b_far = lax.ppermute(b_panel, "factor", [(0, 3), (1, 2)])
+    work = rows * panel * cols
+    (begun,) = call(
+        functools.partial(forward_kernel, 0),
+        at_factor,
+        [panel_inverse, b_panel, b_core],
+        [((rows, cols), F32)],
+        work,
+    )
     (forward,) = call(
-        forward_kernel,
+        functools.partial(forward_kernel, 2),
         at_factor,
-        [panel_inverse, b_panel, b_core, b_across, b_far],
+        [panel_inverse, begun, b_across, b_far],
         [((rows, cols), BF16)],
-        2 * rows * panel * cols,
+        work,
     )
     forward_across = by_xor(forward, "factor", factors, 2)
     late[3], forward_across = lax.optimization_barrier((late[3], forward_across))

time: 100 us -> 105 us (1.050)
  the two profiles are of different devices: /device:TPU:0 before, /device:TPU:30 now
where the time goes in v9:
time: 105 us; the launch traced here: 104 us
  waiting for transfers between devices  45 us (43%)
  starting transfers between devices  30.3 us (29%)
  Pallas kernels  19.6 us (19%)
  local copies, waits for them, and re-layouts  8 us (8%)
    ppermute x20, waiting for transfers between devices, by_xor(): return lax.ppermute(value, axis, [(i, i ^ bits) for i in range(size)])  30.1 us
    pallas_call x13, Pallas kernels, call(): pl.pallas_call(kernel, out_shape=shapes, in_specs=[SMEM] * len(at) + [VME...  19.1 us
    ppermute x20, starting transfers between devices, by_xor(): return lax.ppermute(value, axis, [(i, i ^ bits) for i in range(size)])  18.2 us
    unnamed x17, local copies, waits for them, and re-layouts  8 us
    ppermute x1, waiting for transfers between devices, small_slice(): d = lax.ppermute(b, 'load', [(i, i ^ 2) for i in middle])  5.03 us
    ppermute x1, waiting for transfers between devices, small_slice(): b_far = lax.ppermute(b_panel, 'factor', [(0, 3), (1, 2)])  4.8 us
    ppermute x1, starting transfers between devices, small_slice(): from_across = lax.ppermute(send, 'factor', [(2, 0), (3, 1)])  3.81 us
    ppermute x1, waiting for transfers between devices, small_slice(): d_x = lax.ppermute(d, 'load', [(i, i ^ 1) for i in (0, 1, 6, 7)])  3.15 us
  transfers between devices with their start and end apart: 27, of which 12 were waited for; matrix products, arithmetic and copies ran while one was open for 1% of the time, Pallas kernels for 14%

profile of v9, /device:TPU:30, one launch (start us, length us, event | category | flops | bytes accessed | tf_op | source)
XLA Modules:
  0.0 104.3 jit_solution(11422629546451077641)
XLA Ops:
  0.7 1.2 %copy-done.5 = bf16[256,2048]{1,0:T(8,128)(2,1)S(1)} copy-done((bf16[256,2048]{1,0:T(8,128)(2,1)S(1)}, bf16[256,2048]{1,0:T(8,128)(2,1)}, u32[]{:S(2)}) %copy-start.5) | copy-done | bytes 1048600
  2.8 1.3 %collective-permute-start.1 = (bf16[512,256]{1,0:T(8,128)(2,1)}, bf16[512,256]{1,0:T(8,128)(2,1)S(1)}, u32[]{:S(2)}, u32[]{:S(2)}) collective-permute-start(bf16[512,256]{1,0:T(8,128)(2,1)} %refs_0_), channel_id=1, source_target_pairs={{0,16},{8,24},{1,17},{9,25},{2,18},{10,26},{3,19},{11,27},{4,20},{... | collective-permute-start | bytes 786440 | tf_op jit(solution)/shard_map/ppermute | solution.py:155
  4.1 1.3 %collective-permute-start.2 = (bf16[512,256]{1,0:T(8,128)(2,1)}, bf16[512,256]{1,0:T(8,128)(2,1)S(1)}, u32[]{:S(2)}, u32[]{:S(2)}) collective-permute-start(bf16[512,256]{1,0:T(8,128)(2,1)} %refs_0_), channel_id=1, source_target_pairs={{0,24},{8,16},{1,25},{9,17},{2,26},{10,18},{3,27},{11,19},{4,28},{... | collective-permute-start | bytes 786440 | tf_op jit(solution)/shard_map/ppermute | solution.py:157
  5.8 2.6 %collective-permute-start.4 = (bf16[256,256]{1,0:T(8,128)(2,1)S(1)}, bf16[256,256]{1,0:T(8,128)(2,1)S(1)}, u32[]{:S(2)}, u32[]{:S(2)}) collective-permute-start(bf16[256,256]{1,0:T(8,128)(2,1)S(1)} %get-tuple-element.49), channel_id=1, source_target_pairs={{0,5},{1,4},{2,7},{3,6},{4,1},{5,0},{6,3},{7,2},{8,13},{9,12},{10,... | collective-permute-start | bytes 393224 | tf_op jit(solution)/shard_map/ppermute | solution.py:125
  8.6 1.6 %copy-done = bf16[512,2048]{1,0:T(8,128)(2,1)S(1)} copy-done((bf16[512,2048]{1,0:T(8,128)(2,1)S(1)}, bf16[512,2048]{1,0:T(8,128)(2,1)}, u32[]{:S(2)}) %copy-start) | copy-done | bytes 2097176
  11.2 1.0 shard_map.95.refs_0_
  12.2 1.9 %collective-permute-done.1.refs_1_ = bf16[512,256]{1,0:T(8,128)(2,1)S(1)} collective-permute-done((bf16[512,256]{1,0:T(8,128)(2,1)}, bf16[512,256]{1,0:T(8,128)(2,1)S(1)}, u32[]{:S(2)}, u32[]{:S(2)}) %collective-permute-start.1) | collective-permute-done | bytes 262176 | tf_op jit(solution)/shard_map/ppermute | solution.py:155
  14.0 4.8 %collective-permute-done.2.refs_2_ = bf16[512,256]{1,0:T(8,128)(2,1)S(1)} collective-permute-done((bf16[512,256]{1,0:T(8,128)(2,1)}, bf16[512,256]{1,0:T(8,128)(2,1)S(1)}, u32[]{:S(2)}, u32[]{:S(2)}) %collective-permute-start.2) | collective-permute-done | bytes 262176 | tf_op jit(solution)/shard_map/ppermute | solution.py:157
  18.8 1.0 shard_map.96.forward_ref.refs_0_
  20.6 1.0 collective-permute-start.7
  21.7 1.7 %collective-permute-done.4.refs_2_ = bf16[256,256]{1,0:T(8,128)(2,1)S(1)} collective-permute-done((bf16[256,256]{1,0:T(8,128)(2,1)S(1)}, bf16[256,256]{1,0:T(8,128)(2,1)S(1)}, u32[]{:S(2)}, u32[]{:S(2)}) %collective-permute-start.4) | collective-permute-done | bytes 131104 | tf_op jit(solution)/shard_map/ppermute | solution.py:125
  23.4 6.2 %collective-permute-start.9 = (bf16[256,256]{1,0:T(8,128)(2,1)S(1)}, bf16[256,256]{1,0:T(8,128)(2,1)S(1)}, u32[]{:S(2)}, u32[]{:S(2)}) collective-permute-start(bf16[256,256]{1,0:T(8,128)(2,1)S(1)} %get-tuple-element.54), channel_id=1, source_target_pairs={{0,3},{1,2},{2,1},{3,0},{4,7},{5,6},{6,5},{7,4},{8,11},{9,10},{10,... | collective-permute-start | bytes 393224 | tf_op jit(solution)/shard_map/ppermute | solution.py:125
  29.7 3.4 %copy-done.2 = bf16[2048,2048]{1,0:T(8,128)(2,1)S(1)} copy-done((bf16[2048,2048]{1,0:T(8,128)(2,1)S(1)}, bf16[2048,2048]{1,0:T(8,128)(2,1)}, u32[]{:S(2)}) %copy-start.2) | copy-done | bytes 8388632
  33.6 1.8 %shard_map.98.begun_ref = f32[4,256,512]{2,1,0:T(8,128)S(1)} custom-call(s32[12]{0:T(128)S(1)} %pad_add_fusion.at_ref, bf16[2048,2048]{1,0:T(8,128)(2,1)S(1)} %shard_map.97.factor_ref, bf16[256,256]{1,0:T(8,128)(2,1)S(1)} %get-tuple-element.43.refs_0_, bf16[256,256]{1,0:T(8,128)(2,1)S(1)} %collective-permute-done.3.refs_1_, ...), custom_call_target="tpu_custom_call" | custom-call | flops 1073741824 | bytes 11010048 | tf_op jit(solution)/shard_map/pallas_call | solution.py:22
  35.5 1.3 %shard_map.100 = bf16[2,256,512]{2,1,0:T(8,128)(2,1)S(1)} custom-call(s32[12]{0:T(128)S(1)} %pad_add_fusion.at_ref, bf16[2048,2048]{1,0:T(8,128)(2,1)S(1)} %shard_map.97.factor_ref, f32[4,256,512]{2,1,0:T(8,128)S(1)} %shard_map.98.begun_ref, bf16[256,256]{1,0:T(8,128)(2,1)S(1)} %collective-permute-done.6.refs_0_, ...), custom_call_target="tpu_custom_call" | custom-call | flops 536870912 | bytes 11534336 | tf_op jit(solution)/shard_map/pallas_call | solution.py:22
  36.9 1.3 %shard_map.99.kept_ref = f32[2,256,512]{2,1,0:T(8,128)S(1)} custom-call(s32[12]{0:T(128)S(1)} %pad_add_fusion.at_ref, bf16[2048,2048]{1,0:T(8,128)(2,1)S(1)} %shard_map.97.factor_ref, f32[4,256,512]{2,1,0:T(8,128)S(1)} %shard_map.98.begun_ref, bf16[256,256]{1,0:T(8,128)(2,1)S(1)} %collective-permute-done.6.refs_0_, ...), custom_call_target="tpu_custom_call" | custom-call | flops 536870912 | bytes 12058624 | tf_op jit(solution)/shard_map/pallas_call | solution.py:22
  38.8 2.5 %collective-permute-start.12 = (bf16[256,512]{1,0:T(8,128)(2,1)S(1)}, bf16[256,512]{1,0:T(8,128)(2,1)S(1)}, u32[]{:S(2)}, u32[]{:S(2)}) collective-permute-start(bf16[256,512]{1,0:T(8,128)(2,1)S(1)} %fusion.1), channel_id=1, source_target_pairs={{0,16},{8,24},{16,0},{24,8},{1,17},{9,25},{17,1},{25,9},{2,18},{10... | collective-permute-start | bytes 786440 | tf_op jit(solution)/shard_map/ppermute | solution.py:125
  41.3 6.6 %collective-permute-done.12.across_ref = bf16[256,512]{1,0:T(8,128)(2,1)S(1)} collective-permute-done((bf16[256,512]{1,0:T(8,128)(2,1)S(1)}, bf16[256,512]{1,0:T(8,128)(2,1)S(1)}, u32[]{:S(2)}, u32[]{:S(2)}) %collective-permute-start.12) | collective-permute-done | bytes 262176 | tf_op jit(solution)/shard_map/ppermute | solution.py:125
  50.5 3.8 %collective-permute-start.14 = (bf16[256,512]{1,0:T(8,128)(2,1)S(1)}, bf16[256,512]{1,0:T(8,128)(2,1)S(1)}, u32[]{:S(2)}, u32[]{:S(2)}) collective-permute-start(bf16[256,512]{1,0:T(8,128)(2,1)S(1)} %add_convert_fusion.1), channel_id=1, source_target_pairs={{16,0},{24,8},{17,1},{25,9},{18,2},{26,10},{19,3},{27,11},{20,4},{... | collective-permute-start | bytes 786440 | tf_op jit(solution)/shard_map/ppermute | solution.py:221
  55.3 4.4 %shard_map.103 = bf16[2048,256]{1,0:T(8,128)(2,1)} custom-call(s32[4]{0:T(128)S(1)} %iota_xor_fusion.1.at_ref, bf16[2048,2048]{1,0:T(8,128)(2,1)S(1)} %shard_map.97.factor_ref, bf16[2048,256]{1,0:T(8,128)(2,1)S(1)} %copy-done.4, bf16[512,256]{1,0:T(8,128)(2,1)S(1)} %shard_map.96.forward_ref.refs_0_, bf16[512,256]{1,0:T(8,128)(2,1)S(1)} %collective-permute-done.15.refs_1_, ...), custom_call_target="tpu_custom_call" | custom-call | flops 2147483648 | bytes 11534336 | tf_op jit(solution)/shard_map/pallas_call | solution.py:22
  60.8 1.6 %collective-permute-start.18 = (bf16[256,512]{1,0:T(8,128)(2,1)S(1)}, bf16[256,512]{1,0:T(8,128)(2,1)S(1)}, u32[]{:S(2)}, u32[]{:S(2)}) collective-permute-start(bf16[256,512]{1,0:T(8,128)(2,1)S(1)} %add_convert_fusion.refs_0_), channel_id=1, source_target_pairs={{0,1},{1,0},{2,3},{3,2},{4,5},{5,4},{6,7},{7,6},{8,9},{9,8},{10,11... | collective-permute-start | bytes 786440 | tf_op jit(solution)/shard_map/ppermute | solution.py:125
  62.3 1.1 %collective-permute-start.20 = (bf16[256,512]{1,0:T(8,128)(2,1)S(1)}, bf16[256,512]{1,0:T(8,128)(2,1)S(1)}, u32[]{:S(2)}, u32[]{:S(2)}) collective-permute-start(bf16[256,512]{1,0:T(8,128)(2,1)S(1)} %add_convert_fusion.refs_0_), channel_id=1, source_target_pairs={{0,6},{1,7},{2,4},{3,5},{4,2},{5,3},{6,0},{7,1},{8,14},{9,15},{10,... | collective-permute-start | bytes 786440 | tf_op jit(solution)/shard_map/ppermute | solution.py:125
  63.4 6.1 %collective-permute-done.18.refs_1_ = bf16[256,512]{1,0:T(8,128)(2,1)S(1)} collective-permute-done((bf16[256,512]{1,0:T(8,128)(2,1)S(1)}, bf16[256,512]{1,0:T(8,128)(2,1)S(1)}, u32[]{:S(2)}, u32[]{:S(2)}) %collective-permute-start.18) | collective-permute-done | bytes 262176 | tf_op jit(solution)/shard_map/ppermute | solution.py:125
  69.5 6.8 %collective-permute-done.19.refs_2_ = bf16[256,512]{1,0:T(8,128)(2,1)S(1)} collective-permute-done((bf16[256,512]{1,0:T(8,128)(2,1)S(1)}, bf16[256,512]{1,0:T(8,128)(2,1)S(1)}, u32[]{:S(2)}, u32[]{:S(2)}) %collective-permute-start.19) | collective-permute-done | bytes 262176 | tf_op jit(solution)/shard_map/ppermute | solution.py:125
  77.5 8.0 %collective-permute-done.21.refs_3_ = bf16[256,512]{1,0:T(8,128)(2,1)S(1)} collective-permute-done((bf16[256,512]{1,0:T(8,128)(2,1)S(1)}, bf16[256,512]{1,0:T(8,128)(2,1)S(1)}, u32[]{:S(2)}, u32[]{:S(2)}) %collective-permute-start.21) | collective-permute-done | bytes 262176 | tf_op jit(solution)/shard_map/ppermute | solution.py:125
  85.5 1.3 %collective-permute-start.24 = (bf16[256,512]{1,0:T(8,128)(2,1)S(1)}, bf16[256,512]{1,0:T(8,128)(2,1)S(1)}, u32[]{:S(2)}, u32[]{:S(2)}) collective-permute-start(bf16[256,512]{1,0:T(8,128)(2,1)S(1)} %collective-permute-done.20.refs_4_), channel_id=1, source_target_pairs={{2,0},{3,1},{4,6},{5,7},{10,8},{11,9},{12,14},{13,15},{18,16},{19,... | collective-permute-start | bytes 786440 | tf_op jit(solution)/shard_map/ppermute | solution.py:246
  87.4 1.4 %collective-permute-start.25 = (bf16[256,512]{1,0:T(8,128)(2,1)S(1)}, bf16[256,512]{1,0:T(8,128)(2,1)}, u32[]{:S(2)}, u32[]{:S(2)}) collective-permute-start(bf16[256,512]{1,0:T(8,128)(2,1)S(1)} %collective-permute-done.23.refs_6_), channel_id=1, source_target_pairs={{2,3},{3,2},{4,5},{5,4},{10,11},{11,10},{12,13},{13,12},{18,19},{1... | collective-permute-start | bytes 786440 | tf_op jit(solution)/shard_map/ppermute | solution.py:248
  88.7 5.0 %collective-permute-done.24.refs_7_ = bf16[256,512]{1,0:T(8,128)(2,1)S(1)} collective-permute-done((bf16[256,512]{1,0:T(8,128)(2,1)S(1)}, bf16[256,512]{1,0:T(8,128)(2,1)S(1)}, u32[]{:S(2)}, u32[]{:S(2)}) %collective-permute-start.24) | collective-permute-done | bytes 262176 | tf_op jit(solution)/shard_map/ppermute | solution.py:246
  93.8 2.4 %collective-permute-start.26 = (bf16[256,512]{1,0:T(8,128)(2,1)S(1)}, bf16[256,512]{1,0:T(8,128)(2,1)}, u32[]{:S(2)}, u32[]{:S(2)}) collective-permute-start(bf16[256,512]{1,0:T(8,128)(2,1)S(1)} %collective-permute-done.24.refs_7_), channel_id=1, source_target_pairs={{0,1},{1,0},{6,7},{7,6},{8,9},{9,8},{14,15},{15,14},{16,17},{17,16... | collective-permute-start | bytes 786440 | tf_op jit(solution)/shard_map/ppermute | solution.py:249
  97.1 1.8 %shard_map.106.refs_0_ = f32[384,512]{1,0:T(8,128)S(1)} custom-call(s32[9]{0:T(128)S(1)} %pad_add_fusion.1.at_ref, bf16[384,2048]{1,0:T(8,128)(2,1)S(1)} %copy-done.3, bf16[256,512]{1,0:T(8,128)(2,1)S(1)} %add_convert_fusion.refs_0_, bf16[256,512]{1,0:T(8,128)(2,1)S(1)} %collective-permute-done.18.refs_1_, ...), custom_call_target="tpu_custom_call" | custom-call | flops 704643072 | bytes 4456448 | tf_op jit(solution)/shard_map/pallas_call | solution.py:22
  99.0 3.1 %collective-permute-done.26.refs_2_ = bf16[256,512]{1,0:T(8,128)(2,1)} collective-permute-done((bf16[256,512]{1,0:T(8,128)(2,1)S(1)}, bf16[256,512]{1,0:T(8,128)(2,1)}, u32[]{:S(2)}, u32[]{:S(2)}) %collective-permute-start.26) | collective-permute-done | bytes 262176 | tf_op jit(solution)/shard_map/ppermute | solution.py:249
  102.1 2.2 %shard_map.107 = f32[384,512]{1,0:T(8,128)} custom-call(s32[9]{0:T(128)S(1)} %pad_add_fusion.1.at_ref, bf16[384,2048]{1,0:T(8,128)(2,1)S(1)} %copy-done.3, f32[384,512]{1,0:T(8,128)S(1)} %shard_map.106.refs_0_, bf16[256,512]{1,0:T(8,128)(2,1)} %collective-permute-done.25.refs_1_, bf16[256,512]{1,0:T(8,128)(2,1)} %collective-permute-done.26.refs_2_), custom_call_target="tpu_custom_call" | custom-call | flops 100663296 | bytes 3670016 | tf_op jit(solution)/shard_map/pallas_call | solution.py:22
  (61 shorter events, 12.0 us)
Async XLA Ops:
  2.7 5.6 %collective-permute-start = (bf16[512,256]{1,0:T(8,128)(2,1)}, bf16[512,256]{1,0:T(8,128)(2,1)S(1)}, u32[]{:S(2)}, u32[]{:S(2)}) collective-permute-start(bf16[512,256]{1,0:T(8,128)(2,1)} %refs_0_), channel_id=1, source_target_pairs={{0,8},{8,0},{16,24},{24,16},{1,9},{9,1},{17,25},{25,17},{2,10},{10... | collective-permute-start | bytes 786440 | tf_op jit(solution)/shard_map/ppermute | solution.py:125
  2.8 11.2 %collective-permute-start.1 = (bf16[512,256]{1,0:T(8,128)(2,1)}, bf16[512,256]{1,0:T(8,128)(2,1)S(1)}, u32[]{:S(2)}, u32[]{:S(2)}) collective-permute-start(bf16[512,256]{1,0:T(8,128)(2,1)} %refs_0_), channel_id=1, source_target_pairs={{0,16},{8,24},{1,17},{9,25},{2,18},{10,26},{3,19},{11,27},{4,20},{... | collective-permute-start | bytes 786440 | tf_op jit(solution)/shard_map/ppermute | solution.py:155
  4.1 14.7 %collective-permute-start.2 = (bf16[512,256]{1,0:T(8,128)(2,1)}, bf16[512,256]{1,0:T(8,128)(2,1)S(1)}, u32[]{:S(2)}, u32[]{:S(2)}) collective-permute-start(bf16[512,256]{1,0:T(8,128)(2,1)} %refs_0_), channel_id=1, source_target_pairs={{0,24},{8,16},{1,25},{9,17},{2,26},{10,18},{3,27},{11,19},{4,28},{... | collective-permute-start | bytes 786440 | tf_op jit(solution)/shard_map/ppermute | solution.py:157
  5.4 15.2 %collective-permute-start.3 = (bf16[256,256]{1,0:T(8,128)(2,1)S(1)}, bf16[256,256]{1,0:T(8,128)(2,1)S(1)}, u32[]{:S(2)}, u32[]{:S(2)}) collective-permute-start(bf16[256,256]{1,0:T(8,128)(2,1)S(1)} %get-tuple-element.44), channel_id=1, source_target_pairs={{0,4},{1,5},{2,6},{3,7},{4,0},{5,1},{6,2},{7,3},{8,12},{9,13},{10,... | collective-permute-start | bytes 393224 | tf_op jit(solution)/shard_map/ppermute | solution.py:125
  5.8 17.6 %collective-permute-start.4 = (bf16[256,256]{1,0:T(8,128)(2,1)S(1)}, bf16[256,256]{1,0:T(8,128)(2,1)S(1)}, u32[]{:S(2)}, u32[]{:S(2)}) collective-permute-start(bf16[256,256]{1,0:T(8,128)(2,1)S(1)} %get-tuple-element.49), channel_id=1, source_target_pairs={{0,5},{1,4},{2,7},{3,6},{4,1},{5,0},{6,3},{7,2},{8,13},{9,12},{10,... | collective-permute-start | bytes 393224 | tf_op jit(solution)/shard_map/ppermute | solution.py:125
  8.4 15.0 %collective-permute-start.5 = (bf16[256,256]{1,0:T(8,128)(2,1)S(1)}, bf16[256,256]{1,0:T(8,128)(2,1)S(1)}, u32[]{:S(2)}, u32[]{:S(2)}) collective-permute-start(bf16[256,256]{1,0:T(8,128)(2,1)S(1)} %get-tuple-element.50), channel_id=1, source_target_pairs={{0,6},{1,7},{2,4},{3,5},{4,2},{5,3},{6,0},{7,1},{8,14},{9,15},{10,... | collective-permute-start | bytes 393224 | tf_op jit(solution)/shard_map/ppermute | solution.py:125
  19.8 15.6 %collective-permute-start.10 = (bf16[512,256]{1,0:T(8,128)(2,1)S(1)}, bf16[512,256]{1,0:T(8,128)(2,1)S(1)}, u32[]{:S(2)}, u32[]{:S(2)}) collective-permute-start(bf16[512,256]{1,0:T(8,128)(2,1)S(1)} %shard_map.96.forward_ref.refs_0_), channel_id=1, source_target_pairs={{0,16},{8,24},{16,0},{24,8},{1,17},{9,25},{17,1},{25,9},{2,18},{10... | collective-permute-start | bytes 786440 | tf_op jit(solution)/shard_map/ppermute | solution.py:125
  19.9 15.5 %collective-permute-start.6 = (bf16[256,256]{1,0:T(8,128)(2,1)S(1)}, bf16[256,256]{1,0:T(8,128)(2,1)S(1)}, u32[]{:S(2)}, u32[]{:S(2)}) collective-permute-start(bf16[256,256]{1,0:T(8,128)(2,1)S(1)} %get-tuple-element.51), channel_id=1, source_target_pairs={{0,7},{1,6},{2,5},{3,4},{4,3},{5,2},{6,1},{7,0},{8,15},{9,14},{10,... | collective-permute-start | bytes 393224 | tf_op jit(solution)/shard_map/ppermute | solution.py:125
  20.6 14.8 %collective-permute-start.7 = (bf16[256,256]{1,0:T(8,128)(2,1)S(1)}, bf16[256,256]{1,0:T(8,128)(2,1)S(1)}, u32[]{:S(2)}, u32[]{:S(2)}) collective-permute-start(bf16[256,256]{1,0:T(8,128)(2,1)S(1)} %get-tuple-element.52), channel_id=1, source_target_pairs={{0,1},{1,0},{2,3},{3,2},{4,5},{5,4},{6,7},{7,6},{8,9},{9,8},{10,11... | collective-permute-start | bytes 393224 | tf_op jit(solution)/shard_map/ppermute | solution.py:125
  23.4 12.1 %collective-permute-start.8 = (bf16[256,256]{1,0:T(8,128)(2,1)S(1)}, bf16[256,256]{1,0:T(8,128)(2,1)S(1)}, u32[]{:S(2)}, u32[]{:S(2)}) collective-permute-start(bf16[256,256]{1,0:T(8,128)(2,1)S(1)} %get-tuple-element.53), channel_id=1, source_target_pairs={{0,2},{1,3},{2,0},{3,1},{4,6},{5,7},{6,4},{7,5},{8,10},{9,11},{10,... | collective-permute-start | bytes 393224 | tf_op jit(solution)/shard_map/ppermute | solution.py:125
  23.4 12.0 %collective-permute-start.9 = (bf16[256,256]{1,0:T(8,128)(2,1)S(1)}, bf16[256,256]{1,0:T(8,128)(2,1)S(1)}, u32[]{:S(2)}, u32[]{:S(2)}) collective-permute-start(bf16[256,256]{1,0:T(8,128)(2,1)S(1)} %get-tuple-element.54), channel_id=1, source_target_pairs={{0,3},{1,2},{2,1},{3,0},{4,7},{5,6},{6,5},{7,4},{8,11},{9,10},{10,... | collective-permute-start | bytes 393224 | tf_op jit(solution)/shard_map/ppermute | solution.py:125
  29.7 3.4 %copy-start.2 = (bf16[2048,2048]{1,0:T(8,128)(2,1)S(1)}, bf16[2048,2048]{1,0:T(8,128)(2,1)}, u32[]{:S(2)}) copy-start(bf16[2048,2048]{1,0:T(8,128)(2,1)} %factor_ref.1) | copy-start | bytes 25165828
  36.8 2.0 %collective-permute-start.11 = (bf16[2,256,512]{2,1,0:T(8,128)(2,1)S(1)}, bf16[2,256,512]{2,1,0:T(8,128)(2,1)S(1)}, u32[]{:S(2)}, u32[]{:S(2)}) collective-permute-start(bf16[2,256,512]{2,1,0:T(8,128)(2,1)S(1)} %shard_map.100), channel_id=1, source_target_pairs={{0,8},{8,0},{16,24},{24,16},{1,9},{9,1},{17,25},{25,17},{2,10},{10... | collective-permute-start | bytes 1572872 | tf_op jit(solution)/shard_map/ppermute | solution.py:125
  36.9 11.1 %copy-start.1 = (bf16[512,2048]{1,0:T(8,128)(2,1)S(1)}, bf16[512,2048]{1,0:T(8,128)(2,1)}, u32[]{:S(2)}) copy-start(bf16[512,2048]{1,0:T(8,128)(2,1)} %inverse_ref.11) | copy-start | bytes 6291460
  38.8 9.1 %collective-permute-start.12 = (bf16[256,512]{1,0:T(8,128)(2,1)S(1)}, bf16[256,512]{1,0:T(8,128)(2,1)S(1)}, u32[]{:S(2)}, u32[]{:S(2)}) collective-permute-start(bf16[256,512]{1,0:T(8,128)(2,1)S(1)} %fusion.1), channel_id=1, source_target_pairs={{0,16},{8,24},{16,0},{24,8},{1,17},{9,25},{17,1},{25,9},{2,18},{10... | collective-permute-start | bytes 786440 | tf_op jit(solution)/shard_map/ppermute | solution.py:125
  48.9 1.6 %collective-permute-start.13 = (bf16[256,512]{1,0:T(8,128)(2,1)S(1)}, bf16[256,512]{1,0:T(8,128)(2,1)S(1)}, u32[]{:S(2)}, u32[]{:S(2)}) collective-permute-start(bf16[256,512]{1,0:T(8,128)(2,1)S(1)} %get-tuple-element.57), channel_id=1, source_target_pairs={{0,8},{8,0},{16,24},{24,16},{1,9},{9,1},{17,25},{25,17},{2,10},{10... | collective-permute-start | bytes 786440 | tf_op jit(solution)/shard_map/ppermute | solution.py:125
  48.9 6.4 %collective-permute-start.15 = (bf16[512,256]{1,0:T(8,128)(2,1)S(1)}, bf16[512,256]{1,0:T(8,128)(2,1)S(1)}, u32[]{:S(2)}, u32[]{:S(2)}) collective-permute-start(bf16[512,256]{1,0:T(8,128)(2,1)S(1)} %shard_map.96.forward_ref.refs_0_), channel_id=1, source_target_pairs={{0,8},{8,0},{16,24},{24,16},{1,9},{9,1},{17,25},{25,17},{2,10},{10... | collective-permute-start | bytes 786440 | tf_op jit(solution)/shard_map/ppermute | solution.py:125
  49.4 5.9 %collective-permute-start.16 = (bf16[512,256]{1,0:T(8,128)(2,1)S(1)}, bf16[512,256]{1,0:T(8,128)(2,1)S(1)}, u32[]{:S(2)}, u32[]{:S(2)}) collective-permute-start(bf16[512,256]{1,0:T(8,128)(2,1)S(1)} %collective-permute-done.10.refs_2_), channel_id=1, source_target_pairs={{0,8},{8,0},{16,24},{24,16},{1,9},{9,1},{17,25},{25,17},{2,10},{10... | collective-permute-start | bytes 786440 | tf_op jit(solution)/shard_map/ppermute | solution.py:125
  50.4 5.0 %copy-start.4 = (bf16[2048,256]{1,0:T(8,128)(2,1)S(1)}, bf16[2048,256]{1,0:T(8,128)(2,1)}, u32[]{:S(2)}) copy-start(bf16[2048,256]{1,0:T(8,128)(2,1)} %rhs_ref.1) | copy-start | bytes 3145732
  50.5 10.1 %collective-permute-start.14 = (bf16[256,512]{1,0:T(8,128)(2,1)S(1)}, bf16[256,512]{1,0:T(8,128)(2,1)S(1)}, u32[]{:S(2)}, u32[]{:S(2)}) collective-permute-start(bf16[256,512]{1,0:T(8,128)(2,1)S(1)} %add_convert_fusion.1), channel_id=1, source_target_pairs={{16,0},{24,8},{17,1},{25,9},{18,2},{26,10},{19,3},{27,11},{20,4},{... | collective-permute-start | bytes 786440 | tf_op jit(solution)/shard_map/ppermute | solution.py:221
  55.2 5.4 %collective-permute-start.17 = (bf16[256,512]{1,0:T(8,128)(2,1)S(1)}, bf16[256,512]{1,0:T(8,128)(2,1)S(1)}, u32[]{:S(2)}, u32[]{:S(2)}) collective-permute-start(bf16[256,512]{1,0:T(8,128)(2,1)S(1)} %shard_map.105), channel_id=1, source_target_pairs={{0,8},{8,0},{16,24},{24,16},{1,9},{9,1},{17,25},{25,17},{2,10},{10... | collective-permute-start | bytes 786440 | tf_op jit(solution)/shard_map/ppermute | solution.py:125
  59.8 36.4 %copy-start.7 = (s32[8]{0:T(128)S(1)}, s32[8]{0:T(128)}, u32[]{:S(2)}) copy-start(s32[8]{0:T(128)} %constant.14.clone) | copy-start | bytes 100
  59.8 37.3 %copy-start.3 = (bf16[384,2048]{1,0:T(8,128)(2,1)S(1)}, bf16[384,2048]{1,0:T(8,128)(2,1)}, u32[]{:S(2)}) copy-start(bf16[384,2048]{1,0:T(8,128)(2,1)} %axle_ref.3) | copy-start | bytes 4718596
  60.8 8.7 %collective-permute-start.18 = (bf16[256,512]{1,0:T(8,128)(2,1)S(1)}, bf16[256,512]{1,0:T(8,128)(2,1)S(1)}, u32[]{:S(2)}, u32[]{:S(2)}) collective-permute-start(bf16[256,512]{1,0:T(8,128)(2,1)S(1)} %add_convert_fusion.refs_0_), channel_id=1, source_target_pairs={{0,1},{1,0},{2,3},{3,2},{4,5},{5,4},{6,7},{7,6},{8,9},{9,8},{10,11... | collective-permute-start | bytes 786440 | tf_op jit(solution)/shard_map/ppermute | solution.py:125
  62.3 14.0 %collective-permute-start.19 = (bf16[256,512]{1,0:T(8,128)(2,1)S(1)}, bf16[256,512]{1,0:T(8,128)(2,1)S(1)}, u32[]{:S(2)}, u32[]{:S(2)}) collective-permute-start(bf16[256,512]{1,0:T(8,128)(2,1)S(1)} %add_convert_fusion.refs_0_), channel_id=1, source_target_pairs={{0,2},{1,3},{2,0},{3,1},{4,6},{5,7},{6,4},{7,5},{8,10},{9,11},{10,... | collective-permute-start | bytes 786440 | tf_op jit(solution)/shard_map/ppermute | solution.py:125
  62.3 15.2 %collective-permute-start.20 = (bf16[256,512]{1,0:T(8,128)(2,1)S(1)}, bf16[256,512]{1,0:T(8,128)(2,1)S(1)}, u32[]{:S(2)}, u32[]{:S(2)}) collective-permute-start(bf16[256,512]{1,0:T(8,128)(2,1)S(1)} %add_convert_fusion.refs_0_), channel_id=1, source_target_pairs={{0,6},{1,7},{2,4},{3,5},{4,2},{5,3},{6,0},{7,1},{8,14},{9,15},{10,... | collective-permute-start | bytes 786440 | tf_op jit(solution)/shard_map/ppermute | solution.py:125
  76.3 9.2 %collective-permute-start.21 = (bf16[256,512]{1,0:T(8,128)(2,1)S(1)}, bf16[256,512]{1,0:T(8,128)(2,1)S(1)}, u32[]{:S(2)}, u32[]{:S(2)}) collective-permute-start(bf16[256,512]{1,0:T(8,128)(2,1)S(1)} %collective-permute-done.19.refs_2_), channel_id=1, source_target_pairs={{0,1},{1,0},{2,3},{3,2},{4,5},{5,4},{6,7},{7,6},{8,9},{9,8},{10,11... | collective-permute-start | bytes 786440 | tf_op jit(solution)/shard_map/ppermute | solution.py:125
  76.9 10.5 %collective-permute-start.23 = (bf16[256,512]{1,0:T(8,128)(2,1)S(1)}, bf16[256,512]{1,0:T(8,128)(2,1)S(1)}, u32[]{:S(2)}, u32[]{:S(2)}) collective-permute-start(bf16[256,512]{1,0:T(8,128)(2,1)S(1)} %collective-permute-done.19.refs_2_), channel_id=1, source_target_pairs={{2,4},{3,5},{4,2},{5,3},{10,12},{11,13},{12,10},{13,11},{18,20},{1... | collective-permute-start | bytes 786440 | tf_op jit(solution)/shard_map/ppermute | solution.py:245
  85.5 8.3 %collective-permute-start.24 = (bf16[256,512]{1,0:T(8,128)(2,1)S(1)}, bf16[256,512]{1,0:T(8,128)(2,1)S(1)}, u32[]{:S(2)}, u32[]{:S(2)}) collective-permute-start(bf16[256,512]{1,0:T(8,128)(2,1)S(1)} %collective-permute-done.20.refs_4_), channel_id=1, source_target_pairs={{2,0},{3,1},{4,6},{5,7},{10,8},{11,9},{12,14},{13,15},{18,16},{19,... | collective-permute-start | bytes 786440 | tf_op jit(solution)/shard_map/ppermute | solution.py:246
  86.8 10.3 %collective-permute-start.22 = (bf16[256,512]{1,0:T(8,128)(2,1)S(1)}, bf16[256,512]{1,0:T(8,128)(2,1)}, u32[]{:S(2)}, u32[]{:S(2)}) collective-permute-start(bf16[256,512]{1,0:T(8,128)(2,1)S(1)} %collective-permute-done.20.refs_4_), channel_id=1, source_target_pairs={{0,1},{1,0},{2,3},{3,2},{4,5},{5,4},{6,7},{7,6},{8,9},{9,8},{10,11... | collective-permute-start | bytes 786440 | tf_op jit(solution)/shard_map/ppermute | solution.py:125
  87.4 11.6 %collective-permute-start.25 = (bf16[256,512]{1,0:T(8,128)(2,1)S(1)}, bf16[256,512]{1,0:T(8,128)(2,1)}, u32[]{:S(2)}, u32[]{:S(2)}) collective-permute-start(bf16[256,512]{1,0:T(8,128)(2,1)S(1)} %collective-permute-done.23.refs_6_), channel_id=1, source_target_pairs={{2,3},{3,2},{4,5},{5,4},{10,11},{11,10},{12,13},{13,12},{18,19},{1... | collective-permute-start | bytes 786440 | tf_op jit(solution)/shard_map/ppermute | solution.py:248
  93.8 8.4 %collective-permute-start.26 = (bf16[256,512]{1,0:T(8,128)(2,1)S(1)}, bf16[256,512]{1,0:T(8,128)(2,1)}, u32[]{:S(2)}, u32[]{:S(2)}) collective-permute-start(bf16[256,512]{1,0:T(8,128)(2,1)S(1)} %collective-permute-done.24.refs_7_), channel_id=1, source_target_pairs={{0,1},{1,0},{6,7},{7,6},{8,9},{9,8},{14,15},{15,14},{16,17},{17,16... | collective-permute-start | bytes 786440 | tf_op jit(solution)/shard_map/ppermute | solution.py:249
  (3 other events, 3.8 us)

commit v10 on v9

--- a/solution.py
+++ b/solution.py
@@ -140,8 +140,6 @@
     *pieces, b_panel = lax.optimization_barrier((*pieces, b_panel))
     early = [pieces[0]] + [by_xor(pieces[k], "load", loads, k) for k in (4, 5, 6)]
     late = [by_xor(pieces[7], "load", loads, 7)]
-    early[1], *pieces[1:4] = lax.optimization_barrier((early[1], *pieces[1:4]))
-    late += [by_xor(pieces[k], "load", loads, k) for k in (1, 2, 3)]
     held = pl.pallas_call(
         hold_kernel,
         out_shape=jax.ShapeDtypeStruct((updates, panel), BF16),
@@ -151,6 +149,9 @@
         compiler_params=pltpu.CompilerParams(vmem_limit_bytes=16 * 2**20),
         cost_estimate=pl.CostEstimate(flops=0, bytes_accessed=2 * updates * panel, transcendentals=0),
     )(update_factor)
+    early[1], *pieces[1:4] = lax.optimization_barrier((early[1], *pieces[1:4]))
+    pieces[3], held = lax.optimization_barrier((pieces[3], held))
+    late += [by_xor(pieces[k], "load", loads, k) for k in (1, 2, 3)]
 
     b_across = lax.ppermute(b_panel, "factor", [(0, 2), (1, 3)])
     b_core = by_xor(b_panel, "factor", factors, 1)

time: 105 us -> 101 us (0.962)
  the two profiles are of different devices: /device:TPU:30 before, /device:TPU:0 now
where the time goes in v10:
time: 101 us; the launch traced here: 100 us
  starting transfers between devices  41.8 us (41%)
  waiting for transfers between devices  29.4 us (29%)
  Pallas kernels  19.6 us (19%)
  local copies, waits for them, and re-layouts  8 us (8%)
    ppermute x20, starting transfers between devices, by_xor(): return lax.ppermute(value, axis, [(i, i ^ bits) for i in range(size)])  27.3 us
    ppermute x20, waiting for transfers between devices, by_xor(): return lax.ppermute(value, axis, [(i, i ^ bits) for i in range(size)])  21.6 us
    pallas_call x13, Pallas kernels, call(): pl.pallas_call(kernel, out_shape=shapes, in_specs=[SMEM] * len(at) + [VME...  19.1 us
    unnamed x17, local copies, waits for them, and re-layouts  8 us
    ppermute x1, starting transfers between devices, small_slice(): b_across = lax.ppermute(b_panel, 'factor', [(0, 2), (1, 3)])  4.45 us
    ppermute x1, starting transfers between devices, small_slice(): d_x = lax.ppermute(d, 'load', [(i, i ^ 1) for i in (0, 1, 6, 7)])  3.92 us
    ppermute x1, waiting for transfers between devices, small_slice(): d = lax.ppermute(b, 'load', [(i, i ^ 2) for i in middle])  3.51 us
    ppermute x1, waiting for transfers between devices, small_slice(): from_across = lax.ppermute(send, 'factor', [(2, 0), (3, 1)])  2.6 us
  transfers between devices with their start and end apart: 27, of which 11 were waited for; matrix products, arithmetic and copies ran while one was open for 1% of the time, Pallas kernels for 14%

profile of v10, /device:TPU:0, one launch (start us, length us, event | category | flops | bytes accessed | tf_op | source)
XLA Modules:
  0.0 100.1 jit_solution(10414802782974864353)
XLA Ops:
  0.7 1.2 %copy-done.5 = bf16[256,2048]{1,0:T(8,128)(2,1)S(1)} copy-done((bf16[256,2048]{1,0:T(8,128)(2,1)S(1)}, bf16[256,2048]{1,0:T(8,128)(2,1)}, u32[]{:S(2)}) %copy-start.5) | copy-done | bytes 1048600
  3.3 4.5 %collective-permute-start.1 = (bf16[512,256]{1,0:T(8,128)(2,1)}, bf16[512,256]{1,0:T(8,128)(2,1)S(1)}, u32[]{:S(2)}, u32[]{:S(2)}) collective-permute-start(bf16[512,256]{1,0:T(8,128)(2,1)} %refs_0_), channel_id=1, source_target_pairs={{0,16},{8,24},{1,17},{9,25},{2,18},{10,26},{3,19},{11,27},{4,20},{... | collective-permute-start | bytes 786440 | tf_op jit(solution)/shard_map/ppermute | solution.py:156
  7.7 1.4 %collective-permute-start.2 = (bf16[512,256]{1,0:T(8,128)(2,1)}, bf16[512,256]{1,0:T(8,128)(2,1)S(1)}, u32[]{:S(2)}, u32[]{:S(2)}) collective-permute-start(bf16[512,256]{1,0:T(8,128)(2,1)} %refs_0_), channel_id=1, source_target_pairs={{0,24},{8,16},{1,25},{9,17},{2,26},{10,18},{3,27},{11,19},{4,28},{... | collective-permute-start | bytes 786440 | tf_op jit(solution)/shard_map/ppermute | solution.py:158
  9.1 2.7 %collective-permute-start.3 = (bf16[256,256]{1,0:T(8,128)(2,1)S(1)}, bf16[256,256]{1,0:T(8,128)(2,1)S(1)}, u32[]{:S(2)}, u32[]{:S(2)}) collective-permute-start(bf16[256,256]{1,0:T(8,128)(2,1)S(1)} %get-tuple-element.45), channel_id=1, source_target_pairs={{0,4},{1,5},{2,6},{3,7},{4,0},{5,1},{6,2},{7,3},{8,12},{9,13},{10,... | collective-permute-start | bytes 393224 | tf_op jit(solution)/shard_map/ppermute | solution.py:125
  11.8 1.3 %collective-permute-start.4 = (bf16[256,256]{1,0:T(8,128)(2,1)S(1)}, bf16[256,256]{1,0:T(8,128)(2,1)S(1)}, u32[]{:S(2)}, u32[]{:S(2)}) collective-permute-start(bf16[256,256]{1,0:T(8,128)(2,1)S(1)} %get-tuple-element.53), channel_id=1, source_target_pairs={{0,5},{1,4},{2,7},{3,6},{4,1},{5,0},{6,3},{7,2},{8,13},{9,12},{10,... | collective-permute-start | bytes 393224 | tf_op jit(solution)/shard_map/ppermute | solution.py:125
  13.0 3.6 %collective-permute-start.5 = (bf16[256,256]{1,0:T(8,128)(2,1)S(1)}, bf16[256,256]{1,0:T(8,128)(2,1)S(1)}, u32[]{:S(2)}, u32[]{:S(2)}) collective-permute-start(bf16[256,256]{1,0:T(8,128)(2,1)S(1)} %get-tuple-element.54), channel_id=1, source_target_pairs={{0,6},{1,7},{2,4},{3,5},{4,2},{5,3},{6,0},{7,1},{8,14},{9,15},{10,... | collective-permute-start | bytes 393224 | tf_op jit(solution)/shard_map/ppermute | solution.py:125
  16.6 1.6 %copy-done = bf16[512,2048]{1,0:T(8,128)(2,1)S(1)} copy-done((bf16[512,2048]{1,0:T(8,128)(2,1)S(1)}, bf16[512,2048]{1,0:T(8,128)(2,1)}, u32[]{:S(2)}) %copy-start) | copy-done | bytes 2097176
  21.2 1.7 %collective-permute-start.10 = (bf16[512,256]{1,0:T(8,128)(2,1)S(1)}, bf16[512,256]{1,0:T(8,128)(2,1)S(1)}, u32[]{:S(2)}, u32[]{:S(2)}) collective-permute-start(bf16[512,256]{1,0:T(8,128)(2,1)S(1)} %shard_map.96.forward_ref.refs_0_), channel_id=1, source_target_pairs={{0,16},{8,24},{16,0},{24,8},{1,17},{9,25},{17,1},{25,9},{2,18},{10... | collective-permute-start | bytes 786440 | tf_op jit(solution)/shard_map/ppermute | solution.py:125
  22.9 4.5 %collective-permute-start.6 = (bf16[256,256]{1,0:T(8,128)(2,1)S(1)}, bf16[256,256]{1,0:T(8,128)(2,1)S(1)}, u32[]{:S(2)}, u32[]{:S(2)}) collective-permute-start(bf16[256,256]{1,0:T(8,128)(2,1)S(1)} %get-tuple-element.55), channel_id=1, source_target_pairs={{0,7},{1,6},{2,5},{3,4},{4,3},{5,2},{6,1},{7,0},{8,15},{9,14},{10,... | collective-permute-start | bytes 393224 | tf_op jit(solution)/shard_map/ppermute | solution.py:125
  27.4 3.4 %copy-done.2 = bf16[2048,2048]{1,0:T(8,128)(2,1)S(1)} copy-done((bf16[2048,2048]{1,0:T(8,128)(2,1)S(1)}, bf16[2048,2048]{1,0:T(8,128)(2,1)}, u32[]{:S(2)}) %copy-start.2) | copy-done | bytes 8388632
  32.0 2.9 %collective-permute-start.9 = (bf16[256,256]{1,0:T(8,128)(2,1)S(1)}, bf16[256,256]{1,0:T(8,128)(2,1)S(1)}, u32[]{:S(2)}, u32[]{:S(2)}) collective-permute-start(bf16[256,256]{1,0:T(8,128)(2,1)S(1)} %get-tuple-element.58), channel_id=1, source_target_pairs={{0,3},{1,2},{2,1},{3,0},{4,7},{5,6},{6,5},{7,4},{8,11},{9,10},{10,... | collective-permute-start | bytes 393224 | tf_op jit(solution)/shard_map/ppermute | solution.py:125
  35.0 1.8 %shard_map.98.begun_ref = f32[4,256,512]{2,1,0:T(8,128)S(1)} custom-call(s32[12]{0:T(128)S(1)} %pad_add_fusion.at_ref, bf16[2048,2048]{1,0:T(8,128)(2,1)S(1)} %shard_map.97.factor_ref, bf16[256,256]{1,0:T(8,128)(2,1)S(1)} %get-tuple-element.51.refs_0_, bf16[256,256]{1,0:T(8,128)(2,1)S(1)} %collective-permute-done.3.refs_1_, ...), custom_call_target="tpu_custom_call" | custom-call | flops 1073741824 | bytes 11010048 | tf_op jit(solution)/shard_map/pallas_call | solution.py:22
  36.8 4.0 %collective-permute-done.9.refs_3_ = bf16[256,256]{1,0:T(8,128)(2,1)S(1)} collective-permute-done((bf16[256,256]{1,0:T(8,128)(2,1)S(1)}, bf16[256,256]{1,0:T(8,128)(2,1)S(1)}, u32[]{:S(2)}, u32[]{:S(2)}) %collective-permute-start.9) | collective-permute-done | bytes 131104 | tf_op jit(solution)/shard_map/ppermute | solution.py:125
  40.8 1.3 %shard_map.100 = bf16[2,256,512]{2,1,0:T(8,128)(2,1)S(1)} custom-call(s32[12]{0:T(128)S(1)} %pad_add_fusion.at_ref, bf16[2048,2048]{1,0:T(8,128)(2,1)S(1)} %shard_map.97.factor_ref, f32[4,256,512]{2,1,0:T(8,128)S(1)} %shard_map.98.begun_ref, bf16[256,256]{1,0:T(8,128)(2,1)S(1)} %collective-permute-done.6.refs_0_, ...), custom_call_target="tpu_custom_call" | custom-call | flops 536870912 | bytes 11534336 | tf_op jit(solution)/shard_map/pallas_call | solution.py:22
  42.2 1.3 %shard_map.99.kept_ref = f32[2,256,512]{2,1,0:T(8,128)S(1)} custom-call(s32[12]{0:T(128)S(1)} %pad_add_fusion.at_ref, bf16[2048,2048]{1,0:T(8,128)(2,1)S(1)} %shard_map.97.factor_ref, f32[4,256,512]{2,1,0:T(8,128)S(1)} %shard_map.98.begun_ref, bf16[256,256]{1,0:T(8,128)(2,1)S(1)} %collective-permute-done.6.refs_0_, ...), custom_call_target="tpu_custom_call" | custom-call | flops 536870912 | bytes 12058624 | tf_op jit(solution)/shard_map/pallas_call | solution.py:22
  44.6 8.0 %collective-permute-done.12.across_ref = bf16[256,512]{1,0:T(8,128)(2,1)S(1)} collective-permute-done((bf16[256,512]{1,0:T(8,128)(2,1)S(1)}, bf16[256,512]{1,0:T(8,128)(2,1)S(1)}, u32[]{:S(2)}, u32[]{:S(2)}) %collective-permute-start.12) | collective-permute-done | bytes 262176 | tf_op jit(solution)/shard_map/ppermute | solution.py:125
  55.2 1.4 %collective-permute-start.14 = (bf16[256,512]{1,0:T(8,128)(2,1)S(1)}, bf16[256,512]{1,0:T(8,128)(2,1)S(1)}, u32[]{:S(2)}, u32[]{:S(2)}) collective-permute-start(bf16[256,512]{1,0:T(8,128)(2,1)S(1)} %add_convert_fusion.1), channel_id=1, source_target_pairs={{16,0},{24,8},{17,1},{25,9},{18,2},{26,10},{19,3},{27,11},{20,4},{... | collective-permute-start | bytes 786440 | tf_op jit(solution)/shard_map/ppermute | solution.py:222
  57.9 4.4 %shard_map.103 = bf16[2048,256]{1,0:T(8,128)(2,1)} custom-call(s32[4]{0:T(128)S(1)} %iota_xor_fusion.1.at_ref, bf16[2048,2048]{1,0:T(8,128)(2,1)S(1)} %shard_map.97.factor_ref, bf16[2048,256]{1,0:T(8,128)(2,1)S(1)} %copy-done.4, bf16[512,256]{1,0:T(8,128)(2,1)S(1)} %shard_map.96.forward_ref.refs_0_, bf16[512,256]{1,0:T(8,128)(2,1)S(1)} %collective-permute-done.15.refs_1_, ...), custom_call_target="tpu_custom_call" | custom-call | flops 2147483648 | bytes 11534336 | tf_op jit(solution)/shard_map/pallas_call | solution.py:22
  63.2 2.6 %collective-permute-done.14 = bf16[256,512]{1,0:T(8,128)(2,1)S(1)} collective-permute-done((bf16[256,512]{1,0:T(8,128)(2,1)S(1)}, bf16[256,512]{1,0:T(8,128)(2,1)S(1)}, u32[]{:S(2)}, u32[]{:S(2)}) %collective-permute-start.14) | collective-permute-done | bytes 262176 | tf_op jit(solution)/shard_map/ppermute | solution.py:222
  67.3 2.2 %collective-permute-start.20 = (bf16[256,512]{1,0:T(8,128)(2,1)S(1)}, bf16[256,512]{1,0:T(8,128)(2,1)S(1)}, u32[]{:S(2)}, u32[]{:S(2)}) collective-permute-start(bf16[256,512]{1,0:T(8,128)(2,1)S(1)} %add_convert_fusion.refs_0_), channel_id=1, source_target_pairs={{0,6},{1,7},{2,4},{3,5},{4,2},{5,3},{6,0},{7,1},{8,14},{9,15},{10,... | collective-permute-start | bytes 786440 | tf_op jit(solution)/shard_map/ppermute | solution.py:125
  69.5 4.2 %collective-permute-done.18.refs_1_ = bf16[256,512]{1,0:T(8,128)(2,1)S(1)} collective-permute-done((bf16[256,512]{1,0:T(8,128)(2,1)S(1)}, bf16[256,512]{1,0:T(8,128)(2,1)S(1)}, u32[]{:S(2)}, u32[]{:S(2)}) %collective-permute-start.18) | collective-permute-done | bytes 262176 | tf_op jit(solution)/shard_map/ppermute | solution.py:125
  73.7 1.1 %collective-permute-done.19.refs_2_ = bf16[256,512]{1,0:T(8,128)(2,1)S(1)} collective-permute-done((bf16[256,512]{1,0:T(8,128)(2,1)S(1)}, bf16[256,512]{1,0:T(8,128)(2,1)S(1)}, u32[]{:S(2)}, u32[]{:S(2)}) %collective-permute-start.19) | collective-permute-done | bytes 262176 | tf_op jit(solution)/shard_map/ppermute | solution.py:125
  74.7 2.2 %collective-permute-start.21 = (bf16[256,512]{1,0:T(8,128)(2,1)S(1)}, bf16[256,512]{1,0:T(8,128)(2,1)S(1)}, u32[]{:S(2)}, u32[]{:S(2)}) collective-permute-start(bf16[256,512]{1,0:T(8,128)(2,1)S(1)} %collective-permute-done.19.refs_2_), channel_id=1, source_target_pairs={{0,1},{1,0},{2,3},{3,2},{4,5},{5,4},{6,7},{7,6},{8,9},{9,8},{10,11... | collective-permute-start | bytes 786440 | tf_op jit(solution)/shard_map/ppermute | solution.py:125
  77.6 3.0 %collective-permute-done.20.refs_4_ = bf16[256,512]{1,0:T(8,128)(2,1)S(1)} collective-permute-done((bf16[256,512]{1,0:T(8,128)(2,1)S(1)}, bf16[256,512]{1,0:T(8,128)(2,1)S(1)}, u32[]{:S(2)}, u32[]{:S(2)}) %collective-permute-start.20) | collective-permute-done | bytes 262176 | tf_op jit(solution)/shard_map/ppermute | solution.py:125
  81.3 1.3 %collective-permute-start.24 = (bf16[256,512]{1,0:T(8,128)(2,1)S(1)}, bf16[256,512]{1,0:T(8,128)(2,1)S(1)}, u32[]{:S(2)}, u32[]{:S(2)}) collective-permute-start(bf16[256,512]{1,0:T(8,128)(2,1)S(1)} %collective-permute-done.20.refs_4_), channel_id=1, source_target_pairs={{2,0},{3,1},{4,6},{5,7},{10,8},{11,9},{12,14},{13,15},{18,16},{19,... | collective-permute-start | bytes 786440 | tf_op jit(solution)/shard_map/ppermute | solution.py:247
  82.6 2.1 %collective-permute-start.22 = (bf16[256,512]{1,0:T(8,128)(2,1)S(1)}, bf16[256,512]{1,0:T(8,128)(2,1)}, u32[]{:S(2)}, u32[]{:S(2)}) collective-permute-start(bf16[256,512]{1,0:T(8,128)(2,1)S(1)} %collective-permute-done.20.refs_4_), channel_id=1, source_target_pairs={{0,1},{1,0},{2,3},{3,2},{4,5},{5,4},{6,7},{7,6},{8,9},{9,8},{10,11... | collective-permute-start | bytes 786440 | tf_op jit(solution)/shard_map/ppermute | solution.py:125
  84.7 1.4 %collective-permute-start.25 = (bf16[256,512]{1,0:T(8,128)(2,1)S(1)}, bf16[256,512]{1,0:T(8,128)(2,1)}, u32[]{:S(2)}, u32[]{:S(2)}) collective-permute-start(bf16[256,512]{1,0:T(8,128)(2,1)S(1)} %collective-permute-done.23.refs_6_), channel_id=1, source_target_pairs={{2,3},{3,2},{4,5},{5,4},{10,11},{11,10},{12,13},{13,12},{18,19},{1... | collective-permute-start | bytes 786440 | tf_op jit(solution)/shard_map/ppermute | solution.py:249
  86.1 3.5 %collective-permute-done.24.refs_7_ = bf16[256,512]{1,0:T(8,128)(2,1)S(1)} collective-permute-done((bf16[256,512]{1,0:T(8,128)(2,1)S(1)}, bf16[256,512]{1,0:T(8,128)(2,1)S(1)}, u32[]{:S(2)}, u32[]{:S(2)}) %collective-permute-start.24) | collective-permute-done | bytes 262176 | tf_op jit(solution)/shard_map/ppermute | solution.py:247
  89.6 3.9 %collective-permute-start.26 = (bf16[256,512]{1,0:T(8,128)(2,1)S(1)}, bf16[256,512]{1,0:T(8,128)(2,1)}, u32[]{:S(2)}, u32[]{:S(2)}) collective-permute-start(bf16[256,512]{1,0:T(8,128)(2,1)S(1)} %collective-permute-done.24.refs_7_), channel_id=1, source_target_pairs={{0,1},{1,0},{6,7},{7,6},{8,9},{9,8},{14,15},{15,14},{16,17},{17,16... | collective-permute-start | bytes 786440 | tf_op jit(solution)/shard_map/ppermute | solution.py:250
  94.4 1.8 %shard_map.106.refs_0_ = f32[384,512]{1,0:T(8,128)S(1)} custom-call(s32[9]{0:T(128)S(1)} %pad_add_fusion.1.at_ref, bf16[384,2048]{1,0:T(8,128)(2,1)S(1)} %copy-done.3, bf16[256,512]{1,0:T(8,128)(2,1)S(1)} %add_convert_fusion.refs_0_, bf16[256,512]{1,0:T(8,128)(2,1)S(1)} %collective-permute-done.18.refs_1_, ...), custom_call_target="tpu_custom_call" | custom-call | flops 704643072 | bytes 4456448 | tf_op jit(solution)/shard_map/pallas_call | solution.py:22
  96.3 1.6 %collective-permute-done.26.refs_2_ = bf16[256,512]{1,0:T(8,128)(2,1)} collective-permute-done((bf16[256,512]{1,0:T(8,128)(2,1)S(1)}, bf16[256,512]{1,0:T(8,128)(2,1)}, u32[]{:S(2)}, u32[]{:S(2)}) %collective-permute-start.26) | collective-permute-done | bytes 262176 | tf_op jit(solution)/shard_map/ppermute | solution.py:250
  97.9 2.2 %shard_map.107 = f32[384,512]{1,0:T(8,128)} custom-call(s32[9]{0:T(128)S(1)} %pad_add_fusion.1.at_ref, bf16[384,2048]{1,0:T(8,128)(2,1)S(1)} %copy-done.3, f32[384,512]{1,0:T(8,128)S(1)} %shard_map.106.refs_0_, bf16[256,512]{1,0:T(8,128)(2,1)} %collective-permute-done.25.refs_1_, bf16[256,512]{1,0:T(8,128)(2,1)} %collective-permute-done.26.refs_2_), custom_call_target="tpu_custom_call" | custom-call | flops 100663296 | bytes 3670016 | tf_op jit(solution)/shard_map/pallas_call | solution.py:22
  (61 shorter events, 15.2 us)
Async XLA Ops:
  2.7 10.3 %collective-permute-start = (bf16[512,256]{1,0:T(8,128)(2,1)}, bf16[512,256]{1,0:T(8,128)(2,1)S(1)}, u32[]{:S(2)}, u32[]{:S(2)}) collective-permute-start(bf16[512,256]{1,0:T(8,128)(2,1)} %refs_0_), channel_id=1, source_target_pairs={{0,8},{8,0},{16,24},{24,16},{1,9},{9,1},{17,25},{25,17},{2,10},{10... | collective-permute-start | bytes 786440 | tf_op jit(solution)/shard_map/ppermute | solution.py:125
  3.3 16.9 %collective-permute-start.1 = (bf16[512,256]{1,0:T(8,128)(2,1)}, bf16[512,256]{1,0:T(8,128)(2,1)S(1)}, u32[]{:S(2)}, u32[]{:S(2)}) collective-permute-start(bf16[512,256]{1,0:T(8,128)(2,1)} %refs_0_), channel_id=1, source_target_pairs={{0,16},{8,24},{1,17},{9,25},{2,18},{10,26},{3,19},{11,27},{4,20},{... | collective-permute-start | bytes 786440 | tf_op jit(solution)/shard_map/ppermute | solution.py:156
  7.7 12.5 %collective-permute-start.2 = (bf16[512,256]{1,0:T(8,128)(2,1)}, bf16[512,256]{1,0:T(8,128)(2,1)S(1)}, u32[]{:S(2)}, u32[]{:S(2)}) collective-permute-start(bf16[512,256]{1,0:T(8,128)(2,1)} %refs_0_), channel_id=1, source_target_pairs={{0,24},{8,16},{1,25},{9,17},{2,26},{10,18},{3,27},{11,19},{4,28},{... | collective-permute-start | bytes 786440 | tf_op jit(solution)/shard_map/ppermute | solution.py:158
  9.1 22.2 %collective-permute-start.3 = (bf16[256,256]{1,0:T(8,128)(2,1)S(1)}, bf16[256,256]{1,0:T(8,128)(2,1)S(1)}, u32[]{:S(2)}, u32[]{:S(2)}) collective-permute-start(bf16[256,256]{1,0:T(8,128)(2,1)S(1)} %get-tuple-element.45), channel_id=1, source_target_pairs={{0,4},{1,5},{2,6},{3,7},{4,0},{5,1},{6,2},{7,3},{8,12},{9,13},{10,... | collective-permute-start | bytes 393224 | tf_op jit(solution)/shard_map/ppermute | solution.py:125
  11.8 20.2 %collective-permute-start.4 = (bf16[256,256]{1,0:T(8,128)(2,1)S(1)}, bf16[256,256]{1,0:T(8,128)(2,1)S(1)}, u32[]{:S(2)}, u32[]{:S(2)}) collective-permute-start(bf16[256,256]{1,0:T(8,128)(2,1)S(1)} %get-tuple-element.53), channel_id=1, source_target_pairs={{0,5},{1,4},{2,7},{3,6},{4,1},{5,0},{6,3},{7,2},{8,13},{9,12},{10,... | collective-permute-start | bytes 393224 | tf_op jit(solution)/shard_map/ppermute | solution.py:125
  13.0 18.9 %collective-permute-start.5 = (bf16[256,256]{1,0:T(8,128)(2,1)S(1)}, bf16[256,256]{1,0:T(8,128)(2,1)S(1)}, u32[]{:S(2)}, u32[]{:S(2)}) collective-permute-start(bf16[256,256]{1,0:T(8,128)(2,1)S(1)} %get-tuple-element.54), channel_id=1, source_target_pairs={{0,6},{1,7},{2,4},{3,5},{4,2},{5,3},{6,0},{7,1},{8,14},{9,15},{10,... | collective-permute-start | bytes 393224 | tf_op jit(solution)/shard_map/ppermute | solution.py:125
  21.2 19.6 %collective-permute-start.10 = (bf16[512,256]{1,0:T(8,128)(2,1)S(1)}, bf16[512,256]{1,0:T(8,128)(2,1)S(1)}, u32[]{:S(2)}, u32[]{:S(2)}) collective-permute-start(bf16[512,256]{1,0:T(8,128)(2,1)S(1)} %shard_map.96.forward_ref.refs_0_), channel_id=1, source_target_pairs={{0,16},{8,24},{16,0},{24,8},{1,17},{9,25},{17,1},{25,9},{2,18},{10... | collective-permute-start | bytes 786440 | tf_op jit(solution)/shard_map/ppermute | solution.py:125
  22.9 17.9 %collective-permute-start.6 = (bf16[256,256]{1,0:T(8,128)(2,1)S(1)}, bf16[256,256]{1,0:T(8,128)(2,1)S(1)}, u32[]{:S(2)}, u32[]{:S(2)}) collective-permute-start(bf16[256,256]{1,0:T(8,128)(2,1)S(1)} %get-tuple-element.55), channel_id=1, source_target_pairs={{0,7},{1,6},{2,5},{3,4},{4,3},{5,2},{6,1},{7,0},{8,15},{9,14},{10,... | collective-permute-start | bytes 393224 | tf_op jit(solution)/shard_map/ppermute | solution.py:125
  27.4 3.4 %copy-start.2 = (bf16[2048,2048]{1,0:T(8,128)(2,1)S(1)}, bf16[2048,2048]{1,0:T(8,128)(2,1)}, u32[]{:S(2)}) copy-start(bf16[2048,2048]{1,0:T(8,128)(2,1)} %factor_ref.1) | copy-start | bytes 25165828
  31.4 9.4 %collective-permute-start.7 = (bf16[256,256]{1,0:T(8,128)(2,1)S(1)}, bf16[256,256]{1,0:T(8,128)(2,1)S(1)}, u32[]{:S(2)}, u32[]{:S(2)}) collective-permute-start(bf16[256,256]{1,0:T(8,128)(2,1)S(1)} %get-tuple-element.56), channel_id=1, source_target_pairs={{0,1},{1,0},{2,3},{3,2},{4,5},{5,4},{6,7},{7,6},{8,9},{9,8},{10,11... | collective-permute-start | bytes 393224 | tf_op jit(solution)/shard_map/ppermute | solution.py:125
  32.0 8.8 %collective-permute-start.8 = (bf16[256,256]{1,0:T(8,128)(2,1)S(1)}, bf16[256,256]{1,0:T(8,128)(2,1)S(1)}, u32[]{:S(2)}, u32[]{:S(2)}) collective-permute-start(bf16[256,256]{1,0:T(8,128)(2,1)S(1)} %get-tuple-element.57), channel_id=1, source_target_pairs={{0,2},{1,3},{2,0},{3,1},{4,6},{5,7},{6,4},{7,5},{8,10},{9,11},{10,... | collective-permute-start | bytes 393224 | tf_op jit(solution)/shard_map/ppermute | solution.py:125
  32.0 8.8 %collective-permute-start.9 = (bf16[256,256]{1,0:T(8,128)(2,1)S(1)}, bf16[256,256]{1,0:T(8,128)(2,1)S(1)}, u32[]{:S(2)}, u32[]{:S(2)}) collective-permute-start(bf16[256,256]{1,0:T(8,128)(2,1)S(1)} %get-tuple-element.58), channel_id=1, source_target_pairs={{0,3},{1,2},{2,1},{3,0},{4,7},{5,6},{6,5},{7,4},{8,11},{9,10},{10,... | collective-permute-start | bytes 393224 | tf_op jit(solution)/shard_map/ppermute | solution.py:125
  42.1 2.0 %collective-permute-start.11 = (bf16[2,256,512]{2,1,0:T(8,128)(2,1)S(1)}, bf16[2,256,512]{2,1,0:T(8,128)(2,1)S(1)}, u32[]{:S(2)}, u32[]{:S(2)}) collective-permute-start(bf16[2,256,512]{2,1,0:T(8,128)(2,1)S(1)} %shard_map.100), channel_id=1, source_target_pairs={{0,8},{8,0},{16,24},{24,16},{1,9},{9,1},{17,25},{25,17},{2,10},{10... | collective-permute-start | bytes 1572872 | tf_op jit(solution)/shard_map/ppermute | solution.py:125
  42.2 10.4 %copy-start.1 = (bf16[512,2048]{1,0:T(8,128)(2,1)S(1)}, bf16[512,2048]{1,0:T(8,128)(2,1)}, u32[]{:S(2)}) copy-start(bf16[512,2048]{1,0:T(8,128)(2,1)} %inverse_ref.11) | copy-start | bytes 6291460
  44.1 8.4 %collective-permute-start.12 = (bf16[256,512]{1,0:T(8,128)(2,1)S(1)}, bf16[256,512]{1,0:T(8,128)(2,1)S(1)}, u32[]{:S(2)}, u32[]{:S(2)}) collective-permute-start(bf16[256,512]{1,0:T(8,128)(2,1)S(1)} %fusion.1), channel_id=1, source_target_pairs={{0,16},{8,24},{16,0},{24,8},{1,17},{9,25},{17,1},{25,9},{2,18},{10... | collective-permute-start | bytes 786440 | tf_op jit(solution)/shard_map/ppermute | solution.py:125
  53.5 1.6 %collective-permute-start.13 = (bf16[256,512]{1,0:T(8,128)(2,1)S(1)}, bf16[256,512]{1,0:T(8,128)(2,1)S(1)}, u32[]{:S(2)}, u32[]{:S(2)}) collective-permute-start(bf16[256,512]{1,0:T(8,128)(2,1)S(1)} %get-tuple-element.61), channel_id=1, source_target_pairs={{0,8},{8,0},{16,24},{24,16},{1,9},{9,1},{17,25},{25,17},{2,10},{10... | collective-permute-start | bytes 786440 | tf_op jit(solution)/shard_map/ppermute | solution.py:125
  53.6 4.3 %collective-permute-start.15 = (bf16[512,256]{1,0:T(8,128)(2,1)S(1)}, bf16[512,256]{1,0:T(8,128)(2,1)S(1)}, u32[]{:S(2)}, u32[]{:S(2)}) collective-permute-start(bf16[512,256]{1,0:T(8,128)(2,1)S(1)} %shard_map.96.forward_ref.refs_0_), channel_id=1, source_target_pairs={{0,8},{8,0},{16,24},{24,16},{1,9},{9,1},{17,25},{25,17},{2,10},{10... | collective-permute-start | bytes 786440 | tf_op jit(solution)/shard_map/ppermute | solution.py:125
  54.1 3.8 %collective-permute-start.16 = (bf16[512,256]{1,0:T(8,128)(2,1)S(1)}, bf16[512,256]{1,0:T(8,128)(2,1)S(1)}, u32[]{:S(2)}, u32[]{:S(2)}) collective-permute-start(bf16[512,256]{1,0:T(8,128)(2,1)S(1)} %collective-permute-done.10.refs_2_), channel_id=1, source_target_pairs={{0,8},{8,0},{16,24},{24,16},{1,9},{9,1},{17,25},{25,17},{2,10},{10... | collective-permute-start | bytes 786440 | tf_op jit(solution)/shard_map/ppermute | solution.py:125
  55.0 2.9 %copy-start.4 = (bf16[2048,256]{1,0:T(8,128)(2,1)S(1)}, bf16[2048,256]{1,0:T(8,128)(2,1)}, u32[]{:S(2)}) copy-start(bf16[2048,256]{1,0:T(8,128)(2,1)} %rhs_ref.1) | copy-start | bytes 3145732
  55.2 10.6 %collective-permute-start.14 = (bf16[256,512]{1,0:T(8,128)(2,1)S(1)}, bf16[256,512]{1,0:T(8,128)(2,1)S(1)}, u32[]{:S(2)}, u32[]{:S(2)}) collective-permute-start(bf16[256,512]{1,0:T(8,128)(2,1)S(1)} %add_convert_fusion.1), channel_id=1, source_target_pairs={{16,0},{24,8},{17,1},{25,9},{18,2},{26,10},{19,3},{27,11},{20,4},{... | collective-permute-start | bytes 786440 | tf_op jit(solution)/shard_map/ppermute | solution.py:222
  57.4 8.3 %collective-permute-start.17 = (bf16[256,512]{1,0:T(8,128)(2,1)S(1)}, bf16[256,512]{1,0:T(8,128)(2,1)S(1)}, u32[]{:S(2)}, u32[]{:S(2)}) collective-permute-start(bf16[256,512]{1,0:T(8,128)(2,1)S(1)} %shard_map.105), channel_id=1, source_target_pairs={{0,8},{8,0},{16,24},{24,16},{1,9},{9,1},{17,25},{25,17},{2,10},{10... | collective-permute-start | bytes 786440 | tf_op jit(solution)/shard_map/ppermute | solution.py:125
  62.3 31.2 %copy-start.7 = (s32[8]{0:T(128)S(1)}, s32[8]{0:T(128)}, u32[]{:S(2)}) copy-start(s32[8]{0:T(128)} %constant.14.clone) | copy-start | bytes 100
  62.3 32.1 %copy-start.3 = (bf16[384,2048]{1,0:T(8,128)(2,1)S(1)}, bf16[384,2048]{1,0:T(8,128)(2,1)}, u32[]{:S(2)}) copy-start(bf16[384,2048]{1,0:T(8,128)(2,1)} %axle_ref.3) | copy-start | bytes 4718596
  65.9 7.8 %collective-permute-start.18 = (bf16[256,512]{1,0:T(8,128)(2,1)S(1)}, bf16[256,512]{1,0:T(8,128)(2,1)S(1)}, u32[]{:S(2)}, u32[]{:S(2)}) collective-permute-start(bf16[256,512]{1,0:T(8,128)(2,1)S(1)} %add_convert_fusion.refs_0_), channel_id=1, source_target_pairs={{0,1},{1,0},{2,3},{3,2},{4,5},{5,4},{6,7},{7,6},{8,9},{9,8},{10,11... | collective-permute-start | bytes 786440 | tf_op jit(solution)/shard_map/ppermute | solution.py:125
  66.5 8.3 %collective-permute-start.19 = (bf16[256,512]{1,0:T(8,128)(2,1)S(1)}, bf16[256,512]{1,0:T(8,128)(2,1)S(1)}, u32[]{:S(2)}, u32[]{:S(2)}) collective-permute-start(bf16[256,512]{1,0:T(8,128)(2,1)S(1)} %add_convert_fusion.refs_0_), channel_id=1, source_target_pairs={{0,2},{1,3},{2,0},{3,1},{4,6},{5,7},{6,4},{7,5},{8,10},{9,11},{10,... | collective-permute-start | bytes 786440 | tf_op jit(solution)/shard_map/ppermute | solution.py:125
  67.3 13.4 %collective-permute-start.20 = (bf16[256,512]{1,0:T(8,128)(2,1)S(1)}, bf16[256,512]{1,0:T(8,128)(2,1)S(1)}, u32[]{:S(2)}, u32[]{:S(2)}) collective-permute-start(bf16[256,512]{1,0:T(8,128)(2,1)S(1)} %add_convert_fusion.refs_0_), channel_id=1, source_target_pairs={{0,6},{1,7},{2,4},{3,5},{4,2},{5,3},{6,0},{7,1},{8,14},{9,15},{10,... | collective-permute-start | bytes 786440 | tf_op jit(solution)/shard_map/ppermute | solution.py:125
  74.7 6.6 %collective-permute-start.21 = (bf16[256,512]{1,0:T(8,128)(2,1)S(1)}, bf16[256,512]{1,0:T(8,128)(2,1)S(1)}, u32[]{:S(2)}, u32[]{:S(2)}) collective-permute-start(bf16[256,512]{1,0:T(8,128)(2,1)S(1)} %collective-permute-done.19.refs_2_), channel_id=1, source_target_pairs={{0,1},{1,0},{2,3},{3,2},{4,5},{5,4},{6,7},{7,6},{8,9},{9,8},{10,11... | collective-permute-start | bytes 786440 | tf_op jit(solution)/shard_map/ppermute | solution.py:125
  77.0 7.7 %collective-permute-start.23 = (bf16[256,512]{1,0:T(8,128)(2,1)S(1)}, bf16[256,512]{1,0:T(8,128)(2,1)S(1)}, u32[]{:S(2)}, u32[]{:S(2)}) collective-permute-start(bf16[256,512]{1,0:T(8,128)(2,1)S(1)} %collective-permute-done.19.refs_2_), channel_id=1, source_target_pairs={{2,4},{3,5},{4,2},{5,3},{10,12},{11,13},{12,10},{13,11},{18,20},{1... | collective-permute-start | bytes 786440 | tf_op jit(solution)/shard_map/ppermute | solution.py:246
  81.3 8.3 %collective-permute-start.24 = (bf16[256,512]{1,0:T(8,128)(2,1)S(1)}, bf16[256,512]{1,0:T(8,128)(2,1)S(1)}, u32[]{:S(2)}, u32[]{:S(2)}) collective-permute-start(bf16[256,512]{1,0:T(8,128)(2,1)S(1)} %collective-permute-done.20.refs_4_), channel_id=1, source_target_pairs={{2,0},{3,1},{4,6},{5,7},{10,8},{11,9},{12,14},{13,15},{18,16},{19,... | collective-permute-start | bytes 786440 | tf_op jit(solution)/shard_map/ppermute | solution.py:247
  82.6 11.8 %collective-permute-start.22 = (bf16[256,512]{1,0:T(8,128)(2,1)S(1)}, bf16[256,512]{1,0:T(8,128)(2,1)}, u32[]{:S(2)}, u32[]{:S(2)}) collective-permute-start(bf16[256,512]{1,0:T(8,128)(2,1)S(1)} %collective-permute-done.20.refs_4_), channel_id=1, source_target_pairs={{0,1},{1,0},{2,3},{3,2},{4,5},{5,4},{6,7},{7,6},{8,9},{9,8},{10,11... | collective-permute-start | bytes 786440 | tf_op jit(solution)/shard_map/ppermute | solution.py:125
  84.7 11.6 %collective-permute-start.25 = (bf16[256,512]{1,0:T(8,128)(2,1)S(1)}, bf16[256,512]{1,0:T(8,128)(2,1)}, u32[]{:S(2)}, u32[]{:S(2)}) collective-permute-start(bf16[256,512]{1,0:T(8,128)(2,1)S(1)} %collective-permute-done.23.refs_6_), channel_id=1, source_target_pairs={{2,3},{3,2},{4,5},{5,4},{10,11},{11,10},{12,13},{13,12},{18,19},{1... | collective-permute-start | bytes 786440 | tf_op jit(solution)/shard_map/ppermute | solution.py:249
  89.6 8.4 %collective-permute-start.26 = (bf16[256,512]{1,0:T(8,128)(2,1)S(1)}, bf16[256,512]{1,0:T(8,128)(2,1)}, u32[]{:S(2)}, u32[]{:S(2)}) collective-permute-start(bf16[256,512]{1,0:T(8,128)(2,1)S(1)} %collective-permute-done.24.refs_7_), channel_id=1, source_target_pairs={{0,1},{1,0},{6,7},{7,6},{8,9},{9,8},{14,15},{15,14},{16,17},{17,16... | collective-permute-start | bytes 786440 | tf_op jit(solution)/shard_map/ppermute | solution.py:250
  (3 other events, 3.8 us)
